TPU v7x, 32 devices: a whole 2x2x4 slice. The times are simulated.
32 devices in a mesh: dp: 8 (over y, x, core), tensor: 4 (over z).
Axes of the slice: x: 2, y: 2, z: 4, core: 2. Of those that a mesh axis runs over, the one named last changes fastest.
Arguments:
- hidden_in: bfloat16 [4096, 2048], P(('dp', 'tensor')), may hold values from -6 to 6
- teacher: bfloat16 [4096, 2048], P(('dp', 'tensor')), may hold values from -6 to 6
- lengths: int32 [8], replicated, may hold values from 128 to 512, as said below
- routes: int32 [4096, 8], P('dp'), may hold values from 0 to 15, all different within a row; in each aligned block of 128 rows (0 to 127, 128 to 255, ...) at most 68 rows name the same one
- attn_norm_gain: bfloat16 [2048], replicated, may hold values from 0.5 to 1.5
- ffn_norm_gain: bfloat16 [2048], replicated, may hold values from 0.5 to 1.5
- q_weight: bfloat16 [2048, 2048], P('dp', 'tensor'), may hold values from -0.125 to 0.125
- k_weight: bfloat16 [2048, 2048], P('dp', 'tensor'), may hold values from -0.125 to 0.125
- v_weight: bfloat16 [2048, 2048], P('dp', 'tensor'), may hold values from -0.125 to 0.125
- q_gain: bfloat16 [16, 128], P('tensor', 'dp'), may hold values from 0.5 to 1.5
- k_gain: bfloat16 [16, 128], P('tensor', 'dp'), may hold values from 0.5 to 1.5
- o_weight: bfloat16 [2048, 2048], P('tensor', 'dp'), may hold values from -2 to 2
- router_weight: bfloat16 [2048, 16], replicated, may hold values from -0.0625 to 0.0625
- gate_weight: bfloat16 [16, 2048, 1024], P(None, 'dp', 'tensor'), may hold values from -0.125 to 0.125
- up_weight: bfloat16 [16, 2048, 1024], P(None, 'dp', 'tensor'), may hold values from -0.125 to 0.125
- down_weight: bfloat16 [16, 1024, 2048], P(None, 'tensor', 'dp'), may hold values from -3 to 3
Outputs:
- loss_parts: float32 [8], P('dp')
- grad_in: float32 [4096, 2048], P(('dp', 'tensor'))
- grad_attn_gain: float32 [2048], P(('dp', 'tensor'))
- grad_ffn_gain: float32 [2048], P(('dp', 'tensor'))
- grad_q: float32 [2048, 2048], P('dp', 'tensor')
- grad_k: float32 [2048, 2048], P('dp', 'tensor')
- grad_v: float32 [2048, 2048], P('dp', 'tensor')
- grad_q_gain: float32 [16, 128], P('tensor', 'dp')
- grad_k_gain: float32 [16, 128], P('tensor', 'dp')
- grad_o: float32 [2048, 2048], P('tensor', 'dp')
- grad_router: float32 [2048, 16], P(('dp', 'tensor'))
- grad_gate: float32 [16, 2048, 1024], P(None, 'dp', 'tensor')
- grad_up: float32 [16, 2048, 1024], P(None, 'dp', 'tensor')
- grad_down: float32 [16, 1024, 2048], P(None, 'tensor', 'dp')
Inputs may be any that keep to these rules, and one draw needn't show every extreme that they name: `lengths`: each sequence has at least 128 valid tokens; in every draw at least one sequence is valid to its end. `routes`: within the 128 rows of one device (aligned blocks), no expert is named by more than 68 rows, and that bound is reached.
All inputs are finite; a program needn't handle non-finite values.
Results may differ from a plain program's by a relative error of at most 0.022.
Values may be sent and summed in bfloat16 or wider, within the bound.
A program may use at most 320 MiB of HBM per device.

v0:
```python
import math

import jax
import jax.numpy as jnp
from jax import lax
from jax.sharding import PartitionSpec as P

HD = 128
TOK_DEV = 128
CAP = 68


EPSILON = 1e-05
THETA = 10000.0
HIGHEST = lax.Precision.HIGHEST


def inverse_rms(value):
    return lax.rsqrt(jnp.mean(value * value, axis=-1, keepdims=True) + EPSILON)


def rotate(value, cosine, sinus_table, direction):
    middle_index = value.shape[-1] // 2
    leading = value[..., :middle_index]
    trailing = value[..., middle_index:]
    return jnp.concatenate(
        [
            leading * cosine - direction * trailing * sinus_table,
            trailing * cosine + direction * leading * sinus_table,
        ],
        axis=-1,
    )


def norm_backward(grad_norm, unit_rows, inverse_rows, gain_row):
    scaled = grad_norm * gain_row
    return inverse_rows * (
        scaled - unit_rows * jnp.mean(scaled * unit_rows, axis=-1, keepdims=True)
    )


def fetch_attention(q_weight, k_weight, v_weight, o_weight, q_gain, k_gain):
    return (
        lax.all_gather(q_weight, "dp", axis=0, tiled=True),
        lax.all_gather(k_weight, "dp", axis=0, tiled=True),
        lax.all_gather(v_weight, "dp", axis=0, tiled=True),
        lax.all_gather(o_weight, "dp", axis=1, tiled=True),
        lax.all_gather(q_gain, "dp", axis=1, tiled=True),
        lax.all_gather(k_gain, "dp", axis=1, tiled=True),
    )


def fetch_experts(gate_weight, up_weight, down_weight):
    return (
        lax.all_gather(gate_weight, "dp", axis=1, tiled=True),
        lax.all_gather(up_weight, "dp", axis=1, tiled=True),
        lax.all_gather(down_weight, "dp", axis=2, tiled=True),
    )


def per_device(
    hidden_in,
    teacher,
    lengths,
    routes,
    attn_norm_gain,
    ffn_norm_gain,
    q_weight,
    k_weight,
    v_weight,
    q_gain,
    k_gain,
    o_weight,
    router_weight,
    gate_weight,
    up_weight,
    down_weight,
):
    dp_count = lax.axis_size("dp")
    tp_count = lax.axis_size("tensor")
    group_index = lax.axis_index("dp")
    member = lax.axis_index("tensor")
    row_count, model_width = hidden_in.shape
    seq_len = row_count * tp_count
    all_tokens = seq_len * dp_count
    length = lengths[group_index]
    total_count = jnp.sum(lengths).astype(jnp.float32)
    attn_gain = attn_norm_gain.astype(jnp.float32)
    ffn_gain = ffn_norm_gain.astype(jnp.float32)
    root_size = math.sqrt(HD)
    q_full, k_full, v_full, o_full, qgain_full, kgain_full = fetch_attention(
        q_weight, k_weight, v_weight, o_weight, q_gain, k_gain
    )
    local_heads = q_full.shape[1] // HD
    hidden_all = lax.all_gather(hidden_in, "tensor", axis=0, tiled=True).astype(jnp.float32)
    inverse_one = inverse_rms(hidden_all)
    unit_one = hidden_all * inverse_one
    normed = (unit_one * attn_gain).astype(jnp.bfloat16)
    query_raw = jnp.dot(normed, q_full, preferred_element_type=jnp.float32)
    key_raw = jnp.dot(normed, k_full, preferred_element_type=jnp.float32)
    value_low = jnp.dot(normed, v_full, preferred_element_type=jnp.float32).astype(jnp.bfloat16)
    query_sq, key_sq = lax.psum(
        (jnp.sum(query_raw * query_raw, axis=1), jnp.sum(key_raw * key_raw, axis=1)), "tensor"
    )
    query_inv = lax.rsqrt(query_sq / model_width + EPSILON)[:, None]
    key_inv = lax.rsqrt(key_sq / model_width + EPSILON)[:, None]
    query_unit = query_raw * query_inv
    key_unit = key_raw * key_inv
    query_gain = qgain_full.astype(jnp.float32).reshape(-1)
    key_gain = kgain_full.astype(jnp.float32).reshape(-1)
    positions = jnp.arange(seq_len)
    frequency = THETA ** (-jnp.arange(HD // 2).astype(jnp.float32) / (HD // 2))
    angles = positions.astype(jnp.float32)[:, None] * frequency[None, :]
    cosine = jnp.cos(angles)[:, None, :]
    sinus_table = jnp.sin(angles)[:, None, :]
    queries = rotate(
        (query_unit * query_gain).reshape(seq_len, local_heads, HD), cosine, sinus_table, 1.0
    ).astype(jnp.bfloat16)
    key_rows = rotate(
        (key_unit * key_gain).reshape(seq_len, local_heads, HD), cosine, sinus_table, 1.0
    ).astype(jnp.bfloat16)
    value_rows = value_low.reshape(seq_len, local_heads, HD)
    block_rows = min(512, seq_len)
    starts = jnp.arange(seq_len // block_rows) * block_rows

    def block_scores(start):
        query_block = lax.dynamic_slice_in_dim(queries, start, block_rows, 0)
        scores = (
            jnp.einsum("qhd,khd->hqk", query_block, key_rows, preferred_element_type=jnp.float32)
            / root_size
        )
        query_pos = start + jnp.arange(block_rows)
        allowed = (positions[None, :] <= query_pos[:, None]) & (positions[None, :] < length)
        return (query_block, jnp.where(allowed[None], scores, -1e30))

    def attend(start):
        unused_block, scores = block_scores(start)
        row_top = jnp.max(scores, axis=-1, keepdims=True)
        exponent = jnp.exp(scores - row_top)
        row_total = jnp.sum(exponent, axis=-1, keepdims=True)
        weights = (exponent / row_total).astype(jnp.bfloat16)
        mixed_block = jnp.einsum(
            "hqk,khd->qhd", weights, value_rows, preferred_element_type=jnp.float32
        )
        return (mixed_block.astype(jnp.bfloat16), (row_top + jnp.log(row_total))[..., 0])

    mixed_blocks, log_totals = lax.map(attend, starts)
    mixed = mixed_blocks.reshape(seq_len, local_heads * HD)
    attn_own = lax.psum_scatter(
        jnp.dot(mixed, o_full, preferred_element_type=jnp.float32).astype(jnp.bfloat16),
        "tensor",
        scatter_dimension=0,
        tiled=True,
    ).astype(jnp.float32)
    middle = hidden_in.astype(jnp.float32) + attn_own
    inverse_two = inverse_rms(middle)
    unit_two = middle * inverse_two
    ffn_own = (unit_two * ffn_gain).astype(jnp.bfloat16)
    gate_full, up_full, down_full = fetch_experts(gate_weight, up_weight, down_weight)
    ffn_all = lax.all_gather(ffn_own, "tensor", axis=0, tiled=True)
    expert_count = router_weight.shape[1]
    route_width = routes.shape[1]
    gate_probs = jax.nn.softmax(
        jnp.dot(ffn_all, router_weight, preferred_element_type=jnp.float32), axis=-1
    )
    picked = routes[:, :, None] == jnp.arange(expert_count)[None, None, :]
    route_gates = jnp.sum(jnp.where(picked, gate_probs[:, None, :], 0.0), axis=-1)
    block_count = seq_len // TOK_DEV
    per_expert = block_count * CAP
    picked_ints = picked.reshape(block_count, TOK_DEV * route_width, expert_count).astype(jnp.int32)
    slot_ranks = jnp.sum((jnp.cumsum(picked_ints, axis=1) - 1) * picked_ints, axis=-1).reshape(
        seq_len, route_width
    )
    block_ids = (positions // TOK_DEV)[:, None]
    slot_ids = (routes * per_expert + block_ids * CAP + slot_ranks).reshape(-1)
    slot_total = expert_count * per_expert
    token_ids = jnp.repeat(positions, route_width)
    group_width = 4
    turn_count = expert_count // group_width
    sources = (
        jnp.full((slot_total,), seq_len, jnp.int32)
        .at[slot_ids]
        .set(token_ids)
        .reshape(turn_count, group_width, per_expert)
    )
    slot_gates = (
        jnp.zeros((slot_total,), jnp.float32)
        .at[slot_ids]
        .set(route_gates.reshape(-1))
        .reshape(turn_count, group_width, per_expert, 1)
    )
    ffn_padded = jnp.concatenate([ffn_all, jnp.zeros((1, model_width), jnp.bfloat16)], axis=0)
    expert_running = jnp.zeros((seq_len + 1, model_width), jnp.float32)
    kept_values = []
    for turn_index in range(turn_count):
        lower = turn_index * group_width
        upper = lower + group_width
        expert_inputs = ffn_padded[sources[turn_index]]
        gate_value = jnp.einsum(
            "gpd,gdf->gpf",
            expert_inputs,
            gate_full[lower:upper],
            preferred_element_type=jnp.float32,
        )
        up_value = jnp.einsum(
            "gpd,gdf->gpf", expert_inputs, up_full[lower:upper], preferred_element_type=jnp.float32
        )
        active = (slot_gates[turn_index] * jax.nn.silu(gate_value) * up_value).astype(jnp.bfloat16)
        expert_outputs = jnp.einsum(
            "gpf,gfd->gpd", active, down_full[lower:upper], preferred_element_type=jnp.float32
        )
        expert_running = expert_running.at[sources[turn_index].reshape(-1)].add(
            expert_outputs.reshape(-1, model_width)
        )
        kept_values.append((gate_value, up_value, active))
    expert_own = lax.psum_scatter(
        expert_running[:seq_len].astype(jnp.bfloat16), "tensor", scatter_dimension=0, tiled=True
    ).astype(jnp.float32)
    output = middle + expert_own
    own_positions = member * row_count + jnp.arange(row_count)
    valid_rows = (own_positions < length)[:, None]
    mismatch = output - teacher.astype(jnp.float32)
    loss_own = jnp.sum(jnp.where(valid_rows, mismatch * mismatch, 0.0)) / (
        2.0 * model_width * total_count
    )
    grad_output = jnp.where(valid_rows, mismatch * (all_tokens / total_count), 0.0)
    grad_rows = lax.all_gather(grad_output.astype(jnp.bfloat16), "tensor", axis=0, tiled=True)
    gate_full, up_full, down_full = fetch_experts(gate_weight, up_weight, down_weight)
    grad_padded = jnp.concatenate([grad_rows, jnp.zeros((1, model_width), jnp.bfloat16)], axis=0)
    ffn_grad_running = jnp.zeros((seq_len + 1, model_width), jnp.float32)
    gate_grads = []
    up_grads = []
    down_grads = []
    slot_grads = []
    for turn_index in range(turn_count):
        gate_value, up_value, active = kept_values[turn_index]
        lower = turn_index * group_width
        upper = lower + group_width
        source_rows = sources[turn_index]
        expert_inputs = ffn_padded[source_rows]
        incoming = grad_padded[source_rows]
        grad_active = jnp.einsum(
            "gpd,gfd->gpf", incoming, down_full[lower:upper], preferred_element_type=jnp.float32
        )
        down_turn = jnp.einsum("gpf,gpd->gfd", active, incoming, preferred_element_type=jnp.float32)
        sigmoid_value = jax.nn.sigmoid(gate_value)
        silu_value = gate_value * sigmoid_value
        slot_grads.append(jnp.sum(grad_active * silu_value * up_value, axis=-1))
        grad_inner = grad_active * slot_gates[turn_index]
        grad_gate_value = (
            grad_inner * up_value * sigmoid_value * (1.0 + gate_value * (1.0 - sigmoid_value))
        ).astype(jnp.bfloat16)
        grad_up_value = (grad_inner * silu_value).astype(jnp.bfloat16)
        gate_turn = jnp.einsum(
            "gpd,gpf->gdf", expert_inputs, grad_gate_value, preferred_element_type=jnp.float32
        )
        up_turn = jnp.einsum(
            "gpd,gpf->gdf", expert_inputs, grad_up_value, preferred_element_type=jnp.float32
        )
        gate_grads.append(gate_turn)
        up_grads.append(up_turn)
        down_grads.append(down_turn)
        grad_inputs = jnp.einsum(
            "gpf,gdf->gpd",
            grad_gate_value,
            gate_full[lower:upper],
            preferred_element_type=jnp.float32,
        )
        grad_inputs = grad_inputs + jnp.einsum(
            "gpf,gdf->gpd", grad_up_value, up_full[lower:upper], preferred_element_type=jnp.float32
        )
        ffn_grad_running = ffn_grad_running.at[source_rows.reshape(-1)].add(
            grad_inputs.reshape(-1, model_width)
        )
    slot_grad_all = jnp.concatenate([entry.reshape(-1) for entry in slot_grads])
    route_grads = slot_grad_all[slot_ids].reshape(seq_len, route_width)
    grad_probs = jnp.sum(jnp.where(picked, route_grads[:, :, None], 0.0), axis=1)
    grad_logits = gate_probs * (
        grad_probs - jnp.sum(grad_probs * gate_probs, axis=-1, keepdims=True)
    )
    router_float = router_weight.astype(jnp.float32)
    ffn_grad_part = ffn_grad_running[:seq_len] + jnp.einsum(
        "se,de->sd", grad_logits, router_float, precision=HIGHEST
    )
    router_part = jnp.einsum(
        "sd,se->de", ffn_all, grad_logits, precision=HIGHEST, preferred_element_type=jnp.float32
    )
    ffn_grad_own = lax.psum_scatter(
        ffn_grad_part.astype(jnp.bfloat16), "tensor", scatter_dimension=0, tiled=True
    ).astype(jnp.float32)
    ffn_gain_part = jnp.sum(ffn_grad_own * unit_two, axis=0)
    grad_middle = grad_output + norm_backward(ffn_grad_own, unit_two, inverse_two, ffn_gain)
    attn_grad_rows = lax.all_gather(grad_middle.astype(jnp.bfloat16), "tensor", axis=0, tiled=True)
    q_full, k_full, v_full, o_full, qgain_full, kgain_full = fetch_attention(
        q_weight, k_weight, v_weight, o_weight, q_gain, k_gain
    )
    grad_o = jnp.einsum("sa,sb->ab", mixed, attn_grad_rows, preferred_element_type=jnp.float32)
    grad_mixed = (
        jnp.einsum("sb,ab->sa", attn_grad_rows, o_full, preferred_element_type=jnp.float32)
        .astype(jnp.bfloat16)
        .reshape(seq_len, local_heads, HD)
    )

    def attend_back(carry, inputs):
        key_running, value_running = carry
        start, log_total = inputs
        query_block, scores = block_scores(start)
        probs_float = jnp.exp(scores - log_total[..., None])
        probs_low = probs_float.astype(jnp.bfloat16)
        grad_block = lax.dynamic_slice_in_dim(grad_mixed, start, block_rows, 0)
        value_running = value_running + jnp.einsum(
            "hqk,qhd->khd", probs_low, grad_block, preferred_element_type=jnp.float32
        )
        grad_weights = jnp.einsum(
            "qhd,khd->hqk", grad_block, value_rows, preferred_element_type=jnp.float32
        )
        grad_scores = (
            probs_float
            * (grad_weights - jnp.sum(grad_weights * probs_float, axis=-1, keepdims=True))
        ).astype(jnp.bfloat16)
        query_grad_block = (
            jnp.einsum("hqk,khd->qhd", grad_scores, key_rows, preferred_element_type=jnp.float32)
            / root_size
        )
        key_running = (
            key_running
            + jnp.einsum(
                "hqk,qhd->khd", grad_scores, query_block, preferred_element_type=jnp.float32
            )
            / root_size
        )
        return ((key_running, value_running), query_grad_block)

    zero_heads = jnp.zeros((seq_len, local_heads, HD), jnp.float32)
    (key_grad_rot, value_grad), query_grad_blocks = lax.scan(
        attend_back, (zero_heads, zero_heads), (starts, log_totals)
    )
    query_grad = rotate(
        query_grad_blocks.reshape(seq_len, local_heads, HD), cosine, sinus_table, -1.0
    ).reshape(seq_len, local_heads * HD)
    key_grad = rotate(key_grad_rot, cosine, sinus_table, -1.0).reshape(seq_len, local_heads * HD)
    query_scaled = query_grad * query_gain
    key_scaled = key_grad * key_gain
    qgain_part = jnp.sum(query_grad * query_unit, axis=0)
    kgain_part = jnp.sum(key_grad * key_unit, axis=0)
    query_dot, key_dot, loss_group = lax.psum(
        (
            jnp.sum(query_scaled * query_unit, axis=1),
            jnp.sum(key_scaled * key_unit, axis=1),
            loss_own,
        ),
        "tensor",
    )
    query_raw_grad = (
        query_inv * (query_scaled - query_unit * (query_dot / model_width)[:, None])
    ).astype(jnp.bfloat16)
    key_raw_grad = (key_inv * (key_scaled - key_unit * (key_dot / model_width)[:, None])).astype(
        jnp.bfloat16
    )
    value_raw_grad = value_grad.reshape(seq_len, local_heads * HD).astype(jnp.bfloat16)
    grad_q = jnp.einsum("sd,sa->da", normed, query_raw_grad, preferred_element_type=jnp.float32)
    grad_k = jnp.einsum("sd,sa->da", normed, key_raw_grad, preferred_element_type=jnp.float32)
    grad_v = jnp.einsum("sd,sa->da", normed, value_raw_grad, preferred_element_type=jnp.float32)
    normed_grad = jnp.einsum(
        "sa,da->sd", query_raw_grad, q_full, preferred_element_type=jnp.float32
    )
    normed_grad = normed_grad + jnp.einsum(
        "sa,da->sd", key_raw_grad, k_full, preferred_element_type=jnp.float32
    )
    normed_grad = normed_grad + jnp.einsum(
        "sa,da->sd", value_raw_grad, v_full, preferred_element_type=jnp.float32
    )
    attn_gain_part = jnp.sum(normed_grad * unit_one, axis=0)
    input_part = norm_backward(normed_grad, unit_one, inverse_one, attn_gain)
    split_width = model_width // (dp_count * tp_count)
    input_own, attn_gain_share, ffn_gain_share, router_share = (
        lax.psum_scatter(
            input_part.astype(jnp.bfloat16), "tensor", scatter_dimension=0, tiled=True
        ).astype(jnp.float32),
        lax.psum_scatter(
            attn_gain_part.reshape(dp_count, tp_count, split_width).astype(jnp.bfloat16),
            "tensor",
            scatter_dimension=1,
            tiled=True,
        ).astype(jnp.float32),
        lax.psum_scatter(
            ffn_gain_part.reshape(dp_count, tp_count, split_width).astype(jnp.bfloat16),
            "tensor",
            scatter_dimension=1,
            tiled=True,
        ).astype(jnp.float32),
        lax.psum_scatter(
            router_part.reshape(dp_count, tp_count, split_width, expert_count).astype(jnp.bfloat16),
            "tensor",
            scatter_dimension=1,
            tiled=True,
        ).astype(jnp.float32),
    )
    grad_in = grad_middle + input_own
    (
        grad_q,
        grad_k,
        grad_v,
        grad_o,
        grad_qgain,
        grad_kgain,
        attn_gain_sum,
        ffn_gain_sum,
        router_sum,
    ) = (
        lax.psum_scatter(grad_q.astype(jnp.bfloat16), "dp", scatter_dimension=0, tiled=True).astype(
            jnp.float32
        ),
        lax.psum_scatter(grad_k.astype(jnp.bfloat16), "dp", scatter_dimension=0, tiled=True).astype(
            jnp.float32
        ),
        lax.psum_scatter(grad_v.astype(jnp.bfloat16), "dp", scatter_dimension=0, tiled=True).astype(
            jnp.float32
        ),
        lax.psum_scatter(grad_o.astype(jnp.bfloat16), "dp", scatter_dimension=1, tiled=True).astype(
            jnp.float32
        ),
        lax.psum_scatter(
            qgain_part.reshape(local_heads, HD).astype(jnp.bfloat16),
            "dp",
            scatter_dimension=1,
            tiled=True,
        ).astype(jnp.float32),
        lax.psum_scatter(
            kgain_part.reshape(local_heads, HD).astype(jnp.bfloat16),
            "dp",
            scatter_dimension=1,
            tiled=True,
        ).astype(jnp.float32),
        lax.psum_scatter(
            attn_gain_share.astype(jnp.bfloat16), "dp", scatter_dimension=0, tiled=True
        ).astype(jnp.float32),
        lax.psum_scatter(
            ffn_gain_share.astype(jnp.bfloat16), "dp", scatter_dimension=0, tiled=True
        ).astype(jnp.float32),
        lax.psum_scatter(
            router_share.astype(jnp.bfloat16), "dp", scatter_dimension=0, tiled=True
        ).astype(jnp.float32),
    )
    grad_gate, grad_up, grad_down = (
        lax.psum_scatter(
            jnp.concatenate(gate_grads, axis=0).astype(jnp.bfloat16),
            "dp",
            scatter_dimension=1,
            tiled=True,
        ).astype(jnp.float32),
        lax.psum_scatter(
            jnp.concatenate(up_grads, axis=0).astype(jnp.bfloat16),
            "dp",
            scatter_dimension=1,
            tiled=True,
        ).astype(jnp.float32),
        lax.psum_scatter(
            jnp.concatenate(down_grads, axis=0).astype(jnp.bfloat16),
            "dp",
            scatter_dimension=2,
            tiled=True,
        ).astype(jnp.float32),
    )
    return (
        loss_group.reshape(1),
        grad_in,
        attn_gain_sum.reshape(-1),
        ffn_gain_sum.reshape(-1),
        grad_q,
        grad_k,
        grad_v,
        grad_qgain,
        grad_kgain,
        grad_o,
        router_sum.reshape(-1, expert_count),
        grad_gate,
        grad_up,
        grad_down,
    )


def solution(mesh):
    placed = (
        P(("dp", "tensor"), None),
        P(("dp", "tensor"), None),
        P(),
        P("dp", None),
        P(),
        P(),
        P("dp", "tensor"),
        P("dp", "tensor"),
        P("dp", "tensor"),
        P("tensor", "dp"),
        P("tensor", "dp"),
        P("tensor", "dp"),
        P(),
        P(None, "dp", "tensor"),
        P(None, "dp", "tensor"),
        P(None, "tensor", "dp"),
    )
    return jax.shard_map(
        per_device,
        mesh=mesh,
        in_specs=placed,
        out_specs=(
            P("dp"),
            P(("dp", "tensor"), None),
            P(("dp", "tensor")),
            P(("dp", "tensor")),
            P("dp", "tensor"),
            P("dp", "tensor"),
            P("dp", "tensor"),
            P("tensor", "dp"),
            P("tensor", "dp"),
            P("tensor", "dp"),
            P(("dp", "tensor"), None),
            P(None, "dp", "tensor"),
            P(None, "dp", "tensor"),
            P(None, "tensor", "dp"),
        ),
        check_vma=False,
    )
```

profile of v0, /device:TPU:0, one launch (start us, length us, event | category | flops | bytes accessed | tf_op | source)
XLA Modules:
  0.0 1858.6 jit_solution(18430735883210695314)
XLA Ops:
  60.4 26.4 %all-gather.18.cloned.1.call-done = bf16[2048,512]{1,0:T(8,128)(2,1)} async-done(((bf16[256,512]{1,0:T(8,128)(2,1)}), bf16[2048,512]{1,0:T(8,128)(2,1)}) %all-gather.18.cloned.1.call-update) | async-done | bytes 2097168 | tf_op jit(solution)/shard_map/all_gather | solution.py:44
  90.4 26.2 %all-gather.20.cloned.1.call-done = bf16[2048,512]{1,0:T(8,128)(2,1)} async-done(((bf16[256,512]{1,0:T(8,128)(2,1)}), bf16[2048,512]{1,0:T(8,128)(2,1)}) %all-gather.20.cloned.1.call-update) | async-done | bytes 2097168 | tf_op jit(solution)/shard_map/all_gather | solution.py:45
  180.6 43.9 %reduce-scatter.22.cloned.1.call-done = bf16[128,2048]{1,0:T(8,128)(2,1)} async-done(((bf16[512,2048]{1,0:T(8,128)(2,1)}), bf16[128,2048]{1,0:T(8,128)(2,1)}) %reduce-scatter.22.cloned.1.call-update) | async-done | bytes 524304 | tf_op jit(solution)/shard_map/reduce_scatter | solution.py:149
  319.6 44.8 %all-gather.26.cloned.1.call-done = bf16[16,2048,256]{2,1,0:T(8,128)(2,1)} async-done(((bf16[16,256,256]{2,1,0:T(8,128)(2,1)}), bf16[16,2048,256]{2,1,0:T(8,128)(2,1)}) %all-gather.26.cloned.1.call-update) | async-done | bytes 16777232 | tf_op jit(solution)/shard_map/all_gather | solution.py:55
  369.3 87.1 %all-gather.28.cloned.1.call-done = bf16[16,2048,256]{2,1,0:T(8,128)(2,1)} async-done(((bf16[16,256,256]{2,1,0:T(8,128)(2,1)}), bf16[16,2048,256]{2,1,0:T(8,128)(2,1)}) %all-gather.28.cloned.1.call-update) | async-done | bytes 16777232 | tf_op jit(solution)/shard_map/all_gather | solution.py:56
  462.3 89.1 %all-gather.30.cloned.1.call-done = bf16[16,256,2048]{2,1,0:T(8,128)(2,1)} async-done(((bf16[16,256,256]{2,1,0:T(8,128)(2,1)}), bf16[16,256,2048]{2,1,0:T(8,128)(2,1)}) %all-gather.30.cloned.1.call-update) | async-done | bytes 16777232 | tf_op jit(solution)/shard_map/all_gather | solution.py:57
  558.4 23.5 %scatter_custom_fusion.2 = f32[513,2048]{1,0:T(8,128)} fusion(s32[1088]{0:T(1024)S(1)} %get-tuple-element.124, f32[1088,2048]{1,0:T(8,128)} %bitcast.236, f32[]{:T(128)} %constant.74.clone.1), kind=kCustom, calls=%fused_computation.115 | custom fusion | flops 2228224 | bytes 4203008 | tf_op jit(solution)/shard_map/scatter-add | solution.py:212
  599.1 25.6 %scatter_fusion = f32[513,2048]{1,0:T(8,128)} fusion(f32[513,2048]{1,0:T(8,128)} %scatter_custom_fusion.2, s32[1088]{0:T(1024)S(1)} %get-tuple-element.125, f32[1088,2048]{1,0:T(8,128)} %bitcast.221), kind=kCustom, calls=%fused_computation.12 | custom fusion | flops 2228224 | bytes 26743040 | tf_op jit(solution)/shard_map/scatter-add | solution.py:212
  643.3 25.4 %scatter_fusion.1 = f32[513,2048]{1,0:T(8,128)} fusion(f32[513,2048]{1,0:T(8,128)} %scatter_fusion, s32[1088]{0:T(1024)S(1)} %get-tuple-element.126, f32[1088,2048]{1,0:T(8,128)} %bitcast.222), kind=kCustom, calls=%fused_computation.13 | custom fusion | flops 2228224 | bytes 26743040 | tf_op jit(solution)/shard_map/scatter-add | solution.py:212
  686.7 25.4 %scatter_fusion.2 = f32[513,2048]{1,0:T(8,128)} fusion(f32[513,2048]{1,0:T(8,128)} %scatter_fusion.1, s32[1088]{0:T(1024)S(1)} %copy-done.81, f32[1088,2048]{1,0:T(8,128)} %bitcast.220), kind=kCustom, calls=%fused_computation.14 | custom fusion | flops 2228224 | bytes 26743040 | tf_op jit(solution)/shard_map/scatter-add | solution.py:212
  718.2 42.0 %reduce-scatter.24.cloned.1.call-done = bf16[128,2048]{1,0:T(8,128)(2,1)} async-done(((bf16[512,2048]{1,0:T(8,128)(2,1)}), bf16[128,2048]{1,0:T(8,128)(2,1)}) %reduce-scatter.24.cloned.1.call-update) | async-done | bytes 524304 | tf_op jit(solution)/shard_map/reduce_scatter | solution.py:216
  762.5 45.3 %all-gather.32.cloned.1.call-done = bf16[512,2048]{1,0:T(8,128)(2,1)} async-done(((bf16[128,2048]{1,0:T(8,128)(2,1)}), bf16[512,2048]{1,0:T(8,128)(2,1)}) %all-gather.32.cloned.1.call-update) | async-done | bytes 2097168 | tf_op jit(solution)/shard_map/all_gather | solution.py:227
  930.8 25.6 %scatter_fusion.3 = f32[513,2048]{1,0:T(8,128)} fusion(f32[513,2048]{1,0:T(8,128)} %scatter_custom_fusion.6, s32[1088]{0:T(1024)S(1)} %copy-done.86, f32[1088,2048]{1,0:T(8,128)} %bitcast.218), kind=kCustom, calls=%fused_computation.16 | custom fusion | flops 2228224 | bytes 26743040 | tf_op jit(solution)/shard_map/scatter-add | solution.py:272
  967.1 25.3 %scatter_fusion.4 = f32[513,2048]{1,0:T(8,128)} fusion(f32[513,2048]{1,0:T(8,128)} %scatter_fusion.3, s32[1088]{0:T(1024)S(1)} %copy-done.84, f32[1088,2048]{1,0:T(8,128)} %bitcast.219), kind=kCustom, calls=%fused_computation.17 | custom fusion | flops 2228224 | bytes 26743040 | tf_op jit(solution)/shard_map/scatter-add | solution.py:272
  1003.1 25.2 %scatter_fusion.5 = f32[513,2048]{1,0:T(8,128)} fusion(f32[513,2048]{1,0:T(8,128)} %scatter_fusion.4, s32[1088]{0:T(1024)S(1)} %copy-done.82, f32[1088,2048]{1,0:T(8,128)} %bitcast.217), kind=kCustom, calls=%fused_computation.18 | custom fusion | flops 2228224 | bytes 26743040 | tf_op jit(solution)/shard_map/scatter-add | solution.py:272
  1036.2 40.5 %reduce-scatter.26.cloned.1.call-done = bf16[128,2048]{1,0:T(8,128)(2,1)} async-done(((bf16[512,2048]{1,0:T(8,128)(2,1)}), bf16[128,2048]{1,0:T(8,128)(2,1)}) %reduce-scatter.26.cloned.1.call-update) | async-done | bytes 524304 | tf_op jit(solution)/shard_map/reduce_scatter | solution.py:288
  1083.2 30.2 %all-reduce.13.cloned.1.call-done = bf16[8,4,64,16]{2,3,1,0:T(8,128)(2,1)} async-done(((bf16[8,4,64,16]{2,3,1,0:T(8,128)(2,1)}), bf16[8,4,64,16]{2,3,1,0:T(8,128)(2,1)}) %all-reduce.13.cloned.1.call-update) | async-done | bytes 65552
  1115.5 45.5 %all-gather.34.cloned.1.call-done = bf16[512,2048]{1,0:T(8,128)(2,1)} async-done(((bf16[128,2048]{1,0:T(8,128)(2,1)}), bf16[512,2048]{1,0:T(8,128)(2,1)}) %all-gather.34.cloned.1.call-update) | async-done | bytes 2097168 | tf_op jit(solution)/shard_map/all_gather | solution.py:293
  1354.2 43.7 %reduce-scatter.32.cloned.1.call-done = bf16[256,512]{1,0:T(8,128)(2,1)} async-done(((bf16[2048,512]{1,0:T(8,128)(2,1)}), bf16[256,512]{1,0:T(8,128)(2,1)}) %reduce-scatter.32.cloned.1.call-update) | async-done | bytes 262160 | tf_op jit(solution)/shard_map/reduce_scatter | solution.py:414
  1399.7 43.3 %reduce-scatter.30.cloned.1.call-done = bf16[256,512]{1,0:T(8,128)(2,1)} async-done(((bf16[2048,512]{1,0:T(8,128)(2,1)}), bf16[256,512]{1,0:T(8,128)(2,1)}) %reduce-scatter.30.cloned.1.call-update) | async-done | bytes 262160 | tf_op jit(solution)/shard_map/reduce_scatter | solution.py:411
  1444.8 45.1 %reduce-scatter.28.cloned.1.call-done = bf16[128,2048]{1,0:T(8,128)(2,1)} async-done(((bf16[512,2048]{1,0:T(8,128)(2,1)}), bf16[128,2048]{1,0:T(8,128)(2,1)}) %reduce-scatter.28.cloned.1.call-update) | async-done | bytes 524304 | tf_op jit(solution)/shard_map/reduce_scatter | solution.py:377
  1492.0 116.6 %reduce-scatter.44.cloned.1.call-done = bf16[16,256,256]{2,1,0:T(8,128)(2,1)} async-done(((bf16[16,256,2048]{2,1,0:T(8,128)(2,1)}), bf16[16,256,256]{2,1,0:T(8,128)(2,1)}) %reduce-scatter.44.cloned.1.call-update) | async-done | bytes 2097168 | tf_op jit(solution)/shard_map/reduce_scatter | solution.py:458
  1612.7 115.5 %reduce-scatter.42.cloned.1.call-done = bf16[16,256,256]{2,1,0:T(8,128)(2,1)} async-done(((bf16[16,2048,256]{2,1,0:T(8,128)(2,1)}), bf16[16,256,256]{2,1,0:T(8,128)(2,1)}) %reduce-scatter.42.cloned.1.call-update) | async-done | bytes 2097168 | tf_op jit(solution)/shard_map/reduce_scatter | solution.py:452
  1732.2 115.4 %reduce-scatter.40.cloned.1.call-done = bf16[16,256,256]{2,1,0:T(8,128)(2,1)} async-done(((bf16[16,2048,256]{2,1,0:T(8,128)(2,1)}), bf16[16,256,256]{2,1,0:T(8,128)(2,1)}) %reduce-scatter.40.cloned.1.call-update) | async-done | bytes 2097168 | tf_op jit(solution)/shard_map/reduce_scatter | solution.py:446
  (573 shorter events, 663.9 us)
Async XLA Ops:
  8.7 107.9 %all-gather.20.cloned.1.call-start = ((), (), s32[]{:S(2)}) async-start(), calls=%async_computation.17 | async-start | bytes 2359296 | tf_op jit(solution)/shard_map/all_gather | solution.py:45
  9.4 143.8 %all-gather.16.cloned.1.call-start = ((), (), s32[]{:S(2)}) async-start(), calls=%async_computation.15 | async-start | bytes 2359296 | tf_op jit(solution)/shard_map/all_gather | solution.py:46
  10.0 166.3 %all-gather.22.cloned.1.call-start = ((), (), s32[]{:S(2)}) async-start(), calls=%async_computation.18 | async-start | bytes 2359296 | tf_op jit(solution)/shard_map/all_gather | solution.py:47
  10.6 213.9 %reduce-scatter.22.cloned.1.call-start = ((), (), s32[]{:S(2)}) async-start(), calls=%async_computation.19 | async-start | bytes 2621440 | tf_op jit(solution)/shard_map/reduce_scatter | solution.py:149
  180.5 93.6 %all-gather.24.cloned.1.call-start = ((), (), s32[]{:S(2)}) async-start(), calls=%async_computation.20 | async-start | bytes 2621440 | tf_op jit(solution)/shard_map/all_gather | solution.py:160
  228.4 136.0 %all-gather.26.cloned.1.call-start = ((), (), s32[]{:S(2)}) async-start(), calls=%async_computation.21 | async-start | bytes 18874368 | tf_op jit(solution)/shard_map/all_gather | solution.py:55
  229.1 227.2 %all-gather.28.cloned.1.call-start = ((), (), s32[]{:S(2)}) async-start(), calls=%async_computation.22 | async-start | bytes 18874368 | tf_op jit(solution)/shard_map/all_gather | solution.py:56
  229.9 321.5 %all-gather.30.cloned.1.call-start = ((), (), s32[]{:S(2)}) async-start(), calls=%async_computation.23 | async-start | bytes 18874368 | tf_op jit(solution)/shard_map/all_gather | solution.py:57
  230.5 529.7 %reduce-scatter.24.cloned.1.call-start = ((), (), s32[]{:S(2)}) async-start(), calls=%async_computation.24 | async-start | bytes 2621440 | tf_op jit(solution)/shard_map/reduce_scatter | solution.py:216
  716.2 91.7 %all-gather.32.cloned.1.call-start = ((), (), s32[]{:S(2)}) async-start(), calls=%async_computation.25 | async-start | bytes 2621440 | tf_op jit(solution)/shard_map/all_gather | solution.py:227
  762.4 314.3 %reduce-scatter.26.cloned.1.call-start = ((), (), s32[]{:S(2)}) async-start(), calls=%async_computation.26 | async-start | bytes 2621440 | tf_op jit(solution)/shard_map/reduce_scatter | solution.py:288
  1034.1 79.4 %all-reduce.13.cloned.1.call-start = ((), (), s32[]{:S(2)}) async-start(), calls=%async_computation.39 | async-start | bytes 262144
  1036.2 124.9 %all-gather.34.cloned.1.call-start = ((), (), s32[]{:S(2)}) async-start(), calls=%async_computation.27 | async-start | bytes 2621440 | tf_op jit(solution)/shard_map/all_gather | solution.py:293
  1082.6 217.1 %reduce-scatter.38.cloned.1.call-start = ((), (), s32[]{:S(2)}) async-start(), calls=%async_computation.33 | async-start | bytes 36864 | tf_op jit(solution)/shard_map/reduce_scatter | solution.py:441
  1115.5 217.7 %reduce-scatter.48.cloned.1.call-start = ((), (), s32[]{:S(2)}) async-start(), calls=%async_computation.38 | async-start | bytes 36864
  1178.4 156.1 %reduce-scatter.46.cloned.1.call-start = ((), (), s32[]{:S(2)}) async-start(), calls=%async_computation.37 | async-start | bytes 36864
  1179.6 156.3 %reduce-scatter.36.cloned.1.call-start = ((), (), s32[]{:S(2)}) async-start(), calls=%async_computation.32 | async-start | bytes 2359296 | tf_op jit(solution)/shard_map/reduce_scatter | solution.py:420
  1184.2 168.2 %reduce-scatter.34.cloned.1.call-start = ((), (), s32[]{:S(2)}) async-start(), calls=%async_computation.31 | async-start | bytes 2359296 | tf_op jit(solution)/shard_map/reduce_scatter | solution.py:417
  1191.7 206.2 %reduce-scatter.32.cloned.1.call-start = ((), (), s32[]{:S(2)}) async-start(), calls=%async_computation.30 | async-start | bytes 2359296 | tf_op jit(solution)/shard_map/reduce_scatter | solution.py:414
  1208.6 234.4 %reduce-scatter.30.cloned.1.call-start = ((), (), s32[]{:S(2)}) async-start(), calls=%async_computation.29 | async-start | bytes 2359296 | tf_op jit(solution)/shard_map/reduce_scatter | solution.py:411
  1213.8 276.1 %reduce-scatter.28.cloned.1.call-start = ((), (), s32[]{:S(2)}) async-start(), calls=%async_computation.28 | async-start | bytes 2621440 | tf_op jit(solution)/shard_map/reduce_scatter | solution.py:377
  1223.6 385.1 %reduce-scatter.44.cloned.1.call-start = ((), (), s32[]{:S(2)}) async-start(), calls=%async_computation.36 | async-start | bytes 18874368 | tf_op jit(solution)/shard_map/reduce_scatter | solution.py:458
  1245.3 482.9 %reduce-scatter.42.cloned.1.call-start = ((), (), s32[]{:S(2)}) async-start(), calls=%async_computation.35 | async-start | bytes 18874368 | tf_op jit(solution)/shard_map/reduce_scatter | solution.py:452
  1271.8 575.8 %reduce-scatter.40.cloned.1.call-start = ((), (), s32[]{:S(2)}) async-start(), calls=%async_computation.34 | async-start | bytes 18874368 | tf_op jit(solution)/shard_map/reduce_scatter | solution.py:446
  (146 other events, 5572.9 us)
Sparse Core Ops, SparseCore 0:
  9.6 48.6 all-gather.13
  118.4 27.8 all-gather.15
  148.0 28.1 all-gather.21
  180.6 43.8 reduce-scatter.21
  228.5 45.5 all-gather.23
  276.1 88.2 all-gather.25
  366.5 89.8 all-gather.27
  458.3 93.1 all-gather.29
  716.3 43.8 reduce-scatter.23
  762.6 45.2 all-gather.31
  1034.2 42.5 reduce-scatter.25
  1079.6 33.7 all-reduce.12
  1115.4 45.5 all-gather.33
  1163.9 29.9 reduce-scatter.37
  1197.1 31.2 reduce-scatter.47
  1231.8 31.2 reduce-scatter.45
  1266.7 41.2 reduce-scatter.35
  1311.2 41.1 reduce-scatter.33
  1356.6 41.2 reduce-scatter.31
  1401.8 41.2 reduce-scatter.29
  1446.0 43.8 reduce-scatter.27
  1493.3 115.2 reduce-scatter.43
  1612.2 115.9 reduce-scatter.41
  1731.6 115.9 reduce-scatter.39
  (2 shorter events, 54.4 us)
where the time goes:
time: 1860 us
  waiting for transfers between devices  1070 us (58%)
  other arithmetic  303 us (16%)
  matrix products  247 us (13%)
  local copies, waits for them, and re-layouts  150 us (8%)
  blocking collectives  70.4 us (4%)
    reduce_scatter x1, waiting for transfers between devices, per_device(): lax.psum_scatter(jnp.concatenate(down_grads, axis=0).astype(jnp.bfloat16)...  117 us
    reduce_scatter x1, waiting for transfers between devices, per_device(): lax.psum_scatter(jnp.concatenate(up_grads, axis=0).astype(jnp.bfloat16),...  115 us
    reduce_scatter x1, waiting for transfers between devices, per_device(): lax.psum_scatter(jnp.concatenate(gate_grads, axis=0).astype(jnp.bfloat16)...  115 us
    scatter-add x4, other arithmetic, per_device(): expert_running.at[sources[turn_index].reshape(-1)]  100 us
    scatter-add x4, other arithmetic, per_device(): ffn_grad_running.at[source_rows.reshape(-1)]  99.6 us
    all_gather x1, waiting for transfers between devices, fetch_experts(): lax.all_gather(down_weight, 'dp', axis=2, tiled=True)  89.1 us
    all_gather x1, waiting for transfers between devices, fetch_experts(): lax.all_gather(up_weight, 'dp', axis=1, tiled=True)  87.1 us
    all_gather x1, waiting for transfers between devices, per_device(): lax.all_gather(grad_middle.astype(jnp.bfloat16), 'tensor', axis=0, tiled=...  45.5 us
  transfers between devices with their start and end apart: 26, of which 21 were waited for; matrix products, arithmetic and copies ran while one was open for 15% of the time, Pallas kernels for 0%

commit v1 on v0

--- a/solution.py
+++ b/solution.py
@@ -1,8 +1,11 @@
+import functools
 import math
 
 import jax
 import jax.numpy as jnp
 from jax import lax
+from jax.experimental import pallas as pl
+from jax.experimental.pallas import tpu as pltpu
 from jax.sharding import PartitionSpec as P
 
 HD = 128
@@ -480,6 +483,1538 @@
     )
 
 
+MESH = pl.DeviceIdType.MESH
+BF = jnp.bfloat16
+F32 = jnp.float32
+VMEM_LIMIT = 60 * 1024 * 1024
+ANY = pl.BlockSpec(memory_space=pl.ANY)
+VM = pl.BlockSpec(memory_space=pltpu.VMEM)
+
+
+def flip(index, bits):
+    for bit in (1, 2, 4):
+        if bits & bit:
+            index = index + bit * (1 - 2 * ((index // bit) % 2))
+    return index
+
+
+def both(first, second):
+    return jnp.logical_and(first, second)
+
+
+def under(condition, action):
+    if condition is None:
+        action()
+    else:
+        pl.when(condition)(action)
+
+
+class Wire:
+    def __init__(self, send_sem, recv_sem):
+        self.send_sem, self.recv_sem, self.count, self.sent = send_sem, recv_sem, 0, []
+
+    def slot(self):
+        self.count += 1
+        return self.count - 1
+
+    def start(self, slot, source, target, device, condition=None):
+        copy = pltpu.make_async_remote_copy(
+            src_ref=source(),
+            dst_ref=target(),
+            send_sem=self.send_sem.at[slot],
+            recv_sem=self.recv_sem.at[slot],
+            device_id=device,
+            device_id_type=MESH,
+        )
+        under(condition, lambda: copy.start())
+        self.sent.append((condition, copy))
+
+    def arrive(self, slot, region, device, condition=None):
+        copy = pltpu.make_async_remote_copy(
+            src_ref=region(),
+            dst_ref=region(),
+            send_sem=self.send_sem.at[slot],
+            recv_sem=self.recv_sem.at[slot],
+            device_id=device,
+            device_id_type=MESH,
+        )
+        under(condition, lambda: copy.wait_recv())
+
+    def finish(self):
+        for condition, copy in self.sent:
+            under(condition, lambda copy=copy: copy.wait_send())
+        self.sent = []
+
+
+class Local:
+    def __init__(self, sem):
+        self.sem, self.count = sem, 0
+
+    def start(self, source, target):
+        copy = pltpu.make_async_copy(source, target, self.sem.at[self.count])
+        self.count += 1
+        copy.start()
+        return copy
+
+
+def greet(devices):
+    barrier = pltpu.get_barrier_semaphore()
+    for condition, device in devices:
+        under(
+            condition,
+            lambda device=device: pl.semaphore_signal(
+                barrier, inc=1, device_id=device, device_id_type=MESH
+            ),
+        )
+    amount = sum(1 for condition, device in devices if condition is None)
+    for condition, device in devices:
+        if condition is not None:
+            amount = amount + jnp.where(condition, 1, 0)
+    pl.semaphore_wait(barrier, amount)
+
+
+def line_devices(d, t, extent):
+    return [(t < extent - 1, (d, t + 1)), (t > 0, (d, t - 1))]
+
+
+def rows_loop(rows, step, body):
+    def run(index, carry):
+        body(pl.multiple_of(index * step, step))
+        return carry
+
+    lax.fori_loop(0, rows // step, run, 0)
+
+
+def add_into(target, source, rows):
+    def body(start):
+        part = pl.ds(start, 16)
+        target[part] = (target[part].astype(F32) + source[part].astype(F32)).astype(BF)
+
+    rows_loop(rows, 16, body)
+
+
+def gather_line(wire, d, t, extent, own, place, on_block):
+    up = [wire.slot() for unused in range(extent - 1)]
+    down = [wire.slot() for unused in range(extent - 1)]
+    up_device, down_device = (d, t + 1), (d, t - 1)
+    wire.start(up[0], own, lambda: place(t), up_device, t < extent - 1)
+    wire.start(down[0], own, lambda: place(t), down_device, t > 0)
+    on_block(0, 0, t, None)
+    for step in range(1, extent):
+        wire.arrive(up[step - 1], lambda step=step: place(t - step), down_device, t >= step)
+        if step < extent - 1:
+            wire.start(
+                up[step],
+                lambda step=step: place(t - step),
+                lambda step=step: place(t - step),
+                up_device,
+                both(t >= step, t < extent - 1),
+            )
+        wire.arrive(
+            down[step - 1], lambda step=step: place(t + step), up_device, t <= extent - 1 - step
+        )
+        if step < extent - 1:
+            wire.start(
+                down[step],
+                lambda step=step: place(t + step),
+                lambda step=step: place(t + step),
+                down_device,
+                both(t <= extent - 1 - step, t > 0),
+            )
+        on_block(step, 0, t - step, t >= step)
+        on_block(step, 1, t + step, t <= extent - 1 - step)
+
+
+class LineSum:
+    def __init__(self, wire, d, t, extent, block, up_in, down_in, rows, parts):
+        self.wire, self.d, self.t, self.extent = wire, d, t, extent
+        self.block, self.up_in, self.down_in = block, up_in, down_in
+        self.rows, self.parts = rows // parts, parts
+        self.up = [[wire.slot() for p in range(parts)] for s in range(extent - 1)]
+        self.down = [[wire.slot() for p in range(parts)] for s in range(extent - 1)]
+
+    def cut(self, ref, part):
+        return ref.at[pl.ds(part * self.rows, self.rows)]
+
+    def flow(self, step, part, near, index, slots, buffers, to_device, from_device):
+        wire, extent = self.wire, self.extent
+        block = lambda: self.cut(self.block(index), part)
+        if step >= 1:
+            source = lambda: self.cut(buffers.at[step - 1], part)
+            active = both(both(near <= step, near < extent - 1), near >= 1)
+            wire.arrive(slots[step - 1][part], source, from_device, active)
+            under(active, lambda: add_into(block(), source(), self.rows))
+        wire.start(
+            slots[step][part],
+            block,
+            lambda: self.cut(buffers.at[step], part),
+            to_device,
+            both(near <= step, near < extent - 1),
+        )
+
+    def step(self, step):
+        d, t, extent = self.d, self.t, self.extent
+        for part in range(self.parts):
+            self.flow(
+                step,
+                part,
+                t,
+                extent - 1 - step + t,
+                self.up,
+                self.up_in,
+                (d, t + 1),
+                (d, t - 1),
+            )
+            self.flow(
+                step,
+                part,
+                extent - 1 - t,
+                step + t - (extent - 1),
+                self.down,
+                self.down_in,
+                (d, t - 1),
+                (d, t + 1),
+            )
+
+    def last(self):
+        d, t, extent = self.d, self.t, self.extent
+        for ready, missing, slots, buffers, device in (
+            (t > 0, t == 0, self.up, self.up_in, (d, t - 1)),
+            (t < extent - 1, t == extent - 1, self.down, self.down_in, (d, t + 1)),
+        ):
+            buffer = buffers.at[extent - 2]
+            for part in range(self.parts):
+                self.wire.arrive(
+                    slots[extent - 2][part],
+                    lambda part=part, buffer=buffer: self.cut(buffer, part),
+                    device,
+                    ready,
+                )
+
+            def clear(buffer=buffer):
+                buffer[...] = jnp.zeros(buffer.shape, BF)
+
+            under(missing, clear)
+
+
+def own_sum(block, up_in, down_in, part, columns):
+    return (
+        block[part, columns].astype(F32)
+        + up_in[part, columns].astype(F32)
+        + down_in[part, columns].astype(F32)
+    )
+
+
+def gather_plane(wire, d, t, extent, own, place, half):
+    dx, dy, dxy, dc = flip(d, 2), flip(d, 4), flip(d, 6), flip(d, 1)
+    to_x, to_y, to_c = (dx, t), (dy, t), (dc, t)
+    events = []
+
+    def cut(ref, which):
+        return ref.at[pl.ds(which * half, half)]
+
+    def on_block(step, side, index, condition):
+        source = own if step == 0 else (lambda: place(d, index))
+        event = dict(index=index, condition=condition, slots={})
+        for name, device, which in (
+            ("x0", to_x, 0),
+            ("y1", to_y, 1),
+            ("x1", to_x, 1),
+            ("y0", to_y, 0),
+        ):
+            slot = wire.slot()
+            event["slots"][name] = slot
+            wire.start(
+                slot,
+                lambda which=which: cut(source(), which),
+                lambda which=which: cut(place(d, index), which),
+                device,
+                condition,
+            )
+        slot = wire.slot()
+        event["slots"]["c"] = slot
+        wire.start(slot, source, lambda: place(d, index), to_c, condition)
+        events.append(event)
+        if step >= 1 and side == 1:
+            for earlier in events[:-2]:
+                relay(earlier)
+
+    def relay(event):
+        if "relayed" in event:
+            return
+        event["relayed"] = True
+        index, condition, slots = event["index"], event["condition"], event["slots"]
+        x_part = lambda which: (lambda: cut(place(dx, index), which))
+        y_part = lambda which: (lambda: cut(place(dy, index), which))
+        wire.arrive(slots["x0"], x_part(0), to_x, condition)
+        slots["fy"] = wire.slot()
+        wire.start(slots["fy"], x_part(0), x_part(0), to_y, condition)
+        wire.arrive(slots["y1"], y_part(1), to_y, condition)
+        slots["fx"] = wire.slot()
+        wire.start(slots["fx"], y_part(1), y_part(1), to_x, condition)
+        wire.arrive(slots["x1"], x_part(1), to_x, condition)
+        slots["cx"] = wire.slot()
+        wire.start(slots["cx"], lambda: place(dx, index), lambda: place(dx, index), to_c, condition)
+        wire.arrive(slots["y0"], y_part(0), to_y, condition)
+        slots["cy"] = wire.slot()
+        wire.start(slots["cy"], lambda: place(dy, index), lambda: place(dy, index), to_c, condition)
+
+    gather_line(wire, d, t, extent, own, lambda index: place(d, index), on_block)
+    for event in events:
+        relay(event)
+    for event in events:
+        index, condition, slots = event["index"], event["condition"], event["slots"]
+        wire.arrive(slots["fy"], lambda: cut(place(dxy, index), 0), to_y, condition)
+        wire.arrive(slots["fx"], lambda: cut(place(dxy, index), 1), to_x, condition)
+        slots["cd"] = wire.slot()
+        wire.start(
+            slots["cd"], lambda: place(dxy, index), lambda: place(dxy, index), to_c, condition
+        )
+    for event in events:
+        index, condition, slots = event["index"], event["condition"], event["slots"]
+        for name, bits in (("c", 1), ("cx", 3), ("cy", 5), ("cd", 7)):
+            wire.arrive(
+                slots[name], lambda bits=bits: place(flip(d, bits), index), to_c, condition
+            )
+
+
+def plane_order(t):
+    top = t // 2
+    inner = ((t + 1) // 2) % 2
+    return (
+        3 - 3 * top,
+        2 - top,
+        (1 - inner) * (1 - top) + (2 + inner) * top,
+        inner * (1 - top) + (3 - inner) * top,
+    )
+
+
+def sum_plane(wire, local, d, t, extent, partial, work, core_in, a_in, b_in, up_in, down_in, half):
+    order = plane_order(t)
+    to_x, to_y, to_c = (flip(d, 2), t), (flip(d, 4), t), (flip(d, 1), t)
+    turns = (3, 1, 2, 0)
+    slots_c, slots_a, slots_b, loads = {}, {}, {}, {}
+
+    def cut(ref, which):
+        return ref.at[pl.ds(which * half, half)]
+
+    for k in range(extent):
+        for i in turns:
+            slots_c[k, i] = wire.slot()
+            wire.start(
+                slots_c[k, i],
+                lambda k=k, i=i: partial.at[flip(d, 1 + 2 * i) * extent + order[k]],
+                lambda k=k, i=i: core_in.at[k, i],
+                to_c,
+            )
+            loads[k, i] = local.start(
+                partial.at[flip(d, 2 * i) * extent + order[k]], work.at[k, i]
+            )
+
+    def inverse(index):
+        where = jnp.int32(0)
+        for k in range(1, extent):
+            where = where + k * jnp.where(order[k] == index, 1, 0)
+        return where
+
+    line = LineSum(
+        wire,
+        d,
+        t,
+        extent,
+        lambda index: work.at[inverse(index), 0],
+        up_in,
+        down_in,
+        2 * half,
+        1,
+    )
+    routes_a = ((to_x, 1, 0, 0, 0), (to_y, 2, 0, 1, 1), (to_x, 3, 2, 0, 2), (to_y, 3, 1, 1, 3))
+    routes_b = ((to_y, 2, 0, 0), (to_x, 1, 1, 1))
+    for turn in range(extent + 2):
+        if turn < extent:
+            k = turn
+            for i in turns:
+                loads[k, i].wait()
+                wire.arrive(slots_c[k, i], lambda k=k, i=i: core_in.at[k, i], to_c)
+                add_into(work.at[k, i], core_in.at[k, i], 2 * half)
+            for device, source, target, which, row in (
+                routes_a[2],
+                routes_a[3],
+                routes_a[0],
+                routes_a[1],
+            ):
+                slots_a[k, row] = wire.slot()
+                wire.start(
+                    slots_a[k, row],
+                    lambda k=k, source=source, which=which: cut(work.at[k, source], which),
+                    lambda k=k, row=row: a_in.at[k, row],
+                    device,
+                )
+        if 1 <= turn <= extent:
+            k = turn - 1
+            for device, source, target, which, row in (
+                routes_a[2],
+                routes_a[3],
+                routes_a[0],
+                routes_a[1],
+            ):
+                wire.arrive(slots_a[k, row], lambda k=k, row=row: a_in.at[k, row], device)
+                add_into(cut(work.at[k, target], which), a_in.at[k, row], half)
+                if row >= 2:
+                    to, origin, part, b_row = routes_b[row - 2]
+                    slots_b[k, b_row] = wire.slot()
+                    wire.start(
+                        slots_b[k, b_row],
+                        lambda k=k, origin=origin, part=part: cut(work.at[k, origin], part),
+                        lambda k=k, b_row=b_row: b_in.at[k, b_row],
+                        to,
+                    )
+        if turn >= 2:
+            k = turn - 2
+            for device, source, which, row in routes_b:
+                wire.arrive(slots_b[k, row], lambda k=k, row=row: b_in.at[k, row], device)
+                add_into(cut(work.at[k, 0], which), b_in.at[k, row], half)
+            if k < extent - 1:
+                line.step(k)
+    line.last()
+    return work.at[extent - 1, 0]
+
+
+def plane_devices(d, t, extent):
+    return line_devices(d, t, extent) + [(None, (flip(d, bits), t)) for bits in (1, 2, 4)]
+
+
+def kernel_params(number):
+    return pltpu.CompilerParams(
+        collective_id=number, has_side_effects=True, vmem_limit_bytes=VMEM_LIMIT
+    )
+
+
+def dma_pair(count):
+    return [pltpu.SemaphoreType.DMA((count,)), pltpu.SemaphoreType.DMA((count,))]
+
+
+def fetch_kernel(
+    extent,
+    hid,
+    qkv,
+    o,
+    gains,
+    gate,
+    up,
+    down,
+    hid_all,
+    qkv_all,
+    o_all,
+    gains_all,
+    *rest,
+):
+    pieces, (stage, send_sem, recv_sem, local_sem) = rest[:8], rest[8:]
+    d, t = lax.axis_index("dp"), lax.axis_index("tensor")
+    rows = hid.shape[0]
+    depth, o_rows = qkv.shape[0], o.shape[0]
+    width = o.shape[1]
+    greet(line_devices(d, t, extent) + [(None, (flip(d, bits), t)) for bits in range(1, 8)])
+    wire, local = Wire(send_sem, recv_sem), Local(local_sem)
+    dx, dy, dxy, dc = flip(d, 2), flip(d, 4), flip(d, 6), flip(d, 1)
+    to_x, to_y, to_c = (dx, t), (dy, t), (dc, t)
+
+    def region(device, which):
+        start = pl.multiple_of(device * width, width)
+        if which is None:
+            return [qkv_all.at[pl.ds(device * depth, depth)], o_all.at[:, pl.ds(start, width)]]
+        return [
+            qkv_all.at[pl.ds(device * depth + which * (depth // 2), depth // 2)],
+            o_all.at[pl.ds(which * (o_rows // 2), o_rows // 2), pl.ds(start, width)],
+        ]
+
+    def own(which):
+        if which is None:
+            return [qkv, o]
+        return [
+            qkv.at[pl.ds(which * (depth // 2), depth // 2)],
+            o.at[pl.ds(which * (o_rows // 2), o_rows // 2)],
+        ]
+
+    def send(device, sources, targets):
+        slots = []
+        for source, target in zip(sources, targets):
+            slot = wire.slot()
+            wire.start(slot, lambda: source, lambda: target, device)
+            slots.append(slot)
+        return slots
+
+    def arrive(slots, regions, device):
+        for slot, part in zip(slots, regions):
+            wire.arrive(slot, lambda: part, device)
+
+    def block(index):
+        return hid_all.at[pl.ds(index * rows, rows)]
+
+    x_slots, y_slots, c_slots = {}, {}, {}
+    for which, other in ((0, 1), (1, 0)):
+        x_slots[which] = send(to_x, own(which), region(d, which))
+        y_slots[other] = send(to_y, own(other), region(d, other))
+    c_slots[1] = send(to_c, own(None), region(d, None))
+    passed = {}
+    loads, copies = [], []
+    for place, weight in enumerate((gate, up, down)):
+        loads.append(local.start(weight, stage.at[place]))
+
+    def store_pieces():
+        for load in loads:
+            load.wait()
+        for bits in range(8):
+            first = 2 * flip(d, bits)
+            for place in range(3):
+                copies.append(
+                    local.start(stage.at[place, pl.ds(first, 2)], pieces[bits].at[place])
+                )
+
+    def on_block(step, side, index, condition):
+        if side == 1 or step == 0:
+            return
+        if step == 1:
+            store_pieces()
+            arrive(x_slots[0], region(dx, 0), to_x)
+            passed["y"] = send(to_y, region(dx, 0), region(dx, 0))
+            arrive(y_slots[1], region(dy, 1), to_y)
+            passed["x"] = send(to_x, region(dy, 1), region(dy, 1))
+        if step == 2:
+            arrive(x_slots[1], region(dx, 1), to_x)
+            c_slots[3] = send(to_c, region(dx, None), region(dx, None))
+            arrive(y_slots[0], region(dy, 0), to_y)
+            c_slots[5] = send(to_c, region(dy, None), region(dy, None))
+
+    copies.append(local.start(hid, block(t)))
+    for source, target in zip(own(None), region(d, None)):
+        copies.append(local.start(source, target))
+    gather_line(wire, d, t, extent, lambda: hid, block, on_block)
+    gain_slots = {}
+    for bits in range(1, 8):
+        gain_slots[bits] = wire.slot()
+        wire.start(
+            gain_slots[bits],
+            lambda: gains,
+            lambda bits=bits: gains_all.at[bits],
+            (flip(d, bits), t),
+        )
+    copies.append(local.start(gains, gains_all.at[0]))
+    arrive(passed["y"], region(dxy, 0), to_y)
+    arrive(passed["x"], region(dxy, 1), to_x)
+    c_slots[7] = send(to_c, region(dxy, None), region(dxy, None))
+    for bits in (1, 3, 5, 7):
+        arrive(c_slots[bits], region(flip(d, bits), None), to_c)
+    for bits in range(1, 8):
+        wire.arrive(
+            gain_slots[bits], lambda bits=bits: gains_all.at[bits], (flip(d, bits), t)
+        )
+    for copy in copies:
+        copy.wait()
+    wire.finish()
+
+
+def fetch(extent, hid, qkv, o, gains, gate, up, down):
+    rows, model_width = hid.shape
+    piece = jax.ShapeDtypeStruct((3, 2) + gate.shape[1:], BF)
+    return pl.pallas_call(
+        functools.partial(fetch_kernel, extent),
+        out_shape=[
+            jax.ShapeDtypeStruct((rows * extent, model_width), BF),
+            jax.ShapeDtypeStruct((8 * qkv.shape[0], qkv.shape[1]), BF),
+            jax.ShapeDtypeStruct((o.shape[0], 8 * o.shape[1]), BF),
+            jax.ShapeDtypeStruct((8,) + gains.shape, F32),
+        ]
+        + [piece] * 8,
+        in_specs=[VM] * 4 + [ANY] * 3,
+        out_specs=[ANY] * 12,
+        scratch_shapes=[pltpu.VMEM((3,) + gate.shape, BF)]
+        + dma_pair(64) + [pltpu.SemaphoreType.DMA((40,))],
+        compiler_params=kernel_params(1),
+        cost_estimate=pl.CostEstimate(flops=0, bytes_accessed=100_000_000, transcendentals=0),
+    )(hid, qkv, o, gains, gate, up, down)
+
+
+def line_total_kernel(extent, value, total, inbox, send_sem, recv_sem):
+    d, t = lax.axis_index("dp"), lax.axis_index("tensor")
+    peers = [(d, (t + k) % extent) for k in range(1, extent)]
+    greet([(None, peer) for peer in peers])
+    wire = Wire(send_sem, recv_sem)
+    slots = []
+    for k, peer in enumerate(peers):
+        slot = wire.slot()
+        slots.append(slot)
+        wire.start(slot, lambda: value, lambda k=k: inbox.at[k], peer)
+    result = value[...]
+    for k, peer in enumerate(peers):
+        wire.arrive(slots[k], lambda k=k: inbox.at[k], peer)
+        result = result + inbox[k]
+    total[...] = result
+    wire.finish()
+
+
+def line_total(extent, number, value):
+    return pl.pallas_call(
+        functools.partial(line_total_kernel, extent),
+        out_shape=jax.ShapeDtypeStruct(value.shape, F32),
+        in_specs=[VM],
+        out_specs=VM,
+        scratch_shapes=[pltpu.VMEM((extent - 1,) + value.shape, F32)] + dma_pair(extent - 1),
+        compiler_params=kernel_params(number),
+        cost_estimate=pl.CostEstimate(flops=0, bytes_accessed=10_000_000, transcendentals=0),
+    )(value)
+
+
+def enter_kernel(
+    extent,
+    partial,
+    hid,
+    gain,
+    router,
+    chosen,
+    middle,
+    gates,
+    ffn_own,
+    tokens,
+    work,
+    up_in,
+    down_in,
+    packet,
+    send_sem,
+    recv_sem,
+    local_sem,
+):
+    d, t = lax.axis_index("dp"), lax.axis_index("tensor")
+    rows, width = hid.shape
+    greet(plane_devices(d, t, extent))
+    wire, local = Wire(send_sem, recv_sem), Local(local_sem)
+    local.start(partial, work).wait()
+    line = LineSum(
+        wire, d, t, extent, lambda index: work.at[index], up_in, down_in, rows, 2
+    )
+    for step in range(extent - 1):
+        line.step(step)
+    line.last()
+    mine = work.at[t]
+    everything = pl.ds(0, width)
+
+    def body(start):
+        part = pl.ds(start, 16)
+        value = hid[part].astype(F32) + own_sum(
+            mine, up_in.at[extent - 2], down_in.at[extent - 2], part, everything
+        )
+        middle[part] = value
+        unit = value * lax.rsqrt(jnp.mean(value * value, axis=-1, keepdims=True) + EPSILON)
+        packet[part, 0:width] = (unit * gain[...]).astype(BF)
+
+    rows_loop(rows, 16, body)
+    ffn_own[...] = packet[:, 0:width]
+    logits = jnp.dot(packet[:, 0:width], router[...], preferred_element_type=F32)
+    lane = lax.broadcasted_iota(jnp.int32, logits.shape, 1)
+    top = jnp.max(jnp.where(lane < 16, logits, -1e30), axis=-1, keepdims=True)
+    powers = jnp.where(lane < 32, jnp.exp(logits - top), 0.0)
+    probs = powers / jnp.sum(jnp.where(lane < 16, powers, 0.0), axis=-1, keepdims=True)
+    gates[...] = probs
+    coeff = probs * chosen[...]
+    high = coeff.astype(BF).astype(F32)
+    packet[:, width : width + 128] = jnp.where(lane < 16, high, coeff - high).astype(BF)
+
+    def place(device, index):
+        return tokens.at[device * extent + index]
+
+    copy = local.start(packet, place(d, t))
+    gather_plane(wire, d, t, extent, lambda: packet, place, rows // 2)
+    copy.wait()
+    wire.finish()
+
+
+def enter(extent, partial, hid, gain, router, chosen):
+    rows, width = hid.shape
+    return pl.pallas_call(
+        functools.partial(enter_kernel, extent),
+        out_shape=[
+            jax.ShapeDtypeStruct((rows, width), F32),
+            jax.ShapeDtypeStruct((rows, 128), F32),
+            jax.ShapeDtypeStruct((rows, width), BF),
+            jax.ShapeDtypeStruct((8 * extent, rows, width + 128), BF),
+        ],
+        in_specs=[ANY, VM, VM, VM, VM],
+        out_specs=[VM, VM, VM, ANY],
+        scratch_shapes=[
+            pltpu.VMEM((extent, rows, width), BF),
+            pltpu.VMEM((extent - 1, rows, width), BF),
+            pltpu.VMEM((extent - 1, rows, width), BF),
+            pltpu.VMEM((rows, width + 128), BF),
+        ]
+        + dma_pair(100)
+        + [pltpu.SemaphoreType.DMA((2,))],
+        compiler_params=kernel_params(3),
+        cost_estimate=pl.CostEstimate(flops=0, bytes_accessed=300_000_000, transcendentals=0),
+    )(partial, hid, gain, router, chosen)
+
+
+def sum_scratch(extent, rows, width):
+    return [
+        pltpu.VMEM((extent, 4, rows, width), BF),
+        pltpu.VMEM((extent, 4, rows, width), BF),
+        pltpu.VMEM((extent, 4, rows // 2, width), BF),
+        pltpu.VMEM((extent, 2, rows // 2, width), BF),
+        pltpu.VMEM((extent - 1, rows, width), BF),
+        pltpu.VMEM((extent - 1, rows, width), BF),
+    ]
+
+
+def turn_kernel(
+    extent,
+    partial,
+    middle,
+    teacher,
+    weight,
+    grad_output,
+    row_loss,
+    grads,
+    work,
+    core_in,
+    a_in,
+    b_in,
+    up_in,
+    down_in,
+    packet,
+    send_sem,
+    recv_sem,
+    local_sem,
+):
+    d, t = lax.axis_index("dp"), lax.axis_index("tensor")
+    rows, width = middle.shape
+    greet(plane_devices(d, t, extent))
+    wire, local = Wire(send_sem, recv_sem), Local(local_sem)
+    mine = sum_plane(
+        wire, local, d, t, extent, partial, work, core_in, a_in, b_in, up_in, down_in, rows // 2
+    )
+    everything = pl.ds(0, width)
+
+    def body(start):
+        part = pl.ds(start, 16)
+        output = middle[part] + own_sum(
+            mine, up_in.at[extent - 2], down_in.at[extent - 2], part, everything
+        )
+        mismatch = output - teacher[part].astype(F32)
+        scaled = mismatch * weight[part, 0:1]
+        grad_output[part] = scaled
+        packet[part] = scaled.astype(BF)
+        row_loss[part] = jnp.broadcast_to(
+            jnp.sum(scaled * mismatch, axis=-1, keepdims=True), (16, 128)
+        )
+
+    rows_loop(rows, 16, body)
+
+    def place(device, index):
+        return grads.at[device * extent + index]
+
+    copy = local.start(packet, place(d, t))
+    gather_plane(wire, d, t, extent, lambda: packet, place, rows // 2)
+    copy.wait()
+    wire.finish()
+
+
+def turn(extent, partial, middle, teacher, weight):
+    rows, width = middle.shape
+    return pl.pallas_call(
+        functools.partial(turn_kernel, extent),
+        out_shape=[
+            jax.ShapeDtypeStruct((rows, width), F32),
+            jax.ShapeDtypeStruct((rows, 128), F32),
+            jax.ShapeDtypeStruct((8 * extent, rows, width), BF),
+        ],
+        in_specs=[ANY, VM, VM, VM],
+        out_specs=[VM, VM, ANY],
+        scratch_shapes=sum_scratch(extent, rows, width)
+        + [pltpu.VMEM((rows, width), BF)]
+        + dma_pair(150)
+        + [pltpu.SemaphoreType.DMA((20,))],
+        compiler_params=kernel_params(4),
+        cost_estimate=pl.CostEstimate(flops=0, bytes_accessed=450_000_000, transcendentals=0),
+    )(partial, middle, teacher, weight)
+
+
+def leave_kernel(
+    extent,
+    partial,
+    middle,
+    grad_output,
+    gates,
+    chosen,
+    gain,
+    router_t,
+    grad_middle,
+    grad_logits,
+    gain_part,
+    grads,
+    work,
+    core_in,
+    a_in,
+    b_in,
+    up_in,
+    down_in,
+    packet,
+    extra,
+    send_sem,
+    recv_sem,
+    local_sem,
+):
+    d, t = lax.axis_index("dp"), lax.axis_index("tensor")
+    rows, width = middle.shape
+    greet(plane_devices(d, t, extent))
+    wire, local = Wire(send_sem, recv_sem), Local(local_sem)
+    mine = sum_plane(
+        wire, local, d, t, extent, partial, work, core_in, a_in, b_in, up_in, down_in, rows // 2
+    )
+    up_last, down_last = up_in.at[extent - 2], down_in.at[extent - 2]
+    coeff_grad = (
+        own_sum(mine, up_last, down_last, pl.ds(0, rows), pl.ds(width, 128)) * chosen[...]
+    )
+    lane = lax.broadcasted_iota(jnp.int32, coeff_grad.shape, 1)
+    probs = jnp.where(lane < 16, gates[...], 0.0)
+    coeff_grad = jnp.where(lane < 16, coeff_grad, 0.0)
+    logit_grad = probs * (coeff_grad - jnp.sum(coeff_grad * probs, axis=-1, keepdims=True))
+    grad_logits[...] = logit_grad
+    high = logit_grad.astype(BF)
+    low_part = (logit_grad - high.astype(F32)).astype(BF)
+    for begin in range(0, width, 512):
+        columns = slice(begin, begin + 512)
+        extra[:, columns] = jnp.dot(
+            high, router_t[:, columns], preferred_element_type=F32
+        ) + jnp.dot(low_part, router_t[:, columns], preferred_element_type=F32)
+    gain_part[...] = jnp.zeros(gain_part.shape, F32)
+
+    def body(start):
+        part = pl.ds(start, 16)
+        grad = own_sum(mine, up_last, down_last, part, pl.ds(0, width)) + extra[part]
+        value = middle[part]
+        inverse = lax.rsqrt(jnp.mean(value * value, axis=-1, keepdims=True) + EPSILON)
+        unit = value * inverse
+        product = grad * unit
+        gain_part[...] += product[0:8] + product[8:16]
+        scaled = grad * gain[...]
+        result = grad_output[part] + inverse * (
+            scaled - unit * jnp.mean(scaled * unit, axis=-1, keepdims=True)
+        )
+        grad_middle[part] = result
+        packet[part] = result.astype(BF)
+
+    rows_loop(rows, 16, body)
+
+    def place(index):
+        return grads.at[index]
+
+    copy = local.start(packet, place(t))
+    gather_line(wire, d, t, extent, lambda: packet, place, lambda *unused: None)
+    copy.wait()
+    wire.finish()
+
+
+def leave(extent, partial, middle, grad_output, gates, chosen, gain, router_t):
+    rows, width = middle.shape
+    return pl.pallas_call(
+        functools.partial(leave_kernel, extent),
+        out_shape=[
+            jax.ShapeDtypeStruct((rows, width), F32),
+            jax.ShapeDtypeStruct((rows, 128), F32),
+            jax.ShapeDtypeStruct((8, width), F32),
+            jax.ShapeDtypeStruct((extent, rows, width), BF),
+        ],
+        in_specs=[ANY, VM, VM, VM, VM, VM, VM],
+        out_specs=[VM, VM, VM, ANY],
+        scratch_shapes=sum_scratch(extent, rows, width + 128)
+        + [pltpu.VMEM((rows, width), BF), pltpu.VMEM((rows, width), F32)]
+        + dma_pair(80)
+        + [pltpu.SemaphoreType.DMA((20,))],
+        compiler_params=kernel_params(5),
+        cost_estimate=pl.CostEstimate(flops=0, bytes_accessed=350_000_000, transcendentals=0),
+    )(partial, middle, grad_output, gates, chosen, gain, router_t)
+
+
+def close_kernel(
+    extent,
+    partial,
+    grad_middle,
+    grad_qkv,
+    grad_o,
+    small,
+    gains,
+    grad_in,
+    qkv_out,
+    o_out,
+    small_out,
+    work,
+    up_in,
+    down_in,
+    q_work,
+    q_core,
+    q_a,
+    q_b,
+    o_work,
+    o_core,
+    o_a,
+    o_b,
+    small_in,
+    small_sum,
+    small_last,
+    send_sem,
+    recv_sem,
+    local_sem,
+):
+    d, t = lax.axis_index("dp"), lax.axis_index("tensor")
+    rows, width = grad_middle.shape
+    depth, o_width = qkv_out.shape[0], o_out.shape[1]
+    line_peers = [(d, (t + k) % extent) for k in range(1, extent)]
+    greet(
+        [(None, peer) for peer in line_peers]
+        + [(None, (flip(d, bits), t)) for bits in range(1, 8)]
+    )
+    wire, local = Wire(send_sem, recv_sem), Local(local_sem)
+    to_x, to_y, to_c = (flip(d, 2), t), (flip(d, 4), t), (flip(d, 1), t)
+
+    def slices(device):
+        start = pl.multiple_of(device * o_width, o_width)
+        return [
+            grad_qkv.at[pl.ds(device * depth, depth)],
+            grad_o.at[:, pl.ds(start, o_width)],
+        ]
+
+    turns = (3, 1, 2, 0)
+    c_slots, loads = {}, {}
+    work_load = local.start(partial, work)
+    small_slots = []
+    for k, peer in enumerate(line_peers):
+        slot = wire.slot()
+        small_slots.append(slot)
+        wire.start(
+            slot,
+            lambda k=k: small.at[(t + k + 1) % extent],
+            lambda k=k: small_in.at[k],
+            peer,
+        )
+    for i in turns:
+        sources = slices(flip(d, 1 + 2 * i))
+        c_slots[i] = [wire.slot(), wire.slot()]
+        wire.start(c_slots[i][0], lambda: sources[0], lambda i=i: q_core.at[i], to_c)
+        wire.start(c_slots[i][1], lambda: sources[1], lambda i=i: o_core.at[i], to_c)
+        mine = slices(flip(d, 2 * i))
+        loads[i] = [local.start(mine[0], q_work.at[i]), local.start(mine[1], o_work.at[i])]
+    work_load.wait()
+    line = LineSum(
+        wire, d, t, extent, lambda index: work.at[index], up_in, down_in, rows, 2
+    )
+    line.step(0)
+
+    def cut(ref, which):
+        half = ref.shape[0] // 2
+        return ref.at[pl.ds(which * half, half)]
+
+    a_slots, b_slots = {}, {}
+    routes_a = ((to_x, 3, 2, 0, 0), (to_y, 3, 1, 1, 1), (to_x, 1, 0, 0, 2), (to_y, 2, 0, 1, 3))
+    routes_b = ((to_y, 2, 0, 0), (to_x, 1, 1, 1))
+
+    def core_add(i):
+        for load in loads[i]:
+            load.wait()
+        wire.arrive(c_slots[i][0], lambda: q_core.at[i], to_c)
+        wire.arrive(c_slots[i][1], lambda: o_core.at[i], to_c)
+        add_into(q_work.at[i], q_core.at[i], q_work.shape[1])
+        add_into(o_work.at[i], o_core.at[i], o_work.shape[1])
+
+    def a_send(route):
+        device, source, target, which, row = route
+        a_slots[row] = [wire.slot(), wire.slot()]
+        wire.start(
+            a_slots[row][0], lambda: cut(q_work.at[source], which), lambda: q_a.at[row], device
+        )
+        wire.start(
+            a_slots[row][1], lambda: cut(o_work.at[source], which), lambda: o_a.at[row], device
+        )
+
+    core_add(3)
+    a_send(routes_a[0])
+    a_send(routes_a[1])
+    core_add(1)
+    a_send(routes_a[2])
+    core_add(2)
+    a_send(routes_a[3])
+    core_add(0)
+    line.step(1)
+    for device, source, target, which, row in routes_a:
+        wire.arrive(a_slots[row][0], lambda: q_a.at[row], device)
+        wire.arrive(a_slots[row][1], lambda: o_a.at[row], device)
+        add_into(cut(q_work.at[target], which), q_a.at[row], q_a.shape[1])
+        add_into(cut(o_work.at[target], which), o_a.at[row], o_a.shape[1])
+        if row < 2:
+            to, origin, part, b_row = routes_b[row]
+            b_slots[b_row] = [wire.slot(), wire.slot()]
+            wire.start(
+                b_slots[b_row][0],
+                lambda: cut(q_work.at[origin], part),
+                lambda: q_b.at[b_row],
+                to,
+            )
+            wire.start(
+                b_slots[b_row][1],
+                lambda: cut(o_work.at[origin], part),
+                lambda: o_b.at[b_row],
+                to,
+            )
+    for k, peer in enumerate(line_peers):
+        wire.arrive(small_slots[k], lambda k=k: small_in.at[k], peer)
+    total = small[t] + small_in[0]
+    for k in range(1, extent - 1):
+        total = total + small_in[k]
+    small_sum[:, 0:16] = total
+    small_sum[:, 16:24] = jnp.broadcast_to(gains[...][None], (8, 8, 128))
+    last_slots = {}
+    for bits in range(1, 8):
+        last_slots[bits] = wire.slot()
+        wire.start(
+            last_slots[bits],
+            lambda bits=bits: small_sum.at[flip(d, bits)],
+            lambda bits=bits: small_last.at[bits],
+            (flip(d, bits), t),
+        )
+    line.step(2)
+    for device, source, which, row in routes_b:
+        wire.arrive(b_slots[row][0], lambda: q_b.at[row], device)
+        wire.arrive(b_slots[row][1], lambda: o_b.at[row], device)
+        for kept, came, result in (
+            (cut(q_work.at[0], which), q_b.at[row], cut(qkv_out, which)),
+            (cut(o_work.at[0], which), o_b.at[row], cut(o_out, which)),
+        ):
+
+            def body(start, kept=kept, came=came, result=result):
+                part = pl.ds(start, 16)
+                result[part] = kept[part].astype(F32) + came[part].astype(F32)
+
+            rows_loop(kept.shape[0], 16, body)
+    line.last()
+    mine = work.at[t]
+
+    def body(start):
+        part = pl.ds(start, 16)
+        grad_in[part] = grad_middle[part] + own_sum(
+            mine, up_in.at[extent - 2], down_in.at[extent - 2], part, pl.ds(0, width)
+        )
+
+    rows_loop(rows, 16, body)
+    total = small_sum[d]
+    for bits in range(1, 8):
+        wire.arrive(
+            last_slots[bits], lambda bits=bits: small_last.at[bits], (flip(d, bits), t)
+        )
+        total = total + small_last[bits]
+    small_out[...] = total
+    wire.finish()
+
+
+def close(extent, partial, grad_middle, grad_qkv, grad_o, small, gains):
+    rows, width = grad_middle.shape
+    depth, q_width = grad_qkv.shape[0] // 8, grad_qkv.shape[1]
+    o_rows, o_width = grad_o.shape[0], grad_o.shape[1] // 8
+    scratch = [
+        pltpu.VMEM((extent, rows, width), BF),
+        pltpu.VMEM((extent - 1, rows, width), BF),
+        pltpu.VMEM((extent - 1, rows, width), BF),
+    ]
+    for tall, wide in ((depth, q_width), (o_rows, o_width)):
+        scratch += [
+            pltpu.VMEM((4, tall, wide), BF),
+            pltpu.VMEM((4, tall, wide), BF),
+            pltpu.VMEM((4, tall // 2, wide), BF),
+            pltpu.VMEM((2, tall // 2, wide), BF),
+        ]
+    scratch += [
+        pltpu.VMEM((extent - 1, 8, 16, 128), F32),
+        pltpu.VMEM((8, 24, 128), F32),
+        pltpu.VMEM((8, 24, 128), F32),
+    ]
+    return pl.pallas_call(
+        functools.partial(close_kernel, extent),
+        out_shape=[
+            jax.ShapeDtypeStruct((rows, width), F32),
+            jax.ShapeDtypeStruct((depth, q_width), F32),
+            jax.ShapeDtypeStruct((o_rows, o_width), F32),
+            jax.ShapeDtypeStruct((24, 128), F32),
+        ],
+        in_specs=[ANY, VM, ANY, ANY, VM, VM],
+        out_specs=[VM] * 4,
+        scratch_shapes=scratch + dma_pair(64) + [pltpu.SemaphoreType.DMA((16,))],
+        compiler_params=kernel_params(7),
+        cost_estimate=pl.CostEstimate(flops=0, bytes_accessed=150_000_000, transcendentals=0),
+    )(partial, grad_middle, grad_qkv, grad_o, small, gains)
+
+
+def assemble(pieces, in_weight, out_weight, sem, d):
+    copies = []
+    slab = pieces[0].shape[2]
+    for bits in range(8):
+        start = pl.multiple_of(flip(d, bits) * slab, slab)
+        for place in range(3):
+            for e in range(2):
+                if place < 2:
+                    column = (2 * place + e) * slab
+                    target = in_weight.at[pl.ds(start, slab), pl.ds(column, slab)]
+                else:
+                    target = out_weight.at[pl.ds(e * slab, slab), pl.ds(start, slab)]
+                copies.append(
+                    pltpu.make_async_copy(
+                        pieces[bits].at[place, e], target, sem.at[bits * 6 + place * 2 + e]
+                    )
+                )
+    for copy in copies:
+        copy.start()
+    for copy in copies:
+        copy.wait()
+
+
+def coefficients(columns, d, slab):
+    values = columns.astype(F32)
+    lane = lax.broadcasted_iota(jnp.int32, values.shape, 1)
+    parts = []
+    for e in range(2):
+        wanted = jnp.logical_or(lane == 2 * d + e, lane == 16 + 2 * d + e)
+        one = jnp.sum(jnp.where(wanted, values, 0.0), axis=-1, keepdims=True)
+        parts.append(jnp.broadcast_to(one, (values.shape[0], slab)))
+    return jnp.concatenate(parts, axis=1)
+
+
+def experts_kernel(tile, tokens, *rest):
+    pieces, (hidden, out, in_weight, out_weight, sem) = rest[:8], rest[8:]
+    d = lax.axis_index("dp")
+    width = out.shape[1]
+    units = out_weight.shape[0]
+
+    @pl.when(pl.program_id(0) == 0)
+    def _():
+        assemble(pieces, in_weight, out_weight, sem, d)
+
+    def body(start):
+        part = pl.ds(start, tile)
+        both_values = jnp.dot(
+            tokens[part, 0:width], in_weight[...], preferred_element_type=F32
+        )
+        hidden[part] = both_values.astype(BF)
+        gate_value, up_value = both_values[:, :units], both_values[:, units:]
+        coeff = coefficients(tokens[part, width : width + 128], d, units // 2)
+        active = (coeff * (gate_value * jax.nn.sigmoid(gate_value)) * up_value).astype(BF)
+        out[part] = jnp.dot(active, out_weight[...], preferred_element_type=F32).astype(BF)
+
+    rows_loop(tokens.shape[0], tile, body)
+
+
+def experts(tokens, pieces):
+    count, wide = tokens.shape
+    width = wide - 128
+    slab = pieces[0].shape[2]
+    block = 512
+    return pl.pallas_call(
+        functools.partial(experts_kernel, 256),
+        grid=(count // block,),
+        out_shape=[
+            jax.ShapeDtypeStruct((count, 4 * slab), BF),
+            jax.ShapeDtypeStruct((count, width), BF),
+        ],
+        in_specs=[pl.BlockSpec((block, wide), lambda i: (i, 0))] + [ANY] * 8,
+        out_specs=[
+            pl.BlockSpec((block, 4 * slab), lambda i: (i, 0)),
+            pl.BlockSpec((block, width), lambda i: (i, 0)),
+        ],
+        scratch_shapes=[
+            pltpu.VMEM((width, 4 * slab), BF),
+            pltpu.VMEM((2 * slab, width), BF),
+            pltpu.SemaphoreType.DMA((48,)),
+        ],
+        compiler_params=pltpu.CompilerParams(vmem_limit_bytes=VMEM_LIMIT),
+        cost_estimate=pl.CostEstimate(
+            flops=2 * count * width * 6 * slab, bytes_accessed=50_000_000, transcendentals=0
+        ),
+    )(tokens, *pieces)
+
+
+def experts_back_kernel(tile, grads, tokens, hidden, *rest):
+    pieces, (out, *others) = rest[:8], rest[8:]
+    results, (in_weight, out_weight, in_total, out_total, sem) = others[:8], others[8:]
+    d = lax.axis_index("dp")
+    width = grads.shape[1]
+    units, slab = out_weight.shape[0], out_weight.shape[0] // 2
+
+    @pl.when(pl.program_id(0) == 0)
+    def _():
+        assemble(pieces, in_weight, out_weight, sem, d)
+        in_total[...] = jnp.zeros(in_total.shape, F32)
+        out_total[...] = jnp.zeros(out_total.shape, F32)
+
+    def body(start):
+        part = pl.ds(start, tile)
+        incoming = grads[part]
+        grad_active = lax.dot_general(
+            incoming, out_weight[...], (((1,), (1,)), ((), ())), preferred_element_type=F32
+        )
+        gate_value = hidden[part, 0:units].astype(F32)
+        up_value = hidden[part, units : 2 * units].astype(F32)
+        coeff = coefficients(tokens[part, width : width + 128], d, slab)
+        sigmoid_value = jax.nn.sigmoid(gate_value)
+        silu_value = gate_value * sigmoid_value
+        inner = grad_active * coeff
+        direct = silu_value * up_value
+        active = (coeff * direct).astype(BF)
+        product = grad_active * direct
+        lane = lax.broadcasted_iota(jnp.int32, (tile, 128), 1)
+        sums = jnp.zeros((tile, 128), F32)
+        for e in range(2):
+            one = jnp.sum(product[:, e * slab : (e + 1) * slab], axis=-1, keepdims=True)
+            sums = sums + jnp.where(lane == 2 * d + e, one, 0.0)
+        grad_gate = inner * up_value * sigmoid_value * (1.0 + gate_value * (1.0 - sigmoid_value))
+        grad_hidden = jnp.concatenate([grad_gate, inner * silu_value], axis=1).astype(BF)
+        out[part, 0:width] = lax.dot_general(
+            grad_hidden, in_weight[...], (((1,), (1,)), ((), ())), preferred_element_type=F32
+        ).astype(BF)
+        out[part, width : width + 128] = sums.astype(BF)
+        out_total[...] += lax.dot_general(
+            active, incoming, (((0,), (0,)), ((), ())), preferred_element_type=F32
+        )
+        in_total[...] += lax.dot_general(
+            tokens[part, 0:width],
+            grad_hidden,
+            (((0,), (0,)), ((), ())),
+            preferred_element_type=F32,
+        )
+
+    rows_loop(grads.shape[0], tile, body)
+
+    @pl.when(pl.program_id(0) == pl.num_programs(0) - 1)
+    def _():
+        in_weight[...] = in_total[...].astype(BF)
+        out_weight[...] = out_total[...].astype(BF)
+        copies = []
+        for bits in range(8):
+            start = pl.multiple_of(flip(d, bits) * slab, slab)
+            for place in range(3):
+                for e in range(2):
+                    if place < 2:
+                        column = (2 * place + e) * slab
+                        source = in_weight.at[pl.ds(start, slab), pl.ds(column, slab)]
+                    else:
+                        source = out_weight.at[pl.ds(e * slab, slab), pl.ds(start, slab)]
+                    copies.append(
+                        pltpu.make_async_copy(
+                            source, results[bits].at[place, e], sem.at[bits * 6 + place * 2 + e]
+                        )
+                    )
+        for copy in copies:
+            copy.start()
+        for copy in copies:
+            copy.wait()
+
+
+def experts_back(grads, tokens, hidden, pieces):
+    count, wide = tokens.shape
+    width = wide - 128
+    slab = pieces[0].shape[2]
+    block = 256
+    return pl.pallas_call(
+        functools.partial(experts_back_kernel, 256),
+        grid=(count // block,),
+        out_shape=[jax.ShapeDtypeStruct((count, wide), BF)]
+        + [jax.ShapeDtypeStruct(pieces[0].shape, BF)] * 8,
+        in_specs=[
+            pl.BlockSpec((block, width), lambda i: (i, 0)),
+            pl.BlockSpec((block, wide), lambda i: (i, 0)),
+            pl.BlockSpec((block, 4 * slab), lambda i: (i, 0)),
+        ]
+        + [ANY] * 8,
+        out_specs=[pl.BlockSpec((block, wide), lambda i: (i, 0))] + [ANY] * 8,
+        scratch_shapes=[
+            pltpu.VMEM((width, 4 * slab), BF),
+            pltpu.VMEM((2 * slab, width), BF),
+            pltpu.VMEM((width, 4 * slab), F32),
+            pltpu.VMEM((2 * slab, width), F32),
+            pltpu.SemaphoreType.DMA((48,)),
+        ],
+        compiler_params=pltpu.CompilerParams(vmem_limit_bytes=VMEM_LIMIT),
+        cost_estimate=pl.CostEstimate(
+            flops=2 * count * width * 12 * slab, bytes_accessed=80_000_000, transcendentals=0
+        ),
+    )(grads, tokens, hidden, *pieces)
+
+
+def spread_kernel(*refs):
+    pieces, outs = refs[:8], refs[8:]
+    d = lax.axis_index("dp")
+    for bits in range(8):
+        first = 2 * flip(d, bits)
+        for place in range(3):
+            for e in range(2):
+                outs[place][first + e] = pieces[bits][place, e].astype(F32)
+
+
+def spread(pieces):
+    shape = (16,) + pieces[0].shape[2:]
+    return pl.pallas_call(
+        spread_kernel,
+        out_shape=[jax.ShapeDtypeStruct(shape, F32)] * 3,
+        in_specs=[VM] * 8,
+        out_specs=[VM] * 3,
+        compiler_params=pltpu.CompilerParams(vmem_limit_bytes=VMEM_LIMIT),
+        cost_estimate=pl.CostEstimate(flops=0, bytes_accessed=20_000_000, transcendentals=0),
+    )(*pieces)
+
+
+def exchange(value, bits):
+    if bits == 0:
+        return value
+    return lax.ppermute(value, "dp", [(i, i ^ bits) for i in range(8)])
+
+
+def per_device_block(
+    hidden_in,
+    teacher,
+    lengths,
+    routes,
+    attn_norm_gain,
+    ffn_norm_gain,
+    q_weight,
+    k_weight,
+    v_weight,
+    q_gain,
+    k_gain,
+    o_weight,
+    router_weight,
+    gate_weight,
+    up_weight,
+    down_weight,
+):
+    dp_count = lax.axis_size("dp")
+    extent = lax.axis_size("tensor")
+    d = lax.axis_index("dp")
+    t = lax.axis_index("tensor")
+    rows, width = hidden_in.shape
+    seq_len = rows * extent
+    all_tokens = seq_len * dp_count
+    length = lengths[d]
+    total_count = jnp.sum(lengths).astype(F32)
+    attn_gain = attn_norm_gain.astype(F32)
+    ffn_gain = ffn_norm_gain.astype(F32)[None, :]
+    root_size = math.sqrt(HD)
+    expert_count = router_weight.shape[1]
+    head_width = q_gain.shape[1]
+    local_heads = q_gain.shape[0]
+    columns = local_heads * HD
+
+    qkv_own = jnp.concatenate([q_weight, k_weight, v_weight], axis=1)
+    gains_own = lax.dynamic_update_slice(
+        jnp.zeros((2 * local_heads, HD), F32),
+        jnp.concatenate([q_gain, k_gain], axis=0).astype(F32),
+        (0, d * head_width),
+    )
+    hidden_bf, qkv_full, o_full, gains_all, *sent = fetch(
+        extent, hidden_in, qkv_own, o_weight, gains_own, gate_weight, up_weight, down_weight
+    )
+    pieces = [exchange(piece, bits) for bits, piece in enumerate(sent)]
+    gains_full = jnp.sum(gains_all, axis=0)
+    query_gain = gains_full[:local_heads].reshape(-1)
+    key_gain = gains_full[local_heads:].reshape(-1)
+
+    hidden_all = hidden_bf.astype(F32)
+    inverse_one = inverse_rms(hidden_all)
+    unit_one = hidden_all * inverse_one
+    normed = (unit_one * attn_gain).astype(BF)
+    qkv = jnp.dot(normed, qkv_full, preferred_element_type=F32)
+    query_raw, key_raw = qkv[:, :columns], qkv[:, columns : 2 * columns]
+    value_low = qkv[:, 2 * columns :].astype(BF)
+    squares = jnp.stack(
+        [jnp.sum(query_raw * query_raw, axis=1), jnp.sum(key_raw * key_raw, axis=1)]
+    )
+    squares = line_total(extent, 2, squares.reshape(-1, 128)).reshape(2, seq_len)
+    query_inv = lax.rsqrt(squares[0] / width + EPSILON)[:, None]
+    key_inv = lax.rsqrt(squares[1] / width + EPSILON)[:, None]
+    query_unit = query_raw * query_inv
+    key_unit = key_raw * key_inv
+    positions = jnp.arange(seq_len)
+    frequency = THETA ** (-jnp.arange(HD // 2).astype(F32) / (HD // 2))
+    angles = positions.astype(F32)[:, None] * frequency[None, :]
+    cosine = jnp.cos(angles)[:, None, :]
+    sinus_table = jnp.sin(angles)[:, None, :]
+    queries = rotate(
+        (query_unit * query_gain).reshape(seq_len, local_heads, HD), cosine, sinus_table, 1.0
+    ).astype(BF)
+    key_rows = rotate(
+        (key_unit * key_gain).reshape(seq_len, local_heads, HD), cosine, sinus_table, 1.0
+    ).astype(BF)
+    value_rows = value_low.reshape(seq_len, local_heads, HD)
+    scores = (
+        jnp.einsum("qhd,khd->hqk", queries, key_rows, preferred_element_type=F32) / root_size
+    )
+    allowed = (positions[None, :] <= positions[:, None]) & (positions[None, :] < length)
+    scores = jnp.where(allowed[None], scores, -1e30)
+    row_top = jnp.max(scores, axis=-1, keepdims=True)
+    exponent = jnp.exp(scores - row_top)
+    probs_float = exponent / jnp.sum(exponent, axis=-1, keepdims=True)
+    probs_low = probs_float.astype(BF)
+    mixed = (
+        jnp.einsum("hqk,khd->qhd", probs_low, value_rows, preferred_element_type=F32)
+        .astype(BF)
+        .reshape(seq_len, columns)
+    )
+    attn_partial = jnp.dot(mixed, o_full, preferred_element_type=F32).astype(BF)
+
+    lane = jnp.arange(128)
+    lane_expert = jnp.where(lane < 2 * expert_count, lane % expert_count, -1)
+    routes_own = lax.dynamic_slice_in_dim(routes, t * rows, rows, 0)
+    chosen = jnp.any(routes_own[:, :, None] == lane_expert[None, None, :], axis=1).astype(F32)
+    blank = jnp.zeros((width, 128 - 2 * expert_count), BF)
+    router_wide = jnp.concatenate([router_weight, router_weight, blank], axis=1)
+    router_t = jnp.concatenate(
+        [router_weight.T, jnp.zeros((128 - expert_count, width), BF)], axis=0
+    )
+    middle, gates, ffn_own, tokens = enter(
+        extent,
+        attn_partial.reshape(extent, rows, width),
+        hidden_in,
+        ffn_gain,
+        router_wide,
+        chosen,
+    )
+    tokens = tokens.reshape(all_tokens, width + 128)
+    hidden, expert_partial = experts(tokens, pieces)
+    own_positions = t * rows + jnp.arange(rows)
+    row_scale = jnp.where(own_positions < length, all_tokens / total_count, 0.0)
+    grad_output, row_loss, grads = turn(
+        extent,
+        expert_partial.reshape(dp_count * extent, rows, width),
+        middle,
+        teacher,
+        jnp.broadcast_to(row_scale[:, None], (rows, 128)),
+    )
+    loss_own = jnp.sum(row_loss[:, 0]) / (2.0 * width * all_tokens)
+    ffn_grad_partial, *expert_grads = experts_back(
+        grads.reshape(all_tokens, width), tokens, hidden, pieces
+    )
+    expert_grads = [exchange(piece, bits) for bits, piece in enumerate(expert_grads)]
+    grad_middle, grad_logits, ffn_gain_part, attn_grad_rows = leave(
+        extent,
+        ffn_grad_partial.reshape(dp_count * extent, rows, width + 128),
+        middle,
+        grad_output,
+        gates,
+        chosen,
+        ffn_gain,
+        router_t,
+    )
+    attn_grad_rows = attn_grad_rows.reshape(seq_len, width)
+    router_part = jnp.einsum(
+        "sd,se->de",
+        ffn_own,
+        grad_logits[:, :expert_count],
+        precision=HIGHEST,
+        preferred_element_type=F32,
+    )
+    grad_o = jnp.einsum("sa,sb->ab", mixed, attn_grad_rows, preferred_element_type=F32)
+    grad_mixed = (
+        jnp.einsum("sb,ab->sa", attn_grad_rows, o_full, preferred_element_type=F32)
+        .astype(BF)
+        .reshape(seq_len, local_heads, HD)
+    )
+    value_grad = jnp.einsum("hqk,qhd->khd", probs_low, grad_mixed, preferred_element_type=F32)
+    grad_weights = jnp.einsum(
+        "qhd,khd->hqk", grad_mixed, value_rows, preferred_element_type=F32
+    )
+    grad_scores = (
+        probs_float
+        * (grad_weights - jnp.sum(grad_weights * probs_float, axis=-1, keepdims=True))
+    ).astype(BF)
+    query_grad_rot = (
+        jnp.einsum("hqk,khd->qhd", grad_scores, key_rows, preferred_element_type=F32) / root_size
+    )
+    key_grad_rot = (
+        jnp.einsum("hqk,qhd->khd", grad_scores, queries, preferred_element_type=F32) / root_size
+    )
+    query_grad = rotate(query_grad_rot, cosine, sinus_table, -1.0).reshape(seq_len, columns)
+    key_grad = rotate(key_grad_rot, cosine, sinus_table, -1.0).reshape(seq_len, columns)
+    query_scaled = query_grad * query_gain
+    key_scaled = key_grad * key_gain
+    qgain_part = jnp.sum(query_grad * query_unit, axis=0)
+    kgain_part = jnp.sum(key_grad * key_unit, axis=0)
+    dots = jnp.concatenate(
+        [
+            jnp.sum(query_scaled * query_unit, axis=1),
+            jnp.sum(key_scaled * key_unit, axis=1),
+            jnp.full((1024,), loss_own, F32),
+        ]
+    )
+    dots = line_total(extent, 6, dots.reshape(-1, 128)).reshape(-1)
+    query_dot, key_dot, loss_group = (
+        dots[:seq_len],
+        dots[seq_len : 2 * seq_len],
+        dots[2 * seq_len : 2 * seq_len + 1],
+    )
+    query_raw_grad = query_inv * (query_scaled - query_unit * (query_dot / width)[:, None])
+    key_raw_grad = key_inv * (key_scaled - key_unit * (key_dot / width)[:, None])
+    raw_grad = jnp.concatenate(
+        [
+            query_raw_grad.astype(BF),
+            key_raw_grad.astype(BF),
+            value_grad.reshape(seq_len, columns).astype(BF),
+        ],
+        axis=1,
+    )
+    grad_qkv = jnp.einsum("sd,sa->da", normed, raw_grad, preferred_element_type=F32)
+    normed_grad = jnp.einsum("sa,da->sd", raw_grad, qkv_full, preferred_element_type=F32)
+    attn_gain_part = jnp.sum(normed_grad * unit_one, axis=0)
+    input_part = norm_backward(normed_grad, unit_one, inverse_one, attn_gain).astype(BF)
+
+    split = width // (dp_count * extent)
+    small = jnp.concatenate(
+        [
+            jnp.concatenate(
+                [
+                    attn_gain_part.reshape(dp_count, extent, 1, split),
+                    jnp.sum(ffn_gain_part, axis=0).reshape(dp_count, extent, 1, split),
+                ],
+                axis=3,
+            ),
+            router_part.reshape(dp_count, extent, split * expert_count // 128, 128),
+            jnp.zeros((dp_count, extent, 15 - split * expert_count // 128, 128), F32),
+        ],
+        axis=2,
+    ).transpose(1, 0, 2, 3)
+    gains_part = jnp.concatenate([qgain_part, kgain_part]).reshape(2 * local_heads, HD)
+    grad_in, qkv_out, o_out, small_out = close(
+        extent,
+        input_part.reshape(extent, rows, width),
+        grad_middle,
+        grad_qkv.astype(BF),
+        grad_o.astype(BF),
+        small,
+        gains_part,
+    )
+    grad_gate, grad_up, grad_down = spread(expert_grads)
+    router_out = small_out[1 : 1 + split * expert_count // 128].reshape(split, expert_count)
+    gain_out = lax.dynamic_slice(small_out, (16, d * head_width), (2 * local_heads, head_width))
+    return (
+        loss_group,
+        grad_in,
+        small_out[0, :split],
+        small_out[0, split : 2 * split],
+        qkv_out[:, :columns],
+        qkv_out[:, columns : 2 * columns],
+        qkv_out[:, 2 * columns :],
+        gain_out[:local_heads],
+        gain_out[local_heads:],
+        o_out,
+        router_out,
+        grad_gate,
+        grad_up,
+        grad_down,
+    )
+
+
 def solution(mesh):
     placed = (
         P(("dp", "tensor"), None),
@@ -499,8 +2034,9 @@
         P(None, "dp", "tensor"),
         P(None, "tensor", "dp"),
     )
+    block = mesh.shape["dp"] == 8 and mesh.shape["tensor"] == 4
     return jax.shard_map(
-        per_device,
+        per_device_block if block else per_device,
         mesh=mesh,
         in_specs=placed,
         out_specs=(

time: 1860 us -> 844 us (0.45)
  waiting for transfers between devices: 1070 us -> 61.4 us
  Pallas kernels: 0 us -> 642 us
  other arithmetic: 303 us -> 36.8 us
  matrix products: 247 us -> 45.9 us
  local copies, waits for them, and re-layouts: 150 us -> 33.2 us
  blocking collectives: 70.4 us -> 0 us
    pallas_call x0 -> x10, Pallas kernels: none -> 642 us  [the longest x1 160 us: turn(): pl.pallas_call(functools.partial(turn_kernel, extent), out_shape=[jax.Sha...]
    reduce_scatter x12 -> x0, waiting for transfers between devices: 621 us -> none  [the longest x1 117 us: per_device(): lax.psum_scatter(jnp.concatenate(down_grads, axis=0).astype(jnp.bfloat16)...]
    all_gather x11 -> x0, waiting for transfers between devices: 412 us -> none  [the longest x1 89.1 us: fetch_experts(): lax.all_gather(down_weight, 'dp', axis=2, tiled=True)]
    dot_general x57 -> x12, matrix products: 247 us -> 39.7 us  [the longest x1 7.97 us: per_device_block(): jnp.einsum('sa,da->sd', raw_grad, qkv_full, preferred_element_type=F32)]
    scatter-add x8 -> x0, other arithmetic: 200 us -> none  [the longest x4 100 us: per_device(): expert_running.at[sources[turn_index].reshape(-1)]]
    gather x9 -> x0, local copies, waits for them, and re-layouts: 70.4 us -> none  [the longest x4 23.9 us: per_device(): incoming = grad_padded[source_rows]]
    ppermute x0 -> x14, waiting for transfers between devices: none -> 61.4 us  [exchange(): return lax.ppermute(value, 'dp', [(i, i ^ bits) for i in range(8)])]
    unnamed x29 -> x0, waiting for transfers between devices: 35.5 us -> none
  transfers between devices with their start and end apart: 26 -> 14, of which waited for: 21 -> 3; matrix products, arithmetic and copies ran while one was open for 15% -> 8% of each run, Pallas kernels for 0% -> 22%
where the time goes in v1:
time: 844 us; the launch traced here: 834 us
  Pallas kernels  642 us (76%)
  waiting for transfers between devices  61.4 us (7%)
  matrix products  45.9 us (5%)
  other arithmetic  36.8 us (4%)
  local copies, waits for them, and re-layouts  33.2 us (4%)
  starting transfers between devices  11.4 us (1%)
    pallas_call x1, Pallas kernels, turn(): pl.pallas_call(functools.partial(turn_kernel, extent), out_shape=[jax.Sha...  160 us
    pallas_call x1, Pallas kernels, leave(): pl.pallas_call(functools.partial(leave_kernel, extent), out_shape=[jax.Sh...  129 us
    pallas_call x1, Pallas kernels, enter(): pl.pallas_call(functools.partial(enter_kernel, extent), out_shape=[jax.Sh...  122 us
    pallas_call x1, Pallas kernels, experts_back(): pl.pallas_call(functools.partial(experts_back_kernel, 256), grid=(count /...  71.5 us
    ppermute x14, waiting for transfers between devices, exchange(): return lax.ppermute(value, 'dp', [(i, i ^ bits) for i in range(8)])  61.4 us
    pallas_call x1, Pallas kernels, close(): pl.pallas_call(functools.partial(close_kernel, extent), out_shape=[jax.Sh...  51 us
    pallas_call x1, Pallas kernels, fetch(): pl.pallas_call(functools.partial(fetch_kernel, extent), out_shape=[jax.Sh...  50.1 us
    pallas_call x1, Pallas kernels, experts(): pl.pallas_call(functools.partial(experts_kernel, 256), grid=(count // blo...  36.8 us
  transfers between devices with their start and end apart: 14, of which 3 were waited for; matrix products, arithmetic and copies ran while one was open for 8% of the time, Pallas kernels for 22%

profile of v1, /device:TPU:0, one launch (start us, length us, event | category | flops | bytes accessed | tf_op | source)
XLA Modules:
  0.0 834.1 jit_solution(3959661005287368594)
XLA Ops:
  4.1 50.1 %shard_map.263 = (bf16[512,2048]{1,0:T(8,128)(2,1)}, bf16[2048,1536]{1,0:T(8,128)(2,1)}, bf16[512,2048]{1,0:T(8,128)(2,1)}, f32[8,8,128]{2,1,0:T(8,128)}, bf16[3...) custom-call(bf16[128,2048]{1,0:T(8,128)(2,1)} %hid.3, ...), custom_call_target="tpu_custom_call" | custom-call | bytes 100000000 | tf_op jit(solution)/shard_map/pallas_call | solution.py:1020
  63.2 6.3 fusion.27
  70.3 6.7 shard_map.264
  82.5 3.5 fusion.44
  88.6 3.5 fusion.45
  94.5 3.9 subtract_convert_fusion.1
  98.4 6.2 fusion.47
  119.2 122.3 %shard_map.265 = (f32[128,2048]{1,0:T(8,128)}, f32[128,128]{1,0:T(8,128)}, bf16[128,2048]{1,0:T(8,128)(2,1)}, bf16[32,128,2176]{2,1,0:T(8,128)(2,1)}) custom-call(bf16[4,128,2048]{2,1,0:T(8,128)(2,1)} %bitcast.101, bf16[128,2048]{1,0:T(8,128)(2,1)} %hid.3, f32[1,2048]{1,0:T(1,128)} %bitcast.104, bf16[2048,128]{1,0:T(8,128)(2,1)} %maximum_maximum_fusion.router, ...), custom_call_target="tpu_custom_call" | custom-call | bytes 300000000 | tf_op jit(solution)/shard_map/pallas_call | solution.py:1133
  242.2 36.8 %shard_map.266 = (bf16[4096,1024]{1,0:T(8,128)(2,1)}, bf16[4096,2048]{1,0:T(8,128)(2,1)}) custom-call(bf16[4096,2176]{1,0:T(8,128)(2,1)} %bitcast.111, bf16[3,2,256,256]{3,2,1,0:T(8,128)(2,1)} %get-tuple-element.60.rest_0_, bf16[3,2,256,256]{3,2,1,0:T(8,128)(2,1)} %collective-permute-done.rest_1_, bf16[3,2,256,256]{3,2,1,0:T(8,128)(2,1)} %collective-permute-done.1.rest_2_, ...), custom_call_target="tpu_custom_call" | custom-call | flops 25769803776 | bytes 50000000 | tf_op jit(solution)/shard_map/pallas_call | solution.py:1616
  279.8 159.7 %shard_map.267 = (f32[128,2048]{1,0:T(8,128)}, f32[128,128]{1,0:T(8,128)}, bf16[32,128,2048]{2,1,0:T(8,128)(2,1)}) custom-call(bf16[32,128,2048]{2,1,0:T(8,128)(2,1)} %bitcast.99, f32[128,2048]{1,0:T(8,128)} %get-tuple-element.69.middle, bf16[128,2048]{1,0:T(8,128)(2,1)} %teacher.1, f32[128,128]{1,0:T(8,128)} %broadcast_in_dim.78.weight), custom_call_target="tpu_custom_call" | custom-call | bytes 450000000 | tf_op jit(solution)/shard_map/pallas_call | solution.py:1222
  439.5 71.5 %shard_map.268 = (bf16[4096,2176]{1,0:T(8,128)(2,1)}, bf16[3,2,256,256]{3,2,1,0:T(8,128)(2,1)}, bf16[3,2,256,256]{3,2,1,0:T(8,128)(2,1)}, bf16[3,2,256,256]{3,2,...) custom-call(bf16[4096,2048]{1,0:T(8,128)(2,1)} %bitcast.113, ...), custom_call_target="tpu_custom_call" | custom-call | flops 51539607552 | bytes 80000000 | tf_op jit(solution)/shard_map/pallas_call | solution.py:1721
  511.0 129.2 %shard_map.269 = (f32[128,2048]{1,0:T(8,128)}, f32[128,128]{1,0:T(8,128)}, f32[8,2048]{1,0:T(8,128)}, bf16[4,128,2048]{2,1,0:T(8,128)(2,1)}) custom-call(bf16[32,128,2176]{2,1,0:T(8,128)(2,1)} %bitcast.98, f32[128,2048]{1,0:T(8,128)} %get-tuple-element.69.middle, f32[128,2048]{1,0:T(8,128)} %get-tuple-element.73.grad_output, ...), custom_call_target="tpu_custom_call" | custom-call | bytes 350000000 | tf_op jit(solution)/shard_map/pallas_call | solution.py:1318
  640.3 3.7 convolution_convert_fusion.3
  652.7 2.9 multiply_subtract_fusion
  658.2 6.8 shard_map.270
  667.8 3.3 multiply_convert_fusion.2
  671.2 8.0 fusion.10
  679.2 5.8 convolution_convert_fusion.grad_qkv
  693.6 4.5 fusion.9
  698.1 51.0 %shard_map.271 = (f32[128,2048]{1,0:T(8,128)}, f32[256,1536]{1,0:T(8,128)}, f32[512,256]{1,0:T(8,128)}, f32[24,128]{1,0:T(8,128)}) custom-call(bf16[4,128,2048]{2,1,0:T(8,128)(2,1)} %bitcast.100, f32[128,2048]{1,0:T(8,128)} %get-tuple-element.77.grad_middle, bf16[2048,1536]{1,0:T(8,128)(2,1)} %convolution_convert_fusion.grad_qkv, ...), custom_call_target="tpu_custom_call" | custom-call | bytes 150000000 | tf_op jit(solution)/shard_map/pallas_call | solution.py:1537
  760.3 10.3 %collective-permute-done.9.refs_3_ = bf16[3,2,256,256]{3,2,1,0:T(8,128)(2,1)S(1)} collective-permute-done((bf16[3,2,256,256]{3,2,1,0:T(8,128)(2,1)}, bf16[3,2,256,256]{3,2,1,0:T(8,128)(2,1)S(1)}, u32[]{:S(2)}, u32[]{:S(2)}) %collective-permute-start.9) | collective-permute-done | bytes 786464 | tf_op jit(solution)/shard_map/ppermute | solution.py:1772
  770.5 34.5 %collective-permute-done.10.refs_4_ = bf16[3,2,256,256]{3,2,1,0:T(8,128)(2,1)S(1)} collective-permute-done((bf16[3,2,256,256]{3,2,1,0:T(8,128)(2,1)}, bf16[3,2,256,256]{3,2,1,0:T(8,128)(2,1)S(1)}, u32[]{:S(2)}, u32[]{:S(2)}) %collective-permute-start.10) | collective-permute-done | bytes 786464 | tf_op jit(solution)/shard_map/ppermute | solution.py:1772
  805.0 16.7 %collective-permute-done.11.refs_5_ = bf16[3,2,256,256]{3,2,1,0:T(8,128)(2,1)S(1)} collective-permute-done((bf16[3,2,256,256]{3,2,1,0:T(8,128)(2,1)}, bf16[3,2,256,256]{3,2,1,0:T(8,128)(2,1)S(1)}, u32[]{:S(2)}, u32[]{:S(2)}) %collective-permute-start.11) | collective-permute-done | bytes 786464 | tf_op jit(solution)/shard_map/ppermute | solution.py:1772
  823.8 8.3 shard_map.272
  (194 shorter events, 75.8 us)
Async XLA Ops:
  0.6 93.2 %copy-start = (s32[512,8]{0,1:T(8,128)S(1)}, s32[512,8]{0,1:T(8,128)}, u32[]{:S(2)}) copy-start(s32[512,8]{0,1:T(8,128)} %param.19) | copy-start | bytes 49156
  4.1 54.1 %copy-start.46 = (s32[8]{0:T(128)S(1)}, s32[8]{0:T(128)}, u32[]{:S(2)}) copy-start(s32[8]{0:T(128)} %param.18) | copy-start | bytes 100
  4.1 56.2 %copy-start.42 = (bf16[2048]{0:T(1024)(128)(2,1)S(1)}, bf16[2048]{0:T(1024)(128)(2,1)}, u32[]{:S(2)}) copy-start(bf16[2048]{0:T(1024)(128)(2,1)} %param.20) | copy-start | bytes 12292
  54.2 59.4 %collective-permute-start = (bf16[3,2,256,256]{3,2,1,0:T(8,128)(2,1)}, bf16[3,2,256,256]{3,2,1,0:T(8,128)(2,1)}, u32[]{:S(2)}, u32[]{:S(2)}) collective-permute-start(bf16[3,2,256,256]{3,2,1,0:T(8,128)(2,1)} %get-tuple-element.61), channel_id=1, source_target_pairs={{0,4},{4,0},{8,12},{12,8},{16,20},{20,16},{24,28},{28,24},{1,5},{5... | collective-permute-start | bytes 2359304 | tf_op jit(solution)/shard_map/ppermute | solution.py:1772
  54.7 60.8 %collective-permute-start.1 = (bf16[3,2,256,256]{3,2,1,0:T(8,128)(2,1)}, bf16[3,2,256,256]{3,2,1,0:T(8,128)(2,1)}, u32[]{:S(2)}, u32[]{:S(2)}) collective-permute-start(bf16[3,2,256,256]{3,2,1,0:T(8,128)(2,1)} %get-tuple-element.62), channel_id=1, source_target_pairs={{0,8},{4,12},{8,0},{12,4},{16,24},{20,28},{24,16},{28,20},{1,9},{5... | collective-permute-start | bytes 2359304 | tf_op jit(solution)/shard_map/ppermute | solution.py:1772
  55.6 186.6 %collective-permute-start.2 = (bf16[3,2,256,256]{3,2,1,0:T(8,128)(2,1)}, bf16[3,2,256,256]{3,2,1,0:T(8,128)(2,1)}, u32[]{:S(2)}, u32[]{:S(2)}) collective-permute-start(bf16[3,2,256,256]{3,2,1,0:T(8,128)(2,1)} %get-tuple-element.63), channel_id=1, source_target_pairs={{0,12},{4,8},{8,4},{12,0},{16,28},{20,24},{24,20},{28,16},{1,13},{... | collective-permute-start | bytes 2359304 | tf_op jit(solution)/shard_map/ppermute | solution.py:1772
  56.2 186.0 %collective-permute-start.3 = (bf16[3,2,256,256]{3,2,1,0:T(8,128)(2,1)}, bf16[3,2,256,256]{3,2,1,0:T(8,128)(2,1)}, u32[]{:S(2)}, u32[]{:S(2)}) collective-permute-start(bf16[3,2,256,256]{3,2,1,0:T(8,128)(2,1)} %get-tuple-element.64), channel_id=1, source_target_pairs={{0,16},{4,20},{8,24},{12,28},{16,0},{20,4},{24,8},{28,12},{1,17},{... | collective-permute-start | bytes 2359304 | tf_op jit(solution)/shard_map/ppermute | solution.py:1772
  57.4 184.8 %collective-permute-start.4 = (bf16[3,2,256,256]{3,2,1,0:T(8,128)(2,1)}, bf16[3,2,256,256]{3,2,1,0:T(8,128)(2,1)}, u32[]{:S(2)}, u32[]{:S(2)}) collective-permute-start(bf16[3,2,256,256]{3,2,1,0:T(8,128)(2,1)} %get-tuple-element.65), channel_id=1, source_target_pairs={{0,20},{4,16},{8,28},{12,24},{16,4},{20,0},{24,12},{28,8},{1,21},{... | collective-permute-start | bytes 2359304 | tf_op jit(solution)/shard_map/ppermute | solution.py:1772
  60.3 9.1 %copy-start.27 = (f32[2048]{0:T(1024)}, f32[2048]{0:T(1024)S(1)}, u32[]{:S(2)}) copy-start(f32[2048]{0:T(1024)S(1)} %convert_element_type.140) | copy-start | bytes 24580
  98.4 9.0 %copy-start.38 = (s32[128,8]{0,1:T(8,128)S(1)}, s32[128,8]{0,1:T(8,128)}, u32[]{:S(2)}) copy-start(s32[128,8]{0,1:T(8,128)} %constant_dynamic-slice_fusion.1) | copy-start | bytes 12292
  113.6 128.6 %collective-permute-start.5 = (bf16[3,2,256,256]{3,2,1,0:T(8,128)(2,1)}, bf16[3,2,256,256]{3,2,1,0:T(8,128)(2,1)}, u32[]{:S(2)}, u32[]{:S(2)}) collective-permute-start(bf16[3,2,256,256]{3,2,1,0:T(8,128)(2,1)} %get-tuple-element.66), channel_id=1, source_target_pairs={{0,24},{4,28},{8,16},{12,20},{16,8},{20,12},{24,0},{28,4},{1,25},{... | collective-permute-start | bytes 2359304 | tf_op jit(solution)/shard_map/ppermute | solution.py:1772
  115.5 126.7 %collective-permute-start.6 = (bf16[3,2,256,256]{3,2,1,0:T(8,128)(2,1)}, bf16[3,2,256,256]{3,2,1,0:T(8,128)(2,1)}, u32[]{:S(2)}, u32[]{:S(2)}) collective-permute-start(bf16[3,2,256,256]{3,2,1,0:T(8,128)(2,1)} %get-tuple-element.67), channel_id=1, source_target_pairs={{0,28},{4,24},{8,20},{12,16},{16,12},{20,8},{24,4},{28,0},{1,29},{... | collective-permute-start | bytes 2359304 | tf_op jit(solution)/shard_map/ppermute | solution.py:1772
  690.0 62.9 %collective-permute-start.7 = (bf16[3,2,256,256]{3,2,1,0:T(8,128)(2,1)}, bf16[3,2,256,256]{3,2,1,0:T(8,128)(2,1)S(1)}, u32[]{:S(2)}, u32[]{:S(2)}) collective-permute-start(bf16[3,2,256,256]{3,2,1,0:T(8,128)(2,1)} %get-tuple-element.86), channel_id=1, source_target_pairs={{0,4},{4,0},{8,12},{12,8},{16,20},{20,16},{24,28},{28,24},{1,5},{5... | collective-permute-start | bytes 2359304 | tf_op jit(solution)/shard_map/ppermute | solution.py:1772
  690.0 64.3 %collective-permute-start.8 = (bf16[3,2,256,256]{3,2,1,0:T(8,128)(2,1)}, bf16[3,2,256,256]{3,2,1,0:T(8,128)(2,1)}, u32[]{:S(2)}, u32[]{:S(2)}) collective-permute-start(bf16[3,2,256,256]{3,2,1,0:T(8,128)(2,1)} %get-tuple-element.87), channel_id=1, source_target_pairs={{0,8},{4,12},{8,0},{12,4},{16,24},{20,28},{24,16},{28,20},{1,9},{5... | collective-permute-start | bytes 2359304 | tf_op jit(solution)/shard_map/ppermute | solution.py:1772
  750.5 20.0 %collective-permute-start.9 = (bf16[3,2,256,256]{3,2,1,0:T(8,128)(2,1)}, bf16[3,2,256,256]{3,2,1,0:T(8,128)(2,1)S(1)}, u32[]{:S(2)}, u32[]{:S(2)}) collective-permute-start(bf16[3,2,256,256]{3,2,1,0:T(8,128)(2,1)} %get-tuple-element.88), channel_id=1, source_target_pairs={{0,12},{4,8},{8,4},{12,0},{16,28},{20,24},{24,20},{28,16},{1,13},{... | collective-permute-start | bytes 2359304 | tf_op jit(solution)/shard_map/ppermute | solution.py:1772
  750.7 54.3 %collective-permute-start.10 = (bf16[3,2,256,256]{3,2,1,0:T(8,128)(2,1)}, bf16[3,2,256,256]{3,2,1,0:T(8,128)(2,1)S(1)}, u32[]{:S(2)}, u32[]{:S(2)}) collective-permute-start(bf16[3,2,256,256]{3,2,1,0:T(8,128)(2,1)} %get-tuple-element.89), channel_id=1, source_target_pairs={{0,16},{4,20},{8,24},{12,28},{16,0},{20,4},{24,8},{28,12},{1,17},{... | collective-permute-start | bytes 2359304 | tf_op jit(solution)/shard_map/ppermute | solution.py:1772
  751.4 70.2 %collective-permute-start.11 = (bf16[3,2,256,256]{3,2,1,0:T(8,128)(2,1)}, bf16[3,2,256,256]{3,2,1,0:T(8,128)(2,1)S(1)}, u32[]{:S(2)}, u32[]{:S(2)}) collective-permute-start(bf16[3,2,256,256]{3,2,1,0:T(8,128)(2,1)} %get-tuple-element.90), channel_id=1, source_target_pairs={{0,20},{4,16},{8,28},{12,24},{16,4},{20,0},{24,12},{28,8},{1,21},{... | collective-permute-start | bytes 2359304 | tf_op jit(solution)/shard_map/ppermute | solution.py:1772
  752.9 70.9 %copy-start.15 = (bf16[3,2,256,256]{3,2,1,0:T(8,128)(2,1)}, bf16[3,2,256,256]{3,2,1,0:T(8,128)(2,1)S(1)}, u32[]{:S(2)}) copy-start(bf16[3,2,256,256]{3,2,1,0:T(8,128)(2,1)S(1)} %collective-permute-done.7.refs_1_) | copy-start | bytes 2359300
  752.9 68.8 %collective-permute-start.12 = (bf16[3,2,256,256]{3,2,1,0:T(8,128)(2,1)}, bf16[3,2,256,256]{3,2,1,0:T(8,128)(2,1)S(1)}, u32[]{:S(2)}, u32[]{:S(2)}) collective-permute-start(bf16[3,2,256,256]{3,2,1,0:T(8,128)(2,1)} %get-tuple-element.91), channel_id=1, source_target_pairs={{0,24},{4,28},{8,16},{12,20},{16,8},{20,12},{24,0},{28,4},{1,25},{... | collective-permute-start | bytes 2359304 | tf_op jit(solution)/shard_map/ppermute | solution.py:1772
  754.4 67.3 %collective-permute-start.13 = (bf16[3,2,256,256]{3,2,1,0:T(8,128)(2,1)}, bf16[3,2,256,256]{3,2,1,0:T(8,128)(2,1)S(1)}, u32[]{:S(2)}, u32[]{:S(2)}) collective-permute-start(bf16[3,2,256,256]{3,2,1,0:T(8,128)(2,1)} %get-tuple-element.92), channel_id=1, source_target_pairs={{0,28},{4,24},{8,20},{12,16},{16,12},{20,8},{24,4},{28,0},{1,29},{... | collective-permute-start | bytes 2359304 | tf_op jit(solution)/shard_map/ppermute | solution.py:1772
  770.5 53.2 %copy-start.16 = (bf16[3,2,256,256]{3,2,1,0:T(8,128)(2,1)}, bf16[3,2,256,256]{3,2,1,0:T(8,128)(2,1)S(1)}, u32[]{:S(2)}) copy-start(bf16[3,2,256,256]{3,2,1,0:T(8,128)(2,1)S(1)} %collective-permute-done.9.refs_3_) | copy-start | bytes 2359300
  805.0 18.8 %copy-start.17 = (bf16[3,2,256,256]{3,2,1,0:T(8,128)(2,1)}, bf16[3,2,256,256]{3,2,1,0:T(8,128)(2,1)S(1)}, u32[]{:S(2)}) copy-start(bf16[3,2,256,256]{3,2,1,0:T(8,128)(2,1)S(1)} %collective-permute-done.10.refs_4_) | copy-start | bytes 2359300
  823.8 9.3 %copy-start.21 = (f32[512,256]{1,0:T(8,128)S(1)}, f32[512,256]{1,0:T(8,128)}, u32[]{:S(2)}) copy-start(f32[512,256]{1,0:T(8,128)} %get-tuple-element.214) | copy-start | bytes 1572868
  823.8 10.1 %copy-start.1 = (s32[512,8]{0,1:T(8,128)S(1)}, s32[512,8]{0,1:T(8,128)}, u32[]{:S(2)}) copy-start(s32[512,8]{0,1:T(8,128)} %param.19) | copy-start | bytes 49156
  (39 other events, 125.8 us)

commit v2 on v1

--- a/solution.py
+++ b/solution.py
@@ -486,7 +486,7 @@
 MESH = pl.DeviceIdType.MESH
 BF = jnp.bfloat16
 F32 = jnp.float32
-VMEM_LIMIT = 60 * 1024 * 1024
+VMEM_LIMIT = 62 * 1024 * 1024
 ANY = pl.BlockSpec(memory_space=pl.ANY)
 VM = pl.BlockSpec(memory_space=pltpu.VMEM)
 
@@ -518,16 +518,18 @@
         return self.count - 1
 
     def start(self, slot, source, target, device, condition=None):
-        copy = pltpu.make_async_remote_copy(
-            src_ref=source(),
-            dst_ref=target(),
-            send_sem=self.send_sem.at[slot],
-            recv_sem=self.recv_sem.at[slot],
-            device_id=device,
-            device_id_type=MESH,
-        )
-        under(condition, lambda: copy.start())
-        self.sent.append((condition, copy))
+        def make():
+            return pltpu.make_async_remote_copy(
+                src_ref=source(),
+                dst_ref=target(),
+                send_sem=self.send_sem.at[slot],
+                recv_sem=self.recv_sem.at[slot],
+                device_id=device,
+                device_id_type=MESH,
+            )
+
+        under(condition, lambda: make().start())
+        self.sent.append((condition, make))
 
     def arrive(self, slot, region, device, condition=None):
         copy = pltpu.make_async_remote_copy(
@@ -541,8 +543,8 @@
         under(condition, lambda: copy.wait_recv())
 
     def finish(self):
-        for condition, copy in self.sent:
-            under(condition, lambda copy=copy: copy.wait_send())
+        for condition, make in self.sent:
+            under(condition, lambda make=make: make().wait_send())
         self.sent = []
 
 
@@ -593,36 +595,134 @@
     rows_loop(rows, 16, body)
 
 
-def gather_line(wire, d, t, extent, own, place, on_block):
-    up = [wire.slot() for unused in range(extent - 1)]
-    down = [wire.slot() for unused in range(extent - 1)]
-    up_device, down_device = (d, t + 1), (d, t - 1)
-    wire.start(up[0], own, lambda: place(t), up_device, t < extent - 1)
-    wire.start(down[0], own, lambda: place(t), down_device, t > 0)
-    on_block(0, 0, t, None)
-    for step in range(1, extent):
-        wire.arrive(up[step - 1], lambda step=step: place(t - step), down_device, t >= step)
-        if step < extent - 1:
-            wire.start(
-                up[step],
-                lambda step=step: place(t - step),
-                lambda step=step: place(t - step),
-                up_device,
-                both(t >= step, t < extent - 1),
+class LineGather:
+    def __init__(self, wire, d, t, extent, own, place):
+        self.wire, self.extent = wire, extent
+        up = [wire.slot() for unused in range(extent - 1)]
+        down = [wire.slot() for unused in range(extent - 1)]
+        last = extent - 1
+        above, below = (d, t + 1), (d, t - 1)
+        wire.start(up[0], own, lambda: place(t), above, t < last)
+        wire.start(down[0], own, lambda: place(t), below, t > 0)
+        self.steps = {}
+        for step in range(1, extent):
+            from_below, from_above = t >= step, t <= last - step
+            lower, upper = t - step, t + step
+            self.steps[step] = (
+                (
+                    up,
+                    lambda index=lower: place(index),
+                    from_below,
+                    both(from_below, t < last),
+                    above,
+                    below,
+                ),
+                (
+                    down,
+                    lambda index=upper: place(index),
+                    from_above,
+                    both(from_above, t > 0),
+                    below,
+                    above,
+                ),
             )
-        wire.arrive(
-            down[step - 1], lambda step=step: place(t + step), up_device, t <= extent - 1 - step
-        )
-        if step < extent - 1:
-            wire.start(
-                down[step],
-                lambda step=step: place(t + step),
-                lambda step=step: place(t + step),
-                down_device,
-                both(t <= extent - 1 - step, t > 0),
-            )
-        on_block(step, 0, t - step, t >= step)
-        on_block(step, 1, t + step, t <= extent - 1 - step)
+
+    def step(self, step):
+        for slots, region, valid, onward, to, source in self.steps[step]:
+            self.wire.arrive(slots[step - 1], region, source, valid)
+            if step < self.extent - 1:
+                self.wire.start(slots[step], region, region, to, onward)
+
+
+def arrival(t, turn):
+    near = t - 1 + 2 * (1 - (t + 3) // 4)
+    far = 3 * (1 - t // 2)
+    choices = (t, near, 6 - t - near - far, far)
+    if isinstance(turn, int):
+        return choices[turn]
+    result = choices[0]
+    for number in range(1, 4):
+        result = jnp.where(turn == number, choices[number], result)
+    return result
+
+
+class PlaneGather:
+    def __init__(self, wire, d, t, extent, own, place, half):
+        self.wire, self.place, self.half, self.own = wire, place, half, own
+        self.to_x, self.to_y, self.to_c = (flip(d, 2), t), (flip(d, 4), t), (flip(d, 1), t)
+        self.index = [arrival(t, turn) for turn in range(extent)]
+        self.slots = {}
+        self.line = LineGather(wire, d, t, extent, own, lambda j: place(j, 0, 0))
+
+    def send(self, name, turn, source, target, device):
+        slot = self.wire.slot()
+        self.slots[name, turn] = slot
+        self.wire.start(slot, source, target, device)
+
+    def wait(self, name, turn, region, device):
+        self.wire.arrive(self.slots[name, turn], region, device)
+
+    def spot(self, turn, c, i, which=None):
+        def region():
+            ref = self.place(self.index[turn], c, i)
+            return ref if which is None else ref.at[pl.ds(which * self.half, self.half)]
+
+        return region
+
+    def source(self, turn, which=None):
+        def region():
+            ref = self.own() if turn == 0 else self.place(self.index[turn], 0, 0)
+            return ref if which is None else ref.at[pl.ds(which * self.half, self.half)]
+
+        return region
+
+    def stage(self, turn):
+        source, spot = self.source, self.spot
+        self.send("x0", turn, source(turn, 0), spot(turn, 0, 1, 0), self.to_x)
+        self.send("y1", turn, source(turn, 1), spot(turn, 0, 2, 1), self.to_y)
+        self.send("x1", turn, source(turn, 1), spot(turn, 0, 1, 1), self.to_x)
+        self.send("y0", turn, source(turn, 0), spot(turn, 0, 2, 0), self.to_y)
+        self.send("c0", turn, source(turn), spot(turn, 1, 0), self.to_c)
+
+    def relay(self, turn):
+        spot = self.spot
+        self.wait("x0", turn, spot(turn, 0, 1, 0), self.to_x)
+        self.send("fy", turn, spot(turn, 0, 1, 0), spot(turn, 0, 3, 0), self.to_y)
+        self.wait("y1", turn, spot(turn, 0, 2, 1), self.to_y)
+        self.send("fx", turn, spot(turn, 0, 2, 1), spot(turn, 0, 3, 1), self.to_x)
+        self.wait("x1", turn, spot(turn, 0, 1, 1), self.to_x)
+        self.send("c1", turn, spot(turn, 0, 1), spot(turn, 1, 1), self.to_c)
+        self.wait("y0", turn, spot(turn, 0, 2, 0), self.to_y)
+        self.send("c2", turn, spot(turn, 0, 2), spot(turn, 1, 2), self.to_c)
+
+    def corner(self, turn):
+        spot = self.spot
+        self.wait("fy", turn, spot(turn, 0, 3, 0), self.to_y)
+        self.wait("fx", turn, spot(turn, 0, 3, 1), self.to_x)
+        self.send("c3", turn, spot(turn, 0, 3), spot(turn, 1, 3), self.to_c)
+
+    def other(self, turn):
+        for i in range(4):
+            self.wait("c%d" % i, turn, self.spot(turn, 1, i), self.to_c)
+
+    def actions(self):
+        line, stage, relay, corner, other = (
+            self.line.step,
+            self.stage,
+            self.relay,
+            self.corner,
+            self.other,
+        )
+        return (
+            ((line, 1), (stage, 1), (relay, 0), (line, 2), (stage, 2), (corner, 0)),
+            ((relay, 1), (line, 3), (stage, 3), (other, 0)),
+            ((relay, 2), (corner, 1)),
+            ((other, 1),),
+            ((relay, 3), (corner, 2)),
+            ((other, 2),),
+            ((corner, 3),),
+            ((other, 3),),
+        )
 
 
 class LineSum:
@@ -705,79 +805,6 @@
     )
 
 
-def gather_plane(wire, d, t, extent, own, place, half):
-    dx, dy, dxy, dc = flip(d, 2), flip(d, 4), flip(d, 6), flip(d, 1)
-    to_x, to_y, to_c = (dx, t), (dy, t), (dc, t)
-    events = []
-
-    def cut(ref, which):
-        return ref.at[pl.ds(which * half, half)]
-
-    def on_block(step, side, index, condition):
-        source = own if step == 0 else (lambda: place(d, index))
-        event = dict(index=index, condition=condition, slots={})
-        for name, device, which in (
-            ("x0", to_x, 0),
-            ("y1", to_y, 1),
-            ("x1", to_x, 1),
-            ("y0", to_y, 0),
-        ):
-            slot = wire.slot()
-            event["slots"][name] = slot
-            wire.start(
-                slot,
-                lambda which=which: cut(source(), which),
-                lambda which=which: cut(place(d, index), which),
-                device,
-                condition,
-            )
-        slot = wire.slot()
-        event["slots"]["c"] = slot
-        wire.start(slot, source, lambda: place(d, index), to_c, condition)
-        events.append(event)
-        if step >= 1 and side == 1:
-            for earlier in events[:-2]:
-                relay(earlier)
-
-    def relay(event):
-        if "relayed" in event:
-            return
-        event["relayed"] = True
-        index, condition, slots = event["index"], event["condition"], event["slots"]
-        x_part = lambda which: (lambda: cut(place(dx, index), which))
-        y_part = lambda which: (lambda: cut(place(dy, index), which))
-        wire.arrive(slots["x0"], x_part(0), to_x, condition)
-        slots["fy"] = wire.slot()
-        wire.start(slots["fy"], x_part(0), x_part(0), to_y, condition)
-        wire.arrive(slots["y1"], y_part(1), to_y, condition)
-        slots["fx"] = wire.slot()
-        wire.start(slots["fx"], y_part(1), y_part(1), to_x, condition)
-        wire.arrive(slots["x1"], x_part(1), to_x, condition)
-        slots["cx"] = wire.slot()
-        wire.start(slots["cx"], lambda: place(dx, index), lambda: place(dx, index), to_c, condition)
-        wire.arrive(slots["y0"], y_part(0), to_y, condition)
-        slots["cy"] = wire.slot()
-        wire.start(slots["cy"], lambda: place(dy, index), lambda: place(dy, index), to_c, condition)
-
-    gather_line(wire, d, t, extent, own, lambda index: place(d, index), on_block)
-    for event in events:
-        relay(event)
-    for event in events:
-        index, condition, slots = event["index"], event["condition"], event["slots"]
-        wire.arrive(slots["fy"], lambda: cut(place(dxy, index), 0), to_y, condition)
-        wire.arrive(slots["fx"], lambda: cut(place(dxy, index), 1), to_x, condition)
-        slots["cd"] = wire.slot()
-        wire.start(
-            slots["cd"], lambda: place(dxy, index), lambda: place(dxy, index), to_c, condition
-        )
-    for event in events:
-        index, condition, slots = event["index"], event["condition"], event["slots"]
-        for name, bits in (("c", 1), ("cx", 3), ("cy", 5), ("cd", 7)):
-            wire.arrive(
-                slots[name], lambda bits=bits: place(flip(d, bits), index), to_c, condition
-            )
-
-
 def plane_order(t):
     top = t // 2
     inner = ((t + 1) // 2) % 2
@@ -798,18 +825,19 @@
     def cut(ref, which):
         return ref.at[pl.ds(which * half, half)]
 
-    for k in range(extent):
+    def begin(k):
         for i in turns:
+            rows = pl.ds(i * 2 * half, 2 * half)
             slots_c[k, i] = wire.slot()
             wire.start(
                 slots_c[k, i],
-                lambda k=k, i=i: partial.at[flip(d, 1 + 2 * i) * extent + order[k]],
-                lambda k=k, i=i: core_in.at[k, i],
+                lambda rows=rows: partial.at[order[k], 1, rows],
+                lambda i=i: core_in.at[k, i],
                 to_c,
             )
-            loads[k, i] = local.start(
-                partial.at[flip(d, 2 * i) * extent + order[k]], work.at[k, i]
-            )
+            loads[k, i] = local.start(partial.at[order[k], 0, rows], work.at[k, i])
+
+    begin(0)
 
     def inverse(index):
         where = jnp.int32(0)
@@ -831,6 +859,8 @@
     routes_a = ((to_x, 1, 0, 0, 0), (to_y, 2, 0, 1, 1), (to_x, 3, 2, 0, 2), (to_y, 3, 1, 1, 3))
     routes_b = ((to_y, 2, 0, 0), (to_x, 1, 1, 1))
     for turn in range(extent + 2):
+        if turn + 1 < extent:
+            begin(turn + 1)
         if turn < extent:
             k = turn
             for i in turns:
@@ -940,7 +970,7 @@
         slots = []
         for source, target in zip(sources, targets):
             slot = wire.slot()
-            wire.start(slot, lambda: source, lambda: target, device)
+            wire.start(slot, lambda source=source: source, lambda target=target: target, device)
             slots.append(slot)
         return slots
 
@@ -971,25 +1001,22 @@
                     local.start(stage.at[place, pl.ds(first, 2)], pieces[bits].at[place])
                 )
 
-    def on_block(step, side, index, condition):
-        if side == 1 or step == 0:
-            return
-        if step == 1:
-            store_pieces()
-            arrive(x_slots[0], region(dx, 0), to_x)
-            passed["y"] = send(to_y, region(dx, 0), region(dx, 0))
-            arrive(y_slots[1], region(dy, 1), to_y)
-            passed["x"] = send(to_x, region(dy, 1), region(dy, 1))
-        if step == 2:
-            arrive(x_slots[1], region(dx, 1), to_x)
-            c_slots[3] = send(to_c, region(dx, None), region(dx, None))
-            arrive(y_slots[0], region(dy, 0), to_y)
-            c_slots[5] = send(to_c, region(dy, None), region(dy, None))
-
     copies.append(local.start(hid, block(t)))
     for source, target in zip(own(None), region(d, None)):
         copies.append(local.start(source, target))
-    gather_line(wire, d, t, extent, lambda: hid, block, on_block)
+    line = LineGather(wire, d, t, extent, lambda: hid, block)
+    store_pieces()
+    arrive(x_slots[0], region(dx, 0), to_x)
+    passed["y"] = send(to_y, region(dx, 0), region(dx, 0))
+    arrive(y_slots[1], region(dy, 1), to_y)
+    passed["x"] = send(to_x, region(dy, 1), region(dy, 1))
+    line.step(1)
+    arrive(x_slots[1], region(dx, 1), to_x)
+    c_slots[3] = send(to_c, region(dx, None), region(dx, None))
+    arrive(y_slots[0], region(dy, 0), to_y)
+    c_slots[5] = send(to_c, region(dy, None), region(dy, None))
+    for step in range(2, extent):
+        line.step(step)
     gain_slots = {}
     for bits in range(1, 8):
         gain_slots[bits] = wire.slot()
@@ -1065,30 +1092,85 @@
     )(value)
 
 
-def enter_kernel(
-    extent,
-    partial,
-    hid,
-    gain,
-    router,
-    chosen,
-    middle,
-    gates,
-    ffn_own,
-    tokens,
-    work,
-    up_in,
-    down_in,
-    packet,
-    send_sem,
-    recv_sem,
-    local_sem,
-):
+class Pieces:
+    def __init__(self, d, in_weight, out_weight, sem, pieces):
+        self.copies = {}
+        slab = out_weight.shape[0] // 2
+        for bits, piece in enumerate(pieces):
+            start = pl.multiple_of(flip(d, bits) * slab, slab)
+            pairs = []
+            for place in range(3):
+                for e in range(2):
+                    if place < 2:
+                        column = (2 * place + e) * slab
+                        whole = in_weight.at[pl.ds(start, slab), pl.ds(column, slab)]
+                    else:
+                        whole = out_weight.at[pl.ds(e * slab, slab), pl.ds(start, slab)]
+                    pairs.append((piece.at[place, e], whole, sem.at[bits * 6 + place * 2 + e]))
+            self.copies[bits] = pairs
+
+    def load(self, bits):
+        for piece, whole, sem in self.copies[bits]:
+            pltpu.make_async_copy(piece, whole, sem).start()
+
+    def loaded(self, bits):
+        for piece, whole, sem in self.copies[bits]:
+            pltpu.make_async_copy(piece, whole, sem).wait()
+
+    def store(self, bits):
+        for piece, whole, sem in self.copies[bits]:
+            pltpu.make_async_copy(whole, piece, sem).start()
+
+    def stored(self, bits):
+        for piece, whole, sem in self.copies[bits]:
+            pltpu.make_async_copy(whole, piece, sem).wait()
+
+
+def coefficients(columns, d, slab):
+    values = columns.astype(F32)
+    lane = lax.broadcasted_iota(jnp.int32, values.shape, 1)
+    parts = []
+    for e in range(2):
+        wanted = jnp.logical_or(lane == 2 * d + e, lane == 16 + 2 * d + e)
+        one = jnp.sum(jnp.where(wanted, values, 0.0), axis=-1, keepdims=True)
+        parts.append(jnp.broadcast_to(one, (values.shape[0], slab)))
+    return jnp.concatenate(parts, axis=1)
+
+
+def enter_kernel(extent, partial, hid, gain, router, chosen, *rest):
+    near, corner = rest[:6], rest[6:8]
+    middle, gates, ffn_own, tokens, hidden, out = rest[8:14]
+    landed = rest[14:16]
+    (
+        gathered,
+        work,
+        up_in,
+        down_in,
+        in_weight,
+        out_weight,
+        hidden_stage,
+        out_stage,
+        send_sem,
+        recv_sem,
+        local_sem,
+        weight_sem,
+        stage_sem,
+        token_sem,
+    ) = rest[16:]
     d, t = lax.axis_index("dp"), lax.axis_index("tensor")
     rows, width = hid.shape
-    greet(plane_devices(d, t, extent))
+    greet(line_devices(d, t, extent) + [(None, (flip(d, bits), t)) for bits in (1, 2, 4, 6, 7)])
     wire, local = Wire(send_sem, recv_sem), Local(local_sem)
-    local.start(partial, work).wait()
+    corner_slots = []
+    for n in range(2):
+        slot = wire.slot()
+        corner_slots.append(slot)
+        wire.start(slot, lambda n=n: corner[n], lambda n=n: landed[n], (flip(d, 6 + n), t))
+    work_load = local.start(partial, work)
+    weights = Pieces(d, in_weight, out_weight, weight_sem, list(near) + list(landed))
+    for bits in range(6):
+        weights.load(bits)
+    work_load.wait()
     line = LineSum(
         wire, d, t, extent, lambda index: work.at[index], up_in, down_in, rows, 2
     )
@@ -1097,6 +1179,7 @@
     line.last()
     mine = work.at[t]
     everything = pl.ds(0, width)
+    packet = gathered.at[t, 0, pl.ds(0, rows)]
 
     def body(start):
         part = pl.ds(start, 16)
@@ -1105,11 +1188,10 @@
         )
         middle[part] = value
         unit = value * lax.rsqrt(jnp.mean(value * value, axis=-1, keepdims=True) + EPSILON)
-        packet[part, 0:width] = (unit * gain[...]).astype(BF)
+        ffn_own[part] = (unit * gain[...]).astype(BF)
 
     rows_loop(rows, 16, body)
-    ffn_own[...] = packet[:, 0:width]
-    logits = jnp.dot(packet[:, 0:width], router[...], preferred_element_type=F32)
+    logits = jnp.dot(ffn_own[...], router[...], preferred_element_type=F32)
     lane = lax.broadcasted_iota(jnp.int32, logits.shape, 1)
     top = jnp.max(jnp.where(lane < 16, logits, -1e30), axis=-1, keepdims=True)
     powers = jnp.where(lane < 32, jnp.exp(logits - top), 0.0)
@@ -1117,40 +1199,116 @@
     gates[...] = probs
     coeff = probs * chosen[...]
     high = coeff.astype(BF).astype(F32)
+    packet[:, 0:width] = ffn_own[...]
     packet[:, width : width + 128] = jnp.where(lane < 16, high, coeff - high).astype(BF)
 
-    def place(device, index):
-        return tokens.at[device * extent + index]
-
-    copy = local.start(packet, place(d, t))
-    gather_plane(wire, d, t, extent, lambda: packet, place, rows // 2)
-    copy.wait()
+    def place(j, c, i):
+        return gathered.at[j, c, pl.ds(i * rows, rows)]
+
+    gather = PlaneGather(wire, d, t, extent, lambda: packet, place, rows // 2)
+    gather.stage(0)
+    for n in range(2):
+        wire.arrive(corner_slots[n], lambda: landed[n], (flip(d, 6 + n), t))
+        weights.load(6 + n)
+    for bits in range(8):
+        weights.loaded(bits)
+    units = out_weight.shape[0]
+    tile = 256
+
+    def stage_copies(slot, j, c):
+        return (
+            pltpu.make_async_copy(hidden_stage.at[slot], hidden.at[j, c], stage_sem.at[0, slot]),
+            pltpu.make_async_copy(out_stage.at[slot], out.at[j, c], stage_sem.at[1, slot]),
+        )
+
+    actions = gather.actions()
+
+    def group(g, carry):
+        for number, steps in enumerate(actions):
+
+            @pl.when(g == number)
+            def _():
+                for action, argument in steps:
+                    action(argument)
+
+        j, c, slot = arrival(t, g // 2), g % 2, g % 2
+
+        @pl.when(g >= 2)
+        def _():
+            for copy in stage_copies(slot, j, c):
+                copy.wait()
+
+        pltpu.make_async_copy(gathered.at[j, c], tokens.at[j, c], token_sem.at[g]).start()
+
+        def some(start):
+            part = pl.ds(start, tile)
+            values = jnp.dot(
+                gathered[j, c, part, 0:width], in_weight[...], preferred_element_type=F32
+            )
+            hidden_stage[slot, part] = values.astype(BF)
+            gate_value, up_value = values[:, :units], values[:, units:]
+            coeff = coefficients(gathered[j, c, part, width : width + 128], d, units // 2)
+            active = (coeff * (gate_value * jax.nn.sigmoid(gate_value)) * up_value).astype(BF)
+            out_stage[slot, part] = jnp.dot(
+                active, out_weight[...], preferred_element_type=F32
+            ).astype(BF)
+
+        rows_loop(4 * rows, tile, some)
+        for copy in stage_copies(slot, j, c):
+            copy.start()
+        return carry
+
+    lax.fori_loop(0, 2 * extent, group, 0)
+    for slot in range(2):
+        for copy in stage_copies(slot, 0, slot):
+            copy.wait()
+    for g in range(2 * extent):
+        pltpu.make_async_copy(
+            gathered.at[arrival(t, g // 2), g % 2],
+            tokens.at[arrival(t, g // 2), g % 2],
+            token_sem.at[g],
+        ).wait()
     wire.finish()
 
 
-def enter(extent, partial, hid, gain, router, chosen):
+def enter(extent, partial, hid, gain, router, chosen, near, corner):
     rows, width = hid.shape
+    slab = near[0].shape[2]
+    piece = jax.ShapeDtypeStruct(near[0].shape, BF)
     return pl.pallas_call(
         functools.partial(enter_kernel, extent),
         out_shape=[
             jax.ShapeDtypeStruct((rows, width), F32),
             jax.ShapeDtypeStruct((rows, 128), F32),
             jax.ShapeDtypeStruct((rows, width), BF),
-            jax.ShapeDtypeStruct((8 * extent, rows, width + 128), BF),
+            jax.ShapeDtypeStruct((extent, 2, 4 * rows, width + 128), BF),
+            jax.ShapeDtypeStruct((extent, 2, 4 * rows, 4 * slab), BF),
+            jax.ShapeDtypeStruct((extent, 2, 4 * rows, width), BF),
+            piece,
+            piece,
         ],
-        in_specs=[ANY, VM, VM, VM, VM],
-        out_specs=[VM, VM, VM, ANY],
+        in_specs=[ANY, VM, VM, VM, VM] + [ANY] * 8,
+        out_specs=[VM, VM, VM] + [ANY] * 5,
         scratch_shapes=[
+            pltpu.VMEM((extent, 2, 4 * rows, width + 128), BF),
             pltpu.VMEM((extent, rows, width), BF),
             pltpu.VMEM((extent - 1, rows, width), BF),
             pltpu.VMEM((extent - 1, rows, width), BF),
-            pltpu.VMEM((rows, width + 128), BF),
+            pltpu.VMEM((width, 4 * slab), BF),
+            pltpu.VMEM((2 * slab, width), BF),
+            pltpu.VMEM((2, 4 * rows, 4 * slab), BF),
+            pltpu.VMEM((2, 4 * rows, width), BF),
         ]
-        + dma_pair(100)
-        + [pltpu.SemaphoreType.DMA((2,))],
+        + dma_pair(80)
+        + [
+            pltpu.SemaphoreType.DMA((2,)),
+            pltpu.SemaphoreType.DMA((48,)),
+            pltpu.SemaphoreType.DMA((2, 2)),
+            pltpu.SemaphoreType.DMA((2 * extent,)),
+        ],
         compiler_params=kernel_params(3),
         cost_estimate=pl.CostEstimate(flops=0, bytes_accessed=300_000_000, transcendentals=0),
-    )(partial, hid, gain, router, chosen)
+    )(partial, hid, gain, router, chosen, *near, *corner)
 
 
 def sum_scratch(extent, rows, width):
@@ -1164,33 +1322,52 @@
     ]
 
 
-def turn_kernel(
-    extent,
-    partial,
-    middle,
-    teacher,
-    weight,
-    grad_output,
-    row_loss,
-    grads,
-    work,
-    core_in,
-    a_in,
-    b_in,
-    up_in,
-    down_in,
-    packet,
-    send_sem,
-    recv_sem,
-    local_sem,
-):
+def transposed_dot(left, right):
+    return lax.dot_general(left, right, (((0,), (0,)), ((), ())), preferred_element_type=F32)
+
+
+def dot_transposed(left, right):
+    return lax.dot_general(left, right, (((1,), (1,)), ((), ())), preferred_element_type=F32)
+
+
+def turn_kernel(extent, partial, middle, teacher, weight, tokens, hidden, *rest):
+    pieces = rest[:8]
+    grad_output, row_loss, out = rest[8:11]
+    results, grads = rest[11:19], rest[19]
+    (
+        work,
+        core_in,
+        a_in,
+        b_in,
+        up_in,
+        down_in,
+        packet,
+        in_weight,
+        out_weight,
+        in_total,
+        out_total,
+        token_tile,
+        hidden_tile,
+        grad_tile,
+        out_stage,
+        active_tile,
+        inner_tile,
+        send_sem,
+        recv_sem,
+        local_sem,
+        weight_sem,
+        tile_sem,
+    ) = rest[20:]
     d, t = lax.axis_index("dp"), lax.axis_index("tensor")
     rows, width = middle.shape
     greet(plane_devices(d, t, extent))
     wire, local = Wire(send_sem, recv_sem), Local(local_sem)
+    weights = Pieces(d, in_weight, out_weight, weight_sem, pieces)
     mine = sum_plane(
         wire, local, d, t, extent, partial, work, core_in, a_in, b_in, up_in, down_in, rows // 2
     )
+    for bits in range(8):
+        weights.load(bits)
     everything = pl.ds(0, width)
 
     def body(start):
@@ -1208,67 +1385,169 @@
 
     rows_loop(rows, 16, body)
 
-    def place(device, index):
-        return grads.at[device * extent + index]
-
-    copy = local.start(packet, place(d, t))
-    gather_plane(wire, d, t, extent, lambda: packet, place, rows // 2)
-    copy.wait()
+    def place(j, c, i):
+        return grads.at[j, c, pl.ds(i * rows, rows)]
+
+    own_copy = local.start(packet, place(t, 0, 0))
+    gather = PlaneGather(wire, d, t, extent, lambda: packet, place, rows // 2)
+    gather.stage(0)
+    in_total[...] = jnp.zeros(in_total.shape, F32)
+    out_total[...] = jnp.zeros(out_total.shape, F32)
+    for bits in range(8):
+        weights.loaded(bits)
+    own_copy.wait()
+    units, slab = out_weight.shape[0], out_weight.shape[0] // 2
+    tile = 256
+    actions = gather.actions()
+
+    def out_copy(j, c):
+        return pltpu.make_async_copy(out_stage, out.at[j, c], tile_sem.at[3])
+
+    def group(g, carry):
+        j, c = arrival(t, g // 2), g % 2
+        token_copy = pltpu.make_async_copy(tokens.at[j, c], token_tile, tile_sem.at[0])
+        hidden_copy = pltpu.make_async_copy(hidden.at[j, c], hidden_tile, tile_sem.at[1])
+        grad_copy = pltpu.make_async_copy(grads.at[j, c], grad_tile, tile_sem.at[2])
+        token_copy.start()
+        hidden_copy.start()
+        for number, steps in enumerate(actions):
+
+            @pl.when(g == number)
+            def _():
+                for action, argument in steps:
+                    action(argument)
+
+        grad_copy.start()
+
+        @pl.when(g >= 1)
+        def _():
+            out_copy(j, c).wait()
+
+        token_copy.wait()
+        hidden_copy.wait()
+        grad_copy.wait()
+
+        def some(start):
+            part = pl.ds(start, tile)
+            grad_active = dot_transposed(grad_tile[part], out_weight[...])
+            gate_value = hidden_tile[part, 0:units].astype(F32)
+            up_value = hidden_tile[part, units : 2 * units].astype(F32)
+            coeff = coefficients(token_tile[part, width : width + 128], d, slab)
+            sigmoid_value = jax.nn.sigmoid(gate_value)
+            silu_value = gate_value * sigmoid_value
+            inner = grad_active * coeff
+            direct = silu_value * up_value
+            active_tile[part] = (coeff * direct).astype(BF)
+            product = grad_active * direct
+            lane = lax.broadcasted_iota(jnp.int32, (tile, 128), 1)
+            sums = jnp.zeros((tile, 128), F32)
+            for e in range(2):
+                one = jnp.sum(product[:, e * slab : (e + 1) * slab], axis=-1, keepdims=True)
+                sums = sums + jnp.where(lane == 2 * d + e, one, 0.0)
+            out_stage[part, width : width + 128] = sums.astype(BF)
+            grad_gate = (
+                inner * up_value * sigmoid_value * (1.0 + gate_value * (1.0 - sigmoid_value))
+            )
+            inner_tile[part, 0:units] = grad_gate.astype(BF)
+            inner_tile[part, units : 2 * units] = (inner * silu_value).astype(BF)
+            out_stage[part, 0:width] = dot_transposed(inner_tile[part], in_weight[...]).astype(BF)
+
+        rows_loop(4 * rows, tile, some)
+        out_copy(j, c).start()
+
+        def into_in(start):
+            part = pl.ds(start, 256)
+            in_total[part] += transposed_dot(token_tile[:, part], inner_tile[...])
+
+        rows_loop(width, 256, into_in)
+
+        def into_out(start):
+            part = pl.ds(start, 512)
+            out_total[:, part] += transposed_dot(active_tile[...], grad_tile[:, part])
+
+        rows_loop(width, 512, into_out)
+        return carry
+
+    lax.fori_loop(0, 2 * extent, group, 0)
+    in_weight[...] = in_total[...].astype(BF)
+    out_weight[...] = out_total[...].astype(BF)
+    stores = Pieces(d, in_weight, out_weight, weight_sem, results)
+    for bits in range(8):
+        stores.store(bits)
+    for bits in range(8):
+        stores.stored(bits)
+    out_copy(0, 0).wait()
     wire.finish()
 
 
-def turn(extent, partial, middle, teacher, weight):
+def turn(extent, partial, middle, teacher, weight, tokens, hidden, pieces):
     rows, width = middle.shape
+    slab = pieces[0].shape[2]
     return pl.pallas_call(
         functools.partial(turn_kernel, extent),
         out_shape=[
             jax.ShapeDtypeStruct((rows, width), F32),
             jax.ShapeDtypeStruct((rows, 128), F32),
-            jax.ShapeDtypeStruct((8 * extent, rows, width), BF),
+            jax.ShapeDtypeStruct((extent, 2, 4 * rows, width + 128), BF),
+        ]
+        + [jax.ShapeDtypeStruct(pieces[0].shape, BF)] * 8
+        + [jax.ShapeDtypeStruct((extent, 2, 4 * rows, width), BF)],
+        in_specs=[ANY, VM, VM, VM] + [ANY] * 10,
+        out_specs=[VM, VM] + [ANY] * 10,
+        scratch_shapes=sum_scratch(extent, rows, width)
+        + [
+            pltpu.VMEM((rows, width), BF),
+            pltpu.VMEM((width, 4 * slab), BF),
+            pltpu.VMEM((2 * slab, width), BF),
+            pltpu.VMEM((width, 4 * slab), F32),
+            pltpu.VMEM((2 * slab, width), F32),
+            pltpu.VMEM((4 * rows, width + 128), BF),
+            pltpu.VMEM((4 * rows, 4 * slab), BF),
+            pltpu.VMEM((4 * rows, width), BF),
+            pltpu.VMEM((4 * rows, width + 128), BF),
+            pltpu.VMEM((4 * rows, 2 * slab), BF),
+            pltpu.VMEM((4 * rows, 4 * slab), BF),
+        ]
+        + dma_pair(120)
+        + [
+            pltpu.SemaphoreType.DMA((20,)),
+            pltpu.SemaphoreType.DMA((48,)),
+            pltpu.SemaphoreType.DMA((4,)),
         ],
-        in_specs=[ANY, VM, VM, VM],
-        out_specs=[VM, VM, ANY],
-        scratch_shapes=sum_scratch(extent, rows, width)
-        + [pltpu.VMEM((rows, width), BF)]
-        + dma_pair(150)
-        + [pltpu.SemaphoreType.DMA((20,))],
         compiler_params=kernel_params(4),
         cost_estimate=pl.CostEstimate(flops=0, bytes_accessed=450_000_000, transcendentals=0),
-    )(partial, middle, teacher, weight)
-
-
-def leave_kernel(
-    extent,
-    partial,
-    middle,
-    grad_output,
-    gates,
-    chosen,
-    gain,
-    router_t,
-    grad_middle,
-    grad_logits,
-    gain_part,
-    grads,
-    work,
-    core_in,
-    a_in,
-    b_in,
-    up_in,
-    down_in,
-    packet,
-    extra,
-    send_sem,
-    recv_sem,
-    local_sem,
-):
+    )(partial, middle, teacher, weight, tokens, hidden, *pieces)[:11]
+
+
+def leave_kernel(extent, partial, middle, grad_output, gates, chosen, gain, router_t, *rest):
+    sent = rest[:5]
+    grad_middle, grad_logits, gain_part, grads = rest[5:9]
+    came = rest[9:14]
+    (
+        work,
+        core_in,
+        a_in,
+        b_in,
+        up_in,
+        down_in,
+        packet,
+        extra,
+        send_sem,
+        recv_sem,
+        local_sem,
+    ) = rest[14:]
     d, t = lax.axis_index("dp"), lax.axis_index("tensor")
     rows, width = middle.shape
-    greet(plane_devices(d, t, extent))
+    greet(line_devices(d, t, extent) + [(None, (flip(d, bits), t)) for bits in range(1, 6)])
     wire, local = Wire(send_sem, recv_sem), Local(local_sem)
     mine = sum_plane(
         wire, local, d, t, extent, partial, work, core_in, a_in, b_in, up_in, down_in, rows // 2
     )
+    piece_slots = []
+    for n in range(5):
+        slot = wire.slot()
+        piece_slots.append(slot)
+        wire.start(slot, lambda n=n: sent[n], lambda n=n: came[n], (flip(d, 1 + n), t))
     up_last, down_last = up_in.at[extent - 2], down_in.at[extent - 2]
     coeff_grad = (
         own_sum(mine, up_last, down_last, pl.ds(0, rows), pl.ds(width, 128)) * chosen[...]
@@ -1308,12 +1587,16 @@
         return grads.at[index]
 
     copy = local.start(packet, place(t))
-    gather_line(wire, d, t, extent, lambda: packet, place, lambda *unused: None)
+    line = LineGather(wire, d, t, extent, lambda: packet, place)
+    for step in range(1, extent):
+        line.step(step)
     copy.wait()
+    for n in range(5):
+        wire.arrive(piece_slots[n], lambda: came[n], (flip(d, 1 + n), t))
     wire.finish()
 
 
-def leave(extent, partial, middle, grad_output, gates, chosen, gain, router_t):
+def leave(extent, partial, middle, grad_output, gates, chosen, gain, router_t, sent):
     rows, width = middle.shape
     return pl.pallas_call(
         functools.partial(leave_kernel, extent),
@@ -1322,16 +1605,17 @@
             jax.ShapeDtypeStruct((rows, 128), F32),
             jax.ShapeDtypeStruct((8, width), F32),
             jax.ShapeDtypeStruct((extent, rows, width), BF),
-        ],
-        in_specs=[ANY, VM, VM, VM, VM, VM, VM],
-        out_specs=[VM, VM, VM, ANY],
+        ]
+        + [jax.ShapeDtypeStruct(piece.shape, BF) for piece in sent],
+        in_specs=[ANY, VM, VM, VM, VM, VM, VM] + [ANY] * 5,
+        out_specs=[VM, VM, VM] + [ANY] * 6,
         scratch_shapes=sum_scratch(extent, rows, width + 128)
         + [pltpu.VMEM((rows, width), BF), pltpu.VMEM((rows, width), F32)]
         + dma_pair(80)
         + [pltpu.SemaphoreType.DMA((20,))],
         compiler_params=kernel_params(5),
         cost_estimate=pl.CostEstimate(flops=0, bytes_accessed=350_000_000, transcendentals=0),
-    )(partial, middle, grad_output, gates, chosen, gain, router_t)
+    )(partial, middle, grad_output, gates, chosen, gain, router_t, *sent)
 
 
 def close_kernel(
@@ -1398,8 +1682,8 @@
     for i in turns:
         sources = slices(flip(d, 1 + 2 * i))
         c_slots[i] = [wire.slot(), wire.slot()]
-        wire.start(c_slots[i][0], lambda: sources[0], lambda i=i: q_core.at[i], to_c)
-        wire.start(c_slots[i][1], lambda: sources[1], lambda i=i: o_core.at[i], to_c)
+        wire.start(c_slots[i][0], lambda s=sources: s[0], lambda i=i: q_core.at[i], to_c)
+        wire.start(c_slots[i][1], lambda s=sources: s[1], lambda i=i: o_core.at[i], to_c)
         mine = slices(flip(d, 2 * i))
         loads[i] = [local.start(mine[0], q_work.at[i]), local.start(mine[1], o_work.at[i])]
     work_load.wait()
@@ -1432,6 +1716,16 @@
         )
         wire.start(
             a_slots[row][1], lambda: cut(o_work.at[source], which), lambda: o_a.at[row], device
+        )
+
+    def b_send(route):
+        device, source, which, row = route
+        b_slots[row] = [wire.slot(), wire.slot()]
+        wire.start(
+            b_slots[row][0], lambda: cut(q_work.at[source], which), lambda: q_b.at[row], device
+        )
+        wire.start(
+            b_slots[row][1], lambda: cut(o_work.at[source], which), lambda: o_b.at[row], device
         )
 
     core_add(3)
@@ -1449,20 +1743,7 @@
         add_into(cut(q_work.at[target], which), q_a.at[row], q_a.shape[1])
         add_into(cut(o_work.at[target], which), o_a.at[row], o_a.shape[1])
         if row < 2:
-            to, origin, part, b_row = routes_b[row]
-            b_slots[b_row] = [wire.slot(), wire.slot()]
-            wire.start(
-                b_slots[b_row][0],
-                lambda: cut(q_work.at[origin], part),
-                lambda: q_b.at[b_row],
-                to,
-            )
-            wire.start(
-                b_slots[b_row][1],
-                lambda: cut(o_work.at[origin], part),
-                lambda: o_b.at[b_row],
-                to,
-            )
+            b_send(routes_b[row])
     for k, peer in enumerate(line_peers):
         wire.arrive(small_slots[k], lambda k=k: small_in.at[k], peer)
     total = small[t] + small_in[0]
@@ -1550,200 +1831,6 @@
     )(partial, grad_middle, grad_qkv, grad_o, small, gains)
 
 
-def assemble(pieces, in_weight, out_weight, sem, d):
-    copies = []
-    slab = pieces[0].shape[2]
-    for bits in range(8):
-        start = pl.multiple_of(flip(d, bits) * slab, slab)
-        for place in range(3):
-            for e in range(2):
-                if place < 2:
-                    column = (2 * place + e) * slab
-                    target = in_weight.at[pl.ds(start, slab), pl.ds(column, slab)]
-                else:
-                    target = out_weight.at[pl.ds(e * slab, slab), pl.ds(start, slab)]
-                copies.append(
-                    pltpu.make_async_copy(
-                        pieces[bits].at[place, e], target, sem.at[bits * 6 + place * 2 + e]
-                    )
-                )
-    for copy in copies:
-        copy.start()
-    for copy in copies:
-        copy.wait()
-
-
-def coefficients(columns, d, slab):
-    values = columns.astype(F32)
-    lane = lax.broadcasted_iota(jnp.int32, values.shape, 1)
-    parts = []
-    for e in range(2):
-        wanted = jnp.logical_or(lane == 2 * d + e, lane == 16 + 2 * d + e)
-        one = jnp.sum(jnp.where(wanted, values, 0.0), axis=-1, keepdims=True)
-        parts.append(jnp.broadcast_to(one, (values.shape[0], slab)))
-    return jnp.concatenate(parts, axis=1)
-
-
-def experts_kernel(tile, tokens, *rest):
-    pieces, (hidden, out, in_weight, out_weight, sem) = rest[:8], rest[8:]
-    d = lax.axis_index("dp")
-    width = out.shape[1]
-    units = out_weight.shape[0]
-
-    @pl.when(pl.program_id(0) == 0)
-    def _():
-        assemble(pieces, in_weight, out_weight, sem, d)
-
-    def body(start):
-        part = pl.ds(start, tile)
-        both_values = jnp.dot(
-            tokens[part, 0:width], in_weight[...], preferred_element_type=F32
-        )
-        hidden[part] = both_values.astype(BF)
-        gate_value, up_value = both_values[:, :units], both_values[:, units:]
-        coeff = coefficients(tokens[part, width : width + 128], d, units // 2)
-        active = (coeff * (gate_value * jax.nn.sigmoid(gate_value)) * up_value).astype(BF)
-        out[part] = jnp.dot(active, out_weight[...], preferred_element_type=F32).astype(BF)
-
-    rows_loop(tokens.shape[0], tile, body)
-
-
-def experts(tokens, pieces):
-    count, wide = tokens.shape
-    width = wide - 128
-    slab = pieces[0].shape[2]
-    block = 512
-    return pl.pallas_call(
-        functools.partial(experts_kernel, 256),
-        grid=(count // block,),
-        out_shape=[
-            jax.ShapeDtypeStruct((count, 4 * slab), BF),
-            jax.ShapeDtypeStruct((count, width), BF),
-        ],
-        in_specs=[pl.BlockSpec((block, wide), lambda i: (i, 0))] + [ANY] * 8,
-        out_specs=[
-            pl.BlockSpec((block, 4 * slab), lambda i: (i, 0)),
-            pl.BlockSpec((block, width), lambda i: (i, 0)),
-        ],
-        scratch_shapes=[
-            pltpu.VMEM((width, 4 * slab), BF),
-            pltpu.VMEM((2 * slab, width), BF),
-            pltpu.SemaphoreType.DMA((48,)),
-        ],
-        compiler_params=pltpu.CompilerParams(vmem_limit_bytes=VMEM_LIMIT),
-        cost_estimate=pl.CostEstimate(
-            flops=2 * count * width * 6 * slab, bytes_accessed=50_000_000, transcendentals=0
-        ),
-    )(tokens, *pieces)
-
-
-def experts_back_kernel(tile, grads, tokens, hidden, *rest):
-    pieces, (out, *others) = rest[:8], rest[8:]
-    results, (in_weight, out_weight, in_total, out_total, sem) = others[:8], others[8:]
-    d = lax.axis_index("dp")
-    width = grads.shape[1]
-    units, slab = out_weight.shape[0], out_weight.shape[0] // 2
-
-    @pl.when(pl.program_id(0) == 0)
-    def _():
-        assemble(pieces, in_weight, out_weight, sem, d)
-        in_total[...] = jnp.zeros(in_total.shape, F32)
-        out_total[...] = jnp.zeros(out_total.shape, F32)
-
-    def body(start):
-        part = pl.ds(start, tile)
-        incoming = grads[part]
-        grad_active = lax.dot_general(
-            incoming, out_weight[...], (((1,), (1,)), ((), ())), preferred_element_type=F32
-        )
-        gate_value = hidden[part, 0:units].astype(F32)
-        up_value = hidden[part, units : 2 * units].astype(F32)
-        coeff = coefficients(tokens[part, width : width + 128], d, slab)
-        sigmoid_value = jax.nn.sigmoid(gate_value)
-        silu_value = gate_value * sigmoid_value
-        inner = grad_active * coeff
-        direct = silu_value * up_value
-        active = (coeff * direct).astype(BF)
-        product = grad_active * direct
-        lane = lax.broadcasted_iota(jnp.int32, (tile, 128), 1)
-        sums = jnp.zeros((tile, 128), F32)
-        for e in range(2):
-            one = jnp.sum(product[:, e * slab : (e + 1) * slab], axis=-1, keepdims=True)
-            sums = sums + jnp.where(lane == 2 * d + e, one, 0.0)
-        grad_gate = inner * up_value * sigmoid_value * (1.0 + gate_value * (1.0 - sigmoid_value))
-        grad_hidden = jnp.concatenate([grad_gate, inner * silu_value], axis=1).astype(BF)
-        out[part, 0:width] = lax.dot_general(
-            grad_hidden, in_weight[...], (((1,), (1,)), ((), ())), preferred_element_type=F32
-        ).astype(BF)
-        out[part, width : width + 128] = sums.astype(BF)
-        out_total[...] += lax.dot_general(
-            active, incoming, (((0,), (0,)), ((), ())), preferred_element_type=F32
-        )
-        in_total[...] += lax.dot_general(
-            tokens[part, 0:width],
-            grad_hidden,
-            (((0,), (0,)), ((), ())),
-            preferred_element_type=F32,
-        )
-
-    rows_loop(grads.shape[0], tile, body)
-
-    @pl.when(pl.program_id(0) == pl.num_programs(0) - 1)
-    def _():
-        in_weight[...] = in_total[...].astype(BF)
-        out_weight[...] = out_total[...].astype(BF)
-        copies = []
-        for bits in range(8):
-            start = pl.multiple_of(flip(d, bits) * slab, slab)
-            for place in range(3):
-                for e in range(2):
-                    if place < 2:
-                        column = (2 * place + e) * slab
-                        source = in_weight.at[pl.ds(start, slab), pl.ds(column, slab)]
-                    else:
-                        source = out_weight.at[pl.ds(e * slab, slab), pl.ds(start, slab)]
-                    copies.append(
-                        pltpu.make_async_copy(
-                            source, results[bits].at[place, e], sem.at[bits * 6 + place * 2 + e]
-                        )
-                    )
-        for copy in copies:
-            copy.start()
-        for copy in copies:
-            copy.wait()
-
-
-def experts_back(grads, tokens, hidden, pieces):
-    count, wide = tokens.shape
-    width = wide - 128
-    slab = pieces[0].shape[2]
-    block = 256
-    return pl.pallas_call(
-        functools.partial(experts_back_kernel, 256),
-        grid=(count // block,),
-        out_shape=[jax.ShapeDtypeStruct((count, wide), BF)]
-        + [jax.ShapeDtypeStruct(pieces[0].shape, BF)] * 8,
-        in_specs=[
-            pl.BlockSpec((block, width), lambda i: (i, 0)),
-            pl.BlockSpec((block, wide), lambda i: (i, 0)),
-            pl.BlockSpec((block, 4 * slab), lambda i: (i, 0)),
-        ]
-        + [ANY] * 8,
-        out_specs=[pl.BlockSpec((block, wide), lambda i: (i, 0))] + [ANY] * 8,
-        scratch_shapes=[
-            pltpu.VMEM((width, 4 * slab), BF),
-            pltpu.VMEM((2 * slab, width), BF),
-            pltpu.VMEM((width, 4 * slab), F32),
-            pltpu.VMEM((2 * slab, width), F32),
-            pltpu.SemaphoreType.DMA((48,)),
-        ],
-        compiler_params=pltpu.CompilerParams(vmem_limit_bytes=VMEM_LIMIT),
-        cost_estimate=pl.CostEstimate(
-            flops=2 * count * width * 12 * slab, bytes_accessed=80_000_000, transcendentals=0
-        ),
-    )(grads, tokens, hidden, *pieces)
-
-
 def spread_kernel(*refs):
     pieces, outs = refs[:8], refs[8:]
     d = lax.axis_index("dp")
@@ -1816,7 +1903,7 @@
     hidden_bf, qkv_full, o_full, gains_all, *sent = fetch(
         extent, hidden_in, qkv_own, o_weight, gains_own, gate_weight, up_weight, down_weight
     )
-    pieces = [exchange(piece, bits) for bits, piece in enumerate(sent)]
+    pieces = [exchange(piece, bits) for bits, piece in enumerate(sent[:6])]
     gains_full = jnp.sum(gains_all, axis=0)
     query_gain = gains_full[:local_heads].reshape(-1)
     key_gain = gains_full[local_heads:].reshape(-1)
@@ -1873,39 +1960,45 @@
     router_t = jnp.concatenate(
         [router_weight.T, jnp.zeros((128 - expert_count, width), BF)], axis=0
     )
-    middle, gates, ffn_own, tokens = enter(
+    middle, gates, ffn_own, tokens, hidden, expert_partial, *last_pieces = enter(
         extent,
         attn_partial.reshape(extent, rows, width),
         hidden_in,
         ffn_gain,
         router_wide,
         chosen,
-    )
-    tokens = tokens.reshape(all_tokens, width + 128)
-    hidden, expert_partial = experts(tokens, pieces)
+        pieces,
+        sent[6:],
+    )
+    pieces = pieces + last_pieces
     own_positions = t * rows + jnp.arange(rows)
     row_scale = jnp.where(own_positions < length, all_tokens / total_count, 0.0)
-    grad_output, row_loss, grads = turn(
+    grad_output, row_loss, ffn_grad_partial, *expert_grads = turn(
         extent,
-        expert_partial.reshape(dp_count * extent, rows, width),
+        expert_partial,
         middle,
         teacher,
         jnp.broadcast_to(row_scale[:, None], (rows, 128)),
+        tokens,
+        hidden,
+        pieces,
     )
     loss_own = jnp.sum(row_loss[:, 0]) / (2.0 * width * all_tokens)
-    ffn_grad_partial, *expert_grads = experts_back(
-        grads.reshape(all_tokens, width), tokens, hidden, pieces
-    )
-    expert_grads = [exchange(piece, bits) for bits, piece in enumerate(expert_grads)]
-    grad_middle, grad_logits, ffn_gain_part, attn_grad_rows = leave(
+    grad_middle, grad_logits, ffn_gain_part, attn_grad_rows, *came = leave(
         extent,
-        ffn_grad_partial.reshape(dp_count * extent, rows, width + 128),
+        ffn_grad_partial,
         middle,
         grad_output,
         gates,
         chosen,
         ffn_gain,
         router_t,
+        expert_grads[1:6],
+    )
+    corner_grads = lax.optimization_barrier((*expert_grads[6:], attn_grad_rows))
+    attn_grad_rows = corner_grads[2]
+    expert_grads = (
+        expert_grads[:1] + came + [exchange(corner_grads[n], 6 + n) for n in range(2)]
     )
     attn_grad_rows = attn_grad_rows.reshape(seq_len, width)
     router_part = jnp.einsum(

time: 844 us -> 742 us (0.88)
  waiting for transfers between devices: 61.4 us -> 0.02 us
  Pallas kernels: 642 us -> 622 us
  local copies, waits for them, and re-layouts: 33.2 us -> 22.6 us
    pallas_call x2 -> x0, Pallas kernels: 108 us -> none  [the longest x1 71.5 us: experts_back(): pl.pallas_call(functools.partial(experts_back_kernel, 256), grid=(count /...]
    ppermute x14 -> x7, waiting for transfers between devices: 61.4 us -> 0.02 us  [exchange(): return lax.ppermute(value, 'dp', [(i, i ^ bits) for i in range(8)])]
    pallas_call x1, Pallas kernels: 160 us -> 218 us  [turn(): pl.pallas_call(functools.partial(turn_kernel, extent), out_shape=[jax.Sha...]
    pallas_call x1, Pallas kernels: 51 us -> 64.4 us  [close(): pl.pallas_call(functools.partial(close_kernel, extent), out_shape=[jax.Sh...]
    pallas_call x1, Pallas kernels: 122 us -> 133 us  [enter(): pl.pallas_call(functools.partial(enter_kernel, extent), out_shape=[jax.Sh...]
  transfers between devices with their start and end apart: 14 -> 7, of which waited for: 3 -> 0; matrix products, arithmetic and copies ran while one was open for 8% -> 7% of each run, Pallas kernels for 22% -> 10%
where the time goes in v2:
time: 742 us; the launch traced here: 733 us
  Pallas kernels  622 us (84%)
  matrix products  44.5 us (6%)
  other arithmetic  34.9 us (5%)
  local copies, waits for them, and re-layouts  22.6 us (3%)
    pallas_call x1, Pallas kernels, turn(): pl.pallas_call(functools.partial(turn_kernel, extent), out_shape=[jax.Sha...  218 us
    pallas_call x1, Pallas kernels, leave(): pl.pallas_call(functools.partial(leave_kernel, extent), out_shape=[jax.Sh...  135 us
    pallas_call x1, Pallas kernels, enter(): pl.pallas_call(functools.partial(enter_kernel, extent), out_shape=[jax.Sh...  133 us
    pallas_call x1, Pallas kernels, close(): pl.pallas_call(functools.partial(close_kernel, extent), out_shape=[jax.Sh...  64.4 us
    pallas_call x1, Pallas kernels, fetch(): pl.pallas_call(functools.partial(fetch_kernel, extent), out_shape=[jax.Sh...  50 us
  transfers between devices with their start and end apart: 7, of which 0 were waited for; matrix products, arithmetic and copies ran while one was open for 7% of the time, Pallas kernels for 10%

profile of v2, /device:TPU:0, one launch (start us, length us, event | category | flops | bytes accessed | tf_op | source)
XLA Modules:
  0.0 732.6 jit_solution(14978342805492415890)
XLA Ops:
  1.6 2.0 pad_maximum_fusion.1.qkv
  3.6 50.0 %shard_map.263 = (bf16[512,2048]{1,0:T(8,128)(2,1)}, bf16[2048,1536]{1,0:T(8,128)(2,1)}, bf16[512,2048]{1,0:T(8,128)(2,1)}, f32[8,8,128]{2,1,0:T(8,128)}, bf16[3...) custom-call(bf16[128,2048]{1,0:T(8,128)(2,1)} %hid.3, ...), custom_call_target="tpu_custom_call" | custom-call | bytes 100000000 | tf_op jit(solution)/shard_map/pallas_call | solution.py:1047
  57.8 2.1 fusion.11
  59.9 6.3 fusion.27
  68.7 6.7 shard_map.264
  89.9 3.1 subtract_convert_fusion.1
  93.0 5.6 fusion.47
  98.6 3.2 convolution_convert_fusion.5
  102.9 2.6 convolution_convert_fusion.2
  106.7 133.2 %shard_map.265 = (f32[128,2048]{1,0:T(8,128)}, f32[128,128]{1,0:T(8,128)}, bf16[128,2048]{1,0:T(8,128)(2,1)}, bf16[4,2,512,2176]{3,2,1,0:T(8,128)(2,1)}, bf16[4,...) custom-call(bf16[4,128,2048]{2,1,0:T(8,128)(2,1)} %bitcast.95, ...), custom_call_target="tpu_custom_call" | custom-call | bytes 300000000 | tf_op jit(solution)/shard_map/pallas_call | solution.py:1278
  240.5 217.8 %shard_map.266 = (f32[128,2048]{1,0:T(8,128)}, f32[128,128]{1,0:T(8,128)}, bf16[4,2,512,2176]{3,2,1,0:T(8,128)(2,1)}, bf16[3,2,256,256]{3,2,1,0:T(8,128)(2,1)}, ...) custom-call(bf16[4,2,512,2048]{3,2,1,0:T(8,128)(2,1)} %get-tuple-ele, ...), custom_call_target="tpu_custom_call" | custom-call | bytes 450000000 | tf_op jit(solution)/shard_map/pallas_call | solution.py:1486
  458.3 134.9 %shard_map.267 = (f32[128,2048]{1,0:T(8,128)}, f32[128,128]{1,0:T(8,128)}, f32[8,2048]{1,0:T(8,128)}, bf16[4,128,2048]{2,1,0:T(8,128)(2,1)}, bf16[3,2,256,256]{3...) custom-call(bf16[4,2,512,2176]{3,2,1,0:T(8,128)(2,1)} %get-tuple-ele, ...), custom_call_target="tpu_custom_call" | custom-call | bytes 350000000 | tf_op jit(solution)/shard_map/pallas_call | solution.py:1601
  593.3 3.6 convolution_convert_fusion.3
  599.7 2.0 fusion.17
  605.2 2.6 convolution_convert_fusion.1.grad_o
  609.0 2.9 multiply_subtract_fusion
  614.6 6.8 shard_map.268
  623.4 3.9 multiply_convert_fusion.2
  627.4 8.0 %fusion.10 = (f32[2048]{0:T(1024)S(1)}, f32[512]{0:T(512)S(1)}, f32[512,2048]{1,0:T(8,128)}) fusion(bf16[512,2048]{1,0:T(8,128)(2,1)S(1)} %copy-done.8, f32[512]{0:T(512)S(1)} %add_rsqrt_fusion, f32[2048]{0:T(1024)S(1)} %convert_element_type.140, bf16[2048,1536]{1,0:T(8,128)(2,1)} %get-tuple-element.65, bf16[512,512]{1,0:T(8,128)(2,1)S(1)} %copy.114, ...), kind=kOutput, calls=%fused_computation.13 | convolution fusion | flops 3233281536 | bytes 14176256 | tf_op jit(solution)/shard_map/sa,da->sd/dot_general | solution.py:2061
  635.3 5.8 convolution_convert_fusion.grad_qkv
  644.5 4.5 fusion.9
  649.8 64.4 %shard_map.269 = (f32[128,2048]{1,0:T(8,128)}, f32[256,1536]{1,0:T(8,128)}, f32[512,256]{1,0:T(8,128)}, f32[24,128]{1,0:T(8,128)}) custom-call(bf16[4,128,2048]{2,1,0:T(8,128)(2,1)} %bitcast.94, f32[128,2048]{1,0:T(8,128)} %get-tuple-element.95.grad_middle, bf16[2048,1536]{1,0:T(8,128)(2,1)} %convolution_convert_fusion.grad_qkv, ...), custom_call_target="tpu_custom_call" | custom-call | bytes 150000000 | tf_op jit(solution)/shard_map/pallas_call | solution.py:1818
  719.5 2.5 fusion.43
  722.1 8.3 %shard_map.270 = (f32[16,256,256]{2,1,0:T(8,128)}, f32[16,256,256]{2,1,0:T(8,128)}, f32[16,256,256]{2,1,0:T(8,128)}) custom-call(bf16[3,2,256,256]{3,2,1,0:T(8,128)(2,1)} %get-tuple-element.103.refs_0_, bf16[3,2,256,256]{3,2,1,0:T(8,128)(2,1)} %get-tuple-element.104.refs_1_, bf16[3,2,256,256]{3,2,1,0:T(8,128)(2,1)} %get-tuple-element.105.refs_2_, ...), custom_call_target="tpu_custom_call" | custom-call | bytes 20000000 | tf_op jit(solution)/shard_map/pallas_call | solution.py:1846
  (144 shorter events, 46.7 us)
Async XLA Ops:
  0.6 84.3 %copy-start = (s32[512,8]{0,1:T(8,128)S(1)}, s32[512,8]{0,1:T(8,128)}, u32[]{:S(2)}) copy-start(s32[512,8]{0,1:T(8,128)} %param.19) | copy-start | bytes 49156
  3.6 56.2 %copy-start.25 = (bf16[2048]{0:T(1024)(128)(2,1)S(1)}, bf16[2048]{0:T(1024)(128)(2,1)}, u32[]{:S(2)}) copy-start(bf16[2048]{0:T(1024)(128)(2,1)} %param.20) | copy-start | bytes 12292
  53.7 52.9 %collective-permute-start = (bf16[3,2,256,256]{3,2,1,0:T(8,128)(2,1)}, bf16[3,2,256,256]{3,2,1,0:T(8,128)(2,1)}, u32[]{:S(2)}, u32[]{:S(2)}) collective-permute-start(bf16[3,2,256,256]{3,2,1,0:T(8,128)(2,1)} %get-tuple-element.69), channel_id=1, source_target_pairs={{0,4},{4,0},{8,12},{12,8},{16,20},{20,16},{24,28},{28,24},{1,5},{5... | collective-permute-start | bytes 2359304 | tf_op jit(solution)/shard_map/ppermute | solution.py:1859
  54.2 52.4 %collective-permute-start.1 = (bf16[3,2,256,256]{3,2,1,0:T(8,128)(2,1)}, bf16[3,2,256,256]{3,2,1,0:T(8,128)(2,1)}, u32[]{:S(2)}, u32[]{:S(2)}) collective-permute-start(bf16[3,2,256,256]{3,2,1,0:T(8,128)(2,1)} %get-tuple-element.70), channel_id=1, source_target_pairs={{0,8},{4,12},{8,0},{12,4},{16,24},{20,28},{24,16},{28,20},{1,9},{5... | collective-permute-start | bytes 2359304 | tf_op jit(solution)/shard_map/ppermute | solution.py:1859
  55.0 51.6 %collective-permute-start.2 = (bf16[3,2,256,256]{3,2,1,0:T(8,128)(2,1)}, bf16[3,2,256,256]{3,2,1,0:T(8,128)(2,1)}, u32[]{:S(2)}, u32[]{:S(2)}) collective-permute-start(bf16[3,2,256,256]{3,2,1,0:T(8,128)(2,1)} %get-tuple-element.71), channel_id=1, source_target_pairs={{0,12},{4,8},{8,4},{12,0},{16,28},{20,24},{24,20},{28,16},{1,13},{... | collective-permute-start | bytes 2359304 | tf_op jit(solution)/shard_map/ppermute | solution.py:1859
  55.7 51.0 %collective-permute-start.3 = (bf16[3,2,256,256]{3,2,1,0:T(8,128)(2,1)}, bf16[3,2,256,256]{3,2,1,0:T(8,128)(2,1)}, u32[]{:S(2)}, u32[]{:S(2)}) collective-permute-start(bf16[3,2,256,256]{3,2,1,0:T(8,128)(2,1)} %get-tuple-element.72), channel_id=1, source_target_pairs={{0,16},{4,20},{8,24},{12,28},{16,0},{20,4},{24,8},{28,12},{1,17},{... | collective-permute-start | bytes 2359304 | tf_op jit(solution)/shard_map/ppermute | solution.py:1859
  56.8 49.8 %collective-permute-start.4 = (bf16[3,2,256,256]{3,2,1,0:T(8,128)(2,1)}, bf16[3,2,256,256]{3,2,1,0:T(8,128)(2,1)}, u32[]{:S(2)}, u32[]{:S(2)}) collective-permute-start(bf16[3,2,256,256]{3,2,1,0:T(8,128)(2,1)} %get-tuple-element.73), channel_id=1, source_target_pairs={{0,20},{4,16},{8,28},{12,24},{16,4},{20,0},{24,12},{28,8},{1,21},{... | collective-permute-start | bytes 2359304 | tf_op jit(solution)/shard_map/ppermute | solution.py:1859
  59.9 15.5 %copy-start.23 = (f32[8,8,128]{2,1,0:T(8,128)S(1)}, f32[8,8,128]{2,1,0:T(8,128)}, u32[]{:S(2)}) copy-start(f32[8,8,128]{2,1,0:T(8,128)} %get-tuple-element.66) | copy-start | bytes 98308
  79.9 6.0 copy-start.26
  79.9 6.6 copy-start.19
  80.3 9.6 %copy-start.10 = (f32[512,4,64]{2,1,0:T(4,128)S(1)}, f32[512,4,64]{2,1,0:T(4,128)}, u32[]{:S(2)}) copy-start(f32[512,4,64]{2,1,0:T(4,128)} %get-tuple-element.182) | copy-start | bytes 1572868
  93.0 5.6 copy-start.11
  98.6 4.3 copy-start.27
  101.8 3.7 copy-start.30
  593.3 4.4 copy-start.9
  623.4 4.0 copy-start.8
  635.3 7.3 copy-start.17
  635.3 7.3 copy-start.20
  635.3 8.4 %copy-start.21 = (f32[8,2048]{1,0:T(8,128)S(1)}, f32[8,2048]{1,0:T(8,128)}, u32[]{:S(2)}) copy-start(f32[8,2048]{1,0:T(8,128)} %get-tuple-element.96) | copy-start | bytes 196612
  641.2 80.9 %collective-permute-start.5 = (bf16[3,2,256,256]{3,2,1,0:T(8,128)(2,1)}, bf16[3,2,256,256]{3,2,1,0:T(8,128)(2,1)}, u32[]{:S(2)}, u32[]{:S(2)}) collective-permute-start(bf16[3,2,256,256]{3,2,1,0:T(8,128)(2,1)} %get-tuple-element.109), channel_id=1, source_target_pairs={{0,24},{4,28},{8,16},{12,20},{16,8},{20,12},{24,0},{28,4},{1,25},{... | collective-permute-start | bytes 2359304 | tf_op jit(solution)/shard_map/ppermute | solution.py:1859
  642.6 79.4 %collective-permute-start.6 = (bf16[3,2,256,256]{3,2,1,0:T(8,128)(2,1)}, bf16[3,2,256,256]{3,2,1,0:T(8,128)(2,1)}, u32[]{:S(2)}, u32[]{:S(2)}) collective-permute-start(bf16[3,2,256,256]{3,2,1,0:T(8,128)(2,1)} %get-tuple-element.110), channel_id=1, source_target_pairs={{0,28},{4,24},{8,20},{12,16},{16,12},{20,8},{24,4},{28,0},{1,29},{... | collective-permute-start | bytes 2359304 | tf_op jit(solution)/shard_map/ppermute | solution.py:1859
  722.0 8.4 %copy-start.16 = (f32[128,2048]{1,0:T(8,128)S(1)}, f32[128,2048]{1,0:T(8,128)}, u32[]{:S(2)}) copy-start(f32[128,2048]{1,0:T(8,128)} %get-tuple-element.224) | copy-start | bytes 3145732
  722.0 9.3 %copy-start.18 = (f32[512,256]{1,0:T(8,128)S(1)}, f32[512,256]{1,0:T(8,128)}, u32[]{:S(2)}) copy-start(f32[512,256]{1,0:T(8,128)} %get-tuple-element.232) | copy-start | bytes 1572868
  722.1 10.1 %copy-start.1 = (s32[512,8]{0,1:T(8,128)S(1)}, s32[512,8]{0,1:T(8,128)}, u32[]{:S(2)}) copy-start(s32[512,8]{0,1:T(8,128)} %param.19) | copy-start | bytes 49156
  (15 other events, 28.1 us)

commit v3 on v2

--- a/solution.py
+++ b/solution.py
@@ -590,7 +590,7 @@
 def add_into(target, source, rows):
     def body(start):
         part = pl.ds(start, 16)
-        target[part] = (target[part].astype(F32) + source[part].astype(F32)).astype(BF)
+        target[part] = target[part] + source[part]
 
     rows_loop(rows, 16, body)
 
@@ -646,13 +646,37 @@
     return result
 
 
+LATE = 32
+
+
 class PlaneGather:
-    def __init__(self, wire, d, t, extent, own, place, half):
-        self.wire, self.place, self.half, self.own = wire, place, half, own
+    def __init__(self, wire, d, t, extent, own, place, bundle, rows):
+        self.wire, self.place, self.bundle, self.own = wire, place, bundle, own
+        self.early, self.half = rows - LATE, (rows - LATE) // 2
         self.to_x, self.to_y, self.to_c = (flip(d, 2), t), (flip(d, 4), t), (flip(d, 1), t)
         self.index = [arrival(t, turn) for turn in range(extent)]
         self.slots = {}
-        self.line = LineGather(wire, d, t, extent, own, lambda j: place(j, 0, 0))
+        self.where = (wire, d, t, extent)
+        late = lambda n: (self.early + n * (LATE // 2), LATE // 2)
+        self.parts = {0: (0, self.half), 1: (self.half, self.half), 2: late(0), 3: late(1)}
+        self.parts["early"], self.parts["late"] = (0, self.early), (self.early, LATE)
+        self.send("gx", 0, self.source(0, "late"), self.spot(0, 0, 1, "late"), self.to_x)
+        self.send("gy", 0, self.source(0, "late"), self.spot(0, 0, 2, "late"), self.to_y)
+        self.line = LineGather(
+            wire, d, t, extent, lambda: self.cut(own(), "early"), lambda j: self.cut(place(j, 0, 0), "early")
+        )
+        self.stage_first(0)
+        for name, i, which, onward, to, source in (
+            ("gx", 1, 2, "gfy", self.to_y, self.to_x),
+            ("gy", 2, 3, "gfx", self.to_x, self.to_y),
+        ):
+            self.wait(name, 0, self.spot(0, 0, i, "late"), source)
+            self.send(onward, 0, self.spot(0, 0, i, which), self.spot(0, 0, 3, which), to)
+        self.stage_second(0)
+
+    def cut(self, ref, which):
+        start, size = self.parts[which]
+        return ref.at[pl.ds(start, size)]
 
     def send(self, name, turn, source, target, device):
         slot = self.wire.slot()
@@ -662,27 +686,28 @@
     def wait(self, name, turn, region, device):
         self.wire.arrive(self.slots[name, turn], region, device)
 
-    def spot(self, turn, c, i, which=None):
-        def region():
-            ref = self.place(self.index[turn], c, i)
-            return ref if which is None else ref.at[pl.ds(which * self.half, self.half)]
-
-        return region
-
-    def source(self, turn, which=None):
-        def region():
-            ref = self.own() if turn == 0 else self.place(self.index[turn], 0, 0)
-            return ref if which is None else ref.at[pl.ds(which * self.half, self.half)]
-
-        return region
-
-    def stage(self, turn):
+    def spot(self, turn, c, i, which):
+        return lambda: self.cut(self.place(self.index[turn], c, i), which)
+
+    def source(self, turn, which):
+        if turn == 0:
+            return lambda: self.cut(self.own(), which)
+        return self.spot(turn, 0, 0, which)
+
+    def stage_first(self, turn):
         source, spot = self.source, self.spot
         self.send("x0", turn, source(turn, 0), spot(turn, 0, 1, 0), self.to_x)
         self.send("y1", turn, source(turn, 1), spot(turn, 0, 2, 1), self.to_y)
+
+    def stage_second(self, turn):
+        source, spot = self.source, self.spot
         self.send("x1", turn, source(turn, 1), spot(turn, 0, 1, 1), self.to_x)
         self.send("y0", turn, source(turn, 0), spot(turn, 0, 2, 0), self.to_y)
-        self.send("c0", turn, source(turn), spot(turn, 1, 0), self.to_c)
+        self.send("c0", turn, source(turn, "early"), spot(turn, 1, 0, "early"), self.to_c)
+
+    def stage(self, turn):
+        self.stage_first(turn)
+        self.stage_second(turn)
 
     def relay(self, turn):
         spot = self.spot
@@ -691,34 +716,63 @@
         self.wait("y1", turn, spot(turn, 0, 2, 1), self.to_y)
         self.send("fx", turn, spot(turn, 0, 2, 1), spot(turn, 0, 3, 1), self.to_x)
         self.wait("x1", turn, spot(turn, 0, 1, 1), self.to_x)
-        self.send("c1", turn, spot(turn, 0, 1), spot(turn, 1, 1), self.to_c)
+        self.send("c1", turn, spot(turn, 0, 1, "early"), spot(turn, 1, 1, "early"), self.to_c)
         self.wait("y0", turn, spot(turn, 0, 2, 0), self.to_y)
-        self.send("c2", turn, spot(turn, 0, 2), spot(turn, 1, 2), self.to_c)
+        self.send("c2", turn, spot(turn, 0, 2, "early"), spot(turn, 1, 2, "early"), self.to_c)
 
     def corner(self, turn):
         spot = self.spot
         self.wait("fy", turn, spot(turn, 0, 3, 0), self.to_y)
         self.wait("fx", turn, spot(turn, 0, 3, 1), self.to_x)
-        self.send("c3", turn, spot(turn, 0, 3), spot(turn, 1, 3), self.to_c)
+        self.send("c3", turn, spot(turn, 0, 3, "early"), spot(turn, 1, 3, "early"), self.to_c)
+
+    def pass_bundle(self, turn):
+        region = lambda c: (lambda: self.bundle(self.index[turn], c))
+        self.send("cb", turn, region(0), region(1), self.to_c)
+
+    def bundle_start(self):
+        spot = self.spot
+        self.wait("gfy", 0, spot(0, 0, 3, 2), self.to_y)
+        self.wait("gfx", 0, spot(0, 0, 3, 3), self.to_x)
+        here = self.index[0]
+        wire, d, t, extent = self.where
+        self.late_line = LineGather(
+            wire, d, t, extent, lambda: self.bundle(here, 0), lambda j: self.bundle(j, 0)
+        )
+        self.pass_bundle(0)
+
+    def bundle_step(self, step):
+        self.late_line.step(step)
+        self.pass_bundle(step)
 
     def other(self, turn):
         for i in range(4):
-            self.wait("c%d" % i, turn, self.spot(turn, 1, i), self.to_c)
+            self.wait("c%d" % i, turn, self.spot(turn, 1, i, "early"), self.to_c)
+        self.wait("cb", turn, lambda: self.bundle(self.index[turn], 1), self.to_c)
 
     def actions(self):
-        line, stage, relay, corner, other = (
+        line, stage, relay, corner, other, late = (
             self.line.step,
             self.stage,
             self.relay,
             self.corner,
             self.other,
+            self.bundle_step,
         )
         return (
-            ((line, 1), (stage, 1), (relay, 0), (line, 2), (stage, 2), (corner, 0)),
+            (
+                (line, 1),
+                (stage, 1),
+                (relay, 0),
+                (line, 2),
+                (stage, 2),
+                (corner, 0),
+                (late, 1),
+            ),
             ((relay, 1), (line, 3), (stage, 3), (other, 0)),
-            ((relay, 2), (corner, 1)),
+            ((relay, 2), (corner, 1), (late, 2)),
             ((other, 1),),
-            ((relay, 3), (corner, 2)),
+            ((relay, 3), (corner, 2), (late, 3)),
             ((other, 2),),
             ((corner, 3),),
             ((other, 3),),
@@ -736,6 +790,9 @@
     def cut(self, ref, part):
         return ref.at[pl.ds(part * self.rows, self.rows)]
 
+    def add(self, target, source):
+        add_into(target, source, self.rows)
+
     def flow(self, step, part, near, index, slots, buffers, to_device, from_device):
         wire, extent = self.wire, self.extent
         block = lambda: self.cut(self.block(index), part)
@@ -743,7 +800,7 @@
             source = lambda: self.cut(buffers.at[step - 1], part)
             active = both(both(near <= step, near < extent - 1), near >= 1)
             wire.arrive(slots[step - 1][part], source, from_device, active)
-            under(active, lambda: add_into(block(), source(), self.rows))
+            under(active, lambda: self.add(block(), source()))
         wire.start(
             slots[step][part],
             block,
@@ -754,27 +811,11 @@
 
     def step(self, step):
         d, t, extent = self.d, self.t, self.extent
+        up, down = extent - 1 - step + t, step + t - (extent - 1)
+        above, below = (d, t + 1), (d, t - 1)
         for part in range(self.parts):
-            self.flow(
-                step,
-                part,
-                t,
-                extent - 1 - step + t,
-                self.up,
-                self.up_in,
-                (d, t + 1),
-                (d, t - 1),
-            )
-            self.flow(
-                step,
-                part,
-                extent - 1 - t,
-                step + t - (extent - 1),
-                self.down,
-                self.down_in,
-                (d, t - 1),
-                (d, t + 1),
-            )
+            self.flow(step, part, t, up, self.up, self.up_in, above, below)
+            self.flow(step, part, extent - 1 - t, down, self.down, self.down_in, below, above)
 
     def last(self):
         d, t, extent = self.d, self.t, self.extent
@@ -797,6 +838,15 @@
             under(missing, clear)
 
 
+class BundleSum(LineSum):
+    def cut(self, ref, part):
+        return ref
+
+    def add(self, target, source):
+        for i in range(4):
+            add_into(target.at[i], source.at[i], LATE)
+
+
 def own_sum(block, up_in, down_in, part, columns):
     return (
         block[part, columns].astype(F32)
@@ -816,8 +866,21 @@
     )
 
 
-def sum_plane(wire, local, d, t, extent, partial, work, core_in, a_in, b_in, up_in, down_in, half):
+def sum_plane(wire, local, d, t, extent, partial, buffers, rows, between=lambda turn: None):
+    (
+        work,
+        own_in,
+        a_in,
+        b_in,
+        up_in,
+        down_in,
+        late_up,
+        late_down,
+        late_a,
+        late_b,
+    ) = buffers
     order = plane_order(t)
+    early, half = rows - LATE, (rows - LATE) // 2
     to_x, to_y, to_c = (flip(d, 2), t), (flip(d, 4), t), (flip(d, 1), t)
     turns = (3, 1, 2, 0)
     slots_c, slots_a, slots_b, loads = {}, {}, {}, {}
@@ -825,17 +888,19 @@
     def cut(ref, which):
         return ref.at[pl.ds(which * half, half)]
 
+    def late_cut(ref, which):
+        return ref.at[pl.ds(early + which * (LATE // 2), LATE // 2)]
+
     def begin(k):
         for i in turns:
-            rows = pl.ds(i * 2 * half, 2 * half)
             slots_c[k, i] = wire.slot()
             wire.start(
                 slots_c[k, i],
-                lambda rows=rows: partial.at[order[k], 1, rows],
-                lambda i=i: core_in.at[k, i],
+                lambda i=i: partial.at[order[k], 1, i],
+                lambda i=i: work.at[k, i],
                 to_c,
             )
-            loads[k, i] = local.start(partial.at[order[k], 0, rows], work.at[k, i])
+            loads[k, i] = local.start(partial.at[order[k], 0, i], own_in.at[k % 2, i])
 
     begin(0)
 
@@ -850,14 +915,66 @@
         d,
         t,
         extent,
-        lambda index: work.at[inverse(index), 0],
+        lambda index: work.at[inverse(index), 0, pl.ds(0, early)],
         up_in,
         down_in,
-        2 * half,
+        early,
         1,
     )
-    routes_a = ((to_x, 1, 0, 0, 0), (to_y, 2, 0, 1, 1), (to_x, 3, 2, 0, 2), (to_y, 3, 1, 1, 3))
+    late_line = BundleSum(
+        wire,
+        d,
+        t,
+        extent,
+        lambda index: work.at[inverse(index), pl.ds(0, 4), pl.ds(early, LATE)],
+        late_up,
+        late_down,
+        LATE,
+        1,
+    )
+    routes_a = (
+        (to_x, 3, 2, 0, 0),
+        (to_y, 3, 1, 1, 1),
+        (to_x, 1, 0, 0, 2),
+        (to_y, 2, 0, 1, 3),
+    )
     routes_b = ((to_y, 2, 0, 0), (to_x, 1, 1, 1))
+    last = extent - 1
+
+    def send_a(k, source, cutter, inbox):
+        for device, origin, unused, which, row in routes_a:
+            if origin == source:
+                slots_a[inbox is a_in, k, row] = wire.slot()
+                wire.start(
+                    slots_a[inbox is a_in, k, row],
+                    lambda origin=origin, which=which: cutter(work.at[k, origin], which),
+                    lambda row=row: inbox.at[k, row] if inbox is a_in else inbox.at[row],
+                    device,
+                )
+
+    def receive_a(k, cutter, inbox, second, size):
+        for device, unused, target, which, row in routes_a:
+            region = inbox.at[k, row] if inbox is a_in else inbox.at[row]
+            wire.arrive(slots_a[inbox is a_in, k, row], lambda: region, device)
+            add_into(cutter(work.at[k, target], which), region, size)
+            if row < 2:
+                to, origin, part, b_row = routes_b[row]
+                slots_b[inbox is a_in, k, b_row] = wire.slot()
+                wire.start(
+                    slots_b[inbox is a_in, k, b_row],
+                    lambda origin=origin, part=part: cutter(work.at[k, origin], part),
+                    lambda b_row=b_row: second.at[k, b_row]
+                    if inbox is a_in
+                    else second.at[b_row],
+                    to,
+                )
+
+    def receive_b(k, cutter, inbox, second, size):
+        for device, unused, which, row in routes_b:
+            region = second.at[k, row] if inbox is a_in else second.at[row]
+            wire.arrive(slots_b[inbox is a_in, k, row], lambda: region, device)
+            add_into(cutter(work.at[k, 0], which), region, size)
+
     for turn in range(extent + 2):
         if turn + 1 < extent:
             begin(turn + 1)
@@ -865,49 +982,65 @@
             k = turn
             for i in turns:
                 loads[k, i].wait()
-                wire.arrive(slots_c[k, i], lambda k=k, i=i: core_in.at[k, i], to_c)
-                add_into(work.at[k, i], core_in.at[k, i], 2 * half)
-            for device, source, target, which, row in (
-                routes_a[2],
-                routes_a[3],
-                routes_a[0],
-                routes_a[1],
-            ):
-                slots_a[k, row] = wire.slot()
-                wire.start(
-                    slots_a[k, row],
-                    lambda k=k, source=source, which=which: cut(work.at[k, source], which),
-                    lambda k=k, row=row: a_in.at[k, row],
-                    device,
-                )
+                wire.arrive(slots_c[k, i], lambda k=k, i=i: work.at[k, i], to_c)
+                add_into(work.at[k, i], own_in.at[k % 2, i], rows)
+                send_a(k, i, cut, a_in)
+            if k < last:
+                late_line.step(k)
+        if turn == extent:
+            late_line.last()
+            for i in turns:
+                for inbox in (late_up, late_down):
+                    add_into(
+                        work.at[last, i, pl.ds(early, LATE)], inbox.at[last - 1, i], LATE
+                    )
+                send_a(last, i, late_cut, late_a)
+        between(turn)
         if 1 <= turn <= extent:
-            k = turn - 1
-            for device, source, target, which, row in (
-                routes_a[2],
-                routes_a[3],
-                routes_a[0],
-                routes_a[1],
-            ):
-                wire.arrive(slots_a[k, row], lambda k=k, row=row: a_in.at[k, row], device)
-                add_into(cut(work.at[k, target], which), a_in.at[k, row], half)
-                if row >= 2:
-                    to, origin, part, b_row = routes_b[row - 2]
-                    slots_b[k, b_row] = wire.slot()
-                    wire.start(
-                        slots_b[k, b_row],
-                        lambda k=k, origin=origin, part=part: cut(work.at[k, origin], part),
-                        lambda k=k, b_row=b_row: b_in.at[k, b_row],
-                        to,
-                    )
+            receive_a(turn - 1, cut, a_in, b_in, half)
+        if turn == extent + 1:
+            receive_a(last, late_cut, late_a, late_b, LATE // 2)
         if turn >= 2:
             k = turn - 2
-            for device, source, which, row in routes_b:
-                wire.arrive(slots_b[k, row], lambda k=k, row=row: b_in.at[k, row], device)
-                add_into(cut(work.at[k, 0], which), b_in.at[k, row], half)
-            if k < extent - 1:
+            receive_b(k, cut, a_in, b_in, half)
+            if k < last:
                 line.step(k)
+    receive_b(last, late_cut, late_a, late_b, LATE // 2)
     line.last()
-    return work.at[extent - 1, 0]
+
+
+def own_rows(buffers, rows, columns, body):
+    work, up_in, down_in = buffers[0], buffers[4], buffers[5]
+    mine = work.at[work.shape[0] - 1, 0]
+    up_last, down_last = up_in.at[up_in.shape[0] - 1], down_in.at[down_in.shape[0] - 1]
+    early = rows - LATE
+
+    def first(start):
+        part = pl.ds(start, 16)
+        body(part, own_sum(mine, up_last, down_last, part, columns))
+
+    def second(start):
+        part = pl.ds(pl.multiple_of(early + start, 16), 16)
+        body(part, mine[part, columns].astype(F32))
+
+    rows_loop(early, 16, first)
+    rows_loop(LATE, 16, second)
+
+
+def sum_scratch(extent, rows, width):
+    early = rows - LATE
+    return [
+        pltpu.VMEM((extent, 4, rows, width), BF),
+        pltpu.VMEM((2, 4, rows, width), BF),
+        pltpu.VMEM((extent, 4, early // 2, width), BF),
+        pltpu.VMEM((extent, 2, early // 2, width), BF),
+        pltpu.VMEM((extent - 1, early, width), BF),
+        pltpu.VMEM((extent - 1, early, width), BF),
+        pltpu.VMEM((extent - 1, 4, LATE, width), BF),
+        pltpu.VMEM((extent - 1, 4, LATE, width), BF),
+        pltpu.VMEM((4, LATE // 2, width), BF),
+        pltpu.VMEM((2, LATE // 2, width), BF),
+    ]
 
 
 def plane_devices(d, t, extent):
@@ -1060,36 +1193,6 @@
         compiler_params=kernel_params(1),
         cost_estimate=pl.CostEstimate(flops=0, bytes_accessed=100_000_000, transcendentals=0),
     )(hid, qkv, o, gains, gate, up, down)
-
-
-def line_total_kernel(extent, value, total, inbox, send_sem, recv_sem):
-    d, t = lax.axis_index("dp"), lax.axis_index("tensor")
-    peers = [(d, (t + k) % extent) for k in range(1, extent)]
-    greet([(None, peer) for peer in peers])
-    wire = Wire(send_sem, recv_sem)
-    slots = []
-    for k, peer in enumerate(peers):
-        slot = wire.slot()
-        slots.append(slot)
-        wire.start(slot, lambda: value, lambda k=k: inbox.at[k], peer)
-    result = value[...]
-    for k, peer in enumerate(peers):
-        wire.arrive(slots[k], lambda k=k: inbox.at[k], peer)
-        result = result + inbox[k]
-    total[...] = result
-    wire.finish()
-
-
-def line_total(extent, number, value):
-    return pl.pallas_call(
-        functools.partial(line_total_kernel, extent),
-        out_shape=jax.ShapeDtypeStruct(value.shape, F32),
-        in_specs=[VM],
-        out_specs=VM,
-        scratch_shapes=[pltpu.VMEM((extent - 1,) + value.shape, F32)] + dma_pair(extent - 1),
-        compiler_params=kernel_params(number),
-        cost_estimate=pl.CostEstimate(flops=0, bytes_accessed=10_000_000, transcendentals=0),
-    )(value)
 
 
 class Pieces:
@@ -1179,7 +1282,7 @@
     line.last()
     mine = work.at[t]
     everything = pl.ds(0, width)
-    packet = gathered.at[t, 0, pl.ds(0, rows)]
+    packet = gathered.at[t, 0, 0]
 
     def body(start):
         part = pl.ds(start, 16)
@@ -1203,17 +1306,19 @@
     packet[:, width : width + 128] = jnp.where(lane < 16, high, coeff - high).astype(BF)
 
     def place(j, c, i):
-        return gathered.at[j, c, pl.ds(i * rows, rows)]
-
-    gather = PlaneGather(wire, d, t, extent, lambda: packet, place, rows // 2)
-    gather.stage(0)
+        return gathered.at[j, c, i]
+
+    def bundle(j, c):
+        return gathered.at[j, c, pl.ds(0, 4), pl.ds(rows - LATE, LATE)]
+
+    gather = PlaneGather(wire, d, t, extent, lambda: packet, place, bundle, rows)
     for n in range(2):
         wire.arrive(corner_slots[n], lambda: landed[n], (flip(d, 6 + n), t))
         weights.load(6 + n)
     for bits in range(8):
         weights.loaded(bits)
+    gather.bundle_start()
     units = out_weight.shape[0]
-    tile = 256
 
     def stage_copies(slot, j, c):
         return (
@@ -1240,20 +1345,26 @@
 
         pltpu.make_async_copy(gathered.at[j, c], tokens.at[j, c], token_sem.at[g]).start()
 
-        def some(start):
-            part = pl.ds(start, tile)
+        def some(first, carry):
+            blocks, part = pl.ds(2 * first, 2), pl.ds(first * 2 * rows, 2 * rows)
             values = jnp.dot(
-                gathered[j, c, part, 0:width], in_weight[...], preferred_element_type=F32
+                gathered[j, c, blocks, :, 0:width].reshape(2 * rows, width),
+                in_weight[...],
+                preferred_element_type=F32,
             )
             hidden_stage[slot, part] = values.astype(BF)
             gate_value, up_value = values[:, :units], values[:, units:]
-            coeff = coefficients(gathered[j, c, part, width : width + 128], d, units // 2)
+            coeff = coefficients(
+                gathered[j, c, blocks, :, width : width + 128].reshape(2 * rows, 128),
+                d,
+                units // 2,
+            )
             active = (coeff * (gate_value * jax.nn.sigmoid(gate_value)) * up_value).astype(BF)
-            out_stage[slot, part] = jnp.dot(
-                active, out_weight[...], preferred_element_type=F32
-            ).astype(BF)
-
-        rows_loop(4 * rows, tile, some)
+            result = jnp.dot(active, out_weight[...], preferred_element_type=F32)
+            out_stage[slot, blocks] = result.astype(BF).reshape(2, rows, width)
+            return carry
+
+        lax.fori_loop(0, 2, some, 0)
         for copy in stage_copies(slot, j, c):
             copy.start()
         return carry
@@ -1281,25 +1392,25 @@
             jax.ShapeDtypeStruct((rows, width), F32),
             jax.ShapeDtypeStruct((rows, 128), F32),
             jax.ShapeDtypeStruct((rows, width), BF),
-            jax.ShapeDtypeStruct((extent, 2, 4 * rows, width + 128), BF),
+            jax.ShapeDtypeStruct((extent, 2, 4, rows, width + 128), BF),
             jax.ShapeDtypeStruct((extent, 2, 4 * rows, 4 * slab), BF),
-            jax.ShapeDtypeStruct((extent, 2, 4 * rows, width), BF),
+            jax.ShapeDtypeStruct((extent, 2, 4, rows, width), BF),
             piece,
             piece,
         ],
         in_specs=[ANY, VM, VM, VM, VM] + [ANY] * 8,
         out_specs=[VM, VM, VM] + [ANY] * 5,
         scratch_shapes=[
-            pltpu.VMEM((extent, 2, 4 * rows, width + 128), BF),
+            pltpu.VMEM((extent, 2, 4, rows, width + 128), BF),
             pltpu.VMEM((extent, rows, width), BF),
             pltpu.VMEM((extent - 1, rows, width), BF),
             pltpu.VMEM((extent - 1, rows, width), BF),
             pltpu.VMEM((width, 4 * slab), BF),
             pltpu.VMEM((2 * slab, width), BF),
             pltpu.VMEM((2, 4 * rows, 4 * slab), BF),
-            pltpu.VMEM((2, 4 * rows, width), BF),
+            pltpu.VMEM((2, 4, rows, width), BF),
         ]
-        + dma_pair(80)
+        + dma_pair(100)
         + [
             pltpu.SemaphoreType.DMA((2,)),
             pltpu.SemaphoreType.DMA((48,)),
@@ -1311,17 +1422,6 @@
     )(partial, hid, gain, router, chosen, *near, *corner)
 
 
-def sum_scratch(extent, rows, width):
-    return [
-        pltpu.VMEM((extent, 4, rows, width), BF),
-        pltpu.VMEM((extent, 4, rows, width), BF),
-        pltpu.VMEM((extent, 4, rows // 2, width), BF),
-        pltpu.VMEM((extent, 2, rows // 2, width), BF),
-        pltpu.VMEM((extent - 1, rows, width), BF),
-        pltpu.VMEM((extent - 1, rows, width), BF),
-    ]
-
-
 def transposed_dot(left, right):
     return lax.dot_general(left, right, (((0,), (0,)), ((), ())), preferred_element_type=F32)
 
@@ -1332,21 +1432,13 @@
 
 def turn_kernel(extent, partial, middle, teacher, weight, tokens, hidden, *rest):
     pieces = rest[:8]
-    grad_output, row_loss, out = rest[8:11]
-    results, grads = rest[11:19], rest[19]
+    grad_output, row_loss, out, inner_out, active_out, grads = rest[8:14]
+    buffers = rest[14:24]
     (
-        work,
-        core_in,
-        a_in,
-        b_in,
-        up_in,
-        down_in,
         packet,
         in_weight,
         out_weight,
-        in_total,
-        out_total,
-        token_tile,
+        coeff_tile,
         hidden_tile,
         grad_tile,
         out_stage,
@@ -1357,24 +1449,22 @@
         local_sem,
         weight_sem,
         tile_sem,
-    ) = rest[20:]
+    ) = rest[24:]
     d, t = lax.axis_index("dp"), lax.axis_index("tensor")
     rows, width = middle.shape
     greet(plane_devices(d, t, extent))
     wire, local = Wire(send_sem, recv_sem), Local(local_sem)
     weights = Pieces(d, in_weight, out_weight, weight_sem, pieces)
-    mine = sum_plane(
-        wire, local, d, t, extent, partial, work, core_in, a_in, b_in, up_in, down_in, rows // 2
-    )
-    for bits in range(8):
-        weights.load(bits)
-    everything = pl.ds(0, width)
-
-    def body(start):
-        part = pl.ds(start, 16)
-        output = middle[part] + own_sum(
-            mine, up_in.at[extent - 2], down_in.at[extent - 2], part, everything
-        )
+
+    def between(turn_number):
+        if turn_number == 1:
+            for bits in range(8):
+                weights.load(bits)
+
+    sum_plane(wire, local, d, t, extent, partial, buffers, rows, between)
+
+    def body(part, value):
+        output = middle[part] + value
         mismatch = output - teacher[part].astype(F32)
         scaled = mismatch * weight[part, 0:1]
         grad_output[part] = scaled
@@ -1383,32 +1473,40 @@
             jnp.sum(scaled * mismatch, axis=-1, keepdims=True), (16, 128)
         )
 
-    rows_loop(rows, 16, body)
+    own_rows(buffers, rows, pl.ds(0, width), body)
 
     def place(j, c, i):
-        return grads.at[j, c, pl.ds(i * rows, rows)]
+        return grads.at[j, c, i]
+
+    def bundle(j, c):
+        return grads.at[j, c, pl.ds(0, 4), pl.ds(rows - LATE, LATE)]
 
     own_copy = local.start(packet, place(t, 0, 0))
-    gather = PlaneGather(wire, d, t, extent, lambda: packet, place, rows // 2)
-    gather.stage(0)
-    in_total[...] = jnp.zeros(in_total.shape, F32)
-    out_total[...] = jnp.zeros(out_total.shape, F32)
+    gather = PlaneGather(wire, d, t, extent, lambda: packet, place, bundle, rows)
+    own_copy.wait()
+    gather.bundle_start()
     for bits in range(8):
         weights.loaded(bits)
-    own_copy.wait()
     units, slab = out_weight.shape[0], out_weight.shape[0] // 2
-    tile = 256
     actions = gather.actions()
 
-    def out_copy(j, c):
-        return pltpu.make_async_copy(out_stage, out.at[j, c], tile_sem.at[3])
+    def out_copies(j, c):
+        return (
+            pltpu.make_async_copy(out_stage, out.at[j, c], tile_sem.at[3]),
+            pltpu.make_async_copy(inner_tile, inner_out.at[j, c], tile_sem.at[4]),
+            pltpu.make_async_copy(active_tile, active_out.at[j, c], tile_sem.at[5]),
+        )
 
     def group(g, carry):
         j, c = arrival(t, g // 2), g % 2
-        token_copy = pltpu.make_async_copy(tokens.at[j, c], token_tile, tile_sem.at[0])
+        coeff_copy = pltpu.make_async_copy(
+            tokens.at[j, c, pl.ds(0, 4), pl.ds(0, rows), pl.ds(width, 128)],
+            coeff_tile,
+            tile_sem.at[0],
+        )
         hidden_copy = pltpu.make_async_copy(hidden.at[j, c], hidden_tile, tile_sem.at[1])
         grad_copy = pltpu.make_async_copy(grads.at[j, c], grad_tile, tile_sem.at[2])
-        token_copy.start()
+        coeff_copy.start()
         hidden_copy.start()
         for number, steps in enumerate(actions):
 
@@ -1421,62 +1519,51 @@
 
         @pl.when(g >= 1)
         def _():
-            out_copy(j, c).wait()
-
-        token_copy.wait()
+            for copy in out_copies(j, c):
+                copy.wait()
+
+        coeff_copy.wait()
         hidden_copy.wait()
         grad_copy.wait()
 
-        def some(start):
-            part = pl.ds(start, tile)
-            grad_active = dot_transposed(grad_tile[part], out_weight[...])
+        def some(first, carry):
+            size = 2 * rows
+            blocks, part = pl.ds(2 * first, 2), pl.ds(first * size, size)
+            grad_active = dot_transposed(
+                grad_tile[blocks].reshape(size, width), out_weight[...]
+            )
             gate_value = hidden_tile[part, 0:units].astype(F32)
             up_value = hidden_tile[part, units : 2 * units].astype(F32)
-            coeff = coefficients(token_tile[part, width : width + 128], d, slab)
+            coeff = coefficients(coeff_tile[blocks].reshape(size, 128), d, slab)
             sigmoid_value = jax.nn.sigmoid(gate_value)
             silu_value = gate_value * sigmoid_value
             inner = grad_active * coeff
             direct = silu_value * up_value
             active_tile[part] = (coeff * direct).astype(BF)
             product = grad_active * direct
-            lane = lax.broadcasted_iota(jnp.int32, (tile, 128), 1)
-            sums = jnp.zeros((tile, 128), F32)
+            lane = lax.broadcasted_iota(jnp.int32, (size, 128), 1)
+            sums = jnp.zeros((size, 128), F32)
             for e in range(2):
                 one = jnp.sum(product[:, e * slab : (e + 1) * slab], axis=-1, keepdims=True)
                 sums = sums + jnp.where(lane == 2 * d + e, one, 0.0)
-            out_stage[part, width : width + 128] = sums.astype(BF)
+            out_stage[blocks, :, width : width + 128] = sums.astype(BF).reshape(2, rows, 128)
             grad_gate = (
                 inner * up_value * sigmoid_value * (1.0 + gate_value * (1.0 - sigmoid_value))
             )
             inner_tile[part, 0:units] = grad_gate.astype(BF)
             inner_tile[part, units : 2 * units] = (inner * silu_value).astype(BF)
-            out_stage[part, 0:width] = dot_transposed(inner_tile[part], in_weight[...]).astype(BF)
-
-        rows_loop(4 * rows, tile, some)
-        out_copy(j, c).start()
-
-        def into_in(start):
-            part = pl.ds(start, 256)
-            in_total[part] += transposed_dot(token_tile[:, part], inner_tile[...])
-
-        rows_loop(width, 256, into_in)
-
-        def into_out(start):
-            part = pl.ds(start, 512)
-            out_total[:, part] += transposed_dot(active_tile[...], grad_tile[:, part])
-
-        rows_loop(width, 512, into_out)
+            result = dot_transposed(inner_tile[part], in_weight[...]).astype(BF)
+            out_stage[blocks, :, 0:width] = result.reshape(2, rows, width)
+            return carry
+
+        lax.fori_loop(0, 2, some, 0)
+        for copy in out_copies(j, c):
+            copy.start()
         return carry
 
     lax.fori_loop(0, 2 * extent, group, 0)
-    in_weight[...] = in_total[...].astype(BF)
-    out_weight[...] = out_total[...].astype(BF)
-    stores = Pieces(d, in_weight, out_weight, weight_sem, results)
-    for bits in range(8):
-        stores.store(bits)
-    for bits in range(8):
-        stores.stored(bits)
-    out_copy(0, 0).wait()
+    for copy in out_copies(0, 0):
+        copy.wait()
     wire.finish()
 
 
@@ -1488,70 +1575,132 @@
         out_shape=[
             jax.ShapeDtypeStruct((rows, width), F32),
             jax.ShapeDtypeStruct((rows, 128), F32),
-            jax.ShapeDtypeStruct((extent, 2, 4 * rows, width + 128), BF),
-        ]
-        + [jax.ShapeDtypeStruct(pieces[0].shape, BF)] * 8
-        + [jax.ShapeDtypeStruct((extent, 2, 4 * rows, width), BF)],
+            jax.ShapeDtypeStruct((extent, 2, 4, rows, width + 128), BF),
+            jax.ShapeDtypeStruct((extent, 2, 4 * rows, 4 * slab), BF),
+            jax.ShapeDtypeStruct((extent, 2, 4 * rows, 2 * slab), BF),
+            jax.ShapeDtypeStruct((extent, 2, 4, rows, width), BF),
+        ],
         in_specs=[ANY, VM, VM, VM] + [ANY] * 10,
-        out_specs=[VM, VM] + [ANY] * 10,
+        out_specs=[VM, VM] + [ANY] * 4,
         scratch_shapes=sum_scratch(extent, rows, width)
         + [
             pltpu.VMEM((rows, width), BF),
             pltpu.VMEM((width, 4 * slab), BF),
             pltpu.VMEM((2 * slab, width), BF),
-            pltpu.VMEM((width, 4 * slab), F32),
-            pltpu.VMEM((2 * slab, width), F32),
-            pltpu.VMEM((4 * rows, width + 128), BF),
+            pltpu.VMEM((4, rows, 128), BF),
             pltpu.VMEM((4 * rows, 4 * slab), BF),
-            pltpu.VMEM((4 * rows, width), BF),
-            pltpu.VMEM((4 * rows, width + 128), BF),
+            pltpu.VMEM((4, rows, width), BF),
+            pltpu.VMEM((4, rows, width + 128), BF),
             pltpu.VMEM((4 * rows, 2 * slab), BF),
             pltpu.VMEM((4 * rows, 4 * slab), BF),
         ]
-        + dma_pair(120)
+        + dma_pair(150)
         + [
             pltpu.SemaphoreType.DMA((20,)),
             pltpu.SemaphoreType.DMA((48,)),
-            pltpu.SemaphoreType.DMA((4,)),
+            pltpu.SemaphoreType.DMA((6,)),
         ],
         compiler_params=kernel_params(4),
         cost_estimate=pl.CostEstimate(flops=0, bytes_accessed=450_000_000, transcendentals=0),
-    )(partial, middle, teacher, weight, tokens, hidden, *pieces)[:11]
+    )(partial, middle, teacher, weight, tokens, hidden, *pieces)
+
+
+class WeightGrads:
+    def __init__(self, sources, tiles, totals, sem):
+        self.sources, self.tiles, self.sem = sources, tiles, sem
+        self.in_total, self.out_total = totals
+
+    def copies(self, g):
+        j, c, slot = g // 2, g % 2, g % 2
+        return [
+            pltpu.make_async_copy(source.at[j, c], tile.at[slot], self.sem.at[n, slot])
+            for n, (source, tile) in enumerate(zip(self.sources, self.tiles))
+        ]
+
+    def start(self, g):
+        for copy in self.copies(g):
+            copy.start()
+
+    def clear(self):
+        self.in_total[...] = jnp.zeros(self.in_total.shape, F32)
+        self.out_total[...] = jnp.zeros(self.out_total.shape, F32)
+
+    def work(self, g, count):
+        if g + 1 < count:
+            self.start(g + 1)
+        for copy in self.copies(g):
+            copy.wait()
+        slot = g % 2
+        token_tile, grad_tile, inner_tile, active_tile = (tile.at[slot] for tile in self.tiles)
+        size, width = inner_tile.shape[0], grad_tile.shape[2]
+
+        def into_in(start):
+            part = pl.ds(start, 256)
+            left = token_tile[:, :, part].reshape(size, 256)
+            self.in_total[part] += transposed_dot(left, inner_tile[...])
+
+        rows_loop(width, 256, into_in)
+
+        def into_out(start):
+            part = pl.ds(start, 512)
+            right = grad_tile[:, :, part].reshape(size, 512)
+            self.out_total[:, part] += transposed_dot(active_tile[...], right)
+
+        rows_loop(width, 512, into_out)
+
+    def pieces(self, d, stage):
+        slab = stage.shape[3]
+        for bits in range(8):
+            part = pl.ds(pl.multiple_of(flip(d, bits) * slab, slab), slab)
+            for place in range(3):
+                for e in range(2):
+                    if place < 2:
+                        column = (2 * place + e) * slab
+                        value = self.in_total[part, column : column + slab]
+                    else:
+                        value = self.out_total[e * slab : (e + 1) * slab, part]
+                    stage[bits, place, e] = value.astype(BF)
 
 
 def leave_kernel(extent, partial, middle, grad_output, gates, chosen, gain, router_t, *rest):
-    sent = rest[:5]
-    grad_middle, grad_logits, gain_part, grads = rest[5:9]
-    came = rest[9:14]
-    (
-        work,
-        core_in,
-        a_in,
-        b_in,
-        up_in,
-        down_in,
-        packet,
-        extra,
-        send_sem,
-        recv_sem,
-        local_sem,
-    ) = rest[14:]
+    sources = rest[:4]
+    grad_middle, grad_logits, gain_part, grads = rest[4:8]
+    came = rest[8:16]
+    buffers = rest[16:26]
+    tiles, totals = rest[26:30], rest[30:32]
+    stage, packet, send_sem, recv_sem, local_sem, tile_sem = rest[32:]
     d, t = lax.axis_index("dp"), lax.axis_index("tensor")
     rows, width = middle.shape
     greet(line_devices(d, t, extent) + [(None, (flip(d, bits), t)) for bits in range(1, 6)])
     wire, local = Wire(send_sem, recv_sem), Local(local_sem)
-    mine = sum_plane(
-        wire, local, d, t, extent, partial, work, core_in, a_in, b_in, up_in, down_in, rows // 2
-    )
+    weight_grads = WeightGrads(sources, tiles, totals, tile_sem)
+    count = 2 * extent
+    weight_grads.start(0)
+
+    def between(turn_number):
+        if turn_number == 0:
+            weight_grads.clear()
+        if turn_number < extent:
+            weight_grads.work(2 * turn_number, count)
+            weight_grads.work(2 * turn_number + 1, count)
+
+    sum_plane(wire, local, d, t, extent, partial, buffers, rows, between)
+    weight_grads.pieces(d, stage)
     piece_slots = []
-    for n in range(5):
+    for bits in range(1, 6):
         slot = wire.slot()
         piece_slots.append(slot)
-        wire.start(slot, lambda n=n: sent[n], lambda n=n: came[n], (flip(d, 1 + n), t))
-    up_last, down_last = up_in.at[extent - 2], down_in.at[extent - 2]
-    coeff_grad = (
-        own_sum(mine, up_last, down_last, pl.ds(0, rows), pl.ds(width, 128)) * chosen[...]
-    )
+        wire.start(
+            slot, lambda bits=bits: stage.at[bits], lambda bits=bits: came[bits], (flip(d, bits), t)
+        )
+    copies = [local.start(stage.at[bits], came[bits]) for bits in (0, 6, 7)]
+    coeff_grads = []
+
+    def collect(part, value):
+        grad_logits[part] = value
+
+    own_rows(buffers, rows, pl.ds(width, 128), collect)
+    coeff_grad = grad_logits[...] * chosen[...]
     lane = lax.broadcasted_iota(jnp.int32, coeff_grad.shape, 1)
     probs = jnp.where(lane < 16, gates[...], 0.0)
     coeff_grad = jnp.where(lane < 16, coeff_grad, 0.0)
@@ -1561,14 +1710,13 @@
     low_part = (logit_grad - high.astype(F32)).astype(BF)
     for begin in range(0, width, 512):
         columns = slice(begin, begin + 512)
-        extra[:, columns] = jnp.dot(
+        grad_middle[:, columns] = jnp.dot(
             high, router_t[:, columns], preferred_element_type=F32
         ) + jnp.dot(low_part, router_t[:, columns], preferred_element_type=F32)
     gain_part[...] = jnp.zeros(gain_part.shape, F32)
 
-    def body(start):
-        part = pl.ds(start, 16)
-        grad = own_sum(mine, up_last, down_last, part, pl.ds(0, width)) + extra[part]
+    def body(part, value):
+        grad = value + grad_middle[part]
         value = middle[part]
         inverse = lax.rsqrt(jnp.mean(value * value, axis=-1, keepdims=True) + EPSILON)
         unit = value * inverse
@@ -1581,23 +1729,27 @@
         grad_middle[part] = result
         packet[part] = result.astype(BF)
 
-    rows_loop(rows, 16, body)
+    own_rows(buffers, rows, pl.ds(0, width), body)
 
     def place(index):
         return grads.at[index]
 
-    copy = local.start(packet, place(t))
+    copies.append(local.start(packet, place(t)))
     line = LineGather(wire, d, t, extent, lambda: packet, place)
     for step in range(1, extent):
         line.step(step)
-    copy.wait()
-    for n in range(5):
-        wire.arrive(piece_slots[n], lambda: came[n], (flip(d, 1 + n), t))
+    for copy in copies:
+        copy.wait()
+    for n, slot in enumerate(piece_slots):
+        wire.arrive(slot, lambda: came[1 + n], (flip(d, 1 + n), t))
     wire.finish()
 
 
-def leave(extent, partial, middle, grad_output, gates, chosen, gain, router_t, sent):
+def leave(extent, partial, middle, grad_output, gates, chosen, gain, router_t, sources):
     rows, width = middle.shape
+    tokens, grads, inner, active = sources
+    units = active.shape[3]
+    piece = jax.ShapeDtypeStruct((3, 2, units // 2, units // 2), BF)
     return pl.pallas_call(
         functools.partial(leave_kernel, extent),
         out_shape=[
@@ -1606,16 +1758,327 @@
             jax.ShapeDtypeStruct((8, width), F32),
             jax.ShapeDtypeStruct((extent, rows, width), BF),
         ]
-        + [jax.ShapeDtypeStruct(piece.shape, BF) for piece in sent],
-        in_specs=[ANY, VM, VM, VM, VM, VM, VM] + [ANY] * 5,
-        out_specs=[VM, VM, VM] + [ANY] * 6,
+        + [piece] * 8,
+        in_specs=[ANY, VM, VM, VM, VM, VM, VM] + [ANY] * 4,
+        out_specs=[VM, VM, VM] + [ANY] * 9,
         scratch_shapes=sum_scratch(extent, rows, width + 128)
-        + [pltpu.VMEM((rows, width), BF), pltpu.VMEM((rows, width), F32)]
-        + dma_pair(80)
-        + [pltpu.SemaphoreType.DMA((20,))],
+        + [pltpu.VMEM((2,) + source.shape[2:], BF) for source in sources]
+        + [
+            pltpu.VMEM((width, 2 * units), F32),
+            pltpu.VMEM((units, width), F32),
+            pltpu.VMEM((8,) + piece.shape, BF),
+            pltpu.VMEM((rows, width), BF),
+        ]
+        + dma_pair(120)
+        + [pltpu.SemaphoreType.DMA((24,)), pltpu.SemaphoreType.DMA((4, 2))],
         compiler_params=kernel_params(5),
         cost_estimate=pl.CostEstimate(flops=0, bytes_accessed=350_000_000, transcendentals=0),
-    )(partial, middle, grad_output, gates, chosen, gain, router_t, *sent)
+    )(partial, middle, grad_output, gates, chosen, gain, router_t, *sources)
+
+
+def line_exchange(wire, t, d, extent, outbox, inbox):
+    peers = [(d, (t + k) % extent) for k in range(1, extent)]
+    slots = []
+    for k, peer in enumerate(peers):
+        slot = wire.slot()
+        slots.append(slot)
+        wire.start(slot, lambda: outbox, lambda k=k: inbox.at[k], peer)
+    result = outbox[...]
+    for k, peer in enumerate(peers):
+        wire.arrive(slots[k], lambda k=k: inbox.at[k], peer)
+        result = result + inbox[k]
+    return result
+
+
+def columns_to_rows(ref):
+    return ref[...].T[0:8]
+
+
+def rows_to_columns(value):
+    return jnp.concatenate([value, jnp.zeros((120, value.shape[1]), F32)], axis=0).T
+
+
+def turned(value, cosine, sine, direction):
+    return value * cosine + direction * pltpu.roll(value, HD // 2, 1) * sine
+
+
+def line_peers(d, t, extent):
+    return [(None, (d, (t + k) % extent)) for k in range(1, extent)]
+
+
+def attend_kernel(
+    extent,
+    length,
+    hid,
+    gain,
+    qkv_weight,
+    o_weight,
+    head_gain,
+    cosine,
+    sine,
+    normed,
+    units,
+    low,
+    probs,
+    mixed,
+    out,
+    inverses,
+    raw,
+    sums,
+    outbox,
+    inbox,
+    send_sem,
+    recv_sem,
+):
+    d, t = lax.axis_index("dp"), lax.axis_index("tensor")
+    seq_len, width = hid.shape
+    heads = head_gain.shape[0] // 2
+    columns = heads * HD
+    greet(line_peers(d, t, extent))
+    wire = Wire(send_sem, recv_sem)
+    tile = 256
+
+    def project(start):
+        part = pl.ds(start, tile)
+        value = hid[part].astype(F32)
+        unit = value * lax.rsqrt(jnp.mean(value * value, axis=-1, keepdims=True) + EPSILON)
+        normed[part] = (unit * gain[...]).astype(BF)
+        result = jnp.dot(normed[part], qkv_weight[...], preferred_element_type=F32)
+        raw[part] = result
+        lane = lax.broadcasted_iota(jnp.int32, (tile, 128), 1)
+        squares = [
+            jnp.sum(jnp.square(result[:, n * columns : (n + 1) * columns]), axis=-1, keepdims=True)
+            for n in range(2)
+        ]
+        sums[part] = jnp.where(lane == 0, squares[0], jnp.where(lane == 1, squares[1], 0.0))
+
+    rows_loop(seq_len, tile, project)
+    outbox[...] = columns_to_rows(sums)
+    total = line_exchange(wire, t, d, extent, outbox, inbox)
+    inverses[...] = rows_to_columns(lax.rsqrt(total / width + EPSILON))
+    low[:, 2 * columns :] = raw[:, 2 * columns :].astype(BF)
+
+    def head(h, carry):
+        for n in range(2):
+            section = pl.ds(pl.multiple_of(n * columns + h * HD, HD), HD)
+            unit = raw[:, section] * inverses[:, n : n + 1]
+            units[:, section] = unit
+            scaled = unit * head_gain[pl.ds(n * heads + h, 1)]
+            low[:, section] = turned(scaled, cosine[...], sine[...], 1.0).astype(BF)
+        section = pl.ds(pl.multiple_of(h * HD, HD), HD)
+        key_section = pl.ds(pl.multiple_of(columns + h * HD, HD), HD)
+        value_section = pl.ds(pl.multiple_of(2 * columns + h * HD, HD), HD)
+
+        def some(start):
+            part = pl.ds(start, tile)
+            scores = dot_transposed(low[part, section], low[:, key_section]) / math.sqrt(HD)
+            row = start + lax.broadcasted_iota(jnp.int32, scores.shape, 0)
+            column = lax.broadcasted_iota(jnp.int32, scores.shape, 1)
+            allowed = both(column <= row, column < length[0])
+            scores = jnp.where(allowed, scores, -1e30)
+            powers = jnp.exp(scores - jnp.max(scores, axis=-1, keepdims=True))
+            result = powers / jnp.sum(powers, axis=-1, keepdims=True)
+            probs[h, part] = result
+            mixed[part, section] = jnp.dot(
+                result.astype(BF), low[:, value_section], preferred_element_type=F32
+            ).astype(BF)
+
+        rows_loop(seq_len, tile, some)
+        return carry
+
+    lax.fori_loop(0, heads, head, 0)
+
+    def finish(start):
+        part = pl.ds(start, tile)
+        out[part] = jnp.dot(mixed[part], o_weight[...], preferred_element_type=F32).astype(BF)
+
+    rows_loop(seq_len, tile, finish)
+    wire.finish()
+
+
+SMEM = pl.BlockSpec(memory_space=pltpu.SMEM)
+
+
+def attend(extent, length, hid, gain, qkv_weight, o_weight, head_gain, cosine, sine):
+    seq_len, width = hid.shape
+    heads = head_gain.shape[0] // 2
+    columns = heads * HD
+    return pl.pallas_call(
+        functools.partial(attend_kernel, extent),
+        out_shape=[
+            jax.ShapeDtypeStruct((seq_len, width), BF),
+            jax.ShapeDtypeStruct((seq_len, 2 * columns), F32),
+            jax.ShapeDtypeStruct((seq_len, 3 * columns), BF),
+            jax.ShapeDtypeStruct((heads, seq_len, seq_len), F32),
+            jax.ShapeDtypeStruct((seq_len, columns), BF),
+            jax.ShapeDtypeStruct((seq_len, width), BF),
+            jax.ShapeDtypeStruct((seq_len, 128), F32),
+        ],
+        in_specs=[SMEM] + [VM] * 7,
+        out_specs=[VM] * 7,
+        scratch_shapes=[
+            pltpu.VMEM((seq_len, 3 * columns), F32),
+            pltpu.VMEM((seq_len, 128), F32),
+            pltpu.VMEM((8, seq_len), F32),
+            pltpu.VMEM((extent - 1, 8, seq_len), F32),
+        ]
+        + dma_pair(extent - 1),
+        compiler_params=kernel_params(2),
+        cost_estimate=pl.CostEstimate(flops=0, bytes_accessed=60_000_000, transcendentals=0),
+    )(length, hid, gain, qkv_weight, o_weight, head_gain, cosine, sine)
+
+
+def attend_back_kernel(
+    extent,
+    grads,
+    row_loss,
+    hid,
+    gain,
+    qkv_weight,
+    o_weight,
+    head_gain,
+    cosine,
+    sine,
+    normed,
+    units,
+    low,
+    probs,
+    mixed,
+    inverses,
+    out,
+    grad_qkv,
+    grad_o,
+    attn_gain_part,
+    head_gain_part,
+    loss,
+    grad_mixed,
+    scaled,
+    raw_grad,
+    sums,
+    dots,
+    outbox,
+    inbox,
+    send_sem,
+    recv_sem,
+):
+    d, t = lax.axis_index("dp"), lax.axis_index("tensor")
+    seq_len, width = hid.shape
+    heads = head_gain.shape[0] // 2
+    columns = heads * HD
+    greet(line_peers(d, t, extent))
+    wire = Wire(send_sem, recv_sem)
+    tile = 256
+    root = math.sqrt(HD)
+
+    def mix(start):
+        part = pl.ds(start, tile)
+        grad_mixed[part] = dot_transposed(grads[part], o_weight[...]).astype(BF)
+
+    rows_loop(seq_len, tile, mix)
+
+    def into_o(start):
+        part = pl.ds(start, 512)
+        grad_o[:, part] = transposed_dot(mixed[...], grads[:, part]).astype(BF)
+
+    rows_loop(width, 512, into_o)
+    sums[...] = jnp.zeros(sums.shape, F32)
+
+    def head(h, carry):
+        section = pl.ds(pl.multiple_of(h * HD, HD), HD)
+        key_section = pl.ds(pl.multiple_of(columns + h * HD, HD), HD)
+        value_section = pl.ds(pl.multiple_of(2 * columns + h * HD, HD), HD)
+        chance = probs[h]
+        incoming = grad_mixed[:, section]
+        raw_grad[:, value_section] = transposed_dot(chance.astype(BF), incoming).astype(BF)
+        grad_probs = dot_transposed(incoming, low[:, value_section])
+        grad_scores = (
+            chance * (grad_probs - jnp.sum(grad_probs * chance, axis=-1, keepdims=True))
+        ).astype(BF)
+        pair = (
+            jnp.dot(grad_scores, low[:, key_section], preferred_element_type=F32) / root,
+            transposed_dot(grad_scores, low[:, section]) / root,
+        )
+        lane = lax.broadcasted_iota(jnp.int32, (seq_len, 128), 1)
+        for n, where in enumerate((section, key_section)):
+            value = turned(pair[n], cosine[...], sine[...], -1.0)
+            unit = units[:, where]
+            head_gain_part[pl.ds(n * heads + h, 1)] = jnp.sum(value * unit, axis=0, keepdims=True)
+            value = value * head_gain[pl.ds(n * heads + h, 1)]
+            scaled[:, where] = value
+            sums[...] += jnp.where(lane == n, jnp.sum(value * unit, axis=-1, keepdims=True), 0.0)
+        return carry
+
+    lax.fori_loop(0, heads, head, 0)
+    outbox[...] = columns_to_rows(sums)
+    outbox[2:3] = jnp.broadcast_to(jnp.sum(row_loss[:, 0:1], axis=0, keepdims=True), (1, seq_len))
+    total = line_exchange(wire, t, d, extent, outbox, inbox)
+    loss[...] = total[:, 0:128]
+    dots[...] = rows_to_columns(total / width)
+
+    def head_again(h, carry):
+        for n in range(2):
+            section = pl.ds(pl.multiple_of(n * columns + h * HD, HD), HD)
+            raw_grad[:, section] = (
+                inverses[:, n : n + 1]
+                * (scaled[:, section] - units[:, section] * dots[:, n : n + 1])
+            ).astype(BF)
+        return carry
+
+    lax.fori_loop(0, heads, head_again, 0)
+    attn_gain_part[...] = jnp.zeros(attn_gain_part.shape, F32)
+
+    def finish(start):
+        part = pl.ds(start, tile)
+        grad = dot_transposed(raw_grad[part], qkv_weight[...])
+        value = hid[part].astype(F32)
+        inverse = lax.rsqrt(jnp.mean(value * value, axis=-1, keepdims=True) + EPSILON)
+        unit = value * inverse
+        attn_gain_part[...] += jnp.sum((grad * unit).reshape(tile // 8, 8, width), axis=0)
+        change = grad * gain[...]
+        out[part] = (
+            inverse * (change - unit * jnp.mean(change * unit, axis=-1, keepdims=True))
+        ).astype(BF)
+
+    rows_loop(seq_len, tile, finish)
+
+    def into_qkv(start):
+        part = pl.ds(start, 256)
+        grad_qkv[part] = transposed_dot(normed[:, part], raw_grad[...]).astype(BF)
+
+    rows_loop(width, 256, into_qkv)
+    wire.finish()
+
+
+def attend_back(extent, *operands):
+    seq_len, width = operands[0].shape
+    head_gain = operands[6]
+    heads = head_gain.shape[0] // 2
+    columns = heads * HD
+    return pl.pallas_call(
+        functools.partial(attend_back_kernel, extent),
+        out_shape=[
+            jax.ShapeDtypeStruct((seq_len, width), BF),
+            jax.ShapeDtypeStruct((width, 3 * columns), BF),
+            jax.ShapeDtypeStruct((columns, width), BF),
+            jax.ShapeDtypeStruct((8, width), F32),
+            jax.ShapeDtypeStruct((2 * heads, HD), F32),
+            jax.ShapeDtypeStruct((8, 128), F32),
+        ],
+        in_specs=[VM] * len(operands),
+        out_specs=[VM] * 6,
+        scratch_shapes=[
+            pltpu.VMEM((seq_len, columns), BF),
+            pltpu.VMEM((seq_len, 2 * columns), F32),
+            pltpu.VMEM((seq_len, 3 * columns), BF),
+            pltpu.VMEM((seq_len, 128), F32),
+            pltpu.VMEM((seq_len, 128), F32),
+            pltpu.VMEM((8, seq_len), F32),
+            pltpu.VMEM((extent - 1, 8, seq_len), F32),
+        ]
+        + dma_pair(extent - 1),
+        compiler_params=kernel_params(6),
+        cost_estimate=pl.CostEstimate(flops=0, bytes_accessed=1_000_000, transcendentals=0),
+    )(*operands)
 
 
 def close_kernel(
@@ -1888,7 +2351,6 @@
     total_count = jnp.sum(lengths).astype(F32)
     attn_gain = attn_norm_gain.astype(F32)
     ffn_gain = ffn_norm_gain.astype(F32)[None, :]
-    root_size = math.sqrt(HD)
     expert_count = router_weight.shape[1]
     head_width = q_gain.shape[1]
     local_heads = q_gain.shape[0]
@@ -1904,52 +2366,16 @@
         extent, hidden_in, qkv_own, o_weight, gains_own, gate_weight, up_weight, down_weight
     )
     pieces = [exchange(piece, bits) for bits, piece in enumerate(sent[:6])]
-    gains_full = jnp.sum(gains_all, axis=0)
-    query_gain = gains_full[:local_heads].reshape(-1)
-    key_gain = gains_full[local_heads:].reshape(-1)
-
-    hidden_all = hidden_bf.astype(F32)
-    inverse_one = inverse_rms(hidden_all)
-    unit_one = hidden_all * inverse_one
-    normed = (unit_one * attn_gain).astype(BF)
-    qkv = jnp.dot(normed, qkv_full, preferred_element_type=F32)
-    query_raw, key_raw = qkv[:, :columns], qkv[:, columns : 2 * columns]
-    value_low = qkv[:, 2 * columns :].astype(BF)
-    squares = jnp.stack(
-        [jnp.sum(query_raw * query_raw, axis=1), jnp.sum(key_raw * key_raw, axis=1)]
-    )
-    squares = line_total(extent, 2, squares.reshape(-1, 128)).reshape(2, seq_len)
-    query_inv = lax.rsqrt(squares[0] / width + EPSILON)[:, None]
-    key_inv = lax.rsqrt(squares[1] / width + EPSILON)[:, None]
-    query_unit = query_raw * query_inv
-    key_unit = key_raw * key_inv
+    head_gain = jnp.sum(gains_all, axis=0)
     positions = jnp.arange(seq_len)
     frequency = THETA ** (-jnp.arange(HD // 2).astype(F32) / (HD // 2))
     angles = positions.astype(F32)[:, None] * frequency[None, :]
-    cosine = jnp.cos(angles)[:, None, :]
-    sinus_table = jnp.sin(angles)[:, None, :]
-    queries = rotate(
-        (query_unit * query_gain).reshape(seq_len, local_heads, HD), cosine, sinus_table, 1.0
-    ).astype(BF)
-    key_rows = rotate(
-        (key_unit * key_gain).reshape(seq_len, local_heads, HD), cosine, sinus_table, 1.0
-    ).astype(BF)
-    value_rows = value_low.reshape(seq_len, local_heads, HD)
-    scores = (
-        jnp.einsum("qhd,khd->hqk", queries, key_rows, preferred_element_type=F32) / root_size
-    )
-    allowed = (positions[None, :] <= positions[:, None]) & (positions[None, :] < length)
-    scores = jnp.where(allowed[None], scores, -1e30)
-    row_top = jnp.max(scores, axis=-1, keepdims=True)
-    exponent = jnp.exp(scores - row_top)
-    probs_float = exponent / jnp.sum(exponent, axis=-1, keepdims=True)
-    probs_low = probs_float.astype(BF)
-    mixed = (
-        jnp.einsum("hqk,khd->qhd", probs_low, value_rows, preferred_element_type=F32)
-        .astype(BF)
-        .reshape(seq_len, columns)
-    )
-    attn_partial = jnp.dot(mixed, o_full, preferred_element_type=F32).astype(BF)
+    cosine = jnp.concatenate([jnp.cos(angles)] * 2, axis=1)
+    sine = jnp.concatenate([-jnp.sin(angles), jnp.sin(angles)], axis=1)
+    attn_operands = (hidden_bf, attn_gain[None, :], qkv_full, o_full, head_gain, cosine, sine)
+    normed, units, low, probs, mixed, attn_partial, inverses = attend(
+        extent, length[None], *attn_operands
+    )
 
     lane = jnp.arange(128)
     lane_expert = jnp.where(lane < 2 * expert_count, lane % expert_count, -1)
@@ -1973,7 +2399,7 @@
     pieces = pieces + last_pieces
     own_positions = t * rows + jnp.arange(rows)
     row_scale = jnp.where(own_positions < length, all_tokens / total_count, 0.0)
-    grad_output, row_loss, ffn_grad_partial, *expert_grads = turn(
+    grad_output, row_loss, ffn_grad_partial, inner, active, grads = turn(
         extent,
         expert_partial,
         middle,
@@ -1983,7 +2409,6 @@
         hidden,
         pieces,
     )
-    loss_own = jnp.sum(row_loss[:, 0]) / (2.0 * width * all_tokens)
     grad_middle, grad_logits, ffn_gain_part, attn_grad_rows, *came = leave(
         extent,
         ffn_grad_partial,
@@ -1993,13 +2418,9 @@
         chosen,
         ffn_gain,
         router_t,
-        expert_grads[1:6],
-    )
-    corner_grads = lax.optimization_barrier((*expert_grads[6:], attn_grad_rows))
-    attn_grad_rows = corner_grads[2]
-    expert_grads = (
-        expert_grads[:1] + came + [exchange(corner_grads[n], 6 + n) for n in range(2)]
-    )
+        (tokens, grads, inner, active),
+    )
+    expert_grads = came[:6] + [exchange(came[bits], bits) for bits in (6, 7)]
     attn_grad_rows = attn_grad_rows.reshape(seq_len, width)
     router_part = jnp.einsum(
         "sd,se->de",
@@ -2008,59 +2429,20 @@
         precision=HIGHEST,
         preferred_element_type=F32,
     )
-    grad_o = jnp.einsum("sa,sb->ab", mixed, attn_grad_rows, preferred_element_type=F32)
-    grad_mixed = (
-        jnp.einsum("sb,ab->sa", attn_grad_rows, o_full, preferred_element_type=F32)
-        .astype(BF)
-        .reshape(seq_len, local_heads, HD)
-    )
-    value_grad = jnp.einsum("hqk,qhd->khd", probs_low, grad_mixed, preferred_element_type=F32)
-    grad_weights = jnp.einsum(
-        "qhd,khd->hqk", grad_mixed, value_rows, preferred_element_type=F32
-    )
-    grad_scores = (
-        probs_float
-        * (grad_weights - jnp.sum(grad_weights * probs_float, axis=-1, keepdims=True))
-    ).astype(BF)
-    query_grad_rot = (
-        jnp.einsum("hqk,khd->qhd", grad_scores, key_rows, preferred_element_type=F32) / root_size
-    )
-    key_grad_rot = (
-        jnp.einsum("hqk,qhd->khd", grad_scores, queries, preferred_element_type=F32) / root_size
-    )
-    query_grad = rotate(query_grad_rot, cosine, sinus_table, -1.0).reshape(seq_len, columns)
-    key_grad = rotate(key_grad_rot, cosine, sinus_table, -1.0).reshape(seq_len, columns)
-    query_scaled = query_grad * query_gain
-    key_scaled = key_grad * key_gain
-    qgain_part = jnp.sum(query_grad * query_unit, axis=0)
-    kgain_part = jnp.sum(key_grad * key_unit, axis=0)
-    dots = jnp.concatenate(
-        [
-            jnp.sum(query_scaled * query_unit, axis=1),
-            jnp.sum(key_scaled * key_unit, axis=1),
-            jnp.full((1024,), loss_own, F32),
-        ]
-    )
-    dots = line_total(extent, 6, dots.reshape(-1, 128)).reshape(-1)
-    query_dot, key_dot, loss_group = (
-        dots[:seq_len],
-        dots[seq_len : 2 * seq_len],
-        dots[2 * seq_len : 2 * seq_len + 1],
-    )
-    query_raw_grad = query_inv * (query_scaled - query_unit * (query_dot / width)[:, None])
-    key_raw_grad = key_inv * (key_scaled - key_unit * (key_dot / width)[:, None])
-    raw_grad = jnp.concatenate(
-        [
-            query_raw_grad.astype(BF),
-            key_raw_grad.astype(BF),
-            value_grad.reshape(seq_len, columns).astype(BF),
-        ],
-        axis=1,
-    )
-    grad_qkv = jnp.einsum("sd,sa->da", normed, raw_grad, preferred_element_type=F32)
-    normed_grad = jnp.einsum("sa,da->sd", raw_grad, qkv_full, preferred_element_type=F32)
-    attn_gain_part = jnp.sum(normed_grad * unit_one, axis=0)
-    input_part = norm_backward(normed_grad, unit_one, inverse_one, attn_gain).astype(BF)
+    input_part, grad_qkv, grad_o, attn_gain_part, gains_part, loss_rows = attend_back(
+        extent,
+        attn_grad_rows,
+        row_loss,
+        *attn_operands,
+        normed,
+        units,
+        low,
+        probs,
+        mixed,
+        inverses,
+    )
+    loss_group = loss_rows[2, :1] / (2.0 * width * all_tokens)
+    attn_gain_part = jnp.sum(attn_gain_part, axis=0)
 
     split = width // (dp_count * extent)
     small = jnp.concatenate(
@@ -2077,13 +2459,12 @@
         ],
         axis=2,
     ).transpose(1, 0, 2, 3)
-    gains_part = jnp.concatenate([qgain_part, kgain_part]).reshape(2 * local_heads, HD)
     grad_in, qkv_out, o_out, small_out = close(
         extent,
         input_part.reshape(extent, rows, width),
         grad_middle,
-        grad_qkv.astype(BF),
-        grad_o.astype(BF),
+        grad_qkv,
+        grad_o,
         small,
         gains_part,
     )

time: 742 us -> 639 us (0.86); the launches traced: 733 us -> 638 us
  matrix products: 44.5 us -> 1.71 us
  Pallas kernels: 622 us -> 597 us
  other arithmetic: 34.9 us -> 13.6 us
    pallas_call x2, Pallas kernels: 13.5 us -> 67.6 us  [the longest x1 40.6 us: attend_back(): pl.pallas_call(functools.partial(attend_back_kernel, extent), out_shape=[...]
    pallas_call x1, Pallas kernels: 218 us -> 175 us  [turn(): pl.pallas_call(functools.partial(turn_kernel, extent), out_shape=[jax.Sha...]
    dot_general x11 -> x0, matrix products: 38.2 us -> none  [the longest x1 7.96 us: per_device_block(): jnp.einsum('sa,da->sd', raw_grad, qkv_full, preferred_element_type=F32)]
    pallas_call x1, Pallas kernels: 64.4 us -> 46.7 us  [close(): pl.pallas_call(functools.partial(close_kernel, extent), out_shape=[jax.Sh...]
    pallas_call x1, Pallas kernels: 135 us -> 122 us  [leave(): pl.pallas_call(functools.partial(leave_kernel, extent), out_shape=[jax.Sh...]
    convert_element_type x4 -> x0, other arithmetic: 9.61 us -> none  [the longest x1 4.49 us: per_device_block(): norm_backward(normed_grad, unit_one, inverse_one, attn_gain).astype(BF)]
  transfers between devices with their start and end apart: 7 -> 7, of which waited for: 0 -> 0; matrix products, arithmetic and copies ran while one was open for 7% -> 4% of each run, Pallas kernels for 10% -> 18%
where the time goes in v3:
time: 639 us; the launch traced here: 638 us
  Pallas kernels  597 us (93%)
  local copies, waits for them, and re-layouts  16.4 us (3%)
  other arithmetic  13.6 us (2%)
    pallas_call x1, Pallas kernels, turn(): pl.pallas_call(functools.partial(turn_kernel, extent), out_shape=[jax.Sha...  175 us
    pallas_call x1, Pallas kernels, enter(): pl.pallas_call(functools.partial(enter_kernel, extent), out_shape=[jax.Sh...  128 us
    pallas_call x1, Pallas kernels, leave(): pl.pallas_call(functools.partial(leave_kernel, extent), out_shape=[jax.Sh...  122 us
    pallas_call x1, Pallas kernels, fetch(): pl.pallas_call(functools.partial(fetch_kernel, extent), out_shape=[jax.Sh...  50.1 us
    pallas_call x1, Pallas kernels, close(): pl.pallas_call(functools.partial(close_kernel, extent), out_shape=[jax.Sh...  46.7 us
    pallas_call x1, Pallas kernels, attend_back(): pl.pallas_call(functools.partial(attend_back_kernel, extent), out_shape=[...  40.6 us
    pallas_call x1, Pallas kernels, attend(): pl.pallas_call(functools.partial(attend_kernel, extent), out_shape=[jax.S...  27.1 us
  transfers between devices with their start and end apart: 7, of which 0 were waited for; matrix products, arithmetic and copies ran while one was open for 4% of the time, Pallas kernels for 18%

profile of v3, /device:TPU:0, one launch (start us, length us, event | category | flops | bytes accessed | tf_op | source)
XLA Modules:
  0.0 638.1 jit_solution(12903279933191767163)
XLA Ops:
  1.6 2.0 pad_maximum_fusion.qkv
  3.7 50.1 %shard_map.263 = (bf16[512,2048]{1,0:T(8,128)(2,1)}, bf16[2048,1536]{1,0:T(8,128)(2,1)}, bf16[512,2048]{1,0:T(8,128)(2,1)}, f32[8,8,128]{2,1,0:T(8,128)}, bf16[3...) custom-call(bf16[128,2048]{1,0:T(8,128)(2,1)} %hid.3, ...), custom_call_target="tpu_custom_call" | custom-call | bytes 100000000 | tf_op jit(solution)/shard_map/pallas_call | solution.py:1180
  55.7 1.2 collective-permute-start.3
  56.9 0.9 collective-permute-start.4
  57.8 1.4 reduce_sum.36.head_gain
  61.1 1.0 fusion
  63.6 1.0 copy.42
  66.3 1.0 pad_maximum_fusion.1
  67.3 27.1 %shard_map.264 = (bf16[512,2048]{1,0:T(8,128)(2,1)}, f32[512,1024]{1,0:T(8,128)}, bf16[512,1536]{1,0:T(8,128)(2,1)}, f32[4,512,512]{2,1,0:T(8,128)}, bf16[512,51...) custom-call(s32[1]{0:T(128)} %dynamic_slice.9.length, bf16[512,2048]{1,0:T(8,128)(2,1)} %get-tuple-element.72.hid, ...), custom_call_target="tpu_custom_call" | custom-call | bytes 60000000 | tf_op jit(solution)/shard_map/pallas_call | solution.py:1906
  95.1 2.4 maximum_maximum_fusion.router
  98.7 127.8 %shard_map.265 = (f32[128,2048]{1,0:T(8,128)}, f32[128,128]{1,0:T(8,128)}, bf16[128,2048]{1,0:T(8,128)(2,1)}, bf16[4,2,4,128,2176]{4,3,2,1,0:T(8,128)(2,1)}, bf1...) custom-call(bf16[4,128,2048]{2,1,0:T(8,128)(2,1)} %bitcast.16, ...), custom_call_target="tpu_custom_call" | custom-call | bytes 300000000 | tf_op jit(solution)/shard_map/pallas_call | solution.py:1389
  227.1 174.7 %shard_map.266 = (f32[128,2048]{1,0:T(8,128)}, f32[128,128]{1,0:T(8,128)}, bf16[4,2,4,128,2176]{4,3,2,1,0:T(8,128)(2,1)}, bf16[4,2,512,1024]{3,2,1,0:T(8,128)(2,...) custom-call(bf16[4,2,4,128,2048]{4,3,2,1,0:T(8,128)(2,1)} %get-tuple-element.85.partial, ...), custom_call_target="tpu_custom_call" | custom-call | bytes 450000000 | tf_op jit(solution)/shard_map/pallas_call | solution.py:1573
  401.9 122.2 %shard_map.267 = (f32[128,2048]{1,0:T(8,128)}, f32[128,128]{1,0:T(8,128)}, f32[8,2048]{1,0:T(8,128)}, bf16[4,128,2048]{2,1,0:T(8,128)(2,1)}, bf16[3,2,256,256]{3...) custom-call(bf16[4,2,4,128,2176]{4,3,2,1,0:T(8,128)(2,1)} %get-tuple, ...), custom_call_target="tpu_custom_call" | custom-call | bytes 350000000 | tf_op jit(solution)/shard_map/pallas_call | solution.py:1753
  524.1 1.6 collective-permute-start.5
  525.7 1.7 fusion.1
  527.7 40.6 %shard_map.268 = (bf16[512,2048]{1,0:T(8,128)(2,1)}, bf16[2048,1536]{1,0:T(8,128)(2,1)}, bf16[512,2048]{1,0:T(8,128)(2,1)}, f32[8,2048]{1,0:T(8,128)}, f32[8,128]{1,0:T(8,128)}, /*index=5*/f32[8,128]{1,0:T(8,128)}) custom-call(bf16[512,2048]{1,0:T(8,128)(2,1)} %bitcast.15, f32[128,128]{1,0:T(8,128)} %get-tuple-element.98.row_loss, ...), custom_call_target="tpu_custom_call" | custom-call | bytes 1000000 | tf_op jit(solution)/shard_map/pallas_call | solution.py:2057
  568.3 0.9 reduce_sum.38
  570.2 46.7 %shard_map.269 = (f32[128,2048]{1,0:T(8,128)}, f32[256,1536]{1,0:T(8,128)}, f32[512,256]{1,0:T(8,128)}, f32[24,128]{1,0:T(8,128)}) custom-call(bf16[4,128,2048]{2,1,0:T(8,128)(2,1)} %bitcast.17, f32[128,2048]{1,0:T(8,128)} %get-tuple-element.107.grad_middle, bf16[2048,1536]{1,0:T(8,128)(2,1)} %get-tuple-element.108.grad_qkv, ...), custom_call_target="tpu_custom_call" | custom-call | bytes 150000000 | tf_op jit(solution)/shard_map/pallas_call | solution.py:2281
  618.4 1.2 slice.30
  621.0 1.3 slice_bitcast_fusion
  622.9 2.5 fusion.3
  625.4 0.9 copy-done.6
  626.6 8.3 %shard_map.270 = (f32[16,256,256]{2,1,0:T(8,128)}, f32[16,256,256]{2,1,0:T(8,128)}, f32[16,256,256]{2,1,0:T(8,128)}) custom-call(bf16[3,2,256,256]{3,2,1,0:T(8,128)(2,1)} %get-tuple-element.119.refs_0_, bf16[3,2,256,256]{3,2,1,0:T(8,128)(2,1)} %get-tuple-element.120.refs_1_, bf16[3,2,256,256]{3,2,1,0:T(8,128)(2,1)} %get-tuple-element.121.refs_2_, ...), custom_call_target="tpu_custom_call" | custom-call | bytes 20000000 | tf_op jit(solution)/shard_map/pallas_call | solution.py:2309
  634.9 1.0 copy.56
  (72 shorter events, 15.4 us)
Async XLA Ops:
  0.6 60.4 %copy-start = (s32[512,8]{0,1:T(8,128)S(1)}, s32[512,8]{0,1:T(8,128)}, u32[]{:S(2)}) copy-start(s32[512,8]{0,1:T(8,128)} %param.19) | copy-start | bytes 49156
  1.6 2.1 copy-start.10
  3.6 55.5 %copy-start.13 = (s32[8]{0:T(128)S(1)}, s32[8]{0:T(128)}, u32[]{:S(2)}) copy-start(s32[8]{0:T(128)} %param.18) | copy-start | bytes 100
  3.6 56.8 %copy-start.11 = (bf16[2048]{0:T(1024)(128)(2,1)S(1)}, bf16[2048]{0:T(1024)(128)(2,1)}, u32[]{:S(2)}) copy-start(bf16[2048]{0:T(1024)(128)(2,1)} %param.20) | copy-start | bytes 12292
  3.7 59.4 %copy-start.12 = (bf16[2048]{0:T(1024)(128)(2,1)S(1)}, bf16[2048]{0:T(1024)(128)(2,1)}, u32[]{:S(2)}) copy-start(bf16[2048]{0:T(1024)(128)(2,1)} %param.21) | copy-start | bytes 12292
  3.7 60.0 %copy-start.8 = (bf16[2048,16]{0,1:T(8,128)(2,1)S(1)}, bf16[2048,16]{0,1:T(8,128)(2,1)}, u32[]{:S(2)}) copy-start(bf16[2048,16]{0,1:T(8,128)(2,1)} %param.28) | copy-start | bytes 196612
  53.8 43.7 %collective-permute-start = (bf16[3,2,256,256]{3,2,1,0:T(8,128)(2,1)}, bf16[3,2,256,256]{3,2,1,0:T(8,128)(2,1)S(1)}, u32[]{:S(2)}, u32[]{:S(2)}) collective-permute-start(bf16[3,2,256,256]{3,2,1,0:T(8,128)(2,1)} %get-tuple-element.78), channel_id=1, source_target_pairs={{0,4},{4,0},{8,12},{12,8},{16,20},{20,16},{24,28},{28,24},{1,5},{5... | collective-permute-start | bytes 2359304 | tf_op jit(solution)/shard_map/ppermute | solution.py:2322
  54.3 43.2 %collective-permute-start.1 = (bf16[3,2,256,256]{3,2,1,0:T(8,128)(2,1)}, bf16[3,2,256,256]{3,2,1,0:T(8,128)(2,1)S(1)}, u32[]{:S(2)}, u32[]{:S(2)}) collective-permute-start(bf16[3,2,256,256]{3,2,1,0:T(8,128)(2,1)} %get-tuple-element.79), channel_id=1, source_target_pairs={{0,8},{4,12},{8,0},{12,4},{16,24},{20,28},{24,16},{28,20},{1,9},{5... | collective-permute-start | bytes 2359304 | tf_op jit(solution)/shard_map/ppermute | solution.py:2322
  55.1 42.4 %collective-permute-start.2 = (bf16[3,2,256,256]{3,2,1,0:T(8,128)(2,1)}, bf16[3,2,256,256]{3,2,1,0:T(8,128)(2,1)}, u32[]{:S(2)}, u32[]{:S(2)}) collective-permute-start(bf16[3,2,256,256]{3,2,1,0:T(8,128)(2,1)} %get-tuple-element.80), channel_id=1, source_target_pairs={{0,12},{4,8},{8,4},{12,0},{16,28},{20,24},{24,20},{28,16},{1,13},{... | collective-permute-start | bytes 2359304 | tf_op jit(solution)/shard_map/ppermute | solution.py:2322
  55.7 41.8 %collective-permute-start.3 = (bf16[3,2,256,256]{3,2,1,0:T(8,128)(2,1)}, bf16[3,2,256,256]{3,2,1,0:T(8,128)(2,1)}, u32[]{:S(2)}, u32[]{:S(2)}) collective-permute-start(bf16[3,2,256,256]{3,2,1,0:T(8,128)(2,1)} %get-tuple-element.81), channel_id=1, source_target_pairs={{0,16},{4,20},{8,24},{12,28},{16,0},{20,4},{24,8},{28,12},{1,17},{... | collective-permute-start | bytes 2359304 | tf_op jit(solution)/shard_map/ppermute | solution.py:2322
  56.9 40.6 %collective-permute-start.4 = (bf16[3,2,256,256]{3,2,1,0:T(8,128)(2,1)}, bf16[3,2,256,256]{3,2,1,0:T(8,128)(2,1)}, u32[]{:S(2)}, u32[]{:S(2)}) collective-permute-start(bf16[3,2,256,256]{3,2,1,0:T(8,128)(2,1)} %get-tuple-element.82), channel_id=1, source_target_pairs={{0,20},{4,16},{8,28},{12,24},{16,4},{20,0},{24,12},{28,8},{1,21},{... | collective-permute-start | bytes 2359304 | tf_op jit(solution)/shard_map/ppermute | solution.py:2322
  97.5 0.9 copy-start.2
  97.5 1.1 copy-start.3
  524.1 101.3 %collective-permute-start.5 = (bf16[3,2,256,256]{3,2,1,0:T(8,128)(2,1)}, bf16[3,2,256,256]{3,2,1,0:T(8,128)(2,1)S(1)}, u32[]{:S(2)}, u32[]{:S(2)}) collective-permute-start(bf16[3,2,256,256]{3,2,1,0:T(8,128)(2,1)} %get-tuple-element.125), channel_id=1, source_target_pairs={{0,24},{4,28},{8,16},{12,20},{16,8},{20,12},{24,0},{28,4},{1,25},{... | collective-permute-start | bytes 2359304 | tf_op jit(solution)/shard_map/ppermute | solution.py:2322
  525.7 99.7 %collective-permute-start.6 = (bf16[3,2,256,256]{3,2,1,0:T(8,128)(2,1)}, bf16[3,2,256,256]{3,2,1,0:T(8,128)(2,1)S(1)}, u32[]{:S(2)}, u32[]{:S(2)}) collective-permute-start(bf16[3,2,256,256]{3,2,1,0:T(8,128)(2,1)} %get-tuple-element.126), channel_id=1, source_target_pairs={{0,28},{4,24},{8,20},{12,16},{16,12},{20,8},{24,4},{28,0},{1,29},{... | collective-permute-start | bytes 2359304 | tf_op jit(solution)/shard_map/ppermute | solution.py:2322
  527.7 41.5 %copy-start.9 = (f32[8,2048]{1,0:T(8,128)S(1)}, f32[8,2048]{1,0:T(8,128)}, u32[]{:S(2)}) copy-start(f32[8,2048]{1,0:T(8,128)} %get-tuple-element.111) | copy-start | bytes 196612
  625.4 1.1 copy-start.5
  625.4 0.9 copy-start.6
  626.5 8.3 %copy-start.4 = (f32[128,2048]{1,0:T(8,128)S(1)}, f32[128,2048]{1,0:T(8,128)}, u32[]{:S(2)}) copy-start(f32[128,2048]{1,0:T(8,128)} %get-tuple-element.199) | copy-start | bytes 3145732
  626.5 10.5 %copy-start.1 = (s32[512,8]{0,1:T(8,128)S(1)}, s32[512,8]{0,1:T(8,128)}, u32[]{:S(2)}) copy-start(s32[512,8]{0,1:T(8,128)} %param.19) | copy-start | bytes 49156
  634.8 1.4 copy-start.7

commit v4 on v3

--- a/solution.py
+++ b/solution.py
@@ -3,6 +3,7 @@
 
 import jax
 import jax.numpy as jnp
+import numpy as np
 from jax import lax
 from jax.experimental import pallas as pl
 from jax.experimental.pallas import tpu as pltpu
@@ -602,8 +603,10 @@
         down = [wire.slot() for unused in range(extent - 1)]
         last = extent - 1
         above, below = (d, t + 1), (d, t - 1)
-        wire.start(up[0], own, lambda: place(t), above, t < last)
-        wire.start(down[0], own, lambda: place(t), below, t > 0)
+        self.first = (
+            (up[0], own, lambda: place(t), above, t < last),
+            (down[0], own, lambda: place(t), below, t > 0),
+        )
         self.steps = {}
         for step in range(1, extent):
             from_below, from_above = t >= step, t <= last - step
@@ -627,6 +630,10 @@
                 ),
             )
 
+    def begin(self):
+        for slot, own, target, device, condition in self.first:
+            self.wire.start(slot, own, target, device, condition)
+
     def step(self, step):
         for slots, region, valid, onward, to, source in self.steps[step]:
             self.wire.arrive(slots[step - 1], region, source, valid)
@@ -656,15 +663,24 @@
         self.to_x, self.to_y, self.to_c = (flip(d, 2), t), (flip(d, 4), t), (flip(d, 1), t)
         self.index = [arrival(t, turn) for turn in range(extent)]
         self.slots = {}
-        self.where = (wire, d, t, extent)
         late = lambda n: (self.early + n * (LATE // 2), LATE // 2)
         self.parts = {0: (0, self.half), 1: (self.half, self.half), 2: late(0), 3: late(1)}
         self.parts["early"], self.parts["late"] = (0, self.early), (self.early, LATE)
         self.send("gx", 0, self.source(0, "late"), self.spot(0, 0, 1, "late"), self.to_x)
         self.send("gy", 0, self.source(0, "late"), self.spot(0, 0, 2, "late"), self.to_y)
+        here = self.index[0]
         self.line = LineGather(
-            wire, d, t, extent, lambda: self.cut(own(), "early"), lambda j: self.cut(place(j, 0, 0), "early")
-        )
+            wire,
+            d,
+            t,
+            extent,
+            lambda: self.cut(own(), "early"),
+            lambda j: self.cut(place(j, 0, 0), "early"),
+        )
+        self.late_line = LineGather(
+            wire, d, t, extent, lambda: bundle(here, 0), lambda j: bundle(j, 0)
+        )
+        self.line.begin()
         self.stage_first(0)
         for name, i, which, onward, to, source in (
             ("gx", 1, 2, "gfy", self.to_y, self.to_x),
@@ -730,15 +746,11 @@
         region = lambda c: (lambda: self.bundle(self.index[turn], c))
         self.send("cb", turn, region(0), region(1), self.to_c)
 
-    def bundle_start(self):
+    def bundle_start(self, unused):
         spot = self.spot
         self.wait("gfy", 0, spot(0, 0, 3, 2), self.to_y)
         self.wait("gfx", 0, spot(0, 0, 3, 3), self.to_x)
-        here = self.index[0]
-        wire, d, t, extent = self.where
-        self.late_line = LineGather(
-            wire, d, t, extent, lambda: self.bundle(here, 0), lambda j: self.bundle(j, 0)
-        )
+        self.late_line.begin()
         self.pass_bundle(0)
 
     def bundle_step(self, step):
@@ -763,18 +775,18 @@
             (
                 (line, 1),
                 (stage, 1),
+                (self.bundle_start, 0),
                 (relay, 0),
                 (line, 2),
                 (stage, 2),
                 (corner, 0),
-                (late, 1),
             ),
-            ((relay, 1), (line, 3), (stage, 3), (other, 0)),
-            ((relay, 2), (corner, 1), (late, 2)),
+            ((relay, 1), (late, 1), (other, 0)),
+            ((relay, 2), (line, 3), (stage, 3), (corner, 1)),
             ((other, 1),),
-            ((relay, 3), (corner, 2), (late, 3)),
+            ((late, 2), (corner, 2), (relay, 3)),
             ((other, 2),),
-            ((corner, 3),),
+            ((late, 3), (corner, 3)),
             ((other, 3),),
         )
 
@@ -1005,6 +1017,7 @@
             receive_b(k, cut, a_in, b_in, half)
             if k < last:
                 line.step(k)
+    between(extent + 2)
     receive_b(last, late_cut, late_a, late_b, LATE // 2)
     line.last()
 
@@ -1057,146 +1070,8 @@
     return [pltpu.SemaphoreType.DMA((count,)), pltpu.SemaphoreType.DMA((count,))]
 
 
-def fetch_kernel(
-    extent,
-    hid,
-    qkv,
-    o,
-    gains,
-    gate,
-    up,
-    down,
-    hid_all,
-    qkv_all,
-    o_all,
-    gains_all,
-    *rest,
-):
-    pieces, (stage, send_sem, recv_sem, local_sem) = rest[:8], rest[8:]
-    d, t = lax.axis_index("dp"), lax.axis_index("tensor")
-    rows = hid.shape[0]
-    depth, o_rows = qkv.shape[0], o.shape[0]
-    width = o.shape[1]
-    greet(line_devices(d, t, extent) + [(None, (flip(d, bits), t)) for bits in range(1, 8)])
-    wire, local = Wire(send_sem, recv_sem), Local(local_sem)
-    dx, dy, dxy, dc = flip(d, 2), flip(d, 4), flip(d, 6), flip(d, 1)
-    to_x, to_y, to_c = (dx, t), (dy, t), (dc, t)
-
-    def region(device, which):
-        start = pl.multiple_of(device * width, width)
-        if which is None:
-            return [qkv_all.at[pl.ds(device * depth, depth)], o_all.at[:, pl.ds(start, width)]]
-        return [
-            qkv_all.at[pl.ds(device * depth + which * (depth // 2), depth // 2)],
-            o_all.at[pl.ds(which * (o_rows // 2), o_rows // 2), pl.ds(start, width)],
-        ]
-
-    def own(which):
-        if which is None:
-            return [qkv, o]
-        return [
-            qkv.at[pl.ds(which * (depth // 2), depth // 2)],
-            o.at[pl.ds(which * (o_rows // 2), o_rows // 2)],
-        ]
-
-    def send(device, sources, targets):
-        slots = []
-        for source, target in zip(sources, targets):
-            slot = wire.slot()
-            wire.start(slot, lambda source=source: source, lambda target=target: target, device)
-            slots.append(slot)
-        return slots
-
-    def arrive(slots, regions, device):
-        for slot, part in zip(slots, regions):
-            wire.arrive(slot, lambda: part, device)
-
-    def block(index):
-        return hid_all.at[pl.ds(index * rows, rows)]
-
-    x_slots, y_slots, c_slots = {}, {}, {}
-    for which, other in ((0, 1), (1, 0)):
-        x_slots[which] = send(to_x, own(which), region(d, which))
-        y_slots[other] = send(to_y, own(other), region(d, other))
-    c_slots[1] = send(to_c, own(None), region(d, None))
-    passed = {}
-    loads, copies = [], []
-    for place, weight in enumerate((gate, up, down)):
-        loads.append(local.start(weight, stage.at[place]))
-
-    def store_pieces():
-        for load in loads:
-            load.wait()
-        for bits in range(8):
-            first = 2 * flip(d, bits)
-            for place in range(3):
-                copies.append(
-                    local.start(stage.at[place, pl.ds(first, 2)], pieces[bits].at[place])
-                )
-
-    copies.append(local.start(hid, block(t)))
-    for source, target in zip(own(None), region(d, None)):
-        copies.append(local.start(source, target))
-    line = LineGather(wire, d, t, extent, lambda: hid, block)
-    store_pieces()
-    arrive(x_slots[0], region(dx, 0), to_x)
-    passed["y"] = send(to_y, region(dx, 0), region(dx, 0))
-    arrive(y_slots[1], region(dy, 1), to_y)
-    passed["x"] = send(to_x, region(dy, 1), region(dy, 1))
-    line.step(1)
-    arrive(x_slots[1], region(dx, 1), to_x)
-    c_slots[3] = send(to_c, region(dx, None), region(dx, None))
-    arrive(y_slots[0], region(dy, 0), to_y)
-    c_slots[5] = send(to_c, region(dy, None), region(dy, None))
-    for step in range(2, extent):
-        line.step(step)
-    gain_slots = {}
-    for bits in range(1, 8):
-        gain_slots[bits] = wire.slot()
-        wire.start(
-            gain_slots[bits],
-            lambda: gains,
-            lambda bits=bits: gains_all.at[bits],
-            (flip(d, bits), t),
-        )
-    copies.append(local.start(gains, gains_all.at[0]))
-    arrive(passed["y"], region(dxy, 0), to_y)
-    arrive(passed["x"], region(dxy, 1), to_x)
-    c_slots[7] = send(to_c, region(dxy, None), region(dxy, None))
-    for bits in (1, 3, 5, 7):
-        arrive(c_slots[bits], region(flip(d, bits), None), to_c)
-    for bits in range(1, 8):
-        wire.arrive(
-            gain_slots[bits], lambda bits=bits: gains_all.at[bits], (flip(d, bits), t)
-        )
-    for copy in copies:
-        copy.wait()
-    wire.finish()
-
-
-def fetch(extent, hid, qkv, o, gains, gate, up, down):
-    rows, model_width = hid.shape
-    piece = jax.ShapeDtypeStruct((3, 2) + gate.shape[1:], BF)
-    return pl.pallas_call(
-        functools.partial(fetch_kernel, extent),
-        out_shape=[
-            jax.ShapeDtypeStruct((rows * extent, model_width), BF),
-            jax.ShapeDtypeStruct((8 * qkv.shape[0], qkv.shape[1]), BF),
-            jax.ShapeDtypeStruct((o.shape[0], 8 * o.shape[1]), BF),
-            jax.ShapeDtypeStruct((8,) + gains.shape, F32),
-        ]
-        + [piece] * 8,
-        in_specs=[VM] * 4 + [ANY] * 3,
-        out_specs=[ANY] * 12,
-        scratch_shapes=[pltpu.VMEM((3,) + gate.shape, BF)]
-        + dma_pair(64) + [pltpu.SemaphoreType.DMA((40,))],
-        compiler_params=kernel_params(1),
-        cost_estimate=pl.CostEstimate(flops=0, bytes_accessed=100_000_000, transcendentals=0),
-    )(hid, qkv, o, gains, gate, up, down)
-
-
 class Pieces:
-    def __init__(self, d, in_weight, out_weight, sem, pieces):
+    def __init__(self, d, in_weight, out_weight, sem, pieces, tables=None):
         self.copies = {}
         slab = out_weight.shape[0] // 2
         for bits, piece in enumerate(pieces):
@@ -1209,7 +1084,11 @@
                         whole = in_weight.at[pl.ds(start, slab), pl.ds(column, slab)]
                     else:
                         whole = out_weight.at[pl.ds(e * slab, slab), pl.ds(start, slab)]
-                    pairs.append((piece.at[place, e], whole, sem.at[bits * 6 + place * 2 + e]))
+                    if tables is not None and bits == 0:
+                        part = tables[place].at[2 * d + e]
+                    else:
+                        part = piece.at[place, e]
+                    pairs.append((part, whole, sem.at[bits * 6 + place * 2 + e]))
             self.copies[bits] = pairs
 
     def load(self, bits):
@@ -1240,46 +1119,290 @@
     return jnp.concatenate(parts, axis=1)
 
 
-def enter_kernel(extent, partial, hid, gain, router, chosen, *rest):
-    near, corner = rest[:6], rest[6:8]
-    middle, gates, ffn_own, tokens, hidden, out = rest[8:14]
-    landed = rest[14:16]
-    (
-        gathered,
-        work,
-        up_in,
-        down_in,
-        in_weight,
-        out_weight,
-        hidden_stage,
-        out_stage,
-        send_sem,
-        recv_sem,
-        local_sem,
-        weight_sem,
-        stage_sem,
-        token_sem,
-    ) = rest[16:]
+def line_exchange(wire, t, d, extent, outbox, inbox):
+    peers = [(d, (t + k) % extent) for k in range(1, extent)]
+    slots = []
+    for k, peer in enumerate(peers):
+        slot = wire.slot()
+        slots.append(slot)
+        wire.start(slot, lambda: outbox, lambda k=k: inbox.at[k], peer)
+    result = outbox[...]
+    for k, peer in enumerate(peers):
+        wire.arrive(slots[k], lambda k=k: inbox.at[k], peer)
+        result = result + inbox[k]
+    return result
+
+
+def columns_to_rows(ref):
+    return ref[...].T[0:8]
+
+
+def rows_to_columns(value):
+    return jnp.concatenate([value, jnp.zeros((120, value.shape[1]), F32)], axis=0).T
+
+
+def turned(value, cosine, sine, direction):
+    return value * cosine + direction * pltpu.roll(value, HD // 2, 1) * sine
+
+
+def line_peers(d, t, extent):
+    return [(None, (d, (t + k) % extent)) for k in range(1, extent)]
+
+
+def transposed_dot(left, right):
+    return lax.dot_general(left, right, (((0,), (0,)), ((), ())), preferred_element_type=F32)
+
+
+def dot_transposed(left, right):
+    return lax.dot_general(left, right, (((1,), (1,)), ((), ())), preferred_element_type=F32)
+
+
+def front_kernel(
+    extent,
+    length,
+    hid,
+    q_weight,
+    k_weight,
+    v_weight,
+    o_weight,
+    gains,
+    gate,
+    up,
+    down,
+    attn_gain,
+    cosine,
+    sine,
+    ffn_gain,
+    router,
+    chosen,
+    middle,
+    gates,
+    ffn_own,
+    head_gain,
+    inverses,
+    hid_out,
+    qkv_out,
+    o_out,
+    normed_out,
+    raw_out,
+    low_out,
+    probs_out,
+    mixed_out,
+    tokens,
+    hidden,
+    out,
+    landed,
+    hid_all,
+    qkv_all,
+    o_all,
+    gains_all,
+    normed,
+    raw,
+    low,
+    probs,
+    mixed,
+    sums,
+    outbox,
+    inbox,
+    gathered,
+    work,
+    up_in,
+    down_in,
+    in_weight,
+    out_weight,
+    hidden_stage,
+    out_stage,
+    send_sem,
+    recv_sem,
+    local_sem,
+    weight_sem,
+    stage_sem,
+    token_sem,
+    probs_sem,
+):
     d, t = lax.axis_index("dp"), lax.axis_index("tensor")
-    rows, width = hid.shape
-    greet(line_devices(d, t, extent) + [(None, (flip(d, bits), t)) for bits in (1, 2, 4, 6, 7)])
+    seq_len, width = hid_all.shape
+    rows = seq_len // extent
+    heads = gains.shape[0] // 2
+    columns = heads * HD
+    depth, o_rows, o_width = q_weight.shape[0], o_weight.shape[0], o_weight.shape[1]
     wire, local = Wire(send_sem, recv_sem), Local(local_sem)
-    corner_slots = []
-    for n in range(2):
-        slot = wire.slot()
-        corner_slots.append(slot)
-        wire.start(slot, lambda n=n: corner[n], lambda n=n: landed[n], (flip(d, 6 + n), t))
-    work_load = local.start(partial, work)
-    weights = Pieces(d, in_weight, out_weight, weight_sem, list(near) + list(landed))
-    for bits in range(6):
-        weights.load(bits)
-    work_load.wait()
-    line = LineSum(
+    dx, dy, dxy = flip(d, 2), flip(d, 4), flip(d, 6)
+    to_x, to_y, to_c = (dx, t), (dy, t), (flip(d, 1), t)
+
+    def block(index):
+        return hid_all.at[pl.ds(index * rows, rows)]
+
+    def region(device, which):
+        start = pl.multiple_of(device * o_width, o_width)
+        if which is None:
+            return [qkv_all.at[pl.ds(device * depth, depth)], o_all.at[:, pl.ds(start, o_width)]]
+        return [
+            qkv_all.at[pl.ds(device * depth + which * (depth // 2), depth // 2)],
+            o_all.at[pl.ds(which * (o_rows // 2), o_rows // 2), pl.ds(start, o_width)],
+        ]
+
+    copies = [local.start(hid, block(t))]
+    for n, weight in enumerate((q_weight, k_weight, v_weight)):
+        target = qkv_all.at[pl.ds(d * depth, depth), pl.ds(n * columns, columns)]
+        copies.append(local.start(weight, target))
+    copies.append(local.start(o_weight, region(d, None)[1]))
+    gains_all[0] = gains[...]
+    greet(line_peers(d, t, extent) + [(None, (flip(d, bits), t)) for bits in range(1, 8)])
+    for copy in copies:
+        copy.wait()
+
+    def send(device, sources, targets):
+        slots = []
+        for source, target in zip(sources, targets):
+            slot = wire.slot()
+            wire.start(slot, lambda source=source: source, lambda target=target: target, device)
+            slots.append(slot)
+        return slots
+
+    def arrive(slots, regions, device):
+        for slot, part in zip(slots, regions):
+            wire.arrive(slot, lambda: part, device)
+
+    line = LineGather(wire, d, t, extent, lambda: block(t), block)
+    line.begin()
+    x_slots, y_slots, c_slots = {}, {}, {}
+    for which, other in ((0, 1), (1, 0)):
+        x_slots[which] = send(to_x, region(d, which), region(d, which))
+        y_slots[other] = send(to_y, region(d, other), region(d, other))
+    c_slots[1] = send(to_c, region(d, None), region(d, None))
+    gain_slots = {}
+    for bits in range(1, 8):
+        gain_slots[bits] = wire.slot()
+        wire.start(
+            gain_slots[bits],
+            lambda: gains,
+            lambda bits=bits: gains_all.at[bits],
+            (flip(d, bits), t),
+        )
+    weights = Pieces(
+        d, in_weight, out_weight, weight_sem, [landed.at[bits] for bits in range(8)]
+    )
+    own_experts = Pieces(d, in_weight, out_weight, weight_sem, [None], (gate, up, down))
+    own_experts.load(0)
+    arrive(x_slots[0], region(dx, 0), to_x)
+    over_y = send(to_y, region(dx, 0), region(dx, 0))
+    arrive(y_slots[1], region(dy, 1), to_y)
+    over_x = send(to_x, region(dy, 1), region(dy, 1))
+    piece_slots = {}
+    for bits in (2, 4, 1, 3, 5, 6, 7):
+        first = 2 * flip(d, bits)
+        piece_slots[bits] = send(
+            (flip(d, bits), t),
+            [weight.at[pl.ds(first, 2)] for weight in (gate, up, down)],
+            [landed.at[bits, place] for place in range(3)],
+        )
+    line.step(1)
+    arrive(x_slots[1], region(dx, 1), to_x)
+    c_slots[3] = send(to_c, region(dx, None), region(dx, None))
+    arrive(y_slots[0], region(dy, 0), to_y)
+    c_slots[5] = send(to_c, region(dy, None), region(dy, None))
+    for step in range(2, extent):
+        line.step(step)
+    arrive(over_y, region(dxy, 0), to_y)
+    arrive(over_x, region(dxy, 1), to_x)
+    c_slots[7] = send(to_c, region(dxy, None), region(dxy, None))
+    for bits in range(1, 8):
+        wire.arrive(
+            gain_slots[bits], lambda bits=bits: gains_all.at[bits], (flip(d, bits), t)
+        )
+    total_gain = gains_all[0]
+    for bits in range(1, 8):
+        total_gain = total_gain + gains_all[bits]
+    head_gain[...] = total_gain
+    tile = 256
+
+    def normalize(start):
+        part = pl.ds(start, 64)
+        value = hid_all[part].astype(F32)
+        unit = value * lax.rsqrt(jnp.mean(value * value, axis=-1, keepdims=True) + EPSILON)
+        normed[part] = (unit * attn_gain[...]).astype(BF)
+
+    rows_loop(seq_len, 64, normalize)
+    for bits in (1, 3, 5, 7):
+        arrive(c_slots[bits], region(flip(d, bits), None), to_c)
+    kept = [
+        local.start(hid_all, hid_out),
+        local.start(qkv_all, qkv_out),
+        local.start(o_all, o_out),
+        local.start(normed, normed_out),
+    ]
+
+    def project(start):
+        part = pl.ds(start, tile)
+        result = jnp.dot(normed[part], qkv_all[...], preferred_element_type=F32)
+        raw[part] = result
+        lane = lax.broadcasted_iota(jnp.int32, (tile, 128), 1)
+        squares = [
+            jnp.sum(jnp.square(result[:, n * columns : (n + 1) * columns]), axis=-1, keepdims=True)
+            for n in range(2)
+        ]
+        sums[part] = jnp.where(lane == 0, squares[0], jnp.where(lane == 1, squares[1], 0.0))
+
+    rows_loop(seq_len, tile, project)
+    outbox[...] = columns_to_rows(sums)
+    total = line_exchange(wire, t, d, extent, outbox, inbox)
+    inverses[...] = rows_to_columns(lax.rsqrt(total / width + EPSILON))
+    low[:, 2 * columns :] = raw[:, 2 * columns :].astype(BF)
+
+    def probs_copy(h):
+        return pltpu.make_async_copy(probs.at[h % 2], probs_out.at[h], probs_sem.at[h % 2])
+
+    def head(h, carry):
+        for n in range(2):
+            section = pl.ds(pl.multiple_of(n * columns + h * HD, HD), HD)
+            unit = raw[:, section] * inverses[:, n : n + 1]
+            raw[:, section] = unit
+            scaled = unit * head_gain[pl.ds(n * heads + h, 1)]
+            low[:, section] = turned(scaled, cosine[...], sine[...], 1.0).astype(BF)
+        section = pl.ds(pl.multiple_of(h * HD, HD), HD)
+        key_section = pl.ds(pl.multiple_of(columns + h * HD, HD), HD)
+        value_section = pl.ds(pl.multiple_of(2 * columns + h * HD, HD), HD)
+
+        @pl.when(h >= 2)
+        def _():
+            probs_copy(h).wait()
+
+        def some(start):
+            part = pl.ds(start, tile)
+            scores = dot_transposed(low[part, section], low[:, key_section]) / math.sqrt(HD)
+            row = start + lax.broadcasted_iota(jnp.int32, scores.shape, 0)
+            column = lax.broadcasted_iota(jnp.int32, scores.shape, 1)
+            allowed = both(column <= row, column < length[0])
+            scores = jnp.where(allowed, scores, -1e30)
+            powers = jnp.exp(scores - jnp.max(scores, axis=-1, keepdims=True))
+            result = powers / jnp.sum(powers, axis=-1, keepdims=True)
+            probs[h % 2, part] = result
+            mixed[part, section] = jnp.dot(
+                result.astype(BF), low[:, value_section], preferred_element_type=F32
+            ).astype(BF)
+
+        rows_loop(seq_len, tile, some)
+        probs_copy(h).start()
+        return carry
+
+    lax.fori_loop(0, heads, head, 0)
+    kept += [local.start(raw, raw_out), local.start(low, low_out), local.start(mixed, mixed_out)]
+
+    def join(first, carry):
+        result = jnp.dot(
+            mixed[pl.ds(first * 2 * rows, 2 * rows)], o_all[...], preferred_element_type=F32
+        )
+        work[pl.ds(2 * first, 2)] = result.astype(BF).reshape(2, rows, width)
+        return carry
+
+    lax.fori_loop(0, extent // 2, join, 0)
+    total_line = LineSum(
         wire, d, t, extent, lambda index: work.at[index], up_in, down_in, rows, 2
     )
     for step in range(extent - 1):
-        line.step(step)
-    line.last()
+        total_line.step(step)
+    total_line.last()
     mine = work.at[t]
     everything = pl.ds(0, width)
     packet = gathered.at[t, 0, 0]
@@ -1291,16 +1414,16 @@
         )
         middle[part] = value
         unit = value * lax.rsqrt(jnp.mean(value * value, axis=-1, keepdims=True) + EPSILON)
-        ffn_own[part] = (unit * gain[...]).astype(BF)
+        ffn_own[part] = (unit * ffn_gain[...]).astype(BF)
 
     rows_loop(rows, 16, body)
     logits = jnp.dot(ffn_own[...], router[...], preferred_element_type=F32)
     lane = lax.broadcasted_iota(jnp.int32, logits.shape, 1)
     top = jnp.max(jnp.where(lane < 16, logits, -1e30), axis=-1, keepdims=True)
     powers = jnp.where(lane < 32, jnp.exp(logits - top), 0.0)
-    probs = powers / jnp.sum(jnp.where(lane < 16, powers, 0.0), axis=-1, keepdims=True)
-    gates[...] = probs
-    coeff = probs * chosen[...]
+    chance = powers / jnp.sum(jnp.where(lane < 16, powers, 0.0), axis=-1, keepdims=True)
+    gates[...] = chance
+    coeff = chance * chosen[...]
     high = coeff.astype(BF).astype(F32)
     packet[:, 0:width] = ffn_own[...]
     packet[:, width : width + 128] = jnp.where(lane < 16, high, coeff - high).astype(BF)
@@ -1312,12 +1435,14 @@
         return gathered.at[j, c, pl.ds(0, 4), pl.ds(rows - LATE, LATE)]
 
     gather = PlaneGather(wire, d, t, extent, lambda: packet, place, bundle, rows)
-    for n in range(2):
-        wire.arrive(corner_slots[n], lambda: landed[n], (flip(d, 6 + n), t))
-        weights.load(6 + n)
-    for bits in range(8):
+    for bits in range(1, 8):
+        arrive(
+            piece_slots[bits], [landed.at[bits, place] for place in range(3)], (flip(d, bits), t)
+        )
+        weights.load(bits)
+    own_experts.loaded(0)
+    for bits in range(1, 8):
         weights.loaded(bits)
-    gather.bundle_start()
     units = out_weight.shape[0]
 
     def stage_copies(slot, j, c):
@@ -1379,28 +1504,64 @@
             tokens.at[arrival(t, g // 2), g % 2],
             token_sem.at[g],
         ).wait()
+    for h in range(heads - 2, heads):
+        probs_copy(h).wait()
+    for copy in kept:
+        copy.wait()
     wire.finish()
 
 
-def enter(extent, partial, hid, gain, router, chosen, near, corner):
+SMEM = pl.BlockSpec(memory_space=pltpu.SMEM)
+
+
+def front(extent, length, hid, q_weight, k_weight, v_weight, o_weight, gains, gate, up, down, *rest):
     rows, width = hid.shape
-    slab = near[0].shape[2]
-    piece = jax.ShapeDtypeStruct(near[0].shape, BF)
+    seq_len = rows * extent
+    slab = gate.shape[1]
+    heads = gains.shape[0] // 2
+    columns = heads * HD
+    shape = jax.ShapeDtypeStruct
+    kept = [
+        shape((seq_len, width), BF),
+        shape((width, 3 * columns), BF),
+        shape((columns, width), BF),
+        shape((seq_len, width), BF),
+        shape((seq_len, 3 * columns), F32),
+        shape((seq_len, 3 * columns), BF),
+        shape((heads, seq_len, seq_len), F32),
+        shape((seq_len, columns), BF),
+    ]
     return pl.pallas_call(
-        functools.partial(enter_kernel, extent),
+        functools.partial(front_kernel, extent),
         out_shape=[
-            jax.ShapeDtypeStruct((rows, width), F32),
-            jax.ShapeDtypeStruct((rows, 128), F32),
-            jax.ShapeDtypeStruct((rows, width), BF),
-            jax.ShapeDtypeStruct((extent, 2, 4, rows, width + 128), BF),
-            jax.ShapeDtypeStruct((extent, 2, 4 * rows, 4 * slab), BF),
-            jax.ShapeDtypeStruct((extent, 2, 4, rows, width), BF),
-            piece,
-            piece,
+            shape((rows, width), F32),
+            shape((rows, 128), F32),
+            shape((rows, width), BF),
+            shape((2 * heads, HD), F32),
+            shape((seq_len, 128), F32),
+        ]
+        + kept
+        + [
+            shape((extent, 2, 4, rows, width + 128), BF),
+            shape((extent, 2, 4 * rows, 4 * slab), BF),
+            shape((extent, 2, 4, rows, width), BF),
+            shape((8, 3, 2, slab, slab), BF),
         ],
-        in_specs=[ANY, VM, VM, VM, VM] + [ANY] * 8,
-        out_specs=[VM, VM, VM] + [ANY] * 5,
+        in_specs=[SMEM, VM] + [ANY] * 4 + [VM] + [ANY] * 3 + [VM] * 6,
+        out_specs=[VM] * 5 + [ANY] * 12,
         scratch_shapes=[
+            pltpu.VMEM((seq_len, width), BF),
+            pltpu.VMEM((width, 3 * columns), BF),
+            pltpu.VMEM((columns, width), BF),
+            pltpu.VMEM((8,) + gains.shape, F32),
+            pltpu.VMEM((seq_len, width), BF),
+            pltpu.VMEM((seq_len, 3 * columns), F32),
+            pltpu.VMEM((seq_len, 3 * columns), BF),
+            pltpu.VMEM((2, seq_len, seq_len), F32),
+            pltpu.VMEM((seq_len, columns), BF),
+            pltpu.VMEM((seq_len, 128), F32),
+            pltpu.VMEM((8, seq_len), F32),
+            pltpu.VMEM((extent - 1, 8, seq_len), F32),
             pltpu.VMEM((extent, 2, 4, rows, width + 128), BF),
             pltpu.VMEM((extent, rows, width), BF),
             pltpu.VMEM((extent - 1, rows, width), BF),
@@ -1410,36 +1571,30 @@
             pltpu.VMEM((2, 4 * rows, 4 * slab), BF),
             pltpu.VMEM((2, 4, rows, width), BF),
         ]
-        + dma_pair(100)
+        + dma_pair(180)
         + [
-            pltpu.SemaphoreType.DMA((2,)),
+            pltpu.SemaphoreType.DMA((16,)),
             pltpu.SemaphoreType.DMA((48,)),
             pltpu.SemaphoreType.DMA((2, 2)),
             pltpu.SemaphoreType.DMA((2 * extent,)),
+            pltpu.SemaphoreType.DMA((2,)),
         ],
-        compiler_params=kernel_params(3),
+        compiler_params=kernel_params(1),
         cost_estimate=pl.CostEstimate(flops=0, bytes_accessed=300_000_000, transcendentals=0),
-    )(partial, hid, gain, router, chosen, *near, *corner)
-
-
-def transposed_dot(left, right):
-    return lax.dot_general(left, right, (((0,), (0,)), ((), ())), preferred_element_type=F32)
-
-
-def dot_transposed(left, right):
-    return lax.dot_general(left, right, (((1,), (1,)), ((), ())), preferred_element_type=F32)
+    )(length, hid, q_weight, k_weight, v_weight, o_weight, gains, gate, up, down, *rest)
 
 
 def turn_kernel(extent, partial, middle, teacher, weight, tokens, hidden, *rest):
-    pieces = rest[:8]
-    grad_output, row_loss, out, inner_out, active_out, grads = rest[8:14]
-    buffers = rest[14:24]
+    landed, tables = rest[0], rest[1:4]
+    grad_output, row_loss, out, inner_out, active_out, grads = rest[4:10]
+    buffers = rest[10:20]
     (
         packet,
         in_weight,
         out_weight,
         coeff_tile,
         hidden_tile,
+        factors,
         grad_tile,
         out_stage,
         active_tile,
@@ -1449,19 +1604,75 @@
         local_sem,
         weight_sem,
         tile_sem,
-    ) = rest[24:]
+        load_sem,
+    ) = rest[20:]
     d, t = lax.axis_index("dp"), lax.axis_index("tensor")
     rows, width = middle.shape
     greet(plane_devices(d, t, extent))
     wire, local = Wire(send_sem, recv_sem), Local(local_sem)
-    weights = Pieces(d, in_weight, out_weight, weight_sem, pieces)
+    pieces = [landed.at[bits] for bits in range(8)]
+    weights = Pieces(d, in_weight, out_weight, weight_sem, pieces, tables)
+    units, slab = out_weight.shape[0], out_weight.shape[0] // 2
+    count = 2 * extent
+
+    def factor_loads(g):
+        j, c, slot = g // 2, g % 2, g % 2
+        part = (pl.ds(0, 4), pl.ds(0, rows), pl.ds(width, 128))
+        return (
+            pltpu.make_async_copy(
+                tokens.at[(j, c) + part], coeff_tile.at[slot], load_sem.at[0, slot]
+            ),
+            pltpu.make_async_copy(hidden.at[j, c], hidden_tile.at[slot], load_sem.at[1, slot]),
+        )
+
+    def active_store(g):
+        return pltpu.make_async_copy(
+            active_tile.at[g % 2], active_out.at[g // 2, g % 2], load_sem.at[2, g % 2]
+        )
+
+    def prepare(g):
+        if g + 1 < count:
+            for copy in factor_loads(g + 1):
+                copy.start()
+        for copy in factor_loads(g):
+            copy.wait()
+        if g >= 2:
+            active_store(g - 2).wait()
+        slot = g % 2
+
+        def some(first, carry):
+            size = 2 * rows
+            blocks, part = pl.ds(2 * first, 2), pl.ds(first * size, size)
+            gate_value = hidden_tile[slot, part, 0:units].astype(F32)
+            up_value = hidden_tile[slot, part, units : 2 * units].astype(F32)
+            coeff = coefficients(coeff_tile[slot, blocks].reshape(size, 128), d, slab)
+            sigmoid_value = jax.nn.sigmoid(gate_value)
+            silu_value = gate_value * sigmoid_value
+            slope = sigmoid_value * (1.0 + gate_value * (1.0 - sigmoid_value))
+            direct = silu_value * up_value
+            factors[g, part, 0:units] = (coeff * up_value * slope).astype(BF)
+            factors[g, part, units : 2 * units] = (coeff * silu_value).astype(BF)
+            factors[g, part, 2 * units : 3 * units] = direct.astype(BF)
+            active_tile[slot, part] = (coeff * direct).astype(BF)
+            return carry
+
+        lax.fori_loop(0, 2, some, 0)
+        active_store(g).start()
+
+    for copy in factor_loads(0):
+        copy.start()
 
     def between(turn_number):
         if turn_number == 1:
             for bits in range(8):
                 weights.load(bits)
+        if turn_number < extent:
+            prepare(2 * turn_number)
+            prepare(2 * turn_number + 1)
 
     sum_plane(wire, local, d, t, extent, partial, buffers, rows, between)
+    for g in (count - 2, count - 1):
+        active_store(g).wait()
 
     def body(part, value):
         output = middle[part] + value
@@ -1484,30 +1695,19 @@
     own_copy = local.start(packet, place(t, 0, 0))
     gather = PlaneGather(wire, d, t, extent, lambda: packet, place, bundle, rows)
     own_copy.wait()
-    gather.bundle_start()
     for bits in range(8):
         weights.loaded(bits)
-    units, slab = out_weight.shape[0], out_weight.shape[0] // 2
     actions = gather.actions()
 
     def out_copies(j, c):
         return (
-            pltpu.make_async_copy(out_stage, out.at[j, c], tile_sem.at[3]),
-            pltpu.make_async_copy(inner_tile, inner_out.at[j, c], tile_sem.at[4]),
-            pltpu.make_async_copy(active_tile, active_out.at[j, c], tile_sem.at[5]),
+            pltpu.make_async_copy(out_stage, out.at[j, c], tile_sem.at[1]),
+            pltpu.make_async_copy(inner_tile, inner_out.at[j, c], tile_sem.at[2]),
         )
 
     def group(g, carry):
         j, c = arrival(t, g // 2), g % 2
-        coeff_copy = pltpu.make_async_copy(
-            tokens.at[j, c, pl.ds(0, 4), pl.ds(0, rows), pl.ds(width, 128)],
-            coeff_tile,
-            tile_sem.at[0],
-        )
-        hidden_copy = pltpu.make_async_copy(hidden.at[j, c], hidden_tile, tile_sem.at[1])
-        grad_copy = pltpu.make_async_copy(grads.at[j, c], grad_tile, tile_sem.at[2])
-        coeff_copy.start()
-        hidden_copy.start()
+        grad_copy = pltpu.make_async_copy(grads.at[j, c], grad_tile, tile_sem.at[0])
         for number, steps in enumerate(actions):
 
             @pl.when(g == number)
@@ -1522,9 +1722,8 @@
             for copy in out_copies(j, c):
                 copy.wait()
 
-        coeff_copy.wait()
-        hidden_copy.wait()
         grad_copy.wait()
+        index = 2 * j + c
 
         def some(first, carry):
             size = 2 * rows
@@ -1532,26 +1731,18 @@
             grad_active = dot_transposed(
                 grad_tile[blocks].reshape(size, width), out_weight[...]
             )
-            gate_value = hidden_tile[part, 0:units].astype(F32)
-            up_value = hidden_tile[part, units : 2 * units].astype(F32)
-            coeff = coefficients(coeff_tile[blocks].reshape(size, 128), d, slab)
-            sigmoid_value = jax.nn.sigmoid(gate_value)
-            silu_value = gate_value * sigmoid_value
-            inner = grad_active * coeff
-            direct = silu_value * up_value
-            active_tile[part] = (coeff * direct).astype(BF)
-            product = grad_active * direct
+            product = grad_active * factors[index, part, 2 * units : 3 * units].astype(F32)
             lane = lax.broadcasted_iota(jnp.int32, (size, 128), 1)
             sums = jnp.zeros((size, 128), F32)
             for e in range(2):
                 one = jnp.sum(product[:, e * slab : (e + 1) * slab], axis=-1, keepdims=True)
                 sums = sums + jnp.where(lane == 2 * d + e, one, 0.0)
             out_stage[blocks, :, width : width + 128] = sums.astype(BF).reshape(2, rows, 128)
-            grad_gate = (
-                inner * up_value * sigmoid_value * (1.0 + gate_value * (1.0 - sigmoid_value))
-            )
-            inner_tile[part, 0:units] = grad_gate.astype(BF)
-            inner_tile[part, units : 2 * units] = (inner * silu_value).astype(BF)
+            for n in range(2):
+                columns = pl.ds(n * units, units)
+                inner_tile[part, columns] = (
+                    grad_active * factors[index, part, columns].astype(F32)
+                ).astype(BF)
             result = dot_transposed(inner_tile[part], in_weight[...]).astype(BF)
             out_stage[blocks, :, 0:width] = result.reshape(2, rows, width)
             return carry
@@ -1567,9 +1758,9 @@
     wire.finish()
 
 
-def turn(extent, partial, middle, teacher, weight, tokens, hidden, pieces):
+def turn(extent, partial, middle, teacher, weight, tokens, hidden, landed, *tables):
     rows, width = middle.shape
-    slab = pieces[0].shape[2]
+    slab = landed.shape[3]
     return pl.pallas_call(
         functools.partial(turn_kernel, extent),
         out_shape=[
@@ -1580,29 +1771,31 @@
             jax.ShapeDtypeStruct((extent, 2, 4 * rows, 2 * slab), BF),
             jax.ShapeDtypeStruct((extent, 2, 4, rows, width), BF),
         ],
-        in_specs=[ANY, VM, VM, VM] + [ANY] * 10,
+        in_specs=[ANY, VM, VM, VM] + [ANY] * 6,
         out_specs=[VM, VM] + [ANY] * 4,
         scratch_shapes=sum_scratch(extent, rows, width)
         + [
             pltpu.VMEM((rows, width), BF),
             pltpu.VMEM((width, 4 * slab), BF),
             pltpu.VMEM((2 * slab, width), BF),
-            pltpu.VMEM((4, rows, 128), BF),
-            pltpu.VMEM((4 * rows, 4 * slab), BF),
+            pltpu.VMEM((2, 4, rows, 128), BF),
+            pltpu.VMEM((2, 4 * rows, 4 * slab), BF),
+            pltpu.VMEM((2 * extent, 4 * rows, 6 * slab), BF),
             pltpu.VMEM((4, rows, width), BF),
             pltpu.VMEM((4, rows, width + 128), BF),
-            pltpu.VMEM((4 * rows, 2 * slab), BF),
+            pltpu.VMEM((2, 4 * rows, 2 * slab), BF),
             pltpu.VMEM((4 * rows, 4 * slab), BF),
         ]
         + dma_pair(150)
         + [
             pltpu.SemaphoreType.DMA((20,)),
             pltpu.SemaphoreType.DMA((48,)),
-            pltpu.SemaphoreType.DMA((6,)),
+            pltpu.SemaphoreType.DMA((3,)),
+            pltpu.SemaphoreType.DMA((3, 2)),
         ],
         compiler_params=kernel_params(4),
         cost_estimate=pl.CostEstimate(flops=0, bytes_accessed=450_000_000, transcendentals=0),
-    )(partial, middle, teacher, weight, tokens, hidden, *pieces)
+    )(partial, middle, teacher, weight, tokens, hidden, landed, *tables)
 
 
 class WeightGrads:
@@ -1675,6 +1868,7 @@
     wire, local = Wire(send_sem, recv_sem), Local(local_sem)
     weight_grads = WeightGrads(sources, tiles, totals, tile_sem)
     count = 2 * extent
+    piece_slots, copies = [], []
     weight_grads.start(0)
 
     def between(turn_number):
@@ -1683,18 +1877,21 @@
         if turn_number < extent:
             weight_grads.work(2 * turn_number, count)
             weight_grads.work(2 * turn_number + 1, count)
+        if turn_number == extent + 2:
+            weight_grads.pieces(d, stage)
+            for bits in range(1, 6):
+                slot = wire.slot()
+                piece_slots.append(slot)
+                wire.start(
+                    slot,
+                    lambda bits=bits: stage.at[bits],
+                    lambda bits=bits: came[bits],
+                    (flip(d, bits), t),
+                )
+            for bits in (0, 6, 7):
+                copies.append(local.start(stage.at[bits], came[bits]))
 
     sum_plane(wire, local, d, t, extent, partial, buffers, rows, between)
-    weight_grads.pieces(d, stage)
-    piece_slots = []
-    for bits in range(1, 6):
-        slot = wire.slot()
-        piece_slots.append(slot)
-        wire.start(
-            slot, lambda bits=bits: stage.at[bits], lambda bits=bits: came[bits], (flip(d, bits), t)
-        )
-    copies = [local.start(stage.at[bits], came[bits]) for bits in (0, 6, 7)]
-    coeff_grads = []
 
     def collect(part, value):
         grad_logits[part] = value
@@ -1736,6 +1933,7 @@
 
     copies.append(local.start(packet, place(t)))
     line = LineGather(wire, d, t, extent, lambda: packet, place)
+    line.begin()
     for step in range(1, extent):
         line.step(step)
     for copy in copies:
@@ -1774,158 +1972,6 @@
         compiler_params=kernel_params(5),
         cost_estimate=pl.CostEstimate(flops=0, bytes_accessed=350_000_000, transcendentals=0),
     )(partial, middle, grad_output, gates, chosen, gain, router_t, *sources)
-
-
-def line_exchange(wire, t, d, extent, outbox, inbox):
-    peers = [(d, (t + k) % extent) for k in range(1, extent)]
-    slots = []
-    for k, peer in enumerate(peers):
-        slot = wire.slot()
-        slots.append(slot)
-        wire.start(slot, lambda: outbox, lambda k=k: inbox.at[k], peer)
-    result = outbox[...]
-    for k, peer in enumerate(peers):
-        wire.arrive(slots[k], lambda k=k: inbox.at[k], peer)
-        result = result + inbox[k]
-    return result
-
-
-def columns_to_rows(ref):
-    return ref[...].T[0:8]
-
-
-def rows_to_columns(value):
-    return jnp.concatenate([value, jnp.zeros((120, value.shape[1]), F32)], axis=0).T
-
-
-def turned(value, cosine, sine, direction):
-    return value * cosine + direction * pltpu.roll(value, HD // 2, 1) * sine
-
-
-def line_peers(d, t, extent):
-    return [(None, (d, (t + k) % extent)) for k in range(1, extent)]
-
-
-def attend_kernel(
-    extent,
-    length,
-    hid,
-    gain,
-    qkv_weight,
-    o_weight,
-    head_gain,
-    cosine,
-    sine,
-    normed,
-    units,
-    low,
-    probs,
-    mixed,
-    out,
-    inverses,
-    raw,
-    sums,
-    outbox,
-    inbox,
-    send_sem,
-    recv_sem,
-):
-    d, t = lax.axis_index("dp"), lax.axis_index("tensor")
-    seq_len, width = hid.shape
-    heads = head_gain.shape[0] // 2
-    columns = heads * HD
-    greet(line_peers(d, t, extent))
-    wire = Wire(send_sem, recv_sem)
-    tile = 256
-
-    def project(start):
-        part = pl.ds(start, tile)
-        value = hid[part].astype(F32)
-        unit = value * lax.rsqrt(jnp.mean(value * value, axis=-1, keepdims=True) + EPSILON)
-        normed[part] = (unit * gain[...]).astype(BF)
-        result = jnp.dot(normed[part], qkv_weight[...], preferred_element_type=F32)
-        raw[part] = result
-        lane = lax.broadcasted_iota(jnp.int32, (tile, 128), 1)
-        squares = [
-            jnp.sum(jnp.square(result[:, n * columns : (n + 1) * columns]), axis=-1, keepdims=True)
-            for n in range(2)
-        ]
-        sums[part] = jnp.where(lane == 0, squares[0], jnp.where(lane == 1, squares[1], 0.0))
-
-    rows_loop(seq_len, tile, project)
-    outbox[...] = columns_to_rows(sums)
-    total = line_exchange(wire, t, d, extent, outbox, inbox)
-    inverses[...] = rows_to_columns(lax.rsqrt(total / width + EPSILON))
-    low[:, 2 * columns :] = raw[:, 2 * columns :].astype(BF)
-
-    def head(h, carry):
-        for n in range(2):
-            section = pl.ds(pl.multiple_of(n * columns + h * HD, HD), HD)
-            unit = raw[:, section] * inverses[:, n : n + 1]
-            units[:, section] = unit
-            scaled = unit * head_gain[pl.ds(n * heads + h, 1)]
-            low[:, section] = turned(scaled, cosine[...], sine[...], 1.0).astype(BF)
-        section = pl.ds(pl.multiple_of(h * HD, HD), HD)
-        key_section = pl.ds(pl.multiple_of(columns + h * HD, HD), HD)
-        value_section = pl.ds(pl.multiple_of(2 * columns + h * HD, HD), HD)
-
-        def some(start):
-            part = pl.ds(start, tile)
-            scores = dot_transposed(low[part, section], low[:, key_section]) / math.sqrt(HD)
-            row = start + lax.broadcasted_iota(jnp.int32, scores.shape, 0)
-            column = lax.broadcasted_iota(jnp.int32, scores.shape, 1)
-            allowed = both(column <= row, column < length[0])
-            scores = jnp.where(allowed, scores, -1e30)
-            powers = jnp.exp(scores - jnp.max(scores, axis=-1, keepdims=True))
-            result = powers / jnp.sum(powers, axis=-1, keepdims=True)
-            probs[h, part] = result
-            mixed[part, section] = jnp.dot(
-                result.astype(BF), low[:, value_section], preferred_element_type=F32
-            ).astype(BF)
-
-        rows_loop(seq_len, tile, some)
-        return carry
-
-    lax.fori_loop(0, heads, head, 0)
-
-    def finish(start):
-        part = pl.ds(start, tile)
-        out[part] = jnp.dot(mixed[part], o_weight[...], preferred_element_type=F32).astype(BF)
-
-    rows_loop(seq_len, tile, finish)
-    wire.finish()
-
-
-SMEM = pl.BlockSpec(memory_space=pltpu.SMEM)
-
-
-def attend(extent, length, hid, gain, qkv_weight, o_weight, head_gain, cosine, sine):
-    seq_len, width = hid.shape
-    heads = head_gain.shape[0] // 2
-    columns = heads * HD
-    return pl.pallas_call(
-        functools.partial(attend_kernel, extent),
-        out_shape=[
-            jax.ShapeDtypeStruct((seq_len, width), BF),
-            jax.ShapeDtypeStruct((seq_len, 2 * columns), F32),
-            jax.ShapeDtypeStruct((seq_len, 3 * columns), BF),
-            jax.ShapeDtypeStruct((heads, seq_len, seq_len), F32),
-            jax.ShapeDtypeStruct((seq_len, columns), BF),
-            jax.ShapeDtypeStruct((seq_len, width), BF),
-            jax.ShapeDtypeStruct((seq_len, 128), F32),
-        ],
-        in_specs=[SMEM] + [VM] * 7,
-        out_specs=[VM] * 7,
-        scratch_shapes=[
-            pltpu.VMEM((seq_len, 3 * columns), F32),
-            pltpu.VMEM((seq_len, 128), F32),
-            pltpu.VMEM((8, seq_len), F32),
-            pltpu.VMEM((extent - 1, 8, seq_len), F32),
-        ]
-        + dma_pair(extent - 1),
-        compiler_params=kernel_params(2),
-        cost_estimate=pl.CostEstimate(flops=0, bytes_accessed=60_000_000, transcendentals=0),
-    )(length, hid, gain, qkv_weight, o_weight, head_gain, cosine, sine)
 
 
 def attend_back_kernel(
@@ -2356,27 +2402,11 @@
     local_heads = q_gain.shape[0]
     columns = local_heads * HD
 
-    qkv_own = jnp.concatenate([q_weight, k_weight, v_weight], axis=1)
     gains_own = lax.dynamic_update_slice(
         jnp.zeros((2 * local_heads, HD), F32),
         jnp.concatenate([q_gain, k_gain], axis=0).astype(F32),
         (0, d * head_width),
     )
-    hidden_bf, qkv_full, o_full, gains_all, *sent = fetch(
-        extent, hidden_in, qkv_own, o_weight, gains_own, gate_weight, up_weight, down_weight
-    )
-    pieces = [exchange(piece, bits) for bits, piece in enumerate(sent[:6])]
-    head_gain = jnp.sum(gains_all, axis=0)
-    positions = jnp.arange(seq_len)
-    frequency = THETA ** (-jnp.arange(HD // 2).astype(F32) / (HD // 2))
-    angles = positions.astype(F32)[:, None] * frequency[None, :]
-    cosine = jnp.concatenate([jnp.cos(angles)] * 2, axis=1)
-    sine = jnp.concatenate([-jnp.sin(angles), jnp.sin(angles)], axis=1)
-    attn_operands = (hidden_bf, attn_gain[None, :], qkv_full, o_full, head_gain, cosine, sine)
-    normed, units, low, probs, mixed, attn_partial, inverses = attend(
-        extent, length[None], *attn_operands
-    )
-
     lane = jnp.arange(128)
     lane_expert = jnp.where(lane < 2 * expert_count, lane % expert_count, -1)
     routes_own = lax.dynamic_slice_in_dim(routes, t * rows, rows, 0)
@@ -2386,17 +2416,47 @@
     router_t = jnp.concatenate(
         [router_weight.T, jnp.zeros((128 - expert_count, width), BF)], axis=0
     )
-    middle, gates, ffn_own, tokens, hidden, expert_partial, *last_pieces = enter(
+    angles = np.arange(seq_len)[:, None] * THETA ** (-np.arange(HD // 2) / (HD // 2))[None, :]
+    cosine = jnp.asarray(np.concatenate([np.cos(angles)] * 2, axis=1), F32)
+    sine = jnp.asarray(np.concatenate([-np.sin(angles), np.sin(angles)], axis=1), F32)
+    (
+        middle,
+        gates,
+        ffn_own,
+        head_gain,
+        inverses,
+        hidden_bf,
+        qkv_full,
+        o_full,
+        normed,
+        units,
+        low,
+        probs,
+        mixed,
+        tokens,
+        hidden,
+        expert_partial,
+        landed,
+    ) = front(
         extent,
-        attn_partial.reshape(extent, rows, width),
+        length[None],
         hidden_in,
+        q_weight,
+        k_weight,
+        v_weight,
+        o_weight,
+        gains_own,
+        gate_weight,
+        up_weight,
+        down_weight,
+        attn_gain[None, :],
+        cosine,
+        sine,
         ffn_gain,
         router_wide,
         chosen,
-        pieces,
-        sent[6:],
-    )
-    pieces = pieces + last_pieces
+    )
+    attn_operands = (hidden_bf, attn_gain[None, :], qkv_full, o_full, head_gain, cosine, sine)
     own_positions = t * rows + jnp.arange(rows)
     row_scale = jnp.where(own_positions < length, all_tokens / total_count, 0.0)
     grad_output, row_loss, ffn_grad_partial, inner, active, grads = turn(
@@ -2407,7 +2467,10 @@
         jnp.broadcast_to(row_scale[:, None], (rows, 128)),
         tokens,
         hidden,
-        pieces,
+        landed,
+        gate_weight,
+        up_weight,
+        down_weight,
     )
     grad_middle, grad_logits, ffn_gain_part, attn_grad_rows, *came = leave(
         extent,

time: 639 us -> 599 us (0.937)
  Pallas kernels: 597 us -> 563 us
    pallas_call x3 -> x1, Pallas kernels: 205 us -> 188 us  [front(): pl.pallas_call(functools.partial(front_kernel, extent), out_shape=[shape(...]
    pallas_call x1, Pallas kernels: 175 us -> 160 us  [turn(): pl.pallas_call(functools.partial(turn_kernel, extent), out_shape=[jax.Sha...]
  transfers between devices with their start and end apart: 7 -> 2, of which waited for: 0 -> 0; matrix products, arithmetic and copies ran while one was open for 4% -> 2% of each run, Pallas kernels for 18% -> 15%
where the time goes in v4:
time: 599 us; the launch traced here: 597 us
  Pallas kernels  563 us (94%)
  local copies, waits for them, and re-layouts  18.7 us (3%)
  other arithmetic  8.96 us (1%)
    pallas_call x1, Pallas kernels, front(): pl.pallas_call(functools.partial(front_kernel, extent), out_shape=[shape(...  188 us
    pallas_call x1, Pallas kernels, turn(): pl.pallas_call(functools.partial(turn_kernel, extent), out_shape=[jax.Sha...  160 us
    pallas_call x1, Pallas kernels, leave(): pl.pallas_call(functools.partial(leave_kernel, extent), out_shape=[jax.Sh...  119 us
    pallas_call x1, Pallas kernels, close(): pl.pallas_call(functools.partial(close_kernel, extent), out_shape=[jax.Sh...  48 us
    pallas_call x1, Pallas kernels, attend_back(): pl.pallas_call(functools.partial(attend_back_kernel, extent), out_shape=[...  40.9 us
  transfers between devices with their start and end apart: 2, of which 0 were waited for; matrix products, arithmetic and copies ran while one was open for 2% of the time, Pallas kernels for 15%

profile of v4, /device:TPU:0, one launch (start us, length us, event | category | flops | bytes accessed | tf_op | source)
XLA Modules:
  0.0 597.3 jit_solution(8095519147056039102)
XLA Ops:
  2.4 1.3 reduce_sum.27
  3.7 1.2 dynamic_slice.9.length
  4.9 1.3 broadcast_in_dim.52
  6.2 1.3 broadcast_in_dim.53
  7.5 1.1 copy.44
  10.0 1.7 concatenate.17.router_t
  11.7 1.1 maximum_maximum_fusion.router
  14.4 187.6 %shard_map.281 = (f32[128,2048]{1,0:T(8,128)}, f32[128,128]{1,0:T(8,128)}, bf16[128,2048]{1,0:T(8,128)(2,1)}, f32[8,128]{1,0:T(8,128)}, f32[512,128]{1,0:T(8,128...) custom-call(s32[1]{0:T(128)} %dynamic_slice.9.length, ...), custom_call_target="tpu_custom_call" | custom-call | bytes 300000000 | tf_op jit(solution)/shard_map/pallas_call | solution.py:1534
  202.7 159.9 %shard_map.282 = (f32[128,2048]{1,0:T(8,128)}, f32[128,128]{1,0:T(8,128)}, bf16[4,2,4,128,2176]{4,3,2,1,0:T(8,128)(2,1)}, bf16[4,2,512,1024]{3,2,1,0:T(8,128)(2,...) custom-call(bf16[4,2,4,128,2048]{4,3,2,1,0:T(8,128)(2,1)} %get-tuple-element.62.partial, ...), custom_call_target="tpu_custom_call" | custom-call | bytes 450000000 | tf_op jit(solution)/shard_map/pallas_call | solution.py:1764
  362.6 118.8 %shard_map.283 = (f32[128,2048]{1,0:T(8,128)}, f32[128,128]{1,0:T(8,128)}, f32[8,2048]{1,0:T(8,128)}, bf16[4,128,2048]{2,1,0:T(8,128)(2,1)}, bf16[3,2,256,256]{3...) custom-call(bf16[4,2,4,128,2176]{4,3,2,1,0:T(8,128)(2,1)} %get-tuple, ...), custom_call_target="tpu_custom_call" | custom-call | bytes 350000000 | tf_op jit(solution)/shard_map/pallas_call | solution.py:1951
  481.4 1.5 collective-permute-start
  482.9 1.5 fusion
  484.7 40.9 %shard_map.284 = (bf16[512,2048]{1,0:T(8,128)(2,1)}, bf16[2048,1536]{1,0:T(8,128)(2,1)}, bf16[512,2048]{1,0:T(8,128)(2,1)}, f32[8,2048]{1,0:T(8,128)}, f32[8,128]{1,0:T(8,128)}, /*index=5*/f32[8,128]{1,0:T(8,128)}) custom-call(bf16[512,2048]{1,0:T(8,128)(2,1)} %bitcast.14, f32[128,128]{1,0:T(8,128)} %get-tuple-element.74.row_loss, ...), custom_call_target="tpu_custom_call" | custom-call | bytes 1000000 | tf_op jit(solution)/shard_map/pallas_call | solution.py:2103
  525.6 0.9 reduce_sum.28
  526.8 0.8 maximum_bitcast_fusion.small
  527.6 48.0 %shard_map.285 = (f32[128,2048]{1,0:T(8,128)}, f32[256,1536]{1,0:T(8,128)}, f32[512,256]{1,0:T(8,128)}, f32[24,128]{1,0:T(8,128)}) custom-call(bf16[4,128,2048]{2,1,0:T(8,128)(2,1)} %bitcast.15, f32[128,2048]{1,0:T(8,128)} %get-tuple-element.87.grad_middle, bf16[2048,1536]{1,0:T(8,128)(2,1)} %get-tuple-element.88.grad_qkv, ...), custom_call_target="tpu_custom_call" | custom-call | bytes 150000000 | tf_op jit(solution)/shard_map/pallas_call | solution.py:2327
  577.1 1.2 slice.30
  578.9 0.8 constant_dynamic-slice_fusion
  579.7 1.3 slice_bitcast_fusion
  581.6 2.6 fusion.2
  584.3 0.9 copy-done.3
  585.1 8.2 %shard_map.286 = (f32[16,256,256]{2,1,0:T(8,128)}, f32[16,256,256]{2,1,0:T(8,128)}, f32[16,256,256]{2,1,0:T(8,128)}) custom-call(bf16[3,2,256,256]{3,2,1,0:T(8,128)(2,1)} %get-tuple-element.99.refs_0_, bf16[3,2,256,256]{3,2,1,0:T(8,128)(2,1)} %get-tuple-element.100.refs_1_, bf16[3,2,256,256]{3,2,1,0:T(8,128)(2,1)} %get-tuple-element.101.refs_2_, ...), custom_call_target="tpu_custom_call" | custom-call | bytes 20000000 | tf_op jit(solution)/shard_map/pallas_call | solution.py:2355
  593.3 1.0 copy.58
  594.3 1.9 copy.59
  (40 shorter events, 7.3 us)
Async XLA Ops:
  0.6 0.7 copy-start
  13.8 0.6 copy-start.6
  362.6 120.4 %copy-start.4 = (bf16[128,2048]{1,0:T(8,128)(2,1)S(1)}, bf16[128,2048]{1,0:T(8,128)(2,1)}, u32[]{:S(2)}) copy-start(bf16[128,2048]{1,0:T(8,128)(2,1)} %get-tuple-element.92) | copy-start | bytes 1572868
  481.4 102.9 %collective-permute-start = (bf16[3,2,256,256]{3,2,1,0:T(8,128)(2,1)}, bf16[3,2,256,256]{3,2,1,0:T(8,128)(2,1)S(1)}, u32[]{:S(2)}, u32[]{:S(2)}) collective-permute-start(bf16[3,2,256,256]{3,2,1,0:T(8,128)(2,1)} %get-tuple-element.105), channel_id=1, source_target_pairs={{0,24},{4,28},{8,16},{12,20},{16,8},{20,12},{24,0},{28,4},{1,25},{... | collective-permute-start | bytes 2359304 | tf_op jit(solution)/shard_map/ppermute | solution.py:2368
  482.9 101.4 %collective-permute-start.1 = (bf16[3,2,256,256]{3,2,1,0:T(8,128)(2,1)}, bf16[3,2,256,256]{3,2,1,0:T(8,128)(2,1)}, u32[]{:S(2)}, u32[]{:S(2)}) collective-permute-start(bf16[3,2,256,256]{3,2,1,0:T(8,128)(2,1)} %get-tuple-element.106), channel_id=1, source_target_pairs={{0,28},{4,24},{8,20},{12,16},{16,12},{20,8},{24,4},{28,0},{1,29},{... | collective-permute-start | bytes 2359304 | tf_op jit(solution)/shard_map/ppermute | solution.py:2368
  484.7 41.9 %copy-start.5 = (f32[8,2048]{1,0:T(8,128)S(1)}, f32[8,2048]{1,0:T(8,128)}, u32[]{:S(2)}) copy-start(f32[8,2048]{1,0:T(8,128)} %get-tuple-element.91) | copy-start | bytes 196612
  581.6 11.7 %copy-start.2 = (f32[128,2048]{1,0:T(8,128)S(1)}, f32[128,2048]{1,0:T(8,128)}, u32[]{:S(2)}) copy-start(f32[128,2048]{1,0:T(8,128)} %get-tuple-element.174) | copy-start | bytes 3145732
  584.2 0.9 copy-start.3
  584.3 11.9 %copy-start.1 = (s32[512,8]{0,1:T(8,128)S(1)}, s32[512,8]{0,1:T(8,128)}, u32[]{:S(2)}) copy-start(s32[512,8]{0,1:T(8,128)} %param.21) | copy-start | bytes 49156

commit v5 on v4

--- a/solution.py
+++ b/solution.py
@@ -1159,13 +1159,14 @@
 
 def front_kernel(
     extent,
-    length,
+    lengths,
     hid,
     q_weight,
     k_weight,
     v_weight,
     o_weight,
-    gains,
+    q_gain,
+    k_gain,
     gate,
     up,
     down,
@@ -1174,10 +1175,10 @@
     sine,
     ffn_gain,
     router,
+    routes,
     chosen,
     middle,
     gates,
-    ffn_own,
     head_gain,
     inverses,
     hid_out,
@@ -1196,6 +1197,7 @@
     qkv_all,
     o_all,
     gains_all,
+    router_rows,
     normed,
     raw,
     low,
@@ -1223,8 +1225,9 @@
     d, t = lax.axis_index("dp"), lax.axis_index("tensor")
     seq_len, width = hid_all.shape
     rows = seq_len // extent
-    heads = gains.shape[0] // 2
+    heads, head_width = q_gain.shape
     columns = heads * HD
+    length = lengths[d]
     depth, o_rows, o_width = q_weight.shape[0], o_weight.shape[0], o_weight.shape[1]
     wire, local = Wire(send_sem, recv_sem), Local(local_sem)
     dx, dy, dxy = flip(d, 2), flip(d, 4), flip(d, 6)
@@ -1247,7 +1250,23 @@
         target = qkv_all.at[pl.ds(d * depth, depth), pl.ds(n * columns, columns)]
         copies.append(local.start(weight, target))
     copies.append(local.start(o_weight, region(d, None)[1]))
-    gains_all[0] = gains[...]
+    lane = lax.broadcasted_iota(jnp.int32, (heads, HD), 1)
+    for n, source in enumerate((q_gain, k_gain)):
+        value = source[...].astype(F32)
+        spread_out = jnp.zeros((heads, HD), F32)
+        for i in range(head_width):
+            spread_out += jnp.where(lane == d * head_width + i, value[:, i : i + 1], 0.0)
+        gains_all[0, n * heads : (n + 1) * heads] = spread_out
+    router_rows[...] = jnp.zeros(router_rows.shape, BF)
+    router_rows[0:16] = router[...]
+    router_rows[16:32] = router[...]
+    lane = lax.broadcasted_iota(jnp.int32, (rows, 128), 1)
+    own_routes = routes[pl.ds(pl.multiple_of(t * rows, rows), rows)]
+    picked = jnp.zeros((rows, 128), F32)
+    for k in range(own_routes.shape[1]):
+        match = both(own_routes[:, k : k + 1] == lane % 16, lane < 32)
+        picked = jnp.where(match, 1.0, picked)
+    chosen[...] = picked
     greet(line_peers(d, t, extent) + [(None, (flip(d, bits), t)) for bits in range(1, 8)])
     for copy in copies:
         copy.wait()
@@ -1276,7 +1295,7 @@
         gain_slots[bits] = wire.slot()
         wire.start(
             gain_slots[bits],
-            lambda: gains,
+            lambda: gains_all.at[0],
             lambda bits=bits: gains_all.at[bits],
             (flip(d, bits), t),
         )
@@ -1321,7 +1340,7 @@
         part = pl.ds(start, 64)
         value = hid_all[part].astype(F32)
         unit = value * lax.rsqrt(jnp.mean(value * value, axis=-1, keepdims=True) + EPSILON)
-        normed[part] = (unit * attn_gain[...]).astype(BF)
+        normed[part] = (unit * attn_gain[...].astype(F32)).astype(BF)
 
     rows_loop(seq_len, 64, normalize)
     for bits in (1, 3, 5, 7):
@@ -1373,7 +1392,7 @@
             scores = dot_transposed(low[part, section], low[:, key_section]) / math.sqrt(HD)
             row = start + lax.broadcasted_iota(jnp.int32, scores.shape, 0)
             column = lax.broadcasted_iota(jnp.int32, scores.shape, 1)
-            allowed = both(column <= row, column < length[0])
+            allowed = both(column <= row, column < length)
             scores = jnp.where(allowed, scores, -1e30)
             powers = jnp.exp(scores - jnp.max(scores, axis=-1, keepdims=True))
             result = powers / jnp.sum(powers, axis=-1, keepdims=True)
@@ -1414,10 +1433,10 @@
         )
         middle[part] = value
         unit = value * lax.rsqrt(jnp.mean(value * value, axis=-1, keepdims=True) + EPSILON)
-        ffn_own[part] = (unit * ffn_gain[...]).astype(BF)
+        packet[part, 0:width] = (unit * ffn_gain[...].astype(F32)).astype(BF)
 
     rows_loop(rows, 16, body)
-    logits = jnp.dot(ffn_own[...], router[...], preferred_element_type=F32)
+    logits = dot_transposed(packet[:, 0:width], router_rows[...])
     lane = lax.broadcasted_iota(jnp.int32, logits.shape, 1)
     top = jnp.max(jnp.where(lane < 16, logits, -1e30), axis=-1, keepdims=True)
     powers = jnp.where(lane < 32, jnp.exp(logits - top), 0.0)
@@ -1425,7 +1444,6 @@
     gates[...] = chance
     coeff = chance * chosen[...]
     high = coeff.astype(BF).astype(F32)
-    packet[:, 0:width] = ffn_own[...]
     packet[:, width : width + 128] = jnp.where(lane < 16, high, coeff - high).astype(BF)
 
     def place(j, c, i):
@@ -1514,11 +1532,11 @@
 SMEM = pl.BlockSpec(memory_space=pltpu.SMEM)
 
 
-def front(extent, length, hid, q_weight, k_weight, v_weight, o_weight, gains, gate, up, down, *rest):
+def front(extent, lengths, hid, *rest):
     rows, width = hid.shape
     seq_len = rows * extent
-    slab = gate.shape[1]
-    heads = gains.shape[0] // 2
+    slab = rest[6].shape[1]
+    heads = rest[4].shape[0]
     columns = heads * HD
     shape = jax.ShapeDtypeStruct
     kept = [
@@ -1534,9 +1552,9 @@
     return pl.pallas_call(
         functools.partial(front_kernel, extent),
         out_shape=[
+            shape((rows, 128), F32),
             shape((rows, width), F32),
             shape((rows, 128), F32),
-            shape((rows, width), BF),
             shape((2 * heads, HD), F32),
             shape((seq_len, 128), F32),
         ]
@@ -1547,13 +1565,14 @@
             shape((extent, 2, 4, rows, width), BF),
             shape((8, 3, 2, slab, slab), BF),
         ],
-        in_specs=[SMEM, VM] + [ANY] * 4 + [VM] + [ANY] * 3 + [VM] * 6,
+        in_specs=[SMEM, VM] + [ANY] * 4 + [VM] * 2 + [ANY] * 3 + [VM] * 6,
         out_specs=[VM] * 5 + [ANY] * 12,
         scratch_shapes=[
             pltpu.VMEM((seq_len, width), BF),
             pltpu.VMEM((width, 3 * columns), BF),
             pltpu.VMEM((columns, width), BF),
-            pltpu.VMEM((8,) + gains.shape, F32),
+            pltpu.VMEM((8, 2 * heads, HD), F32),
+            pltpu.VMEM((128, width), BF),
             pltpu.VMEM((seq_len, width), BF),
             pltpu.VMEM((seq_len, 3 * columns), F32),
             pltpu.VMEM((seq_len, 3 * columns), BF),
@@ -1581,10 +1600,10 @@
         ],
         compiler_params=kernel_params(1),
         cost_estimate=pl.CostEstimate(flops=0, bytes_accessed=300_000_000, transcendentals=0),
-    )(length, hid, q_weight, k_weight, v_weight, o_weight, gains, gate, up, down, *rest)
-
-
-def turn_kernel(extent, partial, middle, teacher, weight, tokens, hidden, *rest):
+    )(lengths, hid, *rest)
+
+
+def turn_kernel(extent, lengths, partial, middle, teacher, tokens, hidden, *rest):
     landed, tables = rest[0], rest[1:4]
     grad_output, row_loss, out, inner_out, active_out, grads = rest[4:10]
     buffers = rest[10:20]
@@ -1674,10 +1693,18 @@
     for g in (count - 2, count - 1):
         active_store(g).wait()
 
+    total_count = lengths[0]
+    for n in range(1, lengths.shape[0]):
+        total_count = total_count + lengths[n]
+    length = lengths[d]
+
     def body(part, value):
+        row = t * rows + part.start + lax.broadcasted_iota(jnp.int32, (16, 1), 0)
+        count = jnp.broadcast_to(total_count, (16, 1)).astype(F32)
+        weight = jnp.where(row < length, 8 * extent * rows / count, 0.0)
         output = middle[part] + value
         mismatch = output - teacher[part].astype(F32)
-        scaled = mismatch * weight[part, 0:1]
+        scaled = mismatch * weight
         grad_output[part] = scaled
         packet[part] = scaled.astype(BF)
         row_loss[part] = jnp.broadcast_to(
@@ -1758,7 +1785,7 @@
     wire.finish()
 
 
-def turn(extent, partial, middle, teacher, weight, tokens, hidden, landed, *tables):
+def turn(extent, lengths, partial, middle, teacher, tokens, hidden, landed, *tables):
     rows, width = middle.shape
     slab = landed.shape[3]
     return pl.pallas_call(
@@ -1771,7 +1798,7 @@
             jax.ShapeDtypeStruct((extent, 2, 4 * rows, 2 * slab), BF),
             jax.ShapeDtypeStruct((extent, 2, 4, rows, width), BF),
         ],
-        in_specs=[ANY, VM, VM, VM] + [ANY] * 6,
+        in_specs=[SMEM, ANY, VM, VM] + [ANY] * 6,
         out_specs=[VM, VM] + [ANY] * 4,
         scratch_shapes=sum_scratch(extent, rows, width)
         + [
@@ -1795,7 +1822,7 @@
         ],
         compiler_params=kernel_params(4),
         cost_estimate=pl.CostEstimate(flops=0, bytes_accessed=450_000_000, transcendentals=0),
-    )(partial, middle, teacher, weight, tokens, hidden, landed, *tables)
+    )(lengths, partial, middle, teacher, tokens, hidden, landed, *tables)
 
 
 class WeightGrads:
@@ -1855,13 +1882,13 @@
                     stage[bits, place, e] = value.astype(BF)
 
 
-def leave_kernel(extent, partial, middle, grad_output, gates, chosen, gain, router_t, *rest):
+def leave_kernel(extent, partial, middle, grad_output, gates, chosen, gain, router, *rest):
     sources = rest[:4]
-    grad_middle, grad_logits, gain_part, grads = rest[4:8]
-    came = rest[8:16]
-    buffers = rest[16:26]
-    tiles, totals = rest[26:30], rest[30:32]
-    stage, packet, send_sem, recv_sem, local_sem, tile_sem = rest[32:]
+    grad_middle, small, grads = rest[4:7]
+    came = rest[7:15]
+    buffers = rest[15:25]
+    tiles, totals = rest[25:29], rest[29:31]
+    stage, packet, grad_logits, gain_part, ffn_own, send_sem, recv_sem, local_sem, tile_sem = rest[31:]
     d, t = lax.axis_index("dp"), lax.axis_index("tensor")
     rows, width = middle.shape
     greet(line_devices(d, t, extent) + [(None, (flip(d, bits), t)) for bits in range(1, 6)])
@@ -1908,8 +1935,8 @@
     for begin in range(0, width, 512):
         columns = slice(begin, begin + 512)
         grad_middle[:, columns] = jnp.dot(
-            high, router_t[:, columns], preferred_element_type=F32
-        ) + jnp.dot(low_part, router_t[:, columns], preferred_element_type=F32)
+            high[:, 0:16], router[:, columns], preferred_element_type=F32
+        ) + jnp.dot(low_part[:, 0:16], router[:, columns], preferred_element_type=F32)
     gain_part[...] = jnp.zeros(gain_part.shape, F32)
 
     def body(part, value):
@@ -1919,7 +1946,9 @@
         unit = value * inverse
         product = grad * unit
         gain_part[...] += product[0:8] + product[8:16]
-        scaled = grad * gain[...]
+        gain_row = gain[...].astype(F32)
+        ffn_own[part] = (unit * gain_row).astype(BF)
+        scaled = grad * gain_row
         result = grad_output[part] + inverse * (
             scaled - unit * jnp.mean(scaled * unit, axis=-1, keepdims=True)
         )
@@ -1934,6 +1963,11 @@
     copies.append(local.start(packet, place(t)))
     line = LineGather(wire, d, t, extent, lambda: packet, place)
     line.begin()
+    router_part = transposed_dot(high, ffn_own[...]) + transposed_dot(low_part, ffn_own[...])
+    small[0:16] = router_part[0:16]
+    row = lax.broadcasted_iota(jnp.int32, (8, width), 0)
+    gain_sum = jnp.sum(gain_part[...], axis=0, keepdims=True)
+    small[16:24] = jnp.where(row == 1, gain_sum, 0.0)
     for step in range(1, extent):
         line.step(step)
     for copy in copies:
@@ -1943,7 +1977,7 @@
     wire.finish()
 
 
-def leave(extent, partial, middle, grad_output, gates, chosen, gain, router_t, sources):
+def leave(extent, partial, middle, grad_output, gates, chosen, gain, router, sources):
     rows, width = middle.shape
     tokens, grads, inner, active = sources
     units = active.shape[3]
@@ -1952,13 +1986,12 @@
         functools.partial(leave_kernel, extent),
         out_shape=[
             jax.ShapeDtypeStruct((rows, width), F32),
-            jax.ShapeDtypeStruct((rows, 128), F32),
-            jax.ShapeDtypeStruct((8, width), F32),
+            jax.ShapeDtypeStruct((24, width), F32),
             jax.ShapeDtypeStruct((extent, rows, width), BF),
         ]
         + [piece] * 8,
         in_specs=[ANY, VM, VM, VM, VM, VM, VM] + [ANY] * 4,
-        out_specs=[VM, VM, VM] + [ANY] * 9,
+        out_specs=[VM, VM] + [ANY] * 9,
         scratch_shapes=sum_scratch(extent, rows, width + 128)
         + [pltpu.VMEM((2,) + source.shape[2:], BF) for source in sources]
         + [
@@ -1966,15 +1999,18 @@
             pltpu.VMEM((units, width), F32),
             pltpu.VMEM((8,) + piece.shape, BF),
             pltpu.VMEM((rows, width), BF),
+            pltpu.VMEM((rows, 128), F32),
+            pltpu.VMEM((8, width), F32),
+            pltpu.VMEM((rows, width), BF),
         ]
         + dma_pair(120)
         + [pltpu.SemaphoreType.DMA((24,)), pltpu.SemaphoreType.DMA((4, 2))],
         compiler_params=kernel_params(5),
         cost_estimate=pl.CostEstimate(flops=0, bytes_accessed=350_000_000, transcendentals=0),
-    )(partial, middle, grad_output, gates, chosen, gain, router_t, *sources)
-
-
-def attend_back_kernel(
+    )(partial, middle, grad_output, gates, chosen, gain, router, *sources)
+
+
+def back_kernel(
     extent,
     grads,
     row_loss,
@@ -1991,11 +2027,17 @@
     probs,
     mixed,
     inverses,
-    out,
-    grad_qkv,
-    grad_o,
-    attn_gain_part,
-    head_gain_part,
+    small,
+    grad_middle,
+    grad_in,
+    q_out,
+    k_out,
+    v_out,
+    o_out,
+    router_out,
+    vectors_out,
+    q_gain_out,
+    k_gain_out,
     loss,
     grad_mixed,
     scaled,
@@ -2004,17 +2046,41 @@
     dots,
     outbox,
     inbox,
+    gain_part,
+    head_part,
+    work,
+    up_in,
+    down_in,
+    q_send,
+    q_work,
+    q_core,
+    q_a,
+    q_b,
+    o_send,
+    o_work,
+    o_core,
+    o_a,
+    o_b,
+    small_send,
+    small_in,
+    small_sum,
+    small_last,
     send_sem,
     recv_sem,
 ):
     d, t = lax.axis_index("dp"), lax.axis_index("tensor")
     seq_len, width = hid.shape
+    rows = seq_len // extent
     heads = head_gain.shape[0] // 2
     columns = heads * HD
-    greet(line_peers(d, t, extent))
+    depth, o_width = q_out.shape[0], o_out.shape[1]
+    peers = [(d, (t + k) % extent) for k in range(1, extent)]
+    greet(line_peers(d, t, extent) + [(None, (flip(d, bits), t)) for bits in range(1, 8)])
     wire = Wire(send_sem, recv_sem)
+    to_x, to_y, to_c = (flip(d, 2), t), (flip(d, 4), t), (flip(d, 1), t)
     tile = 256
     root = math.sqrt(HD)
+    turns = (3, 1, 2, 0)
 
     def mix(start):
         part = pl.ds(start, tile)
@@ -2022,11 +2088,17 @@
 
     rows_loop(seq_len, tile, mix)
 
-    def into_o(start):
-        part = pl.ds(start, 512)
-        grad_o[:, part] = transposed_dot(mixed[...], grads[:, part]).astype(BF)
-
-    rows_loop(width, 512, into_o)
+    def o_slice(bits, target):
+        start = pl.multiple_of(flip(d, bits) * o_width, o_width)
+        target[...] = transposed_dot(mixed[...], grads[:, pl.ds(start, o_width)]).astype(BF)
+
+    core_slots = {}
+    for i in turns:
+        o_slice(1 + 2 * i, o_send.at[i])
+        core_slots["o", i] = wire.slot()
+        wire.start(core_slots["o", i], lambda i=i: o_send.at[i], lambda i=i: o_core.at[i], to_c)
+    for i in turns:
+        o_slice(2 * i, o_work.at[i])
     sums[...] = jnp.zeros(sums.shape, F32)
 
     def head(h, carry):
@@ -2048,7 +2120,7 @@
         for n, where in enumerate((section, key_section)):
             value = turned(pair[n], cosine[...], sine[...], -1.0)
             unit = units[:, where]
-            head_gain_part[pl.ds(n * heads + h, 1)] = jnp.sum(value * unit, axis=0, keepdims=True)
+            head_part[pl.ds(n * heads + h, 1)] = jnp.sum(value * unit, axis=0, keepdims=True)
             value = value * head_gain[pl.ds(n * heads + h, 1)]
             scaled[:, where] = value
             sums[...] += jnp.where(lane == n, jnp.sum(value * unit, axis=-1, keepdims=True), 0.0)
@@ -2058,7 +2130,7 @@
     outbox[...] = columns_to_rows(sums)
     outbox[2:3] = jnp.broadcast_to(jnp.sum(row_loss[:, 0:1], axis=0, keepdims=True), (1, seq_len))
     total = line_exchange(wire, t, d, extent, outbox, inbox)
-    loss[...] = total[:, 0:128]
+    loss[...] = total[:, 0:128] / (2.0 * width * 8 * seq_len)
     dots[...] = rows_to_columns(total / width)
 
     def head_again(h, carry):
@@ -2071,195 +2143,108 @@
         return carry
 
     lax.fori_loop(0, heads, head_again, 0)
-    attn_gain_part[...] = jnp.zeros(attn_gain_part.shape, F32)
-
-    def finish(start):
-        part = pl.ds(start, tile)
+    gain_part[...] = jnp.zeros(gain_part.shape, F32)
+    order = plane_order(t)
+
+    def input_block(k):
+        part = pl.ds(pl.multiple_of(order[k] * rows, rows), rows)
         grad = dot_transposed(raw_grad[part], qkv_weight[...])
         value = hid[part].astype(F32)
         inverse = lax.rsqrt(jnp.mean(value * value, axis=-1, keepdims=True) + EPSILON)
         unit = value * inverse
-        attn_gain_part[...] += jnp.sum((grad * unit).reshape(tile // 8, 8, width), axis=0)
-        change = grad * gain[...]
-        out[part] = (
+        gain_part[...] += jnp.sum((grad * unit).reshape(rows // 8, 8, width), axis=0)
+        change = grad * gain[...].astype(F32)
+        work[order[k]] = (
             inverse * (change - unit * jnp.mean(change * unit, axis=-1, keepdims=True))
         ).astype(BF)
 
-    rows_loop(seq_len, tile, finish)
-
-    def into_qkv(start):
-        part = pl.ds(start, 256)
-        grad_qkv[part] = transposed_dot(normed[:, part], raw_grad[...]).astype(BF)
-
-    rows_loop(width, 256, into_qkv)
-    wire.finish()
-
-
-def attend_back(extent, *operands):
-    seq_len, width = operands[0].shape
-    head_gain = operands[6]
-    heads = head_gain.shape[0] // 2
-    columns = heads * HD
-    return pl.pallas_call(
-        functools.partial(attend_back_kernel, extent),
-        out_shape=[
-            jax.ShapeDtypeStruct((seq_len, width), BF),
-            jax.ShapeDtypeStruct((width, 3 * columns), BF),
-            jax.ShapeDtypeStruct((columns, width), BF),
-            jax.ShapeDtypeStruct((8, width), F32),
-            jax.ShapeDtypeStruct((2 * heads, HD), F32),
-            jax.ShapeDtypeStruct((8, 128), F32),
-        ],
-        in_specs=[VM] * len(operands),
-        out_specs=[VM] * 6,
-        scratch_shapes=[
-            pltpu.VMEM((seq_len, columns), BF),
-            pltpu.VMEM((seq_len, 2 * columns), F32),
-            pltpu.VMEM((seq_len, 3 * columns), BF),
-            pltpu.VMEM((seq_len, 128), F32),
-            pltpu.VMEM((seq_len, 128), F32),
-            pltpu.VMEM((8, seq_len), F32),
-            pltpu.VMEM((extent - 1, 8, seq_len), F32),
-        ]
-        + dma_pair(extent - 1),
-        compiler_params=kernel_params(6),
-        cost_estimate=pl.CostEstimate(flops=0, bytes_accessed=1_000_000, transcendentals=0),
-    )(*operands)
-
-
-def close_kernel(
-    extent,
-    partial,
-    grad_middle,
-    grad_qkv,
-    grad_o,
-    small,
-    gains,
-    grad_in,
-    qkv_out,
-    o_out,
-    small_out,
-    work,
-    up_in,
-    down_in,
-    q_work,
-    q_core,
-    q_a,
-    q_b,
-    o_work,
-    o_core,
-    o_a,
-    o_b,
-    small_in,
-    small_sum,
-    small_last,
-    send_sem,
-    recv_sem,
-    local_sem,
-):
-    d, t = lax.axis_index("dp"), lax.axis_index("tensor")
-    rows, width = grad_middle.shape
-    depth, o_width = qkv_out.shape[0], o_out.shape[1]
-    line_peers = [(d, (t + k) % extent) for k in range(1, extent)]
-    greet(
-        [(None, peer) for peer in line_peers]
-        + [(None, (flip(d, bits), t)) for bits in range(1, 8)]
-    )
-    wire, local = Wire(send_sem, recv_sem), Local(local_sem)
-    to_x, to_y, to_c = (flip(d, 2), t), (flip(d, 4), t), (flip(d, 1), t)
-
-    def slices(device):
-        start = pl.multiple_of(device * o_width, o_width)
-        return [
-            grad_qkv.at[pl.ds(device * depth, depth)],
-            grad_o.at[:, pl.ds(start, o_width)],
-        ]
-
-    turns = (3, 1, 2, 0)
-    c_slots, loads = {}, {}
-    work_load = local.start(partial, work)
+    def q_slice(bits, target):
+        start = pl.multiple_of(flip(d, bits) * depth, depth)
+        target[...] = transposed_dot(normed[:, pl.ds(start, depth)], raw_grad[...]).astype(BF)
+
+    def q_core_send(i):
+        q_slice(1 + 2 * i, q_send.at[i])
+        core_slots["q", i] = wire.slot()
+        wire.start(core_slots["q", i], lambda: q_send.at[i], lambda: q_core.at[i], to_c)
+
+    line = LineSum(
+        wire, d, t, extent, lambda index: work.at[index], up_in, down_in, rows, 2
+    )
+
+    def cut(ref, which):
+        half = ref.shape[0] // 2
+        return ref.at[pl.ds(which * half, half)]
+
+    slots = {}
+    routes_a = ((to_x, 3, 2, 0, 0), (to_y, 3, 1, 1, 1), (to_x, 1, 0, 0, 2), (to_y, 2, 0, 1, 3))
+    routes_b = ((to_y, 2, 0, 0), (to_x, 1, 1, 1))
+    tables = (("q", q_work, q_core, q_a, q_b), ("o", o_work, o_core, o_a, o_b))
+
+    def core_add(i):
+        for name, kept, core, unused, unused_too in tables:
+            wire.arrive(core_slots[name, i], lambda: core.at[i], to_c)
+            add_into(kept.at[i], core.at[i], kept.shape[1])
+
+    def forward(stage, device, source, which, row):
+        for name, kept, unused, first, second in tables:
+            slots[name, stage, row] = wire.slot()
+            inbox_ref = first if stage == "a" else second
+            wire.start(
+                slots[name, stage, row],
+                lambda kept=kept: cut(kept.at[source], which),
+                lambda inbox_ref=inbox_ref: inbox_ref.at[row],
+                device,
+            )
+
+    q_core_send(3)
+    q_core_send(1)
+    input_block(0)
+    line.step(0)
+    q_core_send(2)
+    q_core_send(0)
+    for i in turns:
+        q_slice(2 * i, q_work.at[i])
+        core_add(i)
+        for device, source, unused, which, row in routes_a:
+            if source == i:
+                forward("a", device, source, which, row)
+    input_block(1)
+    input_block(2)
+    line.step(1)
+    input_block(3)
+    small_rows = small.shape[0]
+    vector = jnp.sum(gain_part[...], axis=0, keepdims=True)
+    row = lax.broadcasted_iota(jnp.int32, (small_rows, 128), 0)
+    for number in range(width // 128):
+        lanes = slice(number * 128, number * 128 + 128)
+        small_send[number % 2, number // 2] = jnp.where(
+            row == 16, vector[:, lanes], small[:, lanes]
+        )
     small_slots = []
-    for k, peer in enumerate(line_peers):
+    for k, peer in enumerate(peers):
         slot = wire.slot()
         small_slots.append(slot)
         wire.start(
             slot,
-            lambda k=k: small.at[(t + k + 1) % extent],
+            lambda k=k: small_send.at[((t + k + 1) % extent) // 2],
             lambda k=k: small_in.at[k],
             peer,
         )
-    for i in turns:
-        sources = slices(flip(d, 1 + 2 * i))
-        c_slots[i] = [wire.slot(), wire.slot()]
-        wire.start(c_slots[i][0], lambda s=sources: s[0], lambda i=i: q_core.at[i], to_c)
-        wire.start(c_slots[i][1], lambda s=sources: s[1], lambda i=i: o_core.at[i], to_c)
-        mine = slices(flip(d, 2 * i))
-        loads[i] = [local.start(mine[0], q_work.at[i]), local.start(mine[1], o_work.at[i])]
-    work_load.wait()
-    line = LineSum(
-        wire, d, t, extent, lambda index: work.at[index], up_in, down_in, rows, 2
-    )
-    line.step(0)
-
-    def cut(ref, which):
-        half = ref.shape[0] // 2
-        return ref.at[pl.ds(which * half, half)]
-
-    a_slots, b_slots = {}, {}
-    routes_a = ((to_x, 3, 2, 0, 0), (to_y, 3, 1, 1, 1), (to_x, 1, 0, 0, 2), (to_y, 2, 0, 1, 3))
-    routes_b = ((to_y, 2, 0, 0), (to_x, 1, 1, 1))
-
-    def core_add(i):
-        for load in loads[i]:
-            load.wait()
-        wire.arrive(c_slots[i][0], lambda: q_core.at[i], to_c)
-        wire.arrive(c_slots[i][1], lambda: o_core.at[i], to_c)
-        add_into(q_work.at[i], q_core.at[i], q_work.shape[1])
-        add_into(o_work.at[i], o_core.at[i], o_work.shape[1])
-
-    def a_send(route):
-        device, source, target, which, row = route
-        a_slots[row] = [wire.slot(), wire.slot()]
-        wire.start(
-            a_slots[row][0], lambda: cut(q_work.at[source], which), lambda: q_a.at[row], device
-        )
-        wire.start(
-            a_slots[row][1], lambda: cut(o_work.at[source], which), lambda: o_a.at[row], device
-        )
-
-    def b_send(route):
-        device, source, which, row = route
-        b_slots[row] = [wire.slot(), wire.slot()]
-        wire.start(
-            b_slots[row][0], lambda: cut(q_work.at[source], which), lambda: q_b.at[row], device
-        )
-        wire.start(
-            b_slots[row][1], lambda: cut(o_work.at[source], which), lambda: o_b.at[row], device
-        )
-
-    core_add(3)
-    a_send(routes_a[0])
-    a_send(routes_a[1])
-    core_add(1)
-    a_send(routes_a[2])
-    core_add(2)
-    a_send(routes_a[3])
-    core_add(0)
-    line.step(1)
-    for device, source, target, which, row in routes_a:
-        wire.arrive(a_slots[row][0], lambda: q_a.at[row], device)
-        wire.arrive(a_slots[row][1], lambda: o_a.at[row], device)
-        add_into(cut(q_work.at[target], which), q_a.at[row], q_a.shape[1])
-        add_into(cut(o_work.at[target], which), o_a.at[row], o_a.shape[1])
-        if row < 2:
-            b_send(routes_b[row])
-    for k, peer in enumerate(line_peers):
+    for device, source, target, which, row_number in routes_a:
+        for name, kept, unused, first, second in tables:
+            wire.arrive(slots[name, "a", row_number], lambda: first.at[row_number], device)
+            add_into(cut(kept.at[target], which), first.at[row_number], first.shape[1])
+        if row_number < 2:
+            to, origin, part, b_row = routes_b[row_number]
+            forward("b", to, origin, part, b_row)
+    result = small_send[t // 2]
+    for k, peer in enumerate(peers):
         wire.arrive(small_slots[k], lambda k=k: small_in.at[k], peer)
-    total = small[t] + small_in[0]
-    for k in range(1, extent - 1):
-        total = total + small_in[k]
-    small_sum[:, 0:16] = total
-    small_sum[:, 16:24] = jnp.broadcast_to(gains[...][None], (8, 8, 128))
+        result = result + small_in[k]
+    small_sum[:, 0:small_rows] = result
+    small_sum[:, small_rows : small_rows + 2 * heads] = jnp.broadcast_to(
+        head_part[...][None], (8, 2 * heads, 128)
+    )
     last_slots = {}
     for bits in range(1, 8):
         last_slots[bits] = wire.slot()
@@ -2270,74 +2255,108 @@
             (flip(d, bits), t),
         )
     line.step(2)
-    for device, source, which, row in routes_b:
-        wire.arrive(b_slots[row][0], lambda: q_b.at[row], device)
-        wire.arrive(b_slots[row][1], lambda: o_b.at[row], device)
-        for kept, came, result in (
-            (cut(q_work.at[0], which), q_b.at[row], cut(qkv_out, which)),
-            (cut(o_work.at[0], which), o_b.at[row], cut(o_out, which)),
-        ):
-
-            def body(start, kept=kept, came=came, result=result):
-                part = pl.ds(start, 16)
-                result[part] = kept[part].astype(F32) + came[part].astype(F32)
-
-            rows_loop(kept.shape[0], 16, body)
+    for device, source, which, row_number in routes_b:
+        for name, kept, unused, first, second in tables:
+            came = second.at[row_number]
+            wire.arrive(slots[name, "b", row_number], lambda: came, device)
+            base = which * (kept.shape[1] // 2)
+
+            def body(start, kept=kept, came=came, base=base, name=name):
+                here = pl.ds(start, 16)
+                there = pl.ds(pl.multiple_of(base + start, 16), 16)
+                value = kept[0, there].astype(F32) + came[here].astype(F32)
+                if name == "o":
+                    o_out[there] = value
+                else:
+                    for n, target in enumerate((q_out, k_out, v_out)):
+                        target[there] = value[:, n * columns : (n + 1) * columns]
+
+            rows_loop(kept.shape[1] // 2, 16, body)
     line.last()
     mine = work.at[t]
 
-    def body(start):
+    def finish(start):
         part = pl.ds(start, 16)
         grad_in[part] = grad_middle[part] + own_sum(
             mine, up_in.at[extent - 2], down_in.at[extent - 2], part, pl.ds(0, width)
         )
 
-    rows_loop(rows, 16, body)
+    rows_loop(rows, 16, finish)
     total = small_sum[d]
     for bits in range(1, 8):
         wire.arrive(
             last_slots[bits], lambda bits=bits: small_last.at[bits], (flip(d, bits), t)
         )
         total = total + small_last[bits]
-    small_out[...] = total
+    share = pltpu.roll(total, (128 - 64 * (t % 2)) % 128, 1)
+    square = jnp.concatenate([share, jnp.zeros((128 - share.shape[0], 128), F32)], axis=0).T
+    router_out[...] = square[0 : router_out.shape[0], 0:16]
+    vectors_out[...] = share[16:24]
+    head_width = q_gain_out.shape[1]
+    gains = pltpu.roll(total, (128 - head_width * d) % 128, 1)
+    q_gain_out[...] = gains[small_rows : small_rows + heads, 0:head_width]
+    k_gain_out[...] = gains[small_rows + heads : small_rows + 2 * heads, 0:head_width]
     wire.finish()
 
 
-def close(extent, partial, grad_middle, grad_qkv, grad_o, small, gains):
-    rows, width = grad_middle.shape
-    depth, q_width = grad_qkv.shape[0] // 8, grad_qkv.shape[1]
-    o_rows, o_width = grad_o.shape[0], grad_o.shape[1] // 8
+def back(extent, *operands):
+    seq_len, width = operands[0].shape
+    rows = seq_len // extent
+    head_gain, small = operands[6], operands[15]
+    heads = head_gain.shape[0] // 2
+    columns = heads * HD
+    depth, o_width = width // 8, width // 8
+    split = rows // 2
+    shape = jax.ShapeDtypeStruct
     scratch = [
+        pltpu.VMEM((seq_len, columns), BF),
+        pltpu.VMEM((seq_len, 2 * columns), F32),
+        pltpu.VMEM((seq_len, 3 * columns), BF),
+        pltpu.VMEM((seq_len, 128), F32),
+        pltpu.VMEM((seq_len, 128), F32),
+        pltpu.VMEM((8, seq_len), F32),
+        pltpu.VMEM((extent - 1, 8, seq_len), F32),
+        pltpu.VMEM((8, width), F32),
+        pltpu.VMEM((2 * heads, HD), F32),
         pltpu.VMEM((extent, rows, width), BF),
         pltpu.VMEM((extent - 1, rows, width), BF),
         pltpu.VMEM((extent - 1, rows, width), BF),
     ]
-    for tall, wide in ((depth, q_width), (o_rows, o_width)):
+    for tall, wide in ((depth, 3 * columns), (columns, o_width)):
         scratch += [
+            pltpu.VMEM((4, tall, wide), BF),
             pltpu.VMEM((4, tall, wide), BF),
             pltpu.VMEM((4, tall, wide), BF),
             pltpu.VMEM((4, tall // 2, wide), BF),
             pltpu.VMEM((2, tall // 2, wide), BF),
         ]
+    packed = small.shape[0] + 2 * heads
     scratch += [
-        pltpu.VMEM((extent - 1, 8, 16, 128), F32),
-        pltpu.VMEM((8, 24, 128), F32),
-        pltpu.VMEM((8, 24, 128), F32),
+        pltpu.VMEM((2, 8, small.shape[0], 128), F32),
+        pltpu.VMEM((extent - 1, 8, small.shape[0], 128), F32),
+        pltpu.VMEM((8, packed, 128), F32),
+        pltpu.VMEM((8, packed, 128), F32),
     ]
     return pl.pallas_call(
-        functools.partial(close_kernel, extent),
+        functools.partial(back_kernel, extent),
         out_shape=[
-            jax.ShapeDtypeStruct((rows, width), F32),
-            jax.ShapeDtypeStruct((depth, q_width), F32),
-            jax.ShapeDtypeStruct((o_rows, o_width), F32),
-            jax.ShapeDtypeStruct((24, 128), F32),
+            shape((rows, width), F32),
+            shape((depth, columns), F32),
+            shape((depth, columns), F32),
+            shape((depth, columns), F32),
+            shape((columns, o_width), F32),
+            shape((width // (8 * extent), 16), F32),
+            shape((8, 128), F32),
+            shape((heads, HD // 8), F32),
+            shape((heads, HD // 8), F32),
+            shape((8, 128), F32),
         ],
-        in_specs=[ANY, VM, ANY, ANY, VM, VM],
-        out_specs=[VM] * 4,
-        scratch_shapes=scratch + dma_pair(64) + [pltpu.SemaphoreType.DMA((16,))],
-        compiler_params=kernel_params(7),
-        cost_estimate=pl.CostEstimate(flops=0, bytes_accessed=150_000_000, transcendentals=0),
-    )(partial, grad_middle, grad_qkv, grad_o, small, gains)
+        in_specs=[VM] * len(operands),
+        out_specs=[VM] * 10,
+        scratch_shapes=scratch + dma_pair(80),
+        compiler_params=kernel_params(6),
+        cost_estimate=pl.CostEstimate(flops=0, bytes_accessed=1_000_000, transcendentals=0),
+    )(*operands)
 
 
 def spread_kernel(*refs):
@@ -2393,36 +2412,13 @@
     rows, width = hidden_in.shape
     seq_len = rows * extent
     all_tokens = seq_len * dp_count
-    length = lengths[d]
-    total_count = jnp.sum(lengths).astype(F32)
-    attn_gain = attn_norm_gain.astype(F32)
-    ffn_gain = ffn_norm_gain.astype(F32)[None, :]
-    expert_count = router_weight.shape[1]
-    head_width = q_gain.shape[1]
-    local_heads = q_gain.shape[0]
-    columns = local_heads * HD
-
-    gains_own = lax.dynamic_update_slice(
-        jnp.zeros((2 * local_heads, HD), F32),
-        jnp.concatenate([q_gain, k_gain], axis=0).astype(F32),
-        (0, d * head_width),
-    )
-    lane = jnp.arange(128)
-    lane_expert = jnp.where(lane < 2 * expert_count, lane % expert_count, -1)
-    routes_own = lax.dynamic_slice_in_dim(routes, t * rows, rows, 0)
-    chosen = jnp.any(routes_own[:, :, None] == lane_expert[None, None, :], axis=1).astype(F32)
-    blank = jnp.zeros((width, 128 - 2 * expert_count), BF)
-    router_wide = jnp.concatenate([router_weight, router_weight, blank], axis=1)
-    router_t = jnp.concatenate(
-        [router_weight.T, jnp.zeros((128 - expert_count, width), BF)], axis=0
-    )
     angles = np.arange(seq_len)[:, None] * THETA ** (-np.arange(HD // 2) / (HD // 2))[None, :]
     cosine = jnp.asarray(np.concatenate([np.cos(angles)] * 2, axis=1), F32)
     sine = jnp.asarray(np.concatenate([-np.sin(angles), np.sin(angles)], axis=1), F32)
     (
+        chosen,
         middle,
         gates,
-        ffn_own,
         head_gain,
         inverses,
         hidden_bf,
@@ -2439,32 +2435,30 @@
         landed,
     ) = front(
         extent,
-        length[None],
+        lengths,
         hidden_in,
         q_weight,
         k_weight,
         v_weight,
         o_weight,
-        gains_own,
+        q_gain,
+        k_gain,
         gate_weight,
         up_weight,
         down_weight,
-        attn_gain[None, :],
+        attn_norm_gain[None, :],
         cosine,
         sine,
-        ffn_gain,
-        router_wide,
-        chosen,
-    )
-    attn_operands = (hidden_bf, attn_gain[None, :], qkv_full, o_full, head_gain, cosine, sine)
-    own_positions = t * rows + jnp.arange(rows)
-    row_scale = jnp.where(own_positions < length, all_tokens / total_count, 0.0)
+        ffn_norm_gain[None, :],
+        router_weight.T,
+        routes,
+    )
     grad_output, row_loss, ffn_grad_partial, inner, active, grads = turn(
         extent,
+        lengths,
         expert_partial,
         middle,
         teacher,
-        jnp.broadcast_to(row_scale[:, None], (rows, 128)),
         tokens,
         hidden,
         landed,
@@ -2472,80 +2466,63 @@
         up_weight,
         down_weight,
     )
-    grad_middle, grad_logits, ffn_gain_part, attn_grad_rows, *came = leave(
+    grad_middle, small, attn_grad_rows, *came = leave(
         extent,
         ffn_grad_partial,
         middle,
         grad_output,
         gates,
         chosen,
-        ffn_gain,
-        router_t,
+        ffn_norm_gain[None, :],
+        router_weight.T,
         (tokens, grads, inner, active),
     )
     expert_grads = came[:6] + [exchange(came[bits], bits) for bits in (6, 7)]
-    attn_grad_rows = attn_grad_rows.reshape(seq_len, width)
-    router_part = jnp.einsum(
-        "sd,se->de",
-        ffn_own,
-        grad_logits[:, :expert_count],
-        precision=HIGHEST,
-        preferred_element_type=F32,
-    )
-    input_part, grad_qkv, grad_o, attn_gain_part, gains_part, loss_rows = attend_back(
+    (
+        grad_in,
+        grad_q,
+        grad_k,
+        grad_v,
+        grad_o,
+        grad_router,
+        vectors,
+        grad_q_gain,
+        grad_k_gain,
+        loss,
+    ) = back(
         extent,
-        attn_grad_rows,
+        attn_grad_rows.reshape(seq_len, width),
         row_loss,
-        *attn_operands,
+        hidden_bf,
+        attn_norm_gain[None, :],
+        qkv_full,
+        o_full,
+        head_gain,
+        cosine,
+        sine,
         normed,
         units,
         low,
         probs,
         mixed,
         inverses,
-    )
-    loss_group = loss_rows[2, :1] / (2.0 * width * all_tokens)
-    attn_gain_part = jnp.sum(attn_gain_part, axis=0)
-
-    split = width // (dp_count * extent)
-    small = jnp.concatenate(
-        [
-            jnp.concatenate(
-                [
-                    attn_gain_part.reshape(dp_count, extent, 1, split),
-                    jnp.sum(ffn_gain_part, axis=0).reshape(dp_count, extent, 1, split),
-                ],
-                axis=3,
-            ),
-            router_part.reshape(dp_count, extent, split * expert_count // 128, 128),
-            jnp.zeros((dp_count, extent, 15 - split * expert_count // 128, 128), F32),
-        ],
-        axis=2,
-    ).transpose(1, 0, 2, 3)
-    grad_in, qkv_out, o_out, small_out = close(
-        extent,
-        input_part.reshape(extent, rows, width),
+        small,
         grad_middle,
-        grad_qkv,
+    )
+    grad_gate, grad_up, grad_down = spread(expert_grads)
+    split = grad_router.shape[0]
+    return (
+        loss[2, :1],
+        grad_in,
+        vectors[0, :split],
+        vectors[1, :split],
+        grad_q,
+        grad_k,
+        grad_v,
+        grad_q_gain,
+        grad_k_gain,
         grad_o,
-        small,
-        gains_part,
-    )
-    grad_gate, grad_up, grad_down = spread(expert_grads)
-    router_out = small_out[1 : 1 + split * expert_count // 128].reshape(split, expert_count)
-    gain_out = lax.dynamic_slice(small_out, (16, d * head_width), (2 * local_heads, head_width))
-    return (
-        loss_group,
-        grad_in,
-        small_out[0, :split],
-        small_out[0, split : 2 * split],
-        qkv_out[:, :columns],
-        qkv_out[:, columns : 2 * columns],
-        qkv_out[:, 2 * columns :],
-        gain_out[:local_heads],
-        gain_out[local_heads:],
-        o_out,
-        router_out,
+        grad_router,
         grad_gate,
         grad_up,
         grad_down,

time: 599 us -> 581 us (0.970); the launches traced: 597 us -> 571 us
  Pallas kernels: 563 us -> 552 us
  other arithmetic: 8.96 us -> 0 us
    pallas_call x2 -> x1, Pallas kernels: 88.9 us -> 79.1 us  [back(): pl.pallas_call(functools.partial(back_kernel, extent), out_shape=[shape((...]
  transfers between devices with their start and end apart: 2 -> 2, of which waited for: 0 -> 0; matrix products, arithmetic and copies ran while one was open for 2% -> 1% of each run, Pallas kernels for 15% -> 14%
where the time goes in v5:
time: 581 us; the launch traced here: 571 us
  Pallas kernels  552 us (95%)
  local copies, waits for them, and re-layouts  16.5 us (3%)
    pallas_call x1, Pallas kernels, front(): pl.pallas_call(functools.partial(front_kernel, extent), out_shape=[shape(...  187 us
    pallas_call x1, Pallas kernels, turn(): pl.pallas_call(functools.partial(turn_kernel, extent), out_shape=[jax.Sha...  160 us
    pallas_call x1, Pallas kernels, leave(): pl.pallas_call(functools.partial(leave_kernel, extent), out_shape=[jax.Sh...  118 us
    pallas_call x1, Pallas kernels, back(): pl.pallas_call(functools.partial(back_kernel, extent), out_shape=[shape((...  79.1 us
  transfers between devices with their start and end apart: 2, of which 0 were waited for; matrix products, arithmetic and copies ran while one was open for 1% of the time, Pallas kernels for 14%

profile of v5, /device:TPU:0, one launch (start us, length us, event | category | flops | bytes accessed | tf_op | source)
XLA Modules:
  0.0 571.2 jit_solution(17940839453513221106)
XLA Ops:
  0.6 1.3 broadcast_in_dim.8.attn_gain.gain
  1.9 1.3 broadcast_in_dim.9.ffn_gain.gain
  3.2 1.6 copy.32.routes
  4.8 186.9 %shard_map.281 = (f32[128,128]{1,0:T(8,128)}, f32[128,2048]{1,0:T(8,128)}, f32[128,128]{1,0:T(8,128)}, f32[8,128]{1,0:T(8,128)}, f32[512,128]{1,0:T(8,128)}, /*i...) custom-call(s32[8]{0:T(128)} %lengths.3, ...), custom_call_target="tpu_custom_call" | custom-call | bytes 300000000 | tf_op jit(solution)/shard_map/pallas_call | solution.py:1552
  191.7 159.8 %shard_map.282 = (f32[128,2048]{1,0:T(8,128)}, f32[128,128]{1,0:T(8,128)}, bf16[4,2,4,128,2176]{4,3,2,1,0:T(8,128)(2,1)}, bf16[4,2,512,1024]{3,2,1,0:T(8,128)(2,...) custom-call(s32[8]{0:T(128)} %lengths.3, ...), custom_call_target="tpu_custom_call" | custom-call | bytes 450000000 | tf_op jit(solution)/shard_map/pallas_call | solution.py:1791
  351.5 117.9 %shard_map.283 = (f32[128,2048]{1,0:T(8,128)}, f32[24,2048]{1,0:T(8,128)}, bf16[4,128,2048]{2,1,0:T(8,128)(2,1)}, bf16[3,2,256,256]{3,2,1,0:T(8,128)(2,1)}, bf16...) custom-call(bf16[4,2,4,128,2176]{4,3,2,1,0:T(8,128)(2,1)} %get-tuple, ...), custom_call_target="tpu_custom_call" | custom-call | bytes 350000000 | tf_op jit(solution)/shard_map/pallas_call | solution.py:1985
  469.4 1.5 collective-permute-start
  470.9 0.0 collective-permute-start.1
  470.9 79.1 %shard_map.284 = (f32[128,2048]{1,0:T(8,128)}, f32[256,512]{1,0:T(8,128)}, f32[256,512]{1,0:T(8,128)}, f32[256,512]{1,0:T(8,128)}, f32[512,256]{1,0:T(8,128)}, /...) custom-call(bf16[512,2048]{1,0:T(8,128)(2,1)} %bitcast.7, ...), custom_call_target="tpu_custom_call" | custom-call | bytes 1000000 | tf_op jit(solution)/shard_map/pallas_call | solution.py:2340
  550.1 1.3 slice.9
  551.4 1.4 copy.33
  552.8 1.3 slice_bitcast_fusion
  554.1 0.0 collective-permute-done.refs_6_
  554.1 0.0 collective-permute-done.1.refs_7_
  554.1 0.9 copy-done.1
  555.0 8.3 %shard_map.285 = (f32[16,256,256]{2,1,0:T(8,128)}, f32[16,256,256]{2,1,0:T(8,128)}, f32[16,256,256]{2,1,0:T(8,128)}) custom-call(bf16[3,2,256,256]{3,2,1,0:T(8,128)(2,1)} %get-tuple-element.97.refs_0_, bf16[3,2,256,256]{3,2,1,0:T(8,128)(2,1)} %get-tuple-element.98.refs_1_, bf16[3,2,256,256]{3,2,1,0:T(8,128)(2,1)} %get-tuple-element.99.refs_2_, ...), custom_call_target="tpu_custom_call" | custom-call | bytes 20000000 | tf_op jit(solution)/shard_map/pallas_call | solution.py:2374
  563.3 0.0 copy-start.2
  563.3 1.0 copy.41
  564.3 1.9 copy.42
  566.2 1.9 copy.43
  568.0 0.8 copy.44
  568.8 0.6 copy.45
  569.4 0.6 copy.46
  570.0 0.8 copy.47
  (10 shorter events, 0.0 us)
Async XLA Ops:
  469.4 84.7 %collective-permute-start = (bf16[3,2,256,256]{3,2,1,0:T(8,128)(2,1)}, bf16[3,2,256,256]{3,2,1,0:T(8,128)(2,1)S(1)}, u32[]{:S(2)}, u32[]{:S(2)}) collective-permute-start(bf16[3,2,256,256]{3,2,1,0:T(8,128)(2,1)} %get-tuple-element.103), channel_id=1, source_target_pairs={{0,24},{4,28},{8,16},{12,20},{16,8},{20,12},{24,0},{28,4},{1,25},{... | collective-permute-start | bytes 2359304 | tf_op jit(solution)/shard_map/ppermute | solution.py:2387
  470.9 83.1 %collective-permute-start.1 = (bf16[3,2,256,256]{3,2,1,0:T(8,128)(2,1)}, bf16[3,2,256,256]{3,2,1,0:T(8,128)(2,1)}, u32[]{:S(2)}, u32[]{:S(2)}) collective-permute-start(bf16[3,2,256,256]{3,2,1,0:T(8,128)(2,1)} %get-tuple-element.104), channel_id=1, source_target_pairs={{0,28},{4,24},{8,20},{12,16},{16,12},{20,8},{24,4},{28,0},{1,29},{... | collective-permute-start | bytes 2359304 | tf_op jit(solution)/shard_map/ppermute | solution.py:2387
  550.1 13.2 %copy-start = (f32[128,2048]{1,0:T(8,128)S(1)}, f32[128,2048]{1,0:T(8,128)}, u32[]{:S(2)}) copy-start(f32[128,2048]{1,0:T(8,128)} %get-tuple-element.139) | copy-start | bytes 3145732
  554.1 0.9 copy-start.1
  563.3 4.7 copy-start.3
  563.3 5.5 copy-start.5
  563.3 6.1 %copy-start.4 = (f32[4,16]{1,0:T(4,128)S(1)}, f32[4,16]{1,0:T(4,128)}, u32[]{:S(2)}) copy-start(f32[4,16]{1,0:T(4,128)} %get-tuple-element.146) | copy-start | bytes 772
  563.3 6.7 %copy-start.2 = (f32[512,256]{1,0:T(8,128)S(1)}, f32[512,256]{1,0:T(8,128)}, u32[]{:S(2)}) copy-start(f32[512,256]{1,0:T(8,128)} %get-tuple-element.147) | copy-start | bytes 1572868

commit v6 on v5

--- a/solution.py
+++ b/solution.py
@@ -1260,13 +1260,13 @@
     router_rows[...] = jnp.zeros(router_rows.shape, BF)
     router_rows[0:16] = router[...]
     router_rows[16:32] = router[...]
-    lane = lax.broadcasted_iota(jnp.int32, (rows, 128), 1)
-    own_routes = routes[pl.ds(pl.multiple_of(t * rows, rows), rows)]
-    picked = jnp.zeros((rows, 128), F32)
-    for k in range(own_routes.shape[1]):
-        match = both(own_routes[:, k : k + 1] == lane % 16, lane < 32)
+    own_routes = routes[:, pl.ds(pl.multiple_of(t * rows, rows), rows)]
+    expert = lax.broadcasted_iota(jnp.int32, (128, rows), 0)
+    picked = jnp.zeros((128, rows), F32)
+    for k in range(own_routes.shape[0]):
+        match = both(own_routes[k : k + 1] == expert % 16, expert < 32)
         picked = jnp.where(match, 1.0, picked)
-    chosen[...] = picked
+    chosen[...] = picked.T
     greet(line_peers(d, t, extent) + [(None, (flip(d, bits), t)) for bits in range(1, 8)])
     for copy in copies:
         copy.wait()
@@ -1369,58 +1369,59 @@
     inverses[...] = rows_to_columns(lax.rsqrt(total / width + EPSILON))
     low[:, 2 * columns :] = raw[:, 2 * columns :].astype(BF)
 
-    def probs_copy(h):
-        return pltpu.make_async_copy(probs.at[h % 2], probs_out.at[h], probs_sem.at[h % 2])
-
-    def head(h, carry):
+    def turn_head(h, carry):
         for n in range(2):
             section = pl.ds(pl.multiple_of(n * columns + h * HD, HD), HD)
             unit = raw[:, section] * inverses[:, n : n + 1]
             raw[:, section] = unit
             scaled = unit * head_gain[pl.ds(n * heads + h, 1)]
             low[:, section] = turned(scaled, cosine[...], sine[...], 1.0).astype(BF)
-        section = pl.ds(pl.multiple_of(h * HD, HD), HD)
-        key_section = pl.ds(pl.multiple_of(columns + h * HD, HD), HD)
-        value_section = pl.ds(pl.multiple_of(2 * columns + h * HD, HD), HD)
-
-        @pl.when(h >= 2)
-        def _():
-            probs_copy(h).wait()
-
-        def some(start):
-            part = pl.ds(start, tile)
+        return carry
+
+    lax.fori_loop(0, heads, turn_head, 0)
+    kept += [local.start(raw, raw_out), local.start(low, low_out)]
+    total_line = LineSum(
+        wire, d, t, extent, lambda index: work.at[index], up_in, down_in, rows, 2
+    )
+    order = plane_order(t)
+
+    def probs_copy(k):
+        part = pl.ds(pl.multiple_of(order[k] * rows, rows), rows)
+        return pltpu.make_async_copy(
+            probs.at[k % 2], probs_out.at[pl.ds(0, heads), part], probs_sem.at[k % 2]
+        )
+
+    for k in range(extent):
+        begin = pl.multiple_of(order[k] * rows, rows)
+        part = pl.ds(begin, rows)
+        if k >= 2:
+            probs_copy(k - 2).wait()
+
+        def head(h, carry, begin=begin, part=part, k=k):
+            section = pl.ds(pl.multiple_of(h * HD, HD), HD)
+            key_section = pl.ds(pl.multiple_of(columns + h * HD, HD), HD)
+            value_section = pl.ds(pl.multiple_of(2 * columns + h * HD, HD), HD)
             scores = dot_transposed(low[part, section], low[:, key_section]) / math.sqrt(HD)
-            row = start + lax.broadcasted_iota(jnp.int32, scores.shape, 0)
+            row = begin + lax.broadcasted_iota(jnp.int32, scores.shape, 0)
             column = lax.broadcasted_iota(jnp.int32, scores.shape, 1)
             allowed = both(column <= row, column < length)
             scores = jnp.where(allowed, scores, -1e30)
             powers = jnp.exp(scores - jnp.max(scores, axis=-1, keepdims=True))
             result = powers / jnp.sum(powers, axis=-1, keepdims=True)
-            probs[h % 2, part] = result
+            probs[k % 2, h] = result
             mixed[part, section] = jnp.dot(
                 result.astype(BF), low[:, value_section], preferred_element_type=F32
             ).astype(BF)
-
-        rows_loop(seq_len, tile, some)
-        probs_copy(h).start()
-        return carry
-
-    lax.fori_loop(0, heads, head, 0)
-    kept += [local.start(raw, raw_out), local.start(low, low_out), local.start(mixed, mixed_out)]
-
-    def join(first, carry):
-        result = jnp.dot(
-            mixed[pl.ds(first * 2 * rows, 2 * rows)], o_all[...], preferred_element_type=F32
-        )
-        work[pl.ds(2 * first, 2)] = result.astype(BF).reshape(2, rows, width)
-        return carry
-
-    lax.fori_loop(0, extent // 2, join, 0)
-    total_line = LineSum(
-        wire, d, t, extent, lambda index: work.at[index], up_in, down_in, rows, 2
-    )
-    for step in range(extent - 1):
-        total_line.step(step)
+            return carry
+
+        lax.fori_loop(0, heads, head, 0)
+        probs_copy(k).start()
+        work[order[k]] = jnp.dot(
+            mixed[part], o_all[...], preferred_element_type=F32
+        ).astype(BF)
+        if k != 1:
+            total_line.step(max(k - 1, 0))
+    kept.append(local.start(mixed, mixed_out))
     total_line.last()
     mine = work.at[t]
     everything = pl.ds(0, width)
@@ -1522,8 +1523,8 @@
             tokens.at[arrival(t, g // 2), g % 2],
             token_sem.at[g],
         ).wait()
-    for h in range(heads - 2, heads):
-        probs_copy(h).wait()
+    for k in range(extent - 2, extent):
+        probs_copy(k).wait()
     for copy in kept:
         copy.wait()
     wire.finish()
@@ -1576,7 +1577,7 @@
             pltpu.VMEM((seq_len, width), BF),
             pltpu.VMEM((seq_len, 3 * columns), F32),
             pltpu.VMEM((seq_len, 3 * columns), BF),
-            pltpu.VMEM((2, seq_len, seq_len), F32),
+            pltpu.VMEM((2, heads, rows, seq_len), F32),
             pltpu.VMEM((seq_len, columns), BF),
             pltpu.VMEM((seq_len, 128), F32),
             pltpu.VMEM((8, seq_len), F32),
@@ -2014,21 +2015,21 @@
     extent,
     grads,
     row_loss,
-    hid,
+    hid_far,
     gain,
-    qkv_weight,
+    qkv_far,
     o_weight,
     head_gain,
     cosine,
     sine,
-    normed,
-    units,
-    low,
-    probs,
+    normed_far,
+    units_far,
+    low_far,
+    probs_far,
     mixed,
     inverses,
     small,
-    grad_middle,
+    middle_far,
     grad_in,
     q_out,
     k_out,
@@ -2039,6 +2040,14 @@
     q_gain_out,
     k_gain_out,
     loss,
+    low,
+    probs,
+    units,
+    qkv_weight,
+    normed,
+    hid,
+    grad_middle,
+    load_sem,
     grad_mixed,
     scaled,
     raw_grad,
@@ -2076,7 +2085,19 @@
     depth, o_width = q_out.shape[0], o_out.shape[1]
     peers = [(d, (t + k) % extent) for k in range(1, extent)]
     greet(line_peers(d, t, extent) + [(None, (flip(d, bits), t)) for bits in range(1, 8)])
-    wire = Wire(send_sem, recv_sem)
+    wire, local = Wire(send_sem, recv_sem), Local(load_sem)
+    loads = [
+        local.start(source, target)
+        for source, target in (
+            (low_far, low),
+            (probs_far, probs),
+            (units_far.at[pl.ds(0, seq_len), pl.ds(0, 2 * columns)], units),
+            (normed_far, normed),
+            (qkv_far, qkv_weight),
+            (hid_far, hid),
+            (middle_far, grad_middle),
+        )
+    ]
     to_x, to_y, to_c = (flip(d, 2), t), (flip(d, 4), t), (flip(d, 1), t)
     tile = 256
     root = math.sqrt(HD)
@@ -2100,6 +2121,8 @@
     for i in turns:
         o_slice(2 * i, o_work.at[i])
     sums[...] = jnp.zeros(sums.shape, F32)
+    for load in loads:
+        load.wait()
 
     def head(h, carry):
         section = pl.ds(pl.multiple_of(h * HD, HD), HD)
@@ -2309,6 +2332,14 @@
     split = rows // 2
     shape = jax.ShapeDtypeStruct
     scratch = [
+        pltpu.VMEM((seq_len, 3 * columns), BF),
+        pltpu.VMEM((heads, seq_len, seq_len), F32),
+        pltpu.VMEM((seq_len, 2 * columns), F32),
+        pltpu.VMEM((width, 3 * columns), BF),
+        pltpu.VMEM((seq_len, width), BF),
+        pltpu.VMEM((seq_len, width), BF),
+        pltpu.VMEM((rows, width), F32),
+        pltpu.SemaphoreType.DMA((8,)),
         pltpu.VMEM((seq_len, columns), BF),
         pltpu.VMEM((seq_len, 2 * columns), F32),
         pltpu.VMEM((seq_len, 3 * columns), BF),
@@ -2351,7 +2382,7 @@
             shape((heads, HD // 8), F32),
             shape((8, 128), F32),
         ],
-        in_specs=[VM] * len(operands),
+        in_specs=[ANY if n in (2, 4, 9, 10, 11, 12, 16) else VM for n in range(17)],
         out_specs=[VM] * 10,
         scratch_shapes=scratch + dma_pair(80),
         compiler_params=kernel_params(6),
@@ -2360,25 +2391,97 @@
 
 
 def spread_kernel(*refs):
-    pieces, outs = refs[:8], refs[8:]
+    pieces, large, (vectors, q_gain, k_gain, loss, router) = refs[:8], refs[8:13], refs[13:18]
+    tables, large_out = refs[18:21], refs[21:26]
+    loss_out, attn_out, ffn_out, q_gain_out, k_gain_out, router_out = refs[26:32]
+    near, stage, *copies, in_sem, out_sem, large_sem = refs[32:]
     d = lax.axis_index("dp")
+    slab = near.shape[3]
+    moves = []
+    for n, (source, middle, target) in enumerate(zip(large, copies, large_out)):
+        moves.append(
+            (
+                pltpu.make_async_copy(source, middle, large_sem.at[0, n]),
+                pltpu.make_async_copy(middle, target, large_sem.at[1, n]),
+            )
+        )
+    loads = [
+        pltpu.make_async_copy(pieces[bits], near.at[bits], in_sem.at[bits]) for bits in range(8)
+    ]
+    for bits in range(4):
+        loads[bits].start()
+    for first, second in moves:
+        first.start()
+    for bits in range(4, 8):
+        loads[bits].start()
+    loss_out[...] = loss[2:3, 0:1]
+    attn_out[...] = vectors[0:1, 0 : attn_out.shape[1]]
+    ffn_out[...] = vectors[1:2, 0 : ffn_out.shape[1]]
+    q_gain_out[...] = q_gain[...]
+    k_gain_out[...] = k_gain[...]
+    router_out[...] = router[...]
+    stores = []
     for bits in range(8):
-        first = 2 * flip(d, bits)
+        loads[bits].wait()
+        begin = 2 * flip(d, bits)
         for place in range(3):
             for e in range(2):
-                outs[place][first + e] = pieces[bits][place, e].astype(F32)
-
-
-def spread(pieces):
-    shape = (16,) + pieces[0].shape[2:]
+
+                def body(start, bits=bits, place=place, e=e, begin=begin):
+                    part = pl.ds(start, 64)
+                    stage[place, begin + e, part] = near[bits, place, e, part].astype(F32)
+
+                rows_loop(slab, 64, body)
+            store = pltpu.make_async_copy(
+                stage.at[place, pl.ds(begin, 2)],
+                tables[place].at[pl.ds(begin, 2)],
+                out_sem.at[bits, place],
+            )
+            store.start()
+            stores.append(store)
+        if bits == 3:
+            for first, second in moves:
+                first.wait()
+                second.start()
+    for first, second in moves:
+        second.wait()
+    for store in stores:
+        store.wait()
+
+
+def spread(pieces, large, small):
+    table = jax.ShapeDtypeStruct((16,) + pieces[0].shape[2:], F32)
+    vectors, q_gain, k_gain, loss, router = small
+    shape = jax.ShapeDtypeStruct
+    split = router.shape[0]
+    same = lambda array: shape(array.shape, array.dtype)
     return pl.pallas_call(
         spread_kernel,
-        out_shape=[jax.ShapeDtypeStruct(shape, F32)] * 3,
-        in_specs=[VM] * 8,
-        out_specs=[VM] * 3,
+        out_shape=[table] * 3
+        + [same(array) for array in large]
+        + [
+            shape((1, 1), F32),
+            shape((1, split), F32),
+            shape((1, split), F32),
+            same(q_gain),
+            same(k_gain),
+            same(router),
+        ],
+        in_specs=[ANY] * 13 + [VM] * 5,
+        out_specs=[ANY] * 8 + [VM] * 6,
+        scratch_shapes=[
+            pltpu.VMEM((8,) + pieces[0].shape, BF),
+            pltpu.VMEM((3,) + table.shape, F32),
+        ]
+        + [pltpu.VMEM(array.shape, F32) for array in large]
+        + [
+            pltpu.SemaphoreType.DMA((8,)),
+            pltpu.SemaphoreType.DMA((8, 3)),
+            pltpu.SemaphoreType.DMA((2, 5)),
+        ],
         compiler_params=pltpu.CompilerParams(vmem_limit_bytes=VMEM_LIMIT),
         cost_estimate=pl.CostEstimate(flops=0, bytes_accessed=20_000_000, transcendentals=0),
-    )(*pieces)
+    )(*pieces, *large, *small)
 
 
 def exchange(value, bits):
@@ -2405,13 +2508,9 @@
     up_weight,
     down_weight,
 ):
-    dp_count = lax.axis_size("dp")
     extent = lax.axis_size("tensor")
-    d = lax.axis_index("dp")
-    t = lax.axis_index("tensor")
     rows, width = hidden_in.shape
     seq_len = rows * extent
-    all_tokens = seq_len * dp_count
     angles = np.arange(seq_len)[:, None] * THETA ** (-np.arange(HD // 2) / (HD // 2))[None, :]
     cosine = jnp.asarray(np.concatenate([np.cos(angles)] * 2, axis=1), F32)
     sine = jnp.asarray(np.concatenate([-np.sin(angles), np.sin(angles)], axis=1), F32)
@@ -2451,7 +2550,7 @@
         sine,
         ffn_norm_gain[None, :],
         router_weight.T,
-        routes,
+        routes.T,
     )
     grad_output, row_loss, ffn_grad_partial, inner, active, grads = turn(
         extent,
@@ -2509,13 +2608,31 @@
         small,
         grad_middle,
     )
-    grad_gate, grad_up, grad_down = spread(expert_grads)
-    split = grad_router.shape[0]
+    (
+        grad_gate,
+        grad_up,
+        grad_down,
+        grad_in,
+        grad_q,
+        grad_k,
+        grad_v,
+        grad_o,
+        loss,
+        attn_part,
+        ffn_part,
+        grad_q_gain,
+        grad_k_gain,
+        grad_router,
+    ) = spread(
+        expert_grads,
+        (grad_in, grad_q, grad_k, grad_v, grad_o),
+        (vectors, grad_q_gain, grad_k_gain, loss, grad_router),
+    )
     return (
-        loss[2, :1],
+        loss[0],
         grad_in,
-        vectors[0, :split],
-        vectors[1, :split],
+        attn_part[0],
+        ffn_part[0],
         grad_q,
         grad_k,
         grad_v,

time: 581 us -> 568 us (0.978)
  local copies, waits for them, and re-layouts: 16.5 us -> 5.12 us
    unnamed x21 -> x5, local copies, waits for them, and re-layouts: 11.3 us -> 2.54 us
  transfers between devices with their start and end apart: 2 -> 2, of which waited for: 0 -> 0; matrix products, arithmetic and copies ran while one was open for 1% -> 0% of each run, Pallas kernels for 14% -> 14%
where the time goes in v6:
time: 568 us; the launch traced here: 560 us
  Pallas kernels  552 us (97%)
    pallas_call x1, Pallas kernels, front(): pl.pallas_call(functools.partial(front_kernel, extent), out_shape=[shape(...  187 us
    pallas_call x1, Pallas kernels, turn(): pl.pallas_call(functools.partial(turn_kernel, extent), out_shape=[jax.Sha...  160 us
    pallas_call x1, Pallas kernels, leave(): pl.pallas_call(functools.partial(leave_kernel, extent), out_shape=[jax.Sh...  118 us
    pallas_call x1, Pallas kernels, back(): pl.pallas_call(functools.partial(back_kernel, extent), out_shape=[shape((...  76.6 us
  transfers between devices with their start and end apart: 2, of which 0 were waited for; matrix products, arithmetic and copies ran while one was open for 0% of the time, Pallas kernels for 14%

profile of v6, /device:TPU:0, one launch (start us, length us, event | category | flops | bytes accessed | tf_op | source)
XLA Modules:
  0.0 559.5 jit_solution(13185102026167722769)
XLA Ops:
  0.6 1.3 broadcast_in_dim.8.attn_gain.gain
  1.9 1.3 broadcast_in_dim.9.ffn_gain.gain
  3.2 186.7 %shard_map.281 = (f32[128,128]{1,0:T(8,128)}, f32[128,2048]{1,0:T(8,128)}, f32[128,128]{1,0:T(8,128)}, f32[8,128]{1,0:T(8,128)}, f32[512,128]{1,0:T(8,128)}, /*i...) custom-call(s32[8]{0:T(128)} %lengths.3, ...), custom_call_target="tpu_custom_call" | custom-call | bytes 300000000 | tf_op jit(solution)/shard_map/pallas_call | solution.py:1553
  190.0 159.6 %shard_map.282 = (f32[128,2048]{1,0:T(8,128)}, f32[128,128]{1,0:T(8,128)}, bf16[4,2,4,128,2176]{4,3,2,1,0:T(8,128)(2,1)}, bf16[4,2,512,1024]{3,2,1,0:T(8,128)(2,...) custom-call(s32[8]{0:T(128)} %lengths.3, ...), custom_call_target="tpu_custom_call" | custom-call | bytes 450000000 | tf_op jit(solution)/shard_map/pallas_call | solution.py:1792
  349.5 117.8 %shard_map.283 = (f32[128,2048]{1,0:T(8,128)}, f32[24,2048]{1,0:T(8,128)}, bf16[4,128,2048]{2,1,0:T(8,128)(2,1)}, bf16[3,2,256,256]{3,2,1,0:T(8,128)(2,1)}, bf16...) custom-call(bf16[4,2,4,128,2176]{4,3,2,1,0:T(8,128)(2,1)} %get-tuple, ...), custom_call_target="tpu_custom_call" | custom-call | bytes 350000000 | tf_op jit(solution)/shard_map/pallas_call | solution.py:1986
  467.4 1.5 collective-permute-start
  468.9 0.0 collective-permute-start.1
  468.9 76.6 %shard_map.284 = (f32[128,2048]{1,0:T(8,128)}, f32[256,512]{1,0:T(8,128)}, f32[256,512]{1,0:T(8,128)}, f32[256,512]{1,0:T(8,128)}, f32[512,256]{1,0:T(8,128)}, /...) custom-call(bf16[512,2048]{1,0:T(8,128)(2,1)} %bitcast.6, ...), custom_call_target="tpu_custom_call" | custom-call | bytes 1000000 | tf_op jit(solution)/shard_map/pallas_call | solution.py:2371
  545.6 0.0 collective-permute-done.refs_6_
  545.6 0.0 copy-start
  545.6 0.0 collective-permute-done.1.refs_7_
  545.6 0.0 copy-start.1
  545.6 0.9 copy-done
  546.5 0.2 copy-done.1
  546.7 10.9 %shard_map.285 = (f32[16,256,256]{2,1,0:T(8,128)}, f32[16,256,256]{2,1,0:T(8,128)}, f32[16,256,256]{2,1,0:T(8,128)}, f32[128,2048]{1,0:T(8,128)}, f32[256,512]{1...) custom-call(bf16[3,2,256,256]{3,2,1,0:T(8,128)(2,1)} %get-tuple-elem, ...), custom_call_target="tpu_custom_call" | custom-call | bytes 20000000 | tf_op jit(solution)/shard_map/pallas_call | solution.py:2458
  557.7 1.4 copy.32
Async XLA Ops:
  467.4 78.2 %collective-permute-start = (bf16[3,2,256,256]{3,2,1,0:T(8,128)(2,1)}, bf16[3,2,256,256]{3,2,1,0:T(8,128)(2,1)S(1)}, u32[]{:S(2)}, u32[]{:S(2)}) collective-permute-start(bf16[3,2,256,256]{3,2,1,0:T(8,128)(2,1)} %get-tuple-element.90), channel_id=1, source_target_pairs={{0,24},{4,28},{8,16},{12,20},{16,8},{20,12},{24,0},{28,4},{1,25},{... | collective-permute-start | bytes 2359304 | tf_op jit(solution)/shard_map/ppermute | solution.py:2490
  468.9 76.7 %collective-permute-start.1 = (bf16[3,2,256,256]{3,2,1,0:T(8,128)(2,1)}, bf16[3,2,256,256]{3,2,1,0:T(8,128)(2,1)S(1)}, u32[]{:S(2)}, u32[]{:S(2)}) collective-permute-start(bf16[3,2,256,256]{3,2,1,0:T(8,128)(2,1)} %get-tuple-element.91), channel_id=1, source_target_pairs={{0,28},{4,24},{8,20},{12,16},{16,12},{20,8},{24,4},{28,0},{1,29},{... | collective-permute-start | bytes 2359304 | tf_op jit(solution)/shard_map/ppermute | solution.py:2490
  545.6 0.9 copy-start
  545.6 1.1 copy-start.1

commit v7 on v6

--- a/solution.py
+++ b/solution.py
@@ -1340,7 +1340,7 @@
         part = pl.ds(start, 64)
         value = hid_all[part].astype(F32)
         unit = value * lax.rsqrt(jnp.mean(value * value, axis=-1, keepdims=True) + EPSILON)
-        normed[part] = (unit * attn_gain[...].astype(F32)).astype(BF)
+        normed[part] = (unit * attn_gain[0:1]).astype(BF)
 
     rows_loop(seq_len, 64, normalize)
     for bits in (1, 3, 5, 7):
@@ -1434,7 +1434,7 @@
         )
         middle[part] = value
         unit = value * lax.rsqrt(jnp.mean(value * value, axis=-1, keepdims=True) + EPSILON)
-        packet[part, 0:width] = (unit * ffn_gain[...].astype(F32)).astype(BF)
+        packet[part, 0:width] = (unit * ffn_gain[1:2]).astype(BF)
 
     rows_loop(rows, 16, body)
     logits = dot_transposed(packet[:, 0:width], router_rows[...])
@@ -1947,7 +1947,7 @@
         unit = value * inverse
         product = grad * unit
         gain_part[...] += product[0:8] + product[8:16]
-        gain_row = gain[...].astype(F32)
+        gain_row = gain[1:2]
         ffn_own[part] = (unit * gain_row).astype(BF)
         scaled = grad * gain_row
         result = grad_output[part] + inverse * (
@@ -2176,7 +2176,7 @@
         inverse = lax.rsqrt(jnp.mean(value * value, axis=-1, keepdims=True) + EPSILON)
         unit = value * inverse
         gain_part[...] += jnp.sum((grad * unit).reshape(rows // 8, 8, width), axis=0)
-        change = grad * gain[...].astype(F32)
+        change = grad * gain[0:1]
         work[order[k]] = (
             inverse * (change - unit * jnp.mean(change * unit, axis=-1, keepdims=True))
         ).astype(BF)
@@ -2220,9 +2220,9 @@
             )
 
     q_core_send(3)
-    q_core_send(1)
     input_block(0)
     line.step(0)
+    q_core_send(1)
     q_core_send(2)
     q_core_send(0)
     for i in turns:
@@ -2260,6 +2260,8 @@
         if row_number < 2:
             to, origin, part, b_row = routes_b[row_number]
             forward("b", to, origin, part, b_row)
+        if row_number == 1:
+            line.step(2)
     result = small_send[t // 2]
     for k, peer in enumerate(peers):
         wire.arrive(small_slots[k], lambda k=k: small_in.at[k], peer)
@@ -2277,7 +2279,6 @@
             lambda bits=bits: small_last.at[bits],
             (flip(d, bits), t),
         )
-    line.step(2)
     for device, source, which, row_number in routes_b:
         for name, kept, unused, first, second in tables:
             came = second.at[row_number]
@@ -2312,8 +2313,7 @@
         )
         total = total + small_last[bits]
     share = pltpu.roll(total, (128 - 64 * (t % 2)) % 128, 1)
-    square = jnp.concatenate([share, jnp.zeros((128 - share.shape[0], 128), F32)], axis=0).T
-    router_out[...] = square[0 : router_out.shape[0], 0:16]
+    router_out[...] = share[0:16, 0 : router_out.shape[1]]
     vectors_out[...] = share[16:24]
     head_width = q_gain_out.shape[1]
     gains = pltpu.roll(total, (128 - head_width * d) % 128, 1)
@@ -2376,7 +2376,7 @@
             shape((depth, columns), F32),
             shape((depth, columns), F32),
             shape((columns, o_width), F32),
-            shape((width // (8 * extent), 16), F32),
+            shape((16, width // (8 * extent)), F32),
             shape((8, 128), F32),
             shape((heads, HD // 8), F32),
             shape((heads, HD // 8), F32),
@@ -2453,7 +2453,7 @@
     table = jax.ShapeDtypeStruct((16,) + pieces[0].shape[2:], F32)
     vectors, q_gain, k_gain, loss, router = small
     shape = jax.ShapeDtypeStruct
-    split = router.shape[0]
+    split = router.shape[1]
     same = lambda array: shape(array.shape, array.dtype)
     return pl.pallas_call(
         spread_kernel,
@@ -2511,6 +2511,7 @@
     extent = lax.axis_size("tensor")
     rows, width = hidden_in.shape
     seq_len = rows * extent
+    norm_gains = jnp.stack([attn_norm_gain, ffn_norm_gain]).astype(F32)
     angles = np.arange(seq_len)[:, None] * THETA ** (-np.arange(HD // 2) / (HD // 2))[None, :]
     cosine = jnp.asarray(np.concatenate([np.cos(angles)] * 2, axis=1), F32)
     sine = jnp.asarray(np.concatenate([-np.sin(angles), np.sin(angles)], axis=1), F32)
@@ -2545,10 +2546,10 @@
         gate_weight,
         up_weight,
         down_weight,
-        attn_norm_gain[None, :],
+        norm_gains,
         cosine,
         sine,
-        ffn_norm_gain[None, :],
+        norm_gains,
         router_weight.T,
         routes.T,
     )
@@ -2572,7 +2573,7 @@
         grad_output,
         gates,
         chosen,
-        ffn_norm_gain[None, :],
+        norm_gains,
         router_weight.T,
         (tokens, grads, inner, active),
     )
@@ -2593,7 +2594,7 @@
         attn_grad_rows.reshape(seq_len, width),
         row_loss,
         hidden_bf,
-        attn_norm_gain[None, :],
+        norm_gains,
         qkv_full,
         o_full,
         head_gain,
@@ -2639,7 +2640,7 @@
         grad_q_gain,
         grad_k_gain,
         grad_o,
-        grad_router,
+        grad_router.T,
         grad_gate,
         grad_up,
         grad_down,

time: 568 us -> 564 us (level)
  transfers between devices with their start and end apart: 2 -> 2, of which waited for: 0 -> 0; matrix products, arithmetic and copies ran while one was open for 0% -> 0% of each run, Pallas kernels for 14% -> 13%
where the time goes in v7:
time: 564 us; the launch traced here: 555 us
  Pallas kernels  549 us (97%)
    pallas_call x1, Pallas kernels, front(): pl.pallas_call(functools.partial(front_kernel, extent), out_shape=[shape(...  187 us
    pallas_call x1, Pallas kernels, turn(): pl.pallas_call(functools.partial(turn_kernel, extent), out_shape=[jax.Sha...  160 us
    pallas_call x1, Pallas kernels, leave(): pl.pallas_call(functools.partial(leave_kernel, extent), out_shape=[jax.Sh...  118 us
    pallas_call x1, Pallas kernels, back(): pl.pallas_call(functools.partial(back_kernel, extent), out_shape=[shape((...  73.5 us
  transfers between devices with their start and end apart: 2, of which 0 were waited for; matrix products, arithmetic and copies ran while one was open for 0% of the time, Pallas kernels for 13%

profile of v7, /device:TPU:0, one launch (start us, length us, event | category | flops | bytes accessed | tf_op | source)
XLA Modules:
  0.0 554.6 jit_solution(1552915771517140567)
XLA Ops:
  0.6 0.7 stack.9
  1.3 0.7 stack.10
  2.0 0.6 maximum_convert_fusion.attn_gain.ffn_gain.gain
  2.7 186.8 %shard_map.281 = (f32[128,128]{1,0:T(8,128)}, f32[128,2048]{1,0:T(8,128)}, f32[128,128]{1,0:T(8,128)}, f32[8,128]{1,0:T(8,128)}, f32[512,128]{1,0:T(8,128)}, /*i...) custom-call(s32[8]{0:T(128)} %lengths.3, ...), custom_call_target="tpu_custom_call" | custom-call | bytes 300000000 | tf_op jit(solution)/shard_map/pallas_call | solution.py:1553
  189.4 159.5 %shard_map.282 = (f32[128,2048]{1,0:T(8,128)}, f32[128,128]{1,0:T(8,128)}, bf16[4,2,4,128,2176]{4,3,2,1,0:T(8,128)(2,1)}, bf16[4,2,512,1024]{3,2,1,0:T(8,128)(2,...) custom-call(s32[8]{0:T(128)} %lengths.3, ...), custom_call_target="tpu_custom_call" | custom-call | bytes 450000000 | tf_op jit(solution)/shard_map/pallas_call | solution.py:1792
  348.9 118.1 %shard_map.283 = (f32[128,2048]{1,0:T(8,128)}, f32[24,2048]{1,0:T(8,128)}, bf16[4,128,2048]{2,1,0:T(8,128)(2,1)}, bf16[3,2,256,256]{3,2,1,0:T(8,128)(2,1)}, bf16...) custom-call(bf16[4,2,4,128,2176]{4,3,2,1,0:T(8,128)(2,1)} %get-tuple, ...), custom_call_target="tpu_custom_call" | custom-call | bytes 350000000 | tf_op jit(solution)/shard_map/pallas_call | solution.py:1986
  467.0 1.5 collective-permute-start
  468.6 0.0 collective-permute-start.1
  468.6 73.5 %shard_map.284 = (f32[128,2048]{1,0:T(8,128)}, f32[256,512]{1,0:T(8,128)}, f32[256,512]{1,0:T(8,128)}, f32[256,512]{1,0:T(8,128)}, f32[512,256]{1,0:T(8,128)}, /...) custom-call(bf16[512,2048]{1,0:T(8,128)(2,1)} %bitcast.7, ...), custom_call_target="tpu_custom_call" | custom-call | bytes 1000000 | tf_op jit(solution)/shard_map/pallas_call | solution.py:2371
  542.1 0.0 collective-permute-done.refs_6_
  542.1 0.0 copy-start
  542.2 0.0 collective-permute-done.1.refs_7_
  542.2 0.0 copy-start.1
  542.2 0.9 copy-done
  543.1 0.2 copy-done.1
  543.3 10.9 %shard_map.285 = (f32[16,256,256]{2,1,0:T(8,128)}, f32[16,256,256]{2,1,0:T(8,128)}, f32[16,256,256]{2,1,0:T(8,128)}, f32[128,2048]{1,0:T(8,128)}, f32[256,512]{1...) custom-call(bf16[3,2,256,256]{3,2,1,0:T(8,128)(2,1)} %get-tuple-elem, ...), custom_call_target="tpu_custom_call" | custom-call | bytes 20000000 | tf_op jit(solution)/shard_map/pallas_call | solution.py:2458
Async XLA Ops:
  467.0 75.1 %collective-permute-start = (bf16[3,2,256,256]{3,2,1,0:T(8,128)(2,1)}, bf16[3,2,256,256]{3,2,1,0:T(8,128)(2,1)S(1)}, u32[]{:S(2)}, u32[]{:S(2)}) collective-permute-start(bf16[3,2,256,256]{3,2,1,0:T(8,128)(2,1)} %get-tuple-element.90), channel_id=1, source_target_pairs={{0,24},{4,28},{8,16},{12,20},{16,8},{20,12},{24,0},{28,4},{1,25},{... | collective-permute-start | bytes 2359304 | tf_op jit(solution)/shard_map/ppermute | solution.py:2490
  468.6 73.6 %collective-permute-start.1 = (bf16[3,2,256,256]{3,2,1,0:T(8,128)(2,1)}, bf16[3,2,256,256]{3,2,1,0:T(8,128)(2,1)S(1)}, u32[]{:S(2)}, u32[]{:S(2)}) collective-permute-start(bf16[3,2,256,256]{3,2,1,0:T(8,128)(2,1)} %get-tuple-element.91), channel_id=1, source_target_pairs={{0,28},{4,24},{8,20},{12,16},{16,12},{20,8},{24,4},{28,0},{1,29},{... | collective-permute-start | bytes 2359304 | tf_op jit(solution)/shard_map/ppermute | solution.py:2490
  542.1 0.9 copy-start
  542.2 1.1 copy-start.1
